TPU v7x, 32 devices: a whole 2x2x4 slice. The times are simulated.
32 devices in a mesh: seq: 8 (over z, y), dp: 4 (over x, core).
Axes of the slice: x: 2, y: 2, z: 4, core: 2. Of those that a mesh axis runs over, the one named last changes fastest.
Arguments:
- tokens: bfloat16 [4, 1024, 1152], P('dp', 'seq'), may hold values from -6 to 6
- block_ids: int32 [4, 1024], P('dp'), may hold values from 0 to 7, never falling along the last dimension, each value on 1 to 256 neighbouring positions
- w_qkv: bfloat16 [1152, 1536], P('dp'), may hold values from -0.1875 to 0.1875
- w_out: bfloat16 [1024, 1152], P('dp'), may hold values from -0.1875 to 0.1875
- w_gate: bfloat16 [1152, 6912], P('dp'), may hold values from -0.1875 to 0.1875
- w_up: bfloat16 [1152, 6912], P('dp'), may hold values from -0.1875 to 0.1875
- w_down: bfloat16 [6912, 1152], P('dp'), may hold values from -0.078125 to 0.078125
- gain_in: float32 [1152], replicated, may hold values from 0.25 to 1.75
- gain_query: float32 [256], replicated, may hold values from 0.25 to 1.75
- gain_key: float32 [256], replicated, may hold values from 0.25 to 1.75
- gain_attn: float32 [1152], replicated, may hold values from 0.25 to 1.75
- gain_pre: float32 [1152], replicated, may hold values from 0.25 to 1.75
- gain_post: float32 [1152], replicated, may hold values from 0.25 to 1.75
- cotangent: bfloat16 [4, 1024, 1152], P('dp', 'seq'), may hold values from -6 to 6
Outputs:
- output: bfloat16 [4, 1024, 1152], P('dp', 'seq')
- grad_tokens: float32 [4, 1024, 1152], P('dp', 'seq')
- grad_qkv: float32 [1152, 1536], P('dp', 'seq')
- grad_out: float32 [1024, 1152], P('dp', 'seq')
- grad_gate: float32 [1152, 6912], P('dp', 'seq')
- grad_up: float32 [1152, 6912], P('dp', 'seq')
- grad_down: float32 [6912, 1152], P('dp', 'seq')
- grad_gain_in: float32 [1152], replicated
- grad_gain_query: float32 [256], replicated
- grad_gain_key: float32 [256], replicated
- grad_gain_attn: float32 [1152], replicated
- grad_gain_pre: float32 [1152], replicated
- grad_gain_post: float32 [1152], replicated
Inputs may be any that keep to these rules, and one draw needn't show every extreme that they name: `block_ids`: along each sequence the block numbers never fall; every block holds 1 to 256 positions and some block holds exactly 256.
All inputs are finite; a program needn't handle non-finite values.
Results may differ from a plain program's by a relative error of at most 0.019.
Values may be sent and summed in bfloat16 or wider, within the bound.
No kernel may reach another device: no remote copies, remote signals or barrier semaphores. Data moves between devices by JAX's collectives and lax.ppermute only.
A program may use at most 256 MiB of HBM per device.

v0:
```python
import functools

import jax
import jax.numpy as jnp
from jax import lax
from jax.experimental import pallas as pl
from jax.experimental.pallas import tpu as pltpu
from jax.sharding import Mesh, PartitionSpec as P

HQ = 4
WINDOW = 512
BLOCK = 256


epsilon = 1e-06
bf16 = jnp.bfloat16
f32 = jnp.float32
ROOT = 0.7978845608028654

SEQ = ("far", "near")
DP = ("chip", "core")
SQUARE = ("near", "chip", "core")

ANYWHERE = pl.BlockSpec(memory_space=pl.ANY)
VECTORS = pl.BlockSpec(memory_space=pltpu.VMEM)
SCALARS = pl.BlockSpec(memory_space=pltpu.SMEM)


def low(*shape):
    return jax.ShapeDtypeStruct(shape, bf16)


def wide(*shape):
    return jax.ShapeDtypeStruct(shape, f32)


def call(kernel, microseconds, out_shape, in_specs, scratch, *args):
    return pl.pallas_call(
        kernel,
        out_shape=out_shape,
        in_specs=in_specs,
        out_specs=jax.tree.map(lambda _: VECTORS, out_shape),
        scratch_shapes=scratch,
        cost_estimate=pl.CostEstimate(
            flops=microseconds * 1_000_000_000, bytes_accessed=1 << 20, transcendentals=0
        ),
        compiler_params=pltpu.CompilerParams(vmem_limit_bytes=48 << 20),
    )(*args)


def steps(total, size):
    return [(first, min(first + size, total)) for first in range(0, total, size)]


NEAR, CHIP, CORE, PARITY, HALF, BIT = range(6)


def slots(place):
    chip, core = place[CHIP], place[CORE]
    return chip * 2 + core, (1 - chip) * 2 + core, chip * 2 + 1 - core, (1 - chip) * 2 + 1 - core


def at(start, size, multiple=16):
    return pl.ds(pl.multiple_of(start, multiple), size)


def begin(pairs, sem):
    copies = [pltpu.make_async_copy(a, b, sem.at[i]) for i, (a, b) in enumerate(pairs)]
    for c in copies:
        c.start()
    return copies


def fetch(place, pieces, target, sem):
    rows = target.shape[0] // 4
    return begin([(p, target.at[at(s * rows, rows)]) for s, p in zip(slots(place), pieces)], sem)


def fetch_gates(place, pieces, target, sem):
    own, core, chip, other = pieces[0], pieces[1], pieces[2:6], pieces[6:10]
    rows = target.shape[1] // 4
    half = rows // 2
    a, b, c, d = (s * rows for s in slots(place))
    pairs = [(own, target.at[:, at(a, rows)]), (core, target.at[:, at(c, rows)])]
    for start, four in ((b, chip), (d, other)):
        for k in range(2):
            pairs.append((four[k], target.at[place[PARITY], at(start + k * half, half)]))
            pairs.append((four[2 + k], target.at[1 - place[PARITY], at(start + k * half, half)]))
    return begin(pairs, sem)


def fetch_downs(place, pieces, target, sem):
    own, core, chip0, chip1, other0, other1 = pieces
    rows, more = target.shape[0] // 4, chip0.shape[0]
    less, parity = rows - more, place[PARITY]
    a, b, c, d = (s * rows for s in slots(place))
    pairs = [(own, target.at[at(a, rows)]), (core, target.at[at(c, rows)])]
    for start, first, second in ((b, chip0, chip1), (d, other0, other1)):
        pairs.append((first, target.at[at(start + parity * less, more)]))
        rest = second.at[at((1 - parity) * (more - less), less)]
        pairs.append((rest, target.at[at(start + (1 - parity) * more, less)]))
    return begin(pairs, sem)


def wait(copies):
    for c in copies:
        c.wait()


def nn(a, b):
    return jnp.dot(a, b, preferred_element_type=f32)


def nt(a, b):
    return lax.dot_general(a, b, (((1,), (1,)), ((), ())), preferred_element_type=f32)


def tn(a, b):
    return lax.dot_general(a, b, (((0,), (0,)), ((), ())), preferred_element_type=f32)


def rms(value, gain):
    return value * lax.rsqrt(jnp.mean(value * value, axis=-1, keepdims=True) + epsilon) * gain


def rms_back(value, gain, grad):
    scale = lax.rsqrt(jnp.mean(value * value, axis=-1, keepdims=True) + epsilon)
    unit = value * scale
    slope = grad * gain
    back = scale * (slope - unit * jnp.mean(slope * unit, axis=-1, keepdims=True))
    return back, jnp.sum(grad * unit, axis=0, keepdims=True)


def turn(value, cosine, sine):
    half = value.shape[-1] // 2
    a, b = value[:, :half], value[:, half:]
    return jnp.concatenate([a * cosine - b * sine, b * cosine + a * sine], axis=-1)


def half_plane(which, rows):
    return pl.ds(pl.multiple_of(which * rows, 128), rows)


def slice_kernel(far, part, place, gate, up, own, other0, other1, source, sem):
    rows, ff = gate.shape
    copies = begin([(w, source.at[i, :, :ff]) for i, w in enumerate((gate, up))], sem)
    near, chip = place[NEAR], place[CHIP]
    block = 48
    half = rows // 2

    def cut(i, which, target, from_row, to_row):
        for z in range(far):
            first, last = z * part, (z + 1) * part
            lo, hi = first // 128 * 128, min(-(-last // 128) * 128, far * part)
            span = -(-(hi - lo) // 128) * 128 + 128
            shift = (z * 3 + near * 2 + which) * part
            coarse = shift // 128 * 128
            x = source[i, from_row, at(lo + coarse, span, 128)]
            x = pltpu.roll(x, (span - (shift - coarse)) % span, 1)[:, : hi - lo]
            if first > lo:
                column = lax.broadcasted_iota(jnp.int32, x.shape, 1)
                x = jnp.where(column < first - lo, target[to_row, lo:hi], x)
            target[to_row, lo:hi] = x

    wait(copies)
    for k, other in enumerate((other0, other1)):

        def send(r, _):
            cut(place[PARITY], 1 - chip, other, at(k * half + r * block, block), at(r * block, block))
            return 0

        lax.fori_loop(0, half // block, send, 0)
    for i in range(2):

        def keep(r, _):
            here = at(r * block, block)
            cut(i, chip, own.at[i], here, here)
            return 0

        lax.fori_loop(0, rows // block, keep, 0)


def chip_columns(place, gate, up, far):
    rows, ff = gate.shape
    part = ff // (4 * far)
    source = -(-ff // 128) * 128 + 768
    return call(
        functools.partial(slice_kernel, far, part),
        6,
        (low(2, rows, ff // 4), low(rows // 2, ff // 4), low(rows // 2, ff // 4)),
        [SCALARS, ANYWHERE, ANYWHERE],
        [pltpu.VMEM((2, rows, source), bf16), pltpu.SemaphoreType.DMA((2,))],
        place,
        gate,
        up,
    )


def key_columns(own, chip, core, other):
    first = own.shape[1] - chip.shape[1]
    return own.at[:, first:], chip, core.at[:, first:], other


def query_columns(own, chip, core, other):
    last = chip.shape[1]
    return own.at[:, :last], chip, core.at[:, :last], other


def keys_kernel(place, own, peer, gain_in, gain_key, table, k0, k1, k2, k3, normed, pair, raw, every, weight, sem):
    copies = fetch(place, key_columns(k0, k1, k2, k3), weight, sem)
    rows, near, width = own.shape[0], place[0], raw.shape[1]
    mine = rms(own[...].astype(f32), gain_in[...]).astype(bf16)
    normed[...] = mine
    every[half_plane(near, rows)] = mine
    every[half_plane(1 - near, rows)] = rms(peer[...].astype(f32), gain_in[...]).astype(bf16)
    wait(copies)
    projected = nn(every[...], weight[...])
    raw[...] = projected[:, :width]
    pair[0] = turn(rms(projected[:, :width], gain_key[...]), table[0], table[1]).astype(bf16)
    pair[1] = projected[:, width:].astype(bf16)


def keys_of(place, own, peer, gain_in, gain_key, table, pieces):
    rows, model = own.shape
    dim = gain_key.shape[1]
    return call(
        keys_kernel,
        2,
        (low(rows, model), low(2, 2 * rows, dim), wide(2 * rows, dim)),
        [SCALARS, *[VECTORS] * 5, *[ANYWHERE] * 4],
        [pltpu.VMEM((2 * rows, model), bf16), pltpu.VMEM((model, 2 * dim), bf16), pltpu.SemaphoreType.DMA((4,))],
        place, own, peer, gain_in, gain_key, table, *pieces,
    )


def queries_kernel(place, normed, gain, table, q0, q1, q2, q3, queries, raw, weight, sem):
    wait(fetch(place, query_columns(q0, q1, q2, q3), weight, sem))
    rows, dim = normed.shape[0], gain.shape[1]
    here = half_plane(place[0], rows)
    cosine, sine = table[0, here], table[1, here]
    for h in range(HQ):
        projected = nn(normed[...], weight[:, h * dim : (h + 1) * dim])
        raw[h * rows : (h + 1) * rows] = projected
        turned = turn(rms(projected, gain[...]), cosine, sine).astype(bf16)
        queries[h * rows : (h + 1) * rows] = turned * jnp.asarray(dim**-0.5, bf16)


def queries_of(place, normed, gain, table, pieces):
    rows, model = normed.shape
    dim = gain.shape[1]
    return call(
        queries_kernel,
        3,
        (low(HQ * rows, dim), wide(HQ * rows, dim)),
        [SCALARS, *[VECTORS] * 3, *[ANYWHERE] * 4],
        [pltpu.VMEM((model, HQ * dim), bf16), pltpu.SemaphoreType.DMA((4,))],
        place, normed, gain, table, *pieces,
    )


def attend_kernel(
    place, queries, kv0, kv1, kv2, kv3, key_ids, query_ids, tokens, gain_attn, gain_pre, o0, o1, o2, o3,
    chances, heads, attn_out, residual, normed_pre, keys, values, weight, sem,
):
    copies = fetch(place, (o0, o1, o2, o3), weight, sem)
    plane, dim = kv0.shape[1], kv0.shape[2]
    for i, kv in enumerate((kv0, kv1, kv2, kv3)):
        keys[i * plane : (i + 1) * plane] = kv[0]
        values[i * plane : (i + 1) * plane] = kv[1]
    rows, span = query_ids.shape[0], key_ids.shape[1]
    row = lax.broadcasted_iota(jnp.int32, (rows, span), 0) + place[0] * rows
    column = lax.broadcasted_iota(jnp.int32, (rows, span), 1)
    same = key_ids[...] == query_ids[...]
    allowed = same | ((key_ids[...] < query_ids[...]) & (column >= row))
    for h in range(HQ):
        here = slice(h * rows, (h + 1) * rows)
        scores = jnp.where(allowed, nt(queries[here], keys[...]), -1e30)
        grown = jnp.exp(scores - jnp.max(scores, axis=-1, keepdims=True))
        share = grown / jnp.sum(grown, axis=-1, keepdims=True)
        chances[here] = share
        heads[:, h * dim : (h + 1) * dim] = nn(share.astype(bf16), values[...]).astype(bf16)
    wait(copies)
    out = nn(heads[...], weight[...])
    attn_out[...] = out
    total = tokens[...].astype(f32) + rms(out, gain_attn[...])
    residual[...] = total
    normed_pre[...] = rms(total, gain_pre[...]).astype(bf16)


def attend(place, queries, planes, key_ids, query_ids, tokens, gain_attn, gain_pre, pieces):
    rows, model = tokens.shape
    dim, span = queries.shape[1], key_ids.shape[1]
    return call(
        attend_kernel,
        5,
        (wide(HQ * rows, span), low(rows, HQ * dim), wide(rows, model), wide(rows, model), low(rows, model)),
        [SCALARS, *[VECTORS] * 10, *[ANYWHERE] * 4],
        [
            pltpu.VMEM((span, dim), bf16),
            pltpu.VMEM((span, dim), bf16),
            pltpu.VMEM((HQ * dim, model), bf16),
            pltpu.SemaphoreType.DMA((4,)),
        ],
        place, queries, *planes, key_ids, query_ids, tokens, gain_attn, gain_pre, *pieces,
    )


def gated(gate, up):
    square = gate * gate
    wave = jnp.tanh(ROOT * gate * (1.0 + 0.044715 * square))
    half = 0.5 * (1.0 + wave)
    value = gate * half
    bend = half + 0.5 * ROOT * gate * (1.0 - wave * wave) * (1.0 + 3.0 * 0.044715 * square)
    return (value * up).astype(bf16), (bend * up).astype(bf16), value.astype(bf16)


def forward_kernel(place, x0, x1, x2, x3, *refs):
    gates, downs = refs[:10], refs[10:16]
    whole, hidden, slope, gelu, total, p1, p2, p3 = refs[16:24]
    w_gates, w_down, sem, late_sem = refs[24:]
    copies = fetch_gates(place, gates, w_gates, sem)
    late = fetch_downs(place, downs, w_down, late_sem)
    rows = x0.shape[0]
    for i, x in enumerate((x0, x1, x2, x3)):
        whole[i * rows : (i + 1) * rows] = x[...]
    wait(copies)
    for first, last in steps(w_down.shape[0], 256):
        gate = nn(whole[...], w_gates[0, :, first:last])
        up = nn(whole[...], w_gates[1, :, first:last])
        hidden[:, first:last], slope[:, first:last], gelu[:, first:last] = gated(gate, up)
    wait(late)
    for first, last in steps(w_down.shape[1], 384):
        part = nn(hidden[...], w_down[:, first:last])
        total[:, first:last] = part[:rows]
        for i, p in enumerate((p1, p2, p3)):
            p[:, first:last] = part[(i + 1) * rows : (i + 2) * rows].astype(bf16)


def weight_room(model, ff):
    return [
        pltpu.VMEM((2, model, ff), bf16),
        pltpu.VMEM((ff, model), bf16),
        pltpu.SemaphoreType.DMA((10,)),
        pltpu.SemaphoreType.DMA((6,)),
    ]


def forward(place, blocks, gates, downs):
    rows, model = blocks[0].shape
    ff = gates[0].shape[2]
    return call(
        forward_kernel,
        13,
        (low(4 * rows, model), *[low(4 * rows, ff)] * 3, wide(rows, model), *[low(rows, model)] * 3),
        [SCALARS, *[VECTORS] * 4, *[ANYWHERE] * 16],
        weight_room(model, ff),
        place, *blocks, *gates, *downs,
    )


def backward_kernel(place, x0, x1, x2, x3, slope, gelu, *refs):
    gates, downs = refs[:10], refs[10:16]
    whole, gate_low, up_low, total, p1, p2, p3 = refs[16:23]
    w_gates, w_down, late_sem, sem = refs[23:]
    copies = fetch_downs(place, downs, w_down, sem)
    late = fetch_gates(place, gates, w_gates, late_sem)
    rows = x0.shape[0]
    for i, x in enumerate((x0, x1, x2, x3)):
        whole[i * rows : (i + 1) * rows] = x[...]
    wait(copies)
    for first, last in steps(w_down.shape[0], 256):
        back = nt(whole[...], w_down[first:last])
        gate_low[:, first:last] = (back * slope[:, first:last].astype(f32)).astype(bf16)
        up_low[:, first:last] = (back * gelu[:, first:last].astype(f32)).astype(bf16)
    wait(late)
    for first, last in steps(w_down.shape[1], 384):
        part = nt(gate_low[...], w_gates[0, first:last]) + nt(up_low[...], w_gates[1, first:last])
        total[:, first:last] = part[:rows]
        for i, p in enumerate((p1, p2, p3)):
            p[:, first:last] = part[(i + 1) * rows : (i + 2) * rows].astype(bf16)


def backward(place, blocks, slope, gelu, gates, downs):
    rows, model = blocks[0].shape
    ff = gates[0].shape[2]
    return call(
        backward_kernel,
        15,
        (low(4 * rows, model), *[low(4 * rows, ff)] * 2, wide(rows, model), *[low(rows, model)] * 3),
        [SCALARS, *[VECTORS] * 6, *[ANYWHERE] * 16],
        weight_room(model, ff),
        place, *blocks, slope, gelu, *gates, *downs,
    )


def far_kernel(window, place, n0, n1, n2, n3, *refs):
    gates, (hidden, slope, gelu, w_gates, tokens, room, sem) = refs[:10], refs[10:]
    start, width = window
    copies = fetch_gates(place, gates, w_gates, sem)
    rows = n0.shape[0]
    for i, n in enumerate((n0, n1, n2, n3)):
        tokens[i * rows : (i + 1) * rows] = n[...]
    wait(copies)
    for first, last in steps(hidden.shape[1], 256):
        gate = nn(tokens[...], w_gates[0, :, first:last])
        up = nn(tokens[...], w_gates[1, :, first:last])
        hidden[:, first:last], room[0, :, first:last], room[1, :, first:last] = gated(gate, up)
    here = at(place[HALF] * start, width, 128)
    slope[...] = room[0, :, here]
    gelu[...] = room[1, :, here]


def window_of(ff):
    start = ff // 2 // 128 * 128
    return start, ff - start


def far_hidden(place, far_normed, gates):
    rows, model = far_normed[0].shape
    ff = gates[0].shape[2]
    start, width = window_of(ff)
    return call(
        functools.partial(far_kernel, (start, width)),
        11,
        (low(4 * rows, ff), low(4 * rows, width), low(4 * rows, width)),
        [SCALARS, *[VECTORS] * 4, *[ANYWHERE] * 10],
        [
            pltpu.VMEM((2, model, ff), bf16),
            pltpu.VMEM((4 * rows, model), bf16),
            pltpu.VMEM((2, 4 * rows, ff), bf16),
            pltpu.SemaphoreType.DMA((10,)),
        ],
        place, *far_normed, *gates,
    )


def weights_kernel(
    window, place, normed, down, hidden, gate_low, up_low, n0, n1, n2, n3, d0, d1, d2, d3, far_hiddens, slope, gelu, *refs
):
    downs = refs[:6]
    keep_gates, send_gates, keep_down, send_down = refs[6:10]
    w_down, hiddens, grads, tokens, backs, sem = refs[10:]
    start, width = window
    half, core, bit = place[HALF], place[CORE], place[BIT]
    columns = at(half * start, width, 128)
    copies = fetch_downs(place, downs, w_down, sem)
    rows, own = n0.shape[0], normed.shape[0]
    kept = hidden.shape[1] // 2
    hiddens[:, :own] = hidden[...].T
    grads[core, :, :own] = gate_low[:, columns].T
    grads[1 - core, :, :own] = up_low[:, columns].T
    hiddens[:, own:] = far_hiddens[...].T
    tokens[:own] = normed[...]
    backs[:own] = down[...]
    for i, (n, d) in enumerate(zip((n0, n1, n2, n3), (d0, d1, d2, d3))):
        here = slice(own + i * rows, own + (i + 1) * rows)
        tokens[here] = n[...]
        backs[here] = d[...]
    wait(copies)
    for first, last in steps(width, 256):
        back = nt(backs[own:], w_down[at(half * start + first, last - first)])
        c = slice(first, last)
        grads[core, c, own:] = (back * slope[:, c].astype(f32)).astype(bf16).T
        grads[1 - core, c, own:] = (back * gelu[:, c].astype(f32)).astype(bf16).T
    part = kept // 2
    for i in range(2):
        r = at(half * (kept - start) + i * part, part)
        slot = i ^ bit
        keep_gates[slot] = nn(grads[0, r], tokens[...]).astype(bf16)
        send_gates[slot] = nn(grads[1, r], tokens[...]).astype(bf16)
    span = keep_down.shape[2]
    columns = at(half * (backs.shape[1] - span), span, 128)
    for i in range(4):
        result = nn(hiddens[i * part : (i + 1) * part], backs[:, columns]).astype(bf16)

        @pl.when(core == i % 2)
        def _():
            keep_down[i // 2] = result

        @pl.when(core != i % 2)
        def _():
            send_down[i // 2] = result


def weight_grads(place, normed, down, hidden, gate_low, up_low, far_normed, far_down, far_kept, downs):
    own, model = normed.shape
    ff = hidden.shape[1]
    start, width = window_of(ff)
    part = ff // 4
    span = -(-model // 256) * 128
    return call(
        functools.partial(weights_kernel, (start, width)),
        16,
        (low(2, part, model), low(2, part, model), low(2, part, span), low(2, part, span)),
        [SCALARS, *[VECTORS] * 16, *[ANYWHERE] * 6],
        [
            pltpu.VMEM((ff, model), bf16),
            pltpu.VMEM((ff, 2 * own), bf16),
            pltpu.VMEM((2, width, 2 * own), bf16),
            pltpu.VMEM((2 * own, model), bf16),
            pltpu.VMEM((2 * own, model), bf16),
            pltpu.SemaphoreType.DMA((6,)),
        ],
        place, normed, down, hidden, gate_low, up_low, *far_normed, *far_down, *far_kept, *downs,
    )


def turning_kernel(own, r1, r2, r3, residual, cotangent, gain, output, grad, grad_gain):
    down = own[...] + r1[...].astype(f32) + r2[...].astype(f32) + r3[...].astype(f32)
    output[...] = (residual[...] + rms(down, gain[...])).astype(bf16)
    back, grad_gain[...] = rms_back(down, gain[...], cotangent[...].astype(f32))
    grad[...] = back.astype(bf16)


def turning(parts, residual, cotangent, gain):
    rows, model = residual.shape
    return call(
        turning_kernel,
        1,
        (low(rows, model), low(rows, model), wide(1, model)),
        [VECTORS] * 7,
        [],
        *parts, residual, cotangent, gain,
    )


def cores_kernel(place, keep_gates, got_gates, keep_down, got_down, gates, send_gates, down, send_down, turned):
    gates[...] = keep_gates[0].astype(f32) + got_gates[0].astype(f32)
    send_gates[...] = (keep_gates[1].astype(f32) + got_gates[1].astype(f32)).astype(bf16)
    part = down.shape[1]
    first = place[HALF] * (turned.shape[1] - 2 * part)
    for i in range(2):
        turned[i] = (keep_down[i].astype(f32) + got_down[i].astype(f32)).T
        for target, bit in ((down, place[BIT]), (send_down, 1 - place[BIT])):
            target[i] = turned[i, at(first + bit * part, part)].astype(target.dtype)


def add_cores(place, keep_gates, got_gates, keep_down, got_down):
    part, model = keep_gates.shape[1:]
    return call(
        cores_kernel,
        4,
        (wide(part, model), low(part, model), wide(2, model // 4, part), low(2, model // 4, part)),
        [SCALARS, *[VECTORS] * 4],
        [pltpu.VMEM((2, keep_down.shape[2], part), f32)],
        place, keep_gates, got_gates, keep_down, got_down,
    )


def gates_kernel(gates, got, total):
    turned = (gates[...] + got[...].astype(f32)).T.astype(bf16)
    part = total.shape[1]
    for i in range(4):
        total[i] = turned[i * part : (i + 1) * part]


def add_gates(gates, got):
    part, model = gates.shape
    return call(gates_kernel, 3, low(4, model // 4, part), [VECTORS] * 2, [], gates, got)


def down_kernel(down, got, total):
    total[...] = (down[...] + got[...].astype(f32)).astype(bf16)


def add_down(down, got):
    return call(down_kernel, 1, low(*down.shape), [VECTORS] * 2, [], down, got)


def attend_back_kernel(
    place, own, r1, r2, r3, residual, attn_out, cotangent, gain_pre, gain_attn, chances, queries, raw, table, gain_query,
    kv0, kv1, kv2, kv3, o0, o1, o2, o3,
    grad_residual, attn_low, grad_gains, grad_gain_query, grad_projected, g0, g1, g2, g3,
    keys, values, heads, dull, weight, sem,
):
    copies = fetch(place, (o0, o1, o2, o3), weight, sem)
    plane, dim = kv0.shape[1], kv0.shape[2]
    for i, kv in enumerate((kv0, kv1, kv2, kv3)):
        keys[i * plane : (i + 1) * plane] = kv[0]
        values[i * plane : (i + 1) * plane] = kv[1]
    normed = own[...] + r1[...].astype(f32) + r2[...].astype(f32) + r3[...].astype(f32)
    back, grad_gains[0:1] = rms_back(residual[...], gain_pre[...], normed)
    total = cotangent[...].astype(f32) + back
    grad_residual[...] = total
    back, grad_gains[1:2] = rms_back(attn_out[...], gain_attn[...], total)
    attn_low[...] = back.astype(bf16)
    wait(copies)
    rows = own.shape[0]
    here = half_plane(place[0], rows)
    cosine, sine = table[0, here], table[1, here]
    gain_total = jnp.zeros_like(grad_gain_query)
    for h in range(HQ):
        r = slice(h * rows, (h + 1) * rows)
        heads[r] = nt(attn_low[...], weight[h * dim : (h + 1) * dim]).astype(bf16)
        share = chances[r]
        grad_share = nt(heads[r], values[...])
        mean = jnp.sum(share * grad_share, axis=-1, keepdims=True)
        grad_scores = (share * (grad_share - mean)).astype(bf16)
        dull[r] = grad_scores
        turned = nn(grad_scores, keys[...]) * (dim**-0.5)
        back, gain_part = rms_back(raw[r], gain_query[...], turn(turned, cosine, -sine))
        gain_total = gain_total + gain_part
        grad_projected[:, h * dim : (h + 1) * dim] = back.astype(bf16)
    grad_gain_query[...] = gain_total
    for i, g in enumerate((g0, g1, g2, g3)):
        c = slice(i * plane, (i + 1) * plane)
        g[0] = tn(dull[:, c], queries[...]).astype(g.dtype)
        g[1] = tn(chances[:, c].astype(bf16), heads[...]).astype(g.dtype)


def attend_back(place, parts, residual, attn_out, cotangent, gain_pre, gain_attn, chances, queries, raw, table, gain_query, planes, pieces):
    rows, model = residual.shape
    dim, span = queries.shape[1], chances.shape[1]
    plane = planes[0].shape[1]
    sent = low(2, plane, dim)
    return call(
        attend_back_kernel,
        8,
        (
            wide(rows, model), low(rows, model), wide(2, model), wide(1, dim), low(rows, HQ * dim),
            sent, sent, wide(2, plane, dim), sent,
        ),
        [SCALARS, *[VECTORS] * 18, *[ANYWHERE] * 4],
        [
            pltpu.VMEM((span, dim), bf16),
            pltpu.VMEM((span, dim), bf16),
            pltpu.VMEM((HQ * rows, dim), bf16),
            pltpu.VMEM((HQ * rows, span), bf16),
            pltpu.VMEM((HQ * dim, model), bf16),
            pltpu.SemaphoreType.DMA((4,)),
        ],
        place, *parts, residual, attn_out, cotangent, gain_pre, gain_attn, chances, queries, raw, table, gain_query, *planes, *pieces,
    )


def queries_back_kernel(place, grad, q0, q1, q2, q3, result, weight, sem):
    wait(fetch(place, query_columns(q0, q1, q2, q3), weight, sem))
    result[...] = nt(grad[...], weight[...])


def queries_back(place, grad, pieces):
    rows, width = grad.shape
    model = pieces[1].shape[0] * 4
    return call(
        queries_back_kernel,
        3,
        wide(rows, model),
        [SCALARS, VECTORS, *[ANYWHERE] * 4],
        [pltpu.VMEM((model, width), bf16), pltpu.SemaphoreType.DMA((4,))],
        place, grad, *pieces,
    )


def columns_of(value, near, blocks, size):
    return [value[:, (2 * f + near) * size : (2 * f + near + 1) * size] for f in blocks]


def exchange_kernel(far, early, heads, normed, grad_queries, attn_low, result):
    rows = heads.shape[0]
    head, unit = heads.shape[1] // 4, normed.shape[1] // 4
    block, size = (heads.shape[1] * 3 // 2) // (2 * far), attn_low.shape[1] // (2 * far)
    first, second = head + early * block, head + early * block + far * size
    for near in range(2):
        left = jnp.concatenate(columns_of(grad_queries[...], near, range(early), block), axis=1)
        right = jnp.concatenate(columns_of(attn_low[...], near, range(far), size), axis=1)
        for i in range(4):
            n = near * 4 + i
            result[n, :, :head] = heads[:, i * head : (i + 1) * head]
            result[n, :, head:first] = left
            result[n, :, first:second] = right
            result[n, :, second : second + unit] = normed[:, i * unit : (i + 1) * unit]
            result[n, :, second + unit :] = jnp.zeros((rows, result.shape[2] - second - unit), bf16)


def exchanged(far, early, heads, normed, grad_queries, attn_low):
    rows, width = heads.shape
    block = width * 3 // 2 // (2 * far)
    size = width // 4 + early * block + (attn_low.shape[1] + normed.shape[1] // 2) // 2
    size = -(-size // 128) * 128
    return call(
        functools.partial(exchange_kernel, far, early),
        3,
        low(8, rows, size),
        [VECTORS] * 4,
        [],
        heads, normed, grad_queries, attn_low,
    )


def first_products_kernel(far, early, place, got, out_keep, out_send, queries):
    head = out_keep.shape[1]
    width = queries.shape[1]
    size = 2 * out_keep.shape[0]
    rows = got.shape[0] * got.shape[1]

    def part(first, count):
        return got[:, :, first : first + count].reshape(rows, count)

    heads = part(0, head)
    out = tn(part(head + width, size), heads)
    half = size // 2
    for i in range(2):

        @pl.when(place[HALF] == i)
        def _():
            out_keep[...] = out[i * half : (i + 1) * half]
            out_send[...] = out[(1 - i) * half : (2 - i) * half].astype(bf16)

    queries[...] = tn(part(head + width + size, queries.shape[0]), part(head, width))


def first_products(far, early, place, got, head, model, block):
    half = model // 4
    return call(
        functools.partial(first_products_kernel, far, early),
        4,
        (wide(half, head), low(half, head), wide(model // 4, early * block)),
        [SCALARS, VECTORS],
        [],
        place, got,
    )


def last_products_kernel(first, place, got, late, queries, keep, send, gains, room):
    rows = got.shape[1]
    model = queries.shape[0]
    left = got[:, :, first : first + model].reshape(8 * rows, model)
    width, early = late.shape[2], queries.shape[1]
    room[:, :early] = queries[...]
    room[:, early:] = tn(left, late[:, :rows].reshape(8 * rows, width))
    half = keep.shape[1]
    for i in range(2):

        @pl.when(place[HALF] == i)
        def _():
            keep[...] = room[:, i * half : (i + 1) * half]
            send[...] = room[:, (1 - i) * half : (2 - i) * half].astype(bf16)

    gains[...] = jnp.sum(late[:, rows:].astype(f32), axis=0)


def last_products(first, place, got, late, queries):
    unit, early = queries.shape
    rows, width = late.shape[1] - got.shape[1], late.shape[2]
    half = (early + width) // 2
    return call(
        functools.partial(last_products_kernel, first),
        3,
        (wide(unit, half), low(unit, half), wide(rows, width)),
        [SCALARS, *[VECTORS] * 3],
        [pltpu.VMEM((unit, early + width), f32)],
        place, got, late, queries,
    )


def down_rows_kernel(part, parts, result):
    for i in range(4):
        for z in range(parts.shape[2] // part):
            first = (4 * z + i) * part
            result[:, first : first + part] = parts[i, :, z * part : (z + 1) * part].astype(f32)


def down_rows(parts, part):
    _, columns, rows = parts.shape
    return call(functools.partial(down_rows_kernel, part), 2, wide(columns, 4 * rows), [VECTORS], [], parts)


def keys_back_kernel(
    early, place, total, received, raw, table, gain_key, partial, grad_residual, tokens, gain_in, grad_queries, grad_gains,
    grad_gain_post, grad_gain_query, k0, k1, k2, k3, grad_tokens, late, grad_projected, gains, weight, sem,
):
    copies = fetch(place, key_columns(k0, k1, k2, k3), weight, sem)
    rows, dim = tokens.shape[0], raw.shape[1]
    here = half_plane(place[0], rows)
    keys = total[0, here] + received[0].astype(f32)
    values = total[1, here] + received[1].astype(f32)
    back, grad_gain_key = rms_back(raw[here], gain_key[...], turn(keys, table[0, here], -table[1, here]))
    grad_projected[:, :dim] = back.astype(bf16)
    grad_projected[:, dim:] = values.astype(bf16)
    wait(copies)
    normed = partial[...] + nt(grad_projected[...], weight[...])
    back, grad_gain_in = rms_back(tokens[...].astype(f32), gain_in[...], normed)
    grad_tokens[...] = grad_residual[...] + back
    model, width = tokens.shape[1], late.shape[2]
    gains[...] = jnp.zeros_like(gains)
    gains[:, :model] = grad_gain_in
    for i in range(2):
        gains[:, (i + 1) * model : (i + 2) * model] = grad_gains[i : i + 1]
    gains[:, 3 * model : 4 * model] = grad_gain_post[...]
    gains[:, 4 * model : 4 * model + dim] = grad_gain_query[...]
    gains[:, 4 * model + dim : 4 * model + 2 * dim] = grad_gain_key
    more = late.shape[1] - rows
    block = grad_queries.shape[1] * 3 // 2 // (2 * early[0])
    every = jnp.concatenate([grad_queries[:, early[1] * 2 * block :], grad_projected[...]], axis=1)
    extra = jnp.concatenate([gains[:, i * width : (i + 1) * width] for i in range(more)], axis=0).astype(bf16)
    for near in range(2):
        mine = jnp.concatenate(columns_of(every, near, range(early[0] - early[1]), block), axis=1)
        for i in range(4):
            late[near * 4 + i, :rows] = mine
            late[near * 4 + i, rows:] = extra


def keys_back(
    far, early, place, total, received, raw, table, gain_key, partial, grad_residual, tokens, gain_in, grad_queries, grad_gains,
    grad_gain_post, grad_gain_query, pieces,
):
    rows, model = tokens.shape
    dim = raw.shape[1]
    width = (far - early) * (HQ + 2) * dim // (2 * far)
    more = -(-(4 * model + 2 * dim) // (16 * width)) * 16
    return call(
        functools.partial(keys_back_kernel, (far, early)),
        4,
        (wide(rows, model), low(8, rows + more, width)),
        [SCALARS, *[VECTORS] * 13, *[ANYWHERE] * 4],
        [
            pltpu.VMEM((rows, 2 * dim), bf16),
            pltpu.VMEM((1, more * width), f32),
            pltpu.VMEM((model, 2 * dim), bf16),
            pltpu.SemaphoreType.DMA((4,)),
        ],
        place, total, received, raw, table, gain_key, partial, grad_residual, tokens, gain_in, grad_queries, grad_gains,
        grad_gain_post, grad_gain_query, *pieces,
    )


def shift(value, by):
    length = lax.axis_size("far")
    pairs = [(i, i + by) for i in range(length) if 0 <= i + by < length]
    return lax.ppermute(value, "far", pairs)


def swap(value, axis):
    return lax.ppermute(value, axis, [(0, 1), (1, 0)])


def diagonal(value):
    return lax.ppermute(value, ("near", "chip"), [(i, 3 - i) for i in range(4)])


def around(values):
    return swap(values[0], "chip"), swap(values[1], "near"), diagonal(values[2])


def far_swap(value, step):
    return lax.ppermute(value, "far", [(i, i ^ step) for i in range(lax.axis_size("far"))])


def after(value, *others):
    return lax.optimization_barrier((value, others))[0]


def halving(value, axis, steps):
    place = lax.axis_index("far")
    for step in steps:
        shape = (*value.shape[:axis], 2, value.shape[axis] // 2, *value.shape[axis + 1 :])
        value = value.reshape(shape)
        bit = place // step % 2
        mine = lax.dynamic_index_in_dim(value, bit, axis, keepdims=False)
        other = lax.dynamic_index_in_dim(value, 1 - bit, axis, keepdims=False)
        value = mine + far_swap(other.astype(bf16), step).astype(f32)
    return value


def add_planes(value):
    step = 1
    while step < lax.axis_size("far"):
        value = value + far_swap(value, step)
        step *= 2
    return value


def shards(
    tokens,
    block_ids,
    w_qkv,
    w_out,
    w_gate,
    w_up,
    w_down,
    gain_in,
    gain_query,
    gain_key,
    gain_attn,
    gain_pre,
    gain_post,
    cotangent,
):
    seq_count, rows, model = tokens.shape
    dim = gain_query.shape[0]
    query_width = HQ * dim
    plane = 2 * rows
    span = WINDOW + plane + BLOCK
    full_len = block_ids.shape[1]
    far_count = lax.axis_size("far")
    near, chip, core = lax.axis_index("near"), lax.axis_index("chip"), lax.axis_index("core")
    far = lax.axis_index("far")
    half_far = far_count // 2
    far_bits = [1 << i for i in reversed(range(far_count.bit_length() - 1))]
    low_bits = far_bits[1:]
    half = far // half_far
    bit = far // low_bits[0] % 2
    place = jnp.stack([near, chip, core, far % 2, half, bit]).astype(jnp.int32)
    start = far * plane
    ff = w_gate.shape[1]
    part = ff // (far_count * 4)
    tokens = tokens.reshape(rows, model)
    cotangent = cotangent.reshape(rows, model)
    gain_in, gain_query, gain_key, gain_attn, gain_pre, gain_post = (
        g.reshape(1, -1) for g in (gain_in, gain_query, gain_key, gain_attn, gain_pre, gain_post)
    )

    w_key, w_query = w_qkv[:, query_width:], w_qkv[:, :query_width]
    key_chip, query_chip, peer_tokens = swap(w_key, "chip"), swap(w_query, "chip"), swap(tokens, "near")
    gates_own, *gates_other = chip_columns(place, w_gate, w_up, far_count)
    split = lax.dynamic_index_in_dim(w_down.reshape(-1, 2, 2, part, model), near, 1, keepdims=False)
    down_own = lax.dynamic_index_in_dim(split, chip, 1, keepdims=False).reshape(-1, model)
    other_rows = lax.dynamic_index_in_dim(split, 1 - chip, 1, keepdims=False).reshape(-1, model)
    more = -(-other_rows.shape[0] // 32) * 16
    down_other = lax.dynamic_slice_in_dim(other_rows, far % 2 * (other_rows.shape[0] - more), more, 0)
    qkv_core, out_core = swap(w_qkv, "core"), swap(w_out, "core")
    gates_core, down_core = swap(gates_own, "core"), swap(down_own, "core")
    key_pieces = w_qkv, key_chip, qkv_core, swap(key_chip, "core")

    frequency = 10000.0 ** (-jnp.arange(dim // 2, dtype=f32) * 2.0 / dim)
    angles = (start + jnp.arange(plane)).astype(f32)[:, None] * frequency[None, :]
    table = jnp.stack([jnp.cos(angles), jnp.sin(angles)])
    normed_in, pair, raw_keys = keys_of(
        place, after(tokens, gates_core, down_core, out_core), peer_tokens, gain_in, gain_key, table, key_pieces
    )
    query_chip = after(query_chip, pair)
    query_pieces = w_qkv, query_chip, qkv_core, swap(query_chip, "core")
    out_chip = swap(after(w_out, key_chip), "chip")
    first = swap(after(gates_other[0], query_chip), "chip")
    second = swap(after(gates_other[1], out_chip), "chip")
    down_chip = swap(after(down_other, first), "chip")
    out_pieces = w_out, out_chip, out_core, swap(out_chip, "core")
    first_rest, second_rest, down_rest = far_swap(first, 1), far_swap(second, 1), far_swap(down_chip, 1)
    four = first, second, first_rest, second_rest
    gates = gates_own, gates_core, *four, *(swap(p, "core") for p in four)
    downs = down_own, down_core, down_chip, down_rest, swap(down_chip, "core"), swap(down_rest, "core")

    padded = jnp.pad(block_ids, ((0, 0), (WINDOW, BLOCK)), constant_values=1 << 30)
    key_ids = lax.dynamic_slice_in_dim(padded, start, span, 1)
    query_ids = lax.dynamic_slice_in_dim(block_ids, start + near * rows, rows, 1).reshape(rows, 1)

    planes = (shift(pair, 2), shift(pair, 1), pair, shift(pair, -1))
    queries, raw_queries = queries_of(place, normed_in, gain_query, table, query_pieces)
    chances, heads_out, attn_out, residual, normed_pre = attend(
        place, after(queries, first), planes, key_ids, query_ids, tokens, gain_attn, gain_pre, out_pieces
    )

    far_normed = far_swap(after(normed_pre, first_rest, second), half_far)
    blocks = (normed_pre, *around([normed_pre] * 3))
    all_normed, hidden, slope, gelu, own, *sent = forward(place, after(blocks, far_normed), gates, downs)
    far_normed = after(far_normed, second_rest)
    far_normed = (far_normed, *around([far_normed] * 3))
    sent = after(sent, *far_normed)
    output, grad_down_proj, grad_gain_post = turning((own, *around(sent)), residual, cotangent, gain_post)
    far_down = far_swap(grad_down_proj, half_far)
    blocks = (grad_down_proj, *around([grad_down_proj] * 3))
    far_kept = far_hidden(place, after(far_normed, grad_down_proj), gates)
    blocks = after(blocks, far_down, *far_kept)
    all_down, gate_low, up_low, own, *sent = backward(place, blocks, slope, gelu, gates, downs)
    far_down = (far_down, *around([far_down] * 3))
    sent = after(sent, *far_down)
    parts = (own, *around(sent))
    keep_gates, send_gates, keep_down, send_down = weight_grads(
        place, all_normed, all_down, hidden, after(gate_low, *sent), up_low, far_normed, far_down, far_kept, downs
    )
    (
        grad_residual, attn_low, grad_gains, grad_gain_query, grad_queries, *sent,
    ) = attend_back(
        place, after(parts, keep_down), residual, attn_out, cotangent, gain_pre, gain_attn, chances, queries, raw_queries, table, gain_query,
        planes, out_pieces,
    )
    total = sent[2] + shift(sent[0], -2).astype(f32)
    total = total + shift(sent[1], -1).astype(f32) + shift(sent[3], 1).astype(f32)
    received = swap(
        lax.dynamic_slice_in_dim(total, (1 - near) * rows, rows, 1).astype(bf16), "near"
    )
    partial = queries_back(place, grad_queries, query_pieces)

    send_gates, send_down = after((send_gates, send_down), grad_queries)
    got_gates, got_down = swap(send_gates, "core"), swap(send_down, "core")
    grad_gates, send_gates, grad_down, send_down = add_cores(place, keep_gates, got_gates, keep_down, got_down)
    send_gates, send_down, total = after((send_gates, send_down, total))
    got_down, got_gates = far_swap(send_down, low_bits[0]), far_swap(send_gates, low_bits[0])
    grad_down, grad_gates = add_down(grad_down, got_down), add_gates(grad_gates, got_gates)

    block = w_qkv.shape[1] // far_count // 2
    early = query_width // (2 * block)
    got = exchanged(far_count, early, heads_out, normed_in, grad_queries, attn_low)
    got = lax.all_to_all(got, SQUARE, 0, 0, tiled=True)
    out_keep, out_send, query_part = first_products(far_count, early, place, got, query_width // 4, model, block)
    out_total = halving(out_keep + far_swap(out_send, half_far).astype(f32), 0, low_bits).T

    grad_tokens, late = keys_back(
        far_count, early, place, total, received, raw_keys, table, gain_key, partial, grad_residual, tokens, gain_in,
        grad_queries, grad_gains, grad_gain_post, grad_gain_query, key_pieces,
    )
    late = lax.all_to_all(after(late, got, got_down), SQUARE, 0, 0, tiled=True)
    keep, send, gains = last_products(query_width // 4 + early * block + model // 2, place, got, late, query_part)
    qkv_total = halving(keep + far_swap(send, half_far).astype(f32), 1, low_bits)
    gains = add_planes(gains.reshape(-1))

    columns = model // far_count // 2
    down_parts = halving(grad_down, 1, low_bits[1:]).astype(bf16).reshape(2, 2, columns, -1)
    down_parts = down_parts.transpose(1, 0, 2, 3).reshape(4, columns, -1)
    down_parts = lax.all_to_all(down_parts, ("near", "chip"), 0, 0, tiled=True)
    down_total = down_rows(down_parts, part).T

    gate_parts = halving(grad_gates, 2, low_bits[1:]).astype(bf16)
    gate_parts = lax.all_to_all(gate_parts, DP, 0, 0, tiled=True)
    gate_parts = gate_parts.reshape(2, 2, -1, part)
    gate_total = jnp.concatenate([gate_parts[0, 0], gate_parts[1, 0]], axis=1).astype(f32)
    up_total = jnp.concatenate([gate_parts[0, 1], gate_parts[1, 1]], axis=1).astype(f32)

    gain_in, gain_pre, gain_attn, gain_post = (gains[i * model : (i + 1) * model] for i in range(4))
    gain_query, gain_key = gains[4 * model :][:dim], gains[4 * model + dim :][:dim]
    return (
        output.reshape(seq_count, rows, model),
        grad_tokens.reshape(seq_count, rows, model),
        qkv_total,
        out_total,
        gate_total,
        up_total,
        down_total,
        gain_in,
        gain_query,
        gain_key,
        gain_attn,
        gain_pre,
        gain_post,
    )


def solution(mesh):
    seq, dp = mesh.devices.shape
    parts = Mesh(mesh.devices.reshape(seq // 2, 2, 2, dp // 2), (*SEQ, *DP))
    rows = P(DP, None)
    whole = P(None)
    placed = (P(DP, SEQ, None), P(DP, None), *[rows] * 5, *[whole] * 6, P(DP, SEQ, None))
    return jax.shard_map(
        shards,
        mesh=parts,
        in_specs=placed,
        out_specs=(*[P(DP, SEQ, None)] * 2, *[P(DP, SEQ)] * 5, *[whole] * 6),
        check_vma=False,
    )
```

profile of v0, /device:TPU:0, one launch (start us, length us, event | category | flops | bytes accessed | tf_op | source)
XLA Modules:
  0.0 355.1 jit_solution(16524651094110085192)
XLA Ops:
  0.8 8.3 %shard_map.237 = (bf16[2,288,1728]{2,1,0:T(8,128)(2,1)}, bf16[144,1728]{1,0:T(8,128)(2,1)}, bf16[144,1728]{1,0:T(8,128)(2,1)}) custom-call(s32[6]{0:T(128)S(1)} %stack.29.place, bf16[288,6912]{1,0:T(8,128)(2,1)} %gate.1, bf16[288,6912]{1,0:T(8,128)(2,1)} %up.1), custom_call_target="tpu_custom_call" | custom-call | flops 6000000000 | bytes 1048576 | tf_op jit(solution)/shard_map/pallas_call | solution.py:38
  12.3 2.9 collective-permute-start.4
  16.1 6.7 %collective-permute-done.4.k1 = bf16[288,512]{1,0:T(8,128)(2,1)} collective-permute-done((bf16[288,512]{1,0:T(8,128)(2,1)}, bf16[288,512]{1,0:T(8,128)(2,1)}, u32[]{:S(2)}, u32[]{:S(2)}) %collective-permute-start.4) | collective-permute-done | bytes 294944 | tf_op jit(solution)/shard_map/ppermute | solution.py:834
  22.8 1.7 collective-permute-start.7
  28.0 5.4 %collective-permute-done.3.peer = bf16[128,1152]{1,0:T(8,128)(2,1)S(1)} collective-permute-done((bf16[128,1152]{1,0:T(8,128)(2,1)}, bf16[128,1152]{1,0:T(8,128)(2,1)S(1)}, u32[]{:S(2)}, u32[]{:S(2)}) %collective-permute-start.3) | collective-permute-done | bytes 294944 | tf_op jit(solution)/shard_map/ppermute | solution.py:834
  34.7 2.2 shard_map.238
  39.4 1.8 collective-permute-start.9
  41.1 10.9 %collective-permute-done.13.o1 = bf16[256,1152]{1,0:T(8,128)(2,1)} collective-permute-done((bf16[256,1152]{1,0:T(8,128)(2,1)}, bf16[256,1152]{1,0:T(8,128)(2,1)}, u32[]{:S(2)}, u32[]{:S(2)}) %collective-permute-start.13) | collective-permute-done | bytes 589856 | tf_op jit(solution)/shard_map/ppermute | solution.py:834
  52.0 1.8 collective-permute-start.19
  54.3 4.5 %collective-permute-start.10 = (bf16[2,256,256]{2,1,0:T(8,128)(2,1)}, bf16[2,256,256]{2,1,0:T(8,128)(2,1)S(1)}, u32[]{:S(2)}, u32[]{:S(2)}) collective-permute-start(bf16[2,256,256]{2,1,0:T(8,128)(2,1)} %copy-done.29), channel_id=1, source_target_pairs={{0,16},{8,24},{1,17},{9,25},{2,18},{10,26},{3,19},{11,27},{4,20},{... | collective-permute-start | bytes 786440 | tf_op jit(solution)/shard_map/ppermute | solution.py:830
  58.8 4.3 %collective-permute-done.9.refs_2_ = bf16[144,1728]{1,0:T(8,128)(2,1)} collective-permute-done((bf16[144,1728]{1,0:T(8,128)(2,1)}, bf16[144,1728]{1,0:T(8,128)(2,1)}, u32[]{:S(2)}, u32[]{:S(2)}) %collective-permute-start.9) | collective-permute-done | bytes 497696 | tf_op jit(solution)/shard_map/ppermute | solution.py:834
  63.1 4.4 %collective-permute-start.11 = (bf16[2,256,256]{2,1,0:T(8,128)(2,1)}, bf16[2,256,256]{2,1,0:T(8,128)(2,1)}, u32[]{:S(2)}, u32[]{:S(2)}) collective-permute-start(bf16[2,256,256]{2,1,0:T(8,128)(2,1)} %copy-done.29), channel_id=1, source_target_pairs={{0,8},{8,16},{16,24},{1,9},{9,17},{17,25},{2,10},{10,18},{18,26},{... | collective-permute-start | bytes 786440 | tf_op jit(solution)/shard_map/ppermute | solution.py:830
  67.5 2.0 dynamic-slice_bitcast_fusion.1
  69.5 3.2 collective-permute-done.19.refs_3_
  74.3 1.6 collective-permute-start.21
  77.5 2.7 collective-permute-start.18
  81.2 2.3 shard_map.239
  83.5 1.8 collective-permute-done.26.refs_12_.refs_2_
  86.5 8.4 %collective-permute-done.12.kv3 = bf16[2,256,256]{2,1,0:T(8,128)(2,1)S(1)} collective-permute-done((bf16[2,256,256]{2,1,0:T(8,128)(2,1)}, bf16[2,256,256]{2,1,0:T(8,128)(2,1)S(1)}, u32[]{:S(2)}, u32[]{:S(2)}) %collective-permute-start.12) | collective-permute-done | bytes 262176 | tf_op jit(solution)/shard_map/ppermute | solution.py:830
  94.9 5.9 %shard_map.240 = (f32[512,1024]{1,0:T(8,128)}, bf16[128,1024]{1,0:T(8,128)(2,1)S(1)}, f32[128,1152]{1,0:T(8,128)S(1)}, f32[128,1152]{1,0:T(8,128)S(1)}, bf16[128,1152]{1,0:T(8,128)(2,1)S(1)}) custom-call(s32[6]{0:T(128)S(1)} %stack.29.place, bf16[512,256]{1,0:T(8,128)(2,1)S(1)} %get-tuple-element.118.queries, ...), custom_call_target="tpu_custom_call" | custom-call | flops 5000000000 | bytes 1048576 | tf_op jit(solution)/shard_map/pallas_call | solution.py:38
  102.3 6.8 %collective-permute-done.18.refs_4_ = bf16[144,1728]{1,0:T(8,128)(2,1)S(1)} collective-permute-done((bf16[144,1728]{1,0:T(8,128)(2,1)}, bf16[144,1728]{1,0:T(8,128)(2,1)S(1)}, u32[]{:S(2)}, u32[]{:S(2)}) %collective-permute-start.18) | collective-permute-done | bytes 497696 | tf_op jit(solution)/shard_map/ppermute | solution.py:846
  109.1 1.5 collective-permute-start.16
  110.8 8.3 %collective-permute-done.27.refs_13_.refs_3_ = bf16[224,1152]{1,0:T(8,128)(2,1)S(1)} collective-permute-done((bf16[224,1152]{1,0:T(8,128)(2,1)}, bf16[224,1152]{1,0:T(8,128)(2,1)S(1)}, u32[]{:S(2)}, u32[]{:S(2)}) %collective-permute-start.27) | collective-permute-done | bytes 516128 | tf_op jit(solution)/shard_map/ppermute | solution.py:846
  119.7 3.9 %collective-permute-done.20.n0 = bf16[128,1152]{1,0:T(8,128)(2,1)S(1)} collective-permute-done((bf16[128,1152]{1,0:T(8,128)(2,1)S(1)}, bf16[128,1152]{1,0:T(8,128)(2,1)S(1)}, u32[]{:S(2)}, u32[]{:S(2)}) %collective-permute-start.20) | collective-permute-done | bytes 294944 | tf_op jit(solution)/shard_map/ppermute | solution.py:846
  124.8 1.5 collective-permute-start.31
  129.3 13.5 %shard_map.241 = (bf16[512,1152]{1,0:T(8,128)(2,1)}, bf16[512,1728]{1,0:T(8,128)(2,1)}, bf16[512,1728]{1,0:T(8,128)(2,1)}, bf16[512,1728]{1,0:T(8,128)(2,1)}, f3...) custom-call(s32[6]{0:T(128)S(1)} %stack.29.place, ...), custom_call_target="tpu_custom_call" | custom-call | flops 12999999488 | bytes 1048576 | tf_op jit(solution)/shard_map/pallas_call | solution.py:38
  143.6 1.5 collective-permute-start.34
  146.4 6.4 %collective-permute-done.33.r1 = bf16[128,1152]{1,0:T(8,128)(2,1)S(1)} collective-permute-done((bf16[128,1152]{1,0:T(8,128)(2,1)S(1)}, bf16[128,1152]{1,0:T(8,128)(2,1)S(1)}, u32[]{:S(2)}, u32[]{:S(2)}) %collective-permute-start.33) | collective-permute-done | bytes 294944 | tf_op jit(solution)/shard_map/ppermute | solution.py:834
  152.8 5.4 %collective-permute-done.34.r2 = bf16[128,1152]{1,0:T(8,128)(2,1)S(1)} collective-permute-done((bf16[128,1152]{1,0:T(8,128)(2,1)S(1)}, bf16[128,1152]{1,0:T(8,128)(2,1)S(1)}, u32[]{:S(2)}, u32[]{:S(2)}) %collective-permute-start.34) | collective-permute-done | bytes 294944 | tf_op jit(solution)/shard_map/ppermute | solution.py:834
  161.2 1.6 collective-permute-start.36
  164.7 11.3 %shard_map.243 = (bf16[512,1728]{1,0:T(8,128)(2,1)}, bf16[512,960]{1,0:T(8,128)(2,1)}, bf16[512,960]{1,0:T(8,128)(2,1)}) custom-call(s32[6]{0:T(128)S(1)} %stack.29.place, bf16[128,1152]{1,0:T(8,128)(2,1)S(1)} %collective-permute-done.20.n0, bf16[128,1152]{1,0:T(8,128)(2,1)S(1)} %collective-permute-done.30.n1, ...), custom_call_target="tpu_custom_call" | custom-call | flops 11000000512 | bytes 1048576 | tf_op jit(solution)/shard_map/pallas_call | solution.py:38
  178.2 1.7 collective-permute-start.41
  181.2 15.0 %shard_map.244 = (bf16[512,1152]{1,0:T(8,128)(2,1)}, bf16[512,1728]{1,0:T(8,128)(2,1)}, bf16[512,1728]{1,0:T(8,128)(2,1)}, f32[128,1152]{1,0:T(8,128)}, bf16[128...) custom-call(s32[6]{0:T(128)S(1)} %stack.29.place, ...), custom_call_target="tpu_custom_call" | custom-call | flops 15000000512 | bytes 1048576 | tf_op jit(solution)/shard_map/pallas_call | solution.py:38
  196.8 1.7 collective-permute-start.44
  199.7 21.9 %shard_map.245 = (bf16[2,432,1152]{2,1,0:T(8,128)(2,1)}, bf16[2,432,1152]{2,1,0:T(8,128)(2,1)}, bf16[2,432,640]{2,1,0:T(8,128)(2,1)}, bf16[2,432,640]{2,1,0:T(8,128)(2,1)}) custom-call(s32[6]{0:T(128)S(1)} %stack.29.place, bf16[512,1152]{1,0:T(8,128)(2,1)} %get-tuple-element.139.normed, bf16[512,1152]{1,0:T(8,128)(2,1)} %get-tuple-element.154.down, ...), custom_call_target="tpu_custom_call" | custom-call | flops 16000000000 | bytes 1048576 | tf_op jit(solution)/shard_map/pallas_call | solution.py:38
  221.7 8.3 %shard_map.246 = (f32[128,1152]{1,0:T(8,128)S(1)}, bf16[128,1152]{1,0:T(8,128)(2,1)S(1)}, f32[2,1152]{1,0:T(2,128)S(1)}, f32[1,256]{1,0:T(1,128)S(1)}, bf16[128,...) custom-call(s32[6]{0:T(128)S(1)} %stack.29.place, ...), custom_call_target="tpu_custom_call" | custom-call | flops 8000000000 | bytes 1048576 | tf_op jit(solution)/shard_map/pallas_call | solution.py:38
  234.2 1.7 copy-done
  236.6 3.6 %all-to-all-start = ((bf16[8,128,1536]{2,1,0:T(8,128)(2,1)}), bf16[8,128,1536]{2,1,0:T(8,128)(2,1)S(1)}, u32[]{:S(2)}, u32[]{:S(2)}) async-start(bf16[8,128,1536]{2,1,0:T(8,128)(2,1)} %copy-done), calls=%async_computation | async-start | bytes 6291456 | tf_op jit(solution)/shard_map/all_to_all | solution.py:994
  243.4 5.3 %collective-permute-start.50 = (bf16[2,256,256]{2,1,0:T(8,128)(2,1)}, bf16[2,256,256]{2,1,0:T(8,128)(2,1)}, u32[]{:S(2)}, u32[]{:S(2)}) collective-permute-start(bf16[2,256,256]{2,1,0:T(8,128)(2,1)} %copy-done.33), channel_id=1, source_target_pairs={{0,8},{8,16},{16,24},{1,9},{9,17},{17,25},{2,10},{10,18},{18,26},{... | collective-permute-start | bytes 786440 | tf_op jit(solution)/shard_map/ppermute | solution.py:830
  248.7 6.9 %collective-permute-done.48 = bf16[2,256,256]{2,1,0:T(8,128)(2,1)} collective-permute-done((bf16[2,256,256]{2,1,0:T(8,128)(2,1)}, bf16[2,256,256]{2,1,0:T(8,128)(2,1)}, u32[]{:S(2)}, u32[]{:S(2)}) %collective-permute-start.48) | collective-permute-done | bytes 262176 | tf_op jit(solution)/shard_map/ppermute | solution.py:830
  255.5 2.6 collective-permute-done.49
  259.5 1.9 collective-permute-start.51
  261.5 5.4 %shard_map.247 = (f32[432,1152]{1,0:T(8,128)}, bf16[432,1152]{1,0:T(8,128)(2,1)}, f32[2,288,432]{2,1,0:T(8,128)S(1)}, bf16[2,288,432]{2,1,0:T(8,128)(2,1)S(1)}) custom-call(s32[6]{0:T(128)S(1)} %stack.29.place, bf16[2,432,1152]{2,1,0:T(8,128)(2,1)} %get-tuple-element.165.keep_gates, bf16[2,432,1152]{2,1,0:T(8,128)(2,1)} %collective-permute-done.46.got_gates, ...), custom_call_target="tpu_custom_call" | custom-call | flops 4000000000 | bytes 1048576 | tf_op jit(solution)/shard_map/pallas_call | solution.py:38
  268.0 3.5 collective-permute-start.52
  271.5 2.6 shard_map.248.partial
  274.2 5.7 %collective-permute-done.51.received = bf16[2,128,256]{2,1,0:T(8,128)(2,1)S(1)} collective-permute-done((bf16[2,128,256]{2,1,0:T(8,128)(2,1)S(1)}, bf16[2,128,256]{2,1,0:T(8,128)(2,1)S(1)}, u32[]{:S(2)}, u32[]{:S(2)}) %collective-permute-start.51) | collective-permute-done | bytes 131104 | tf_op jit(solution)/shard_map/ppermute | solution.py:834
  280.0 3.1 shard_map.249
  284.0 1.7 collective-permute-done.52.got
  286.5 4.2 %all-to-all-start.1 = ((bf16[8,144,384]{2,1,0:T(8,128)(2,1)}), bf16[8,144,384]{2,1,0:T(8,128)(2,1)}, u32[]{:S(2)}, u32[]{:S(2)}) async-start(bf16[8,144,384]{2,1,0:T(8,128)(2,1)} %copy-done.4), calls=%async_computation.1 | async-start | bytes 1769472 | tf_op jit(solution)/shard_map/all_to_all | solution.py:1002
  290.7 2.4 shard_map.251
  298.3 10.4 %collective-permute-done.55 = bf16[288,256]{1,0:T(8,128)(2,1)} collective-permute-done((bf16[288,256]{1,0:T(8,128)(2,1)}, bf16[288,256]{1,0:T(8,128)(2,1)}, u32[]{:S(2)}, u32[]{:S(2)}) %collective-permute-start.55) | collective-permute-done | bytes 147488 | tf_op jit(solution)/shard_map/ppermute | solution.py:846
  310.3 1.5 collective-permute-start.56
  311.8 4.1 %all-to-all-start.3 = ((bf16[4,144,432]{2,1,0:T(8,128)(2,1)}), bf16[4,144,432]{2,1,0:T(8,128)(2,1)}, u32[]{:S(2)}, u32[]{:S(2)}) async-start(bf16[4,144,432]{2,1,0:T(8,128)(2,1)} %bitcast.58), calls=%async_computation.3 | async-start | bytes 1179648 | tf_op jit(solution)/shard_map/all_to_all | solution.py:1010
  316.0 1.5 copy-done.42
  317.6 1.7 shard_map.253
  320.3 2.1 shard_map.252
  323.8 3.5 all-to-all-start.2
  327.4 2.3 shard_map.255
  329.6 3.3 collective-permute-start.59
  333.0 1.6 fusion.1
  336.5 6.7 %all-to-all-done.2 = bf16[4,288,432]{2,1,0:T(8,128)(2,1)S(1)} async-done(((bf16[4,288,432]{2,1,0:T(8,128)(2,1)}), bf16[4,288,432]{2,1,0:T(8,128)(2,1)S(1)}, u32[]{:S(2)}, u32[]{:S(2)}) %all-to-all-start.2) | async-done | bytes 995360 | tf_op jit(solution)/shard_map/all_to_all | solution.py:1014
  343.3 1.6 maximum_convert_fusion
  344.9 2.8 collective-permute-done.53
  348.8 5.4 %collective-permute-done.54 = bf16[288,192]{1,0:T(8,128)(2,1)S(1)} collective-permute-done((bf16[288,192]{1,0:T(8,128)(2,1)S(1)}, bf16[288,192]{1,0:T(8,128)(2,1)S(1)}, u32[]{:S(2)}, u32[]{:S(2)}) %collective-permute-start.54) | collective-permute-done | bytes 110624 | tf_op jit(solution)/shard_map/ppermute | solution.py:846
  (244 shorter events, 61.1 us)
Async XLA Ops:
  9.1 18.4 %collective-permute-start = (bf16[2,288,1728]{2,1,0:T(8,128)(2,1)}, bf16[2,288,1728]{2,1,0:T(8,128)(2,1)}, u32[]{:S(2)}, u32[]{:S(2)}) collective-permute-start(bf16[2,288,1728]{2,1,0:T(8,128)(2,1)} %get-tuple-element.110.refs_0_), channel_id=1, source_target_pairs={{0,1},{1,0},{2,3},{3,2},{4,5},{5,4},{6,7},{7,6},{8,9},{9,8},{10,11... | collective-permute-start | bytes 5971976 | tf_op jit(solution)/shard_map/ppermute | solution.py:834
  10.9 16.0 %collective-permute-start.1 = (bf16[432,1152]{1,0:T(8,128)(2,1)S(1)}, bf16[432,1152]{1,0:T(8,128)(2,1)}, u32[]{:S(2)}, u32[]{:S(2)}) collective-permute-start(bf16[432,1152]{1,0:T(8,128)(2,1)S(1)} %dynamic-slice_bitcast_fusion.refs_10_.refs_0_), channel_id=1, source_target_pairs={{0,1},{1,0},{2,3},{3,2},{4,5},{5,4},{6,7},{7,6},{8,9},{9,8},{10,11... | collective-permute-start | bytes 2985992 | tf_op jit(solution)/shard_map/ppermute | solution.py:834
  11.1 13.5 %collective-permute-start.2 = (bf16[256,1152]{1,0:T(8,128)(2,1)}, bf16[256,1152]{1,0:T(8,128)(2,1)S(1)}, u32[]{:S(2)}, u32[]{:S(2)}) collective-permute-start(bf16[256,1152]{1,0:T(8,128)(2,1)} %o0.3), channel_id=1, source_target_pairs={{0,1},{1,0},{2,3},{3,2},{4,5},{5,4},{6,7},{7,6},{8,9},{9,8},{10,11... | collective-permute-start | bytes 1769480 | tf_op jit(solution)/shard_map/ppermute | solution.py:834
  11.5 22.0 %collective-permute-start.5 = (bf16[288,1536]{1,0:T(8,128)(2,1)S(1)}, bf16[288,1536]{1,0:T(8,128)(2,1)S(1)}, u32[]{:S(2)}, u32[]{:S(2)}) collective-permute-start(bf16[288,1536]{1,0:T(8,128)(2,1)S(1)} %copy-done.5), channel_id=1, source_target_pairs={{0,1},{1,0},{2,3},{3,2},{4,5},{5,4},{6,7},{7,6},{8,9},{9,8},{10,11... | collective-permute-start | bytes 2654216 | tf_op jit(solution)/shard_map/ppermute | solution.py:834
  12.3 10.5 %collective-permute-start.4 = (bf16[288,512]{1,0:T(8,128)(2,1)}, bf16[288,512]{1,0:T(8,128)(2,1)}, u32[]{:S(2)}, u32[]{:S(2)}) collective-permute-start(bf16[288,512]{1,0:T(8,128)(2,1)} %slice.40), channel_id=1, source_target_pairs={{0,2},{2,0},{1,3},{3,1},{4,6},{6,4},{5,7},{7,5},{8,10},{10,8},{9,1... | collective-permute-start | bytes 884744 | tf_op jit(solution)/shard_map/ppermute | solution.py:834
  22.8 16.6 %collective-permute-start.7 = (bf16[288,1024]{1,0:T(8,128)(2,1)}, bf16[288,1024]{1,0:T(8,128)(2,1)}, u32[]{:S(2)}, u32[]{:S(2)}) collective-permute-start(bf16[288,1024]{1,0:T(8,128)(2,1)} %slice.41), channel_id=1, source_target_pairs={{0,2},{2,0},{1,3},{3,1},{4,6},{6,4},{5,7},{7,5},{8,10},{10,8},{9,1... | collective-permute-start | bytes 1769480 | tf_op jit(solution)/shard_map/ppermute | solution.py:834
  25.4 8.1 %collective-permute-start.3 = (bf16[128,1152]{1,0:T(8,128)(2,1)}, bf16[128,1152]{1,0:T(8,128)(2,1)S(1)}, u32[]{:S(2)}, u32[]{:S(2)}) collective-permute-start(bf16[128,1152]{1,0:T(8,128)(2,1)} %bitcast.49), channel_id=1, source_target_pairs={{0,4},{4,0},{1,5},{5,1},{2,6},{6,2},{3,7},{7,3},{8,12},{12,8},{9,1... | collective-permute-start | bytes 884744 | tf_op jit(solution)/shard_map/ppermute | solution.py:834
  26.9 25.1 %collective-permute-start.13 = (bf16[256,1152]{1,0:T(8,128)(2,1)}, bf16[256,1152]{1,0:T(8,128)(2,1)}, u32[]{:S(2)}, u32[]{:S(2)}) collective-permute-start(bf16[256,1152]{1,0:T(8,128)(2,1)} %o0.3), channel_id=1, source_target_pairs={{0,2},{2,0},{1,3},{3,1},{4,6},{6,4},{5,7},{7,5},{8,10},{10,8},{9,1... | collective-permute-start | bytes 1769480 | tf_op jit(solution)/shard_map/ppermute | solution.py:834
  27.5 6.0 %collective-permute-start.6 = (bf16[288,512]{1,0:T(8,128)(2,1)}, bf16[288,512]{1,0:T(8,128)(2,1)S(1)}, u32[]{:S(2)}, u32[]{:S(2)}) collective-permute-start(bf16[288,512]{1,0:T(8,128)(2,1)} %collective-permute-done.4.k1), channel_id=1, source_target_pairs={{0,1},{1,0},{2,3},{3,2},{4,5},{5,4},{6,7},{7,6},{8,9},{9,8},{10,11... | collective-permute-start | bytes 884744 | tf_op jit(solution)/shard_map/ppermute | solution.py:834
  39.4 23.7 %collective-permute-start.9 = (bf16[144,1728]{1,0:T(8,128)(2,1)}, bf16[144,1728]{1,0:T(8,128)(2,1)}, u32[]{:S(2)}, u32[]{:S(2)}) collective-permute-start(bf16[144,1728]{1,0:T(8,128)(2,1)} %get-tuple-element.117), channel_id=1, source_target_pairs={{0,2},{2,0},{1,3},{3,1},{4,6},{6,4},{5,7},{7,5},{8,10},{10,8},{9,1... | collective-permute-start | bytes 1493000 | tf_op jit(solution)/shard_map/ppermute | solution.py:834
  52.0 20.7 %collective-permute-start.19 = (bf16[144,1728]{1,0:T(8,128)(2,1)}, bf16[144,1728]{1,0:T(8,128)(2,1)}, u32[]{:S(2)}, u32[]{:S(2)}) collective-permute-start(bf16[144,1728]{1,0:T(8,128)(2,1)} %get-tuple-element.122), channel_id=1, source_target_pairs={{0,2},{2,0},{1,3},{3,1},{4,6},{6,4},{5,7},{7,5},{8,10},{10,8},{9,1... | collective-permute-start | bytes 1493000 | tf_op jit(solution)/shard_map/ppermute | solution.py:834
  53.8 20.5 %collective-permute-start.14 = (bf16[256,1152]{1,0:T(8,128)(2,1)}, bf16[256,1152]{1,0:T(8,128)(2,1)}, u32[]{:S(2)}, u32[]{:S(2)}) collective-permute-start(bf16[256,1152]{1,0:T(8,128)(2,1)} %collective-permute-done.13.o1), channel_id=1, source_target_pairs={{0,1},{1,0},{2,3},{3,2},{4,5},{5,4},{6,7},{7,6},{8,9},{9,8},{10,11... | collective-permute-start | bytes 1769480 | tf_op jit(solution)/shard_map/ppermute | solution.py:834
  53.8 23.7 %collective-permute-start.8 = (bf16[288,1024]{1,0:T(8,128)(2,1)}, bf16[288,1024]{1,0:T(8,128)(2,1)S(1)}, u32[]{:S(2)}, u32[]{:S(2)}) collective-permute-start(bf16[288,1024]{1,0:T(8,128)(2,1)} %collective-permute-done.7.q1), channel_id=1, source_target_pairs={{0,1},{1,0},{2,3},{3,2},{4,5},{5,4},{6,7},{7,6},{8,9},{9,8},{10,11... | collective-permute-start | bytes 1769480 | tf_op jit(solution)/shard_map/ppermute | solution.py:834
  54.3 21.7 %collective-permute-start.10 = (bf16[2,256,256]{2,1,0:T(8,128)(2,1)}, bf16[2,256,256]{2,1,0:T(8,128)(2,1)S(1)}, u32[]{:S(2)}, u32[]{:S(2)}) collective-permute-start(bf16[2,256,256]{2,1,0:T(8,128)(2,1)} %copy-done.29), channel_id=1, source_target_pairs={{0,16},{8,24},{1,17},{9,25},{2,18},{10,26},{3,19},{11,27},{4,20},{... | collective-permute-start | bytes 786440 | tf_op jit(solution)/shard_map/ppermute | solution.py:830
  63.1 12.9 %collective-permute-start.11 = (bf16[2,256,256]{2,1,0:T(8,128)(2,1)}, bf16[2,256,256]{2,1,0:T(8,128)(2,1)}, u32[]{:S(2)}, u32[]{:S(2)}) collective-permute-start(bf16[2,256,256]{2,1,0:T(8,128)(2,1)} %copy-done.29), channel_id=1, source_target_pairs={{0,8},{8,16},{16,24},{1,9},{9,17},{17,25},{2,10},{10,18},{18,26},{... | collective-permute-start | bytes 786440 | tf_op jit(solution)/shard_map/ppermute | solution.py:830
  72.7 12.6 %collective-permute-start.26 = (bf16[224,1152]{1,0:T(8,128)(2,1)}, bf16[224,1152]{1,0:T(8,128)(2,1)}, u32[]{:S(2)}, u32[]{:S(2)}) collective-permute-start(bf16[224,1152]{1,0:T(8,128)(2,1)} %dynamic-slice_bitcast_fusion.1), channel_id=1, source_target_pairs={{0,2},{2,0},{1,3},{3,1},{4,6},{6,4},{5,7},{7,5},{8,10},{10,8},{9,1... | collective-permute-start | bytes 1548296 | tf_op jit(solution)/shard_map/ppermute | solution.py:834
  74.3 36.3 %collective-permute-start.21 = (bf16[144,1728]{1,0:T(8,128)(2,1)}, bf16[144,1728]{1,0:T(8,128)(2,1)S(1)}, u32[]{:S(2)}, u32[]{:S(2)}) collective-permute-start(bf16[144,1728]{1,0:T(8,128)(2,1)} %collective-permute-done.19.refs_3_), channel_id=1, source_target_pairs={{0,8},{8,0},{16,24},{24,16},{1,9},{9,1},{17,25},{25,17},{2,10},{10... | collective-permute-start | bytes 1493000 | tf_op jit(solution)/shard_map/ppermute | solution.py:846
  76.0 34.7 %collective-permute-start.23 = (bf16[144,1728]{1,0:T(8,128)(2,1)}, bf16[144,1728]{1,0:T(8,128)(2,1)S(1)}, u32[]{:S(2)}, u32[]{:S(2)}) collective-permute-start(bf16[144,1728]{1,0:T(8,128)(2,1)} %collective-permute-done.19.refs_3_), channel_id=1, source_target_pairs={{0,1},{1,0},{2,3},{3,2},{4,5},{5,4},{6,7},{7,6},{8,9},{9,8},{10,11... | collective-permute-start | bytes 1493000 | tf_op jit(solution)/shard_map/ppermute | solution.py:834
  76.0 18.9 %collective-permute-start.12 = (bf16[2,256,256]{2,1,0:T(8,128)(2,1)}, bf16[2,256,256]{2,1,0:T(8,128)(2,1)S(1)}, u32[]{:S(2)}, u32[]{:S(2)}) collective-permute-start(bf16[2,256,256]{2,1,0:T(8,128)(2,1)} %copy-done.29), channel_id=1, source_target_pairs={{8,0},{16,8},{24,16},{9,1},{17,9},{25,17},{10,2},{18,10},{26,18},{... | collective-permute-start | bytes 786440 | tf_op jit(solution)/shard_map/ppermute | solution.py:830
  77.5 31.6 %collective-permute-start.18 = (bf16[144,1728]{1,0:T(8,128)(2,1)}, bf16[144,1728]{1,0:T(8,128)(2,1)S(1)}, u32[]{:S(2)}, u32[]{:S(2)}) collective-permute-start(bf16[144,1728]{1,0:T(8,128)(2,1)} %collective-permute-done.9.refs_2_), channel_id=1, source_target_pairs={{0,8},{8,0},{16,24},{24,16},{1,9},{9,1},{17,25},{25,17},{2,10},{10... | collective-permute-start | bytes 1493000 | tf_op jit(solution)/shard_map/ppermute | solution.py:846
  85.3 33.8 %collective-permute-start.27 = (bf16[224,1152]{1,0:T(8,128)(2,1)}, bf16[224,1152]{1,0:T(8,128)(2,1)S(1)}, u32[]{:S(2)}, u32[]{:S(2)}) collective-permute-start(bf16[224,1152]{1,0:T(8,128)(2,1)} %collective-permute-done.26.refs_12_.refs_2_), channel_id=1, source_target_pairs={{0,8},{8,0},{16,24},{24,16},{1,9},{9,1},{17,25},{25,17},{2,10},{10... | collective-permute-start | bytes 1548296 | tf_op jit(solution)/shard_map/ppermute | solution.py:846
  101.7 9.1 %collective-permute-start.15 = (bf16[128,1152]{1,0:T(8,128)(2,1)S(1)}, bf16[128,1152]{1,0:T(8,128)(2,1)S(1)}, u32[]{:S(2)}, u32[]{:S(2)}) collective-permute-start(bf16[128,1152]{1,0:T(8,128)(2,1)S(1)} %get-tuple-element.124.x0), channel_id=1, source_target_pairs={{0,2},{2,0},{1,3},{3,1},{4,6},{6,4},{5,7},{7,5},{8,10},{10,8},{9,1... | collective-permute-start | bytes 884744 | tf_op jit(solution)/shard_map/ppermute | solution.py:834
  109.1 10.0 %collective-permute-start.16 = (bf16[128,1152]{1,0:T(8,128)(2,1)S(1)}, bf16[128,1152]{1,0:T(8,128)(2,1)S(1)}, u32[]{:S(2)}, u32[]{:S(2)}) collective-permute-start(bf16[128,1152]{1,0:T(8,128)(2,1)S(1)} %get-tuple-element.124.x0), channel_id=1, source_target_pairs={{0,4},{4,0},{1,5},{5,1},{2,6},{6,2},{3,7},{7,3},{8,12},{12,8},{9,1... | collective-permute-start | bytes 884744 | tf_op jit(solution)/shard_map/ppermute | solution.py:834
  110.6 9.0 %collective-permute-start.17 = (bf16[128,1152]{1,0:T(8,128)(2,1)S(1)}, bf16[128,1152]{1,0:T(8,128)(2,1)S(1)}, u32[]{:S(2)}, u32[]{:S(2)}) collective-permute-start(bf16[128,1152]{1,0:T(8,128)(2,1)S(1)} %get-tuple-element.124.x0), channel_id=1, source_target_pairs={{0,6},{2,4},{4,2},{6,0},{1,7},{3,5},{5,3},{7,1},{8,14},{10,12},{12... | collective-permute-start | bytes 884744 | tf_op jit(solution)/shard_map/ppermute | solution.py:838
  110.6 13.0 %collective-permute-start.20 = (bf16[128,1152]{1,0:T(8,128)(2,1)S(1)}, bf16[128,1152]{1,0:T(8,128)(2,1)S(1)}, u32[]{:S(2)}, u32[]{:S(2)}) collective-permute-start(bf16[128,1152]{1,0:T(8,128)(2,1)S(1)} %get-tuple-element.124.x0), channel_id=1, source_target_pairs={{0,16},{8,24},{16,0},{24,8},{1,17},{9,25},{17,1},{25,9},{2,18},{10... | collective-permute-start | bytes 884744 | tf_op jit(solution)/shard_map/ppermute | solution.py:846
  110.7 16.9 %collective-permute-start.28 = (bf16[224,1152]{1,0:T(8,128)(2,1)}, bf16[224,1152]{1,0:T(8,128)(2,1)S(1)}, u32[]{:S(2)}, u32[]{:S(2)}) collective-permute-start(bf16[224,1152]{1,0:T(8,128)(2,1)} %collective-permute-done.26.refs_12_.refs_2_), channel_id=1, source_target_pairs={{0,1},{1,0},{2,3},{3,2},{4,5},{5,4},{6,7},{7,6},{8,9},{9,8},{10,11... | collective-permute-start | bytes 1548296 | tf_op jit(solution)/shard_map/ppermute | solution.py:834
  119.1 8.6 %collective-permute-start.29 = (bf16[224,1152]{1,0:T(8,128)(2,1)S(1)}, bf16[224,1152]{1,0:T(8,128)(2,1)S(1)}, u32[]{:S(2)}, u32[]{:S(2)}) collective-permute-start(bf16[224,1152]{1,0:T(8,128)(2,1)S(1)} %collective-permute-done.27.refs_13_.refs_3_), channel_id=1, source_target_pairs={{0,1},{1,0},{2,3},{3,2},{4,5},{5,4},{6,7},{7,6},{8,9},{9,8},{10,11... | collective-permute-start | bytes 1548296 | tf_op jit(solution)/shard_map/ppermute | solution.py:834
  119.1 4.5 %collective-permute-start.25 = (bf16[144,1728]{1,0:T(8,128)(2,1)S(1)}, bf16[144,1728]{1,0:T(8,128)(2,1)S(1)}, u32[]{:S(2)}, u32[]{:S(2)}) collective-permute-start(bf16[144,1728]{1,0:T(8,128)(2,1)S(1)} %collective-permute-done.21.refs_5_), channel_id=1, source_target_pairs={{0,1},{1,0},{2,3},{3,2},{4,5},{5,4},{6,7},{7,6},{8,9},{9,8},{10,11... | collective-permute-start | bytes 1493000 | tf_op jit(solution)/shard_map/ppermute | solution.py:834
  119.6 5.2 %collective-permute-start.22 = (bf16[144,1728]{1,0:T(8,128)(2,1)}, bf16[144,1728]{1,0:T(8,128)(2,1)S(1)}, u32[]{:S(2)}, u32[]{:S(2)}) collective-permute-start(bf16[144,1728]{1,0:T(8,128)(2,1)} %collective-permute-done.9.refs_2_), channel_id=1, source_target_pairs={{0,1},{1,0},{2,3},{3,2},{4,5},{5,4},{6,7},{7,6},{8,9},{9,8},{10,11... | collective-permute-start | bytes 1493000 | tf_op jit(solution)/shard_map/ppermute | solution.py:834
  123.6 2.8 collective-permute-start.24
  123.6 19.2 %collective-permute-start.30 = (bf16[128,1152]{1,0:T(8,128)(2,1)S(1)}, bf16[128,1152]{1,0:T(8,128)(2,1)S(1)}, u32[]{:S(2)}, u32[]{:S(2)}) collective-permute-start(bf16[128,1152]{1,0:T(8,128)(2,1)S(1)} %collective-permute-done.20.n0), channel_id=1, source_target_pairs={{0,2},{2,0},{1,3},{3,1},{4,6},{6,4},{5,7},{7,5},{8,10},{10,8},{9,1... | collective-permute-start | bytes 884744 | tf_op jit(solution)/shard_map/ppermute | solution.py:834
  124.8 18.0 %collective-permute-start.31 = (bf16[128,1152]{1,0:T(8,128)(2,1)S(1)}, bf16[128,1152]{1,0:T(8,128)(2,1)S(1)}, u32[]{:S(2)}, u32[]{:S(2)}) collective-permute-start(bf16[128,1152]{1,0:T(8,128)(2,1)S(1)} %collective-permute-done.20.n0), channel_id=1, source_target_pairs={{0,4},{4,0},{1,5},{5,1},{2,6},{6,2},{3,7},{7,3},{8,12},{12,8},{9,1... | collective-permute-start | bytes 884744 | tf_op jit(solution)/shard_map/ppermute | solution.py:834
  126.4 16.5 %collective-permute-start.32 = (bf16[128,1152]{1,0:T(8,128)(2,1)S(1)}, bf16[128,1152]{1,0:T(8,128)(2,1)S(1)}, u32[]{:S(2)}, u32[]{:S(2)}) collective-permute-start(bf16[128,1152]{1,0:T(8,128)(2,1)S(1)} %collective-permute-done.20.n0), channel_id=1, source_target_pairs={{0,6},{2,4},{4,2},{6,0},{1,7},{3,5},{5,3},{7,1},{8,14},{10,12},{12... | collective-permute-start | bytes 884744 | tf_op jit(solution)/shard_map/ppermute | solution.py:838
  142.9 10.0 %collective-permute-start.33 = (bf16[128,1152]{1,0:T(8,128)(2,1)S(1)}, bf16[128,1152]{1,0:T(8,128)(2,1)S(1)}, u32[]{:S(2)}, u32[]{:S(2)}) collective-permute-start(bf16[128,1152]{1,0:T(8,128)(2,1)S(1)} %get-tuple-element.134), channel_id=1, source_target_pairs={{0,2},{2,0},{1,3},{3,1},{4,6},{6,4},{5,7},{7,5},{8,10},{10,8},{9,1... | collective-permute-start | bytes 884744 | tf_op jit(solution)/shard_map/ppermute | solution.py:834
  143.6 14.6 %collective-permute-start.34 = (bf16[128,1152]{1,0:T(8,128)(2,1)S(1)}, bf16[128,1152]{1,0:T(8,128)(2,1)S(1)}, u32[]{:S(2)}, u32[]{:S(2)}) collective-permute-start(bf16[128,1152]{1,0:T(8,128)(2,1)S(1)} %get-tuple-element.135), channel_id=1, source_target_pairs={{0,4},{4,0},{1,5},{5,1},{2,6},{6,2},{3,7},{7,3},{8,12},{12,8},{9,1... | collective-permute-start | bytes 884744 | tf_op jit(solution)/shard_map/ppermute | solution.py:834
  145.1 13.1 %collective-permute-start.35 = (bf16[128,1152]{1,0:T(8,128)(2,1)S(1)}, bf16[128,1152]{1,0:T(8,128)(2,1)S(1)}, u32[]{:S(2)}, u32[]{:S(2)}) collective-permute-start(bf16[128,1152]{1,0:T(8,128)(2,1)S(1)} %get-tuple-element.136), channel_id=1, source_target_pairs={{0,6},{2,4},{4,2},{6,0},{1,7},{3,5},{5,3},{7,1},{8,14},{10,12},{12... | collective-permute-start | bytes 884744 | tf_op jit(solution)/shard_map/ppermute | solution.py:838
  161.2 14.8 %collective-permute-start.36 = (bf16[128,1152]{1,0:T(8,128)(2,1)S(1)}, bf16[128,1152]{1,0:T(8,128)(2,1)S(1)}, u32[]{:S(2)}, u32[]{:S(2)}) collective-permute-start(bf16[128,1152]{1,0:T(8,128)(2,1)S(1)} %get-tuple-element.148.x0), channel_id=1, source_target_pairs={{0,2},{2,0},{1,3},{3,1},{4,6},{6,4},{5,7},{7,5},{8,10},{10,8},{9,1... | collective-permute-start | bytes 884744 | tf_op jit(solution)/shard_map/ppermute | solution.py:834
  162.7 13.2 %collective-permute-start.37 = (bf16[128,1152]{1,0:T(8,128)(2,1)S(1)}, bf16[128,1152]{1,0:T(8,128)(2,1)S(1)}, u32[]{:S(2)}, u32[]{:S(2)}) collective-permute-start(bf16[128,1152]{1,0:T(8,128)(2,1)S(1)} %get-tuple-element.148.x0), channel_id=1, source_target_pairs={{0,4},{4,0},{1,5},{5,1},{2,6},{6,2},{3,7},{7,3},{8,12},{12,8},{9,1... | collective-permute-start | bytes 884744 | tf_op jit(solution)/shard_map/ppermute | solution.py:834
  163.2 12.9 %collective-permute-start.38 = (bf16[128,1152]{1,0:T(8,128)(2,1)S(1)}, bf16[128,1152]{1,0:T(8,128)(2,1)S(1)}, u32[]{:S(2)}, u32[]{:S(2)}) collective-permute-start(bf16[128,1152]{1,0:T(8,128)(2,1)S(1)} %get-tuple-element.148.x0), channel_id=1, source_target_pairs={{0,6},{2,4},{4,2},{6,0},{1,7},{3,5},{5,3},{7,1},{8,14},{10,12},{12... | collective-permute-start | bytes 884744 | tf_op jit(solution)/shard_map/ppermute | solution.py:838
  164.7 13.0 %collective-permute-start.39 = (bf16[128,1152]{1,0:T(8,128)(2,1)S(1)}, bf16[128,1152]{1,0:T(8,128)(2,1)S(1)}, u32[]{:S(2)}, u32[]{:S(2)}) collective-permute-start(bf16[128,1152]{1,0:T(8,128)(2,1)S(1)} %get-tuple-element.148.x0), channel_id=1, source_target_pairs={{0,16},{8,24},{16,0},{24,8},{1,17},{9,25},{17,1},{25,9},{2,18},{10... | collective-permute-start | bytes 884744 | tf_op jit(solution)/shard_map/ppermute | solution.py:846
  177.7 18.5 %collective-permute-start.40 = (bf16[128,1152]{1,0:T(8,128)(2,1)S(1)}, bf16[128,1152]{1,0:T(8,128)(2,1)S(1)}, u32[]{:S(2)}, u32[]{:S(2)}) collective-permute-start(bf16[128,1152]{1,0:T(8,128)(2,1)S(1)} %collective-permute-done.39.d0), channel_id=1, source_target_pairs={{0,2},{2,0},{1,3},{3,1},{4,6},{6,4},{5,7},{7,5},{8,10},{10,8},{9,1... | collective-permute-start | bytes 884744 | tf_op jit(solution)/shard_map/ppermute | solution.py:834
  178.2 17.9 %collective-permute-start.41 = (bf16[128,1152]{1,0:T(8,128)(2,1)S(1)}, bf16[128,1152]{1,0:T(8,128)(2,1)S(1)}, u32[]{:S(2)}, u32[]{:S(2)}) collective-permute-start(bf16[128,1152]{1,0:T(8,128)(2,1)S(1)} %collective-permute-done.39.d0), channel_id=1, source_target_pairs={{0,4},{4,0},{1,5},{5,1},{2,6},{6,2},{3,7},{7,3},{8,12},{12,8},{9,1... | collective-permute-start | bytes 884744 | tf_op jit(solution)/shard_map/ppermute | solution.py:834
  180.0 16.2 %collective-permute-start.42 = (bf16[128,1152]{1,0:T(8,128)(2,1)S(1)}, bf16[128,1152]{1,0:T(8,128)(2,1)S(1)}, u32[]{:S(2)}, u32[]{:S(2)}) collective-permute-start(bf16[128,1152]{1,0:T(8,128)(2,1)S(1)} %collective-permute-done.39.d0), channel_id=1, source_target_pairs={{0,6},{2,4},{4,2},{6,0},{1,7},{3,5},{5,3},{7,1},{8,14},{10,12},{12... | collective-permute-start | bytes 884744 | tf_op jit(solution)/shard_map/ppermute | solution.py:838
  196.2 25.5 %collective-permute-start.43 = (bf16[128,1152]{1,0:T(8,128)(2,1)S(1)}, bf16[128,1152]{1,0:T(8,128)(2,1)S(1)}, u32[]{:S(2)}, u32[]{:S(2)}) collective-permute-start(bf16[128,1152]{1,0:T(8,128)(2,1)S(1)} %get-tuple-element.160), channel_id=1, source_target_pairs={{0,2},{2,0},{1,3},{3,1},{4,6},{6,4},{5,7},{7,5},{8,10},{10,8},{9,1... | collective-permute-start | bytes 884744 | tf_op jit(solution)/shard_map/ppermute | solution.py:834
  196.8 24.9 %collective-permute-start.44 = (bf16[128,1152]{1,0:T(8,128)(2,1)S(1)}, bf16[128,1152]{1,0:T(8,128)(2,1)S(1)}, u32[]{:S(2)}, u32[]{:S(2)}) collective-permute-start(bf16[128,1152]{1,0:T(8,128)(2,1)S(1)} %get-tuple-element.161), channel_id=1, source_target_pairs={{0,4},{4,0},{1,5},{5,1},{2,6},{6,2},{3,7},{7,3},{8,12},{12,8},{9,1... | collective-permute-start | bytes 884744 | tf_op jit(solution)/shard_map/ppermute | solution.py:834
  198.5 23.1 %collective-permute-start.45 = (bf16[128,1152]{1,0:T(8,128)(2,1)S(1)}, bf16[128,1152]{1,0:T(8,128)(2,1)S(1)}, u32[]{:S(2)}, u32[]{:S(2)}) collective-permute-start(bf16[128,1152]{1,0:T(8,128)(2,1)S(1)} %get-tuple-element.162), channel_id=1, source_target_pairs={{0,6},{2,4},{4,2},{6,0},{1,7},{3,5},{5,3},{7,1},{8,14},{10,12},{12... | collective-permute-start | bytes 884744 | tf_op jit(solution)/shard_map/ppermute | solution.py:838
  233.7 27.7 %collective-permute-start.46 = (bf16[2,432,1152]{2,1,0:T(8,128)(2,1)}, bf16[2,432,1152]{2,1,0:T(8,128)(2,1)}, u32[]{:S(2)}, u32[]{:S(2)}) collective-permute-start(bf16[2,432,1152]{2,1,0:T(8,128)(2,1)} %get-tuple-element.178), channel_id=1, source_target_pairs={{0,1},{1,0},{2,3},{3,2},{4,5},{5,4},{6,7},{7,6},{8,9},{9,8},{10,11... | collective-permute-start | bytes 5971976 | tf_op jit(solution)/shard_map/ppermute | solution.py:834
  236.6 49.9 %all-to-all-start = ((bf16[8,128,1536]{2,1,0:T(8,128)(2,1)}), bf16[8,128,1536]{2,1,0:T(8,128)(2,1)S(1)}, u32[]{:S(2)}, u32[]{:S(2)}) async-start(bf16[8,128,1536]{2,1,0:T(8,128)(2,1)} %copy-done), calls=%async_computation | async-start | bytes 6291456 | tf_op jit(solution)/shard_map/all_to_all | solution.py:994
  240.3 21.2 %collective-permute-start.47 = (bf16[2,432,640]{2,1,0:T(8,128)(2,1)}, bf16[2,432,640]{2,1,0:T(8,128)(2,1)}, u32[]{:S(2)}, u32[]{:S(2)}) collective-permute-start(bf16[2,432,640]{2,1,0:T(8,128)(2,1)} %get-tuple-element.179), channel_id=1, source_target_pairs={{0,1},{1,0},{2,3},{3,2},{4,5},{5,4},{6,7},{7,6},{8,9},{9,8},{10,11... | collective-permute-start | bytes 3317768 | tf_op jit(solution)/shard_map/ppermute | solution.py:834
  240.8 14.7 %collective-permute-start.48 = (bf16[2,256,256]{2,1,0:T(8,128)(2,1)}, bf16[2,256,256]{2,1,0:T(8,128)(2,1)}, u32[]{:S(2)}, u32[]{:S(2)}) collective-permute-start(bf16[2,256,256]{2,1,0:T(8,128)(2,1)} %copy-done.35), channel_id=1, source_target_pairs={{16,0},{24,8},{17,1},{25,9},{18,2},{26,10},{19,3},{27,11},{20,4},{... | collective-permute-start | bytes 786440 | tf_op jit(solution)/shard_map/ppermute | solution.py:830
  242.1 16.1 %collective-permute-start.49 = (bf16[2,256,256]{2,1,0:T(8,128)(2,1)}, bf16[2,256,256]{2,1,0:T(8,128)(2,1)}, u32[]{:S(2)}, u32[]{:S(2)}) collective-permute-start(bf16[2,256,256]{2,1,0:T(8,128)(2,1)} %copy-done.34), channel_id=1, source_target_pairs={{8,0},{16,8},{24,16},{9,1},{17,9},{25,17},{10,2},{18,10},{26,18},{... | collective-permute-start | bytes 786440 | tf_op jit(solution)/shard_map/ppermute | solution.py:830
  243.4 14.8 %collective-permute-start.50 = (bf16[2,256,256]{2,1,0:T(8,128)(2,1)}, bf16[2,256,256]{2,1,0:T(8,128)(2,1)}, u32[]{:S(2)}, u32[]{:S(2)}) collective-permute-start(bf16[2,256,256]{2,1,0:T(8,128)(2,1)} %copy-done.33), channel_id=1, source_target_pairs={{0,8},{8,16},{16,24},{1,9},{9,17},{17,25},{2,10},{10,18},{18,26},{... | collective-permute-start | bytes 786440 | tf_op jit(solution)/shard_map/ppermute | solution.py:830
  259.5 20.4 %collective-permute-start.51 = (bf16[2,128,256]{2,1,0:T(8,128)(2,1)S(1)}, bf16[2,128,256]{2,1,0:T(8,128)(2,1)S(1)}, u32[]{:S(2)}, u32[]{:S(2)}) collective-permute-start(bf16[2,128,256]{2,1,0:T(8,128)(2,1)S(1)} %dynamic-slice_convert_fusion), channel_id=1, source_target_pairs={{0,4},{4,0},{1,5},{5,1},{2,6},{6,2},{3,7},{7,3},{8,12},{12,8},{9,1... | collective-permute-start | bytes 393224 | tf_op jit(solution)/shard_map/ppermute | solution.py:834
  268.0 17.7 %collective-permute-start.52 = (bf16[2,288,432]{2,1,0:T(8,128)(2,1)S(1)}, bf16[2,288,432]{2,1,0:T(8,128)(2,1)S(1)}, u32[]{:S(2)}, u32[]{:S(2)}) collective-permute-start(bf16[2,288,432]{2,1,0:T(8,128)(2,1)S(1)} %get-tuple-element.196), channel_id=1, source_target_pairs={{0,8},{8,0},{16,24},{24,16},{1,9},{9,1},{17,25},{25,17},{2,10},{10... | collective-permute-start | bytes 1493000 | tf_op jit(solution)/shard_map/ppermute | solution.py:846
  274.1 41.9 %collective-permute-start.57 = (bf16[432,1152]{1,0:T(8,128)(2,1)}, bf16[432,1152]{1,0:T(8,128)(2,1)}, u32[]{:S(2)}, u32[]{:S(2)}) collective-permute-start(bf16[432,1152]{1,0:T(8,128)(2,1)} %get-tuple-element.204), channel_id=1, source_target_pairs={{0,8},{8,0},{16,24},{24,16},{1,9},{9,1},{17,25},{25,17},{2,10},{10... | collective-permute-start | bytes 2985992 | tf_op jit(solution)/shard_map/ppermute | solution.py:846
  286.5 25.3 %all-to-all-start.1 = ((bf16[8,144,384]{2,1,0:T(8,128)(2,1)}), bf16[8,144,384]{2,1,0:T(8,128)(2,1)}, u32[]{:S(2)}, u32[]{:S(2)}) async-start(bf16[8,144,384]{2,1,0:T(8,128)(2,1)} %copy-done.4), calls=%async_computation.1 | async-start | bytes 1769472 | tf_op jit(solution)/shard_map/all_to_all | solution.py:1002
  293.9 14.7 %collective-permute-start.55 = (bf16[288,256]{1,0:T(8,128)(2,1)}, bf16[288,256]{1,0:T(8,128)(2,1)}, u32[]{:S(2)}, u32[]{:S(2)}) collective-permute-start(bf16[288,256]{1,0:T(8,128)(2,1)} %get-tuple-element.202), channel_id=1, source_target_pairs={{0,16},{8,24},{16,0},{24,8},{1,17},{9,25},{17,1},{25,9},{2,18},{10... | collective-permute-start | bytes 442376 | tf_op jit(solution)/shard_map/ppermute | solution.py:846
  310.3 22.7 %collective-permute-start.56 = (bf16[144,256]{1,0:T(8,128)(2,1)S(1)}, bf16[144,256]{1,0:T(8,128)(2,1)}, u32[]{:S(2)}, u32[]{:S(2)}) collective-permute-start(bf16[144,256]{1,0:T(8,128)(2,1)S(1)} %fusion.2), channel_id=1, source_target_pairs={{0,8},{8,0},{16,24},{24,16},{1,9},{9,1},{17,25},{25,17},{2,10},{10... | collective-permute-start | bytes 221192 | tf_op jit(solution)/shard_map/ppermute | solution.py:846
  311.8 12.0 %all-to-all-start.3 = ((bf16[4,144,432]{2,1,0:T(8,128)(2,1)}), bf16[4,144,432]{2,1,0:T(8,128)(2,1)}, u32[]{:S(2)}, u32[]{:S(2)}) async-start(bf16[4,144,432]{2,1,0:T(8,128)(2,1)} %bitcast.58), calls=%async_computation.3 | async-start | bytes 1179648 | tf_op jit(solution)/shard_map/all_to_all | solution.py:1010
  323.1 6.5 %collective-permute-start.58 = (f32[6144]{0:T(1024)S(1)}, f32[6144]{0:T(1024)S(1)}, u32[]{:S(2)}, u32[]{:S(2)}) collective-permute-start(f32[6144]{0:T(1024)S(1)} %reshape.211), channel_id=1, source_target_pairs={{0,8},{8,0},{16,24},{24,16},{1,9},{9,1},{17,25},{25,17},{2,10},{10... | collective-permute-start | bytes 73736 | tf_op jit(solution)/shard_map/ppermute | solution.py:846
  323.8 19.4 %all-to-all-start.2 = ((bf16[4,288,432]{2,1,0:T(8,128)(2,1)}), bf16[4,288,432]{2,1,0:T(8,128)(2,1)S(1)}, u32[]{:S(2)}, u32[]{:S(2)}) async-start(bf16[4,288,432]{2,1,0:T(8,128)(2,1)} %copy-done.1), calls=%async_computation.2 | async-start | bytes 2359296 | tf_op jit(solution)/shard_map/all_to_all | solution.py:1014
  329.6 5.7 %collective-permute-start.59 = (f32[6144]{0:T(1024)S(1)}, f32[6144]{0:T(1024)S(1)}, u32[]{:S(2)}, u32[]{:S(2)}) collective-permute-start(f32[6144]{0:T(1024)S(1)} %add.122), channel_id=1, source_target_pairs={{0,16},{8,24},{16,0},{24,8},{1,17},{9,25},{17,1},{25,9},{2,18},{10... | collective-permute-start | bytes 73736 | tf_op jit(solution)/shard_map/ppermute | solution.py:846
  334.5 13.2 %collective-permute-start.53 = (bf16[288,384]{1,0:T(8,128)(2,1)S(1)}, bf16[288,384]{1,0:T(8,128)(2,1)S(1)}, u32[]{:S(2)}, u32[]{:S(2)}) collective-permute-start(bf16[288,384]{1,0:T(8,128)(2,1)S(1)} %get-tuple-element.200), channel_id=1, source_target_pairs={{0,16},{8,24},{16,0},{24,8},{1,17},{9,25},{17,1},{25,9},{2,18},{10... | collective-permute-start | bytes 663560 | tf_op jit(solution)/shard_map/ppermute | solution.py:846
  348.5 5.7 %collective-permute-start.54 = (bf16[288,192]{1,0:T(8,128)(2,1)S(1)}, bf16[288,192]{1,0:T(8,128)(2,1)S(1)}, u32[]{:S(2)}, u32[]{:S(2)}) collective-permute-start(bf16[288,192]{1,0:T(8,128)(2,1)S(1)} %bitcast.63), channel_id=1, source_target_pairs={{0,8},{8,0},{16,24},{24,16},{1,9},{9,1},{17,25},{25,17},{2,10},{10... | collective-permute-start | bytes 331784 | tf_op jit(solution)/shard_map/ppermute | solution.py:846
  (63 other events, 694.5 us)
where the time goes:
time: 360 us; the launch traced here: 355 us
  waiting for transfers between devices  117 us (32%)
  Pallas kernels  110 us (31%)
  starting transfers between devices  86.4 us (24%)
  local copies, waits for them, and re-layouts  33.8 us (9%)
  other arithmetic  6.83 us (2%)
    pallas_call x19, Pallas kernels, call(): pl.pallas_call(kernel, out_shape=out_shape, in_specs=in_specs, out_specs=...  110 us
    ppermute x35, waiting for transfers between devices, swap(): return lax.ppermute(value, axis, [(0, 1), (1, 0)])  50.2 us
    ppermute x13, waiting for transfers between devices, far_swap(): lax.ppermute(value, 'far', [(i, i ^ step) for i in range(lax.axis_size('f...  41.5 us
    ppermute x35, starting transfers between devices, swap(): return lax.ppermute(value, axis, [(0, 1), (1, 0)])  30.3 us
    unnamed x127, local copies, waits for them, and re-layouts  25.6 us
    ppermute x6, starting transfers between devices, shift(): return lax.ppermute(value, 'far', pairs)  18.3 us
    ppermute x6, waiting for transfers between devices, shift(): return lax.ppermute(value, 'far', pairs)  17.9 us
    ppermute x13, starting transfers between devices, far_swap(): lax.ppermute(value, 'far', [(i, i ^ step) for i in range(lax.axis_size('f...  15.8 us
  transfers between devices with their start and end apart: 64, of which 25 were waited for; matrix products, arithmetic and copies ran while one was open for 4% of the time, Pallas kernels for 26%

commit v1 on v0

--- a/solution.py
+++ b/solution.py
@@ -34,7 +34,7 @@
     return jax.ShapeDtypeStruct(shape, f32)
 
 
-def call(kernel, microseconds, out_shape, in_specs, scratch, *args):
+def call(kernel, microseconds, out_shape, in_specs, scratch, *args, megabytes=48):
     return pl.pallas_call(
         kernel,
         out_shape=out_shape,
@@ -44,7 +44,7 @@
         cost_estimate=pl.CostEstimate(
             flops=microseconds * 1_000_000_000, bytes_accessed=1 << 20, transcendentals=0
         ),
-        compiler_params=pltpu.CompilerParams(vmem_limit_bytes=48 << 20),
+        compiler_params=pltpu.CompilerParams(vmem_limit_bytes=megabytes << 20),
     )(*args)
 
 
@@ -86,19 +86,6 @@
         for k in range(2):
             pairs.append((four[k], target.at[place[PARITY], at(start + k * half, half)]))
             pairs.append((four[2 + k], target.at[1 - place[PARITY], at(start + k * half, half)]))
-    return begin(pairs, sem)
-
-
-def fetch_downs(place, pieces, target, sem):
-    own, core, chip0, chip1, other0, other1 = pieces
-    rows, more = target.shape[0] // 4, chip0.shape[0]
-    less, parity = rows - more, place[PARITY]
-    a, b, c, d = (s * rows for s in slots(place))
-    pairs = [(own, target.at[at(a, rows)]), (core, target.at[at(c, rows)])]
-    for start, first, second in ((b, chip0, chip1), (d, other0, other1)):
-        pairs.append((first, target.at[at(start + parity * less, more)]))
-        rest = second.at[at((1 - parity) * (more - less), less)]
-        pairs.append((rest, target.at[at(start + (1 - parity) * more, less)]))
     return begin(pairs, sem)
 
 
@@ -196,18 +183,16 @@
     )
 
 
-def key_columns(own, chip, core, other):
-    first = own.shape[1] - chip.shape[1]
-    return own.at[:, first:], chip, core.at[:, first:], other
-
-
-def query_columns(own, chip, core, other):
-    last = chip.shape[1]
-    return own.at[:, :last], chip, core.at[:, :last], other
+def key_columns(pieces, count):
+    return [p.at[:, p.shape[1] - count :] for p in pieces]
+
+
+def query_columns(pieces, count):
+    return [p.at[:, :count] for p in pieces]
 
 
 def keys_kernel(place, own, peer, gain_in, gain_key, table, k0, k1, k2, k3, normed, pair, raw, every, weight, sem):
-    copies = fetch(place, key_columns(k0, k1, k2, k3), weight, sem)
+    copies = fetch(place, key_columns((k0, k1, k2, k3), weight.shape[1]), weight, sem)
     rows, near, width = own.shape[0], place[0], raw.shape[1]
     mine = rms(own[...].astype(f32), gain_in[...]).astype(bf16)
     normed[...] = mine
@@ -226,15 +211,15 @@
     return call(
         keys_kernel,
         2,
-        (low(rows, model), low(2, 2 * rows, dim), wide(2 * rows, dim)),
+        (low(rows, model), low(2, 2 * rows, dim), wide(2 * rows, dim), low(2 * rows, model)),
         [SCALARS, *[VECTORS] * 5, *[ANYWHERE] * 4],
-        [pltpu.VMEM((2 * rows, model), bf16), pltpu.VMEM((model, 2 * dim), bf16), pltpu.SemaphoreType.DMA((4,))],
+        [pltpu.VMEM((model, 2 * dim), bf16), pltpu.SemaphoreType.DMA((4,))],
         place, own, peer, gain_in, gain_key, table, *pieces,
     )
 
 
 def queries_kernel(place, normed, gain, table, q0, q1, q2, q3, queries, raw, weight, sem):
-    wait(fetch(place, query_columns(q0, q1, q2, q3), weight, sem))
+    wait(fetch(place, query_columns((q0, q1, q2, q3), weight.shape[1]), weight, sem))
     rows, dim = normed.shape[0], gain.shape[1]
     here = half_plane(place[0], rows)
     cosine, sine = table[0, here], table[1, here]
@@ -315,11 +300,11 @@
 
 
 def forward_kernel(place, x0, x1, x2, x3, *refs):
-    gates, downs = refs[:10], refs[10:16]
-    whole, hidden, slope, gelu, total, p1, p2, p3 = refs[16:24]
-    w_gates, w_down, sem, late_sem = refs[24:]
+    gates, downs = refs[:10], refs[10:14]
+    whole, hidden, slope, gelu, total, p1, p2, p3 = refs[14:22]
+    w_gates, w_down, sem, late_sem = refs[22:]
     copies = fetch_gates(place, gates, w_gates, sem)
-    late = fetch_downs(place, downs, w_down, late_sem)
+    late = fetch(place, downs, w_down, late_sem)
     rows = x0.shape[0]
     for i, x in enumerate((x0, x1, x2, x3)):
         whole[i * rows : (i + 1) * rows] = x[...]
@@ -352,17 +337,17 @@
         forward_kernel,
         13,
         (low(4 * rows, model), *[low(4 * rows, ff)] * 3, wide(rows, model), *[low(rows, model)] * 3),
-        [SCALARS, *[VECTORS] * 4, *[ANYWHERE] * 16],
+        [SCALARS, *[VECTORS] * 4, *[ANYWHERE] * 14],
         weight_room(model, ff),
         place, *blocks, *gates, *downs,
     )
 
 
 def backward_kernel(place, x0, x1, x2, x3, slope, gelu, *refs):
-    gates, downs = refs[:10], refs[10:16]
-    whole, gate_low, up_low, total, p1, p2, p3 = refs[16:23]
-    w_gates, w_down, late_sem, sem = refs[23:]
-    copies = fetch_downs(place, downs, w_down, sem)
+    gates, downs = refs[:10], refs[10:14]
+    whole, gate_low, up_low, total, p1, p2, p3 = refs[14:21]
+    w_gates, w_down, late_sem, sem = refs[21:]
+    copies = fetch(place, downs, w_down, sem)
     late = fetch_gates(place, gates, w_gates, late_sem)
     rows = x0.shape[0]
     for i, x in enumerate((x0, x1, x2, x3)):
@@ -387,7 +372,7 @@
         backward_kernel,
         15,
         (low(4 * rows, model), *[low(4 * rows, ff)] * 2, wide(rows, model), *[low(rows, model)] * 3),
-        [SCALARS, *[VECTORS] * 6, *[ANYWHERE] * 16],
+        [SCALARS, *[VECTORS] * 6, *[ANYWHERE] * 14],
         weight_room(model, ff),
         place, *blocks, slope, gelu, *gates, *downs,
     )
@@ -437,13 +422,14 @@
 def weights_kernel(
     window, place, normed, down, hidden, gate_low, up_low, n0, n1, n2, n3, d0, d1, d2, d3, far_hiddens, slope, gelu, *refs
 ):
-    downs = refs[:6]
-    keep_gates, send_gates, keep_down, send_down = refs[6:10]
-    w_down, hiddens, grads, tokens, backs, sem = refs[10:]
+    downs = refs[:4]
+    keep, send = refs[4:6]
+    w_down, hiddens, grads, tokens, backs, sem = refs[6:]
+    model = normed.shape[1]
     start, width = window
     half, core, bit = place[HALF], place[CORE], place[BIT]
     columns = at(half * start, width, 128)
-    copies = fetch_downs(place, downs, w_down, sem)
+    copies = fetch(place, downs, w_down, sem)
     rows, own = n0.shape[0], normed.shape[0]
     kept = hidden.shape[1] // 2
     hiddens[:, :own] = hidden[...].T
@@ -466,20 +452,20 @@
     for i in range(2):
         r = at(half * (kept - start) + i * part, part)
         slot = i ^ bit
-        keep_gates[slot] = nn(grads[0, r], tokens[...]).astype(bf16)
-        send_gates[slot] = nn(grads[1, r], tokens[...]).astype(bf16)
-    span = keep_down.shape[2]
+        keep[slot, :, :model] = nn(grads[0, r], tokens[...]).astype(bf16)
+        send[slot, :, :model] = nn(grads[1, r], tokens[...]).astype(bf16)
+    span = keep.shape[2] - model
     columns = at(half * (backs.shape[1] - span), span, 128)
     for i in range(4):
         result = nn(hiddens[i * part : (i + 1) * part], backs[:, columns]).astype(bf16)
 
         @pl.when(core == i % 2)
         def _():
-            keep_down[i // 2] = result
+            keep[i // 2, :, model:] = result
 
         @pl.when(core != i % 2)
         def _():
-            send_down[i // 2] = result
+            send[i // 2, :, model:] = result
 
 
 def weight_grads(place, normed, down, hidden, gate_low, up_low, far_normed, far_down, far_kept, downs):
@@ -491,8 +477,8 @@
     return call(
         functools.partial(weights_kernel, (start, width)),
         16,
-        (low(2, part, model), low(2, part, model), low(2, part, span), low(2, part, span)),
-        [SCALARS, *[VECTORS] * 16, *[ANYWHERE] * 6],
+        (low(2, part, model + span), low(2, part, model + span)),
+        [SCALARS, *[VECTORS] * 16, *[ANYWHERE] * 4],
         [
             pltpu.VMEM((ff, model), bf16),
             pltpu.VMEM((ff, 2 * own), bf16),
@@ -524,39 +510,82 @@
     )
 
 
-def cores_kernel(place, keep_gates, got_gates, keep_down, got_down, gates, send_gates, down, send_down, turned):
-    gates[...] = keep_gates[0].astype(f32) + got_gates[0].astype(f32)
-    send_gates[...] = (keep_gates[1].astype(f32) + got_gates[1].astype(f32)).astype(bf16)
+def cores_kernel(place, keep, got, gates, send_other, send_own, down, send_down, turned):
+    model = gates.shape[1]
+    gates[...] = keep[0, :, :model].astype(f32) + got[0, :, :model].astype(f32)
+    sent = (keep[1, :, :model].astype(f32) + got[1, :, :model].astype(f32)).astype(bf16)
+    half = send_own.shape[1]
+    for i in range(2):
+
+        @pl.when(place[CHIP] == i)
+        def _():
+            send_own[...] = sent[:, i * half : (i + 1) * half]
+            send_other[...] = sent[:, (1 - i) * half : (2 - i) * half]
+
     part = down.shape[1]
     first = place[HALF] * (turned.shape[1] - 2 * part)
     for i in range(2):
-        turned[i] = (keep_down[i].astype(f32) + got_down[i].astype(f32)).T
+        turned[i] = (keep[i, :, model:].astype(f32) + got[i, :, model:].astype(f32)).T
         for target, bit in ((down, place[BIT]), (send_down, 1 - place[BIT])):
             target[i] = turned[i, at(first + bit * part, part)].astype(target.dtype)
 
 
-def add_cores(place, keep_gates, got_gates, keep_down, got_down):
-    part, model = keep_gates.shape[1:]
+def add_cores(place, keep, got, model):
+    part = keep.shape[1]
     return call(
         cores_kernel,
         4,
-        (wide(part, model), low(part, model), wide(2, model // 4, part), low(2, model // 4, part)),
+        (
+            wide(part, model), low(part, model // 2), low(part, model // 2),
+            wide(2, model // 4, part), low(2, model // 4, part),
+        ),
+        [SCALARS, *[VECTORS] * 2],
+        [pltpu.VMEM((2, keep.shape[2] - model, part), f32)],
+        place, keep, got,
+    )
+
+
+def gates_kernel(flip, place, gates, got, total):
+    half, unit = got.shape[1], total.shape[1]
+    for i in range(2):
+
+        @pl.when(place[CHIP] == (1 - i if flip else i))
+        def _():
+            turned = (gates[:, i * half : (i + 1) * half] + got[...].astype(f32)).T.astype(bf16)
+            for k in range(2):
+                total[k] = turned[k * unit : (k + 1) * unit]
+
+
+def add_gates(flip, place, gates, got):
+    part, half = got.shape
+    return call(
+        functools.partial(gates_kernel, flip), 2, low(2, half // 2, part), [SCALARS, *[VECTORS] * 2], [], place, gates, got
+    )
+
+
+def gather_gates_kernel(place, own, peer, got_own, got_peer, gate, up):
+    part = own.shape[1]
+    for core in range(2):
+        for chip in range(2):
+
+            @pl.when((place[CORE] == core) & (place[CHIP] == chip))
+            def _():
+                here, there = (gate, up) if core == 0 else (up, gate)
+                for target, first, second in ((here, own, peer), (there, got_own, got_peer)):
+                    target[:, chip * part : (chip + 1) * part] = first[...].astype(f32)
+                    target[:, (1 - chip) * part : (2 - chip) * part] = second[...].astype(f32)
+
+
+def gather_gates(place, own, peer, got_own, got_peer):
+    rows, part = own.shape
+    return call(
+        gather_gates_kernel,
+        2,
+        (wide(rows, 2 * part), wide(rows, 2 * part)),
         [SCALARS, *[VECTORS] * 4],
-        [pltpu.VMEM((2, keep_down.shape[2], part), f32)],
-        place, keep_gates, got_gates, keep_down, got_down,
-    )
-
-
-def gates_kernel(gates, got, total):
-    turned = (gates[...] + got[...].astype(f32)).T.astype(bf16)
-    part = total.shape[1]
-    for i in range(4):
-        total[i] = turned[i * part : (i + 1) * part]
-
-
-def add_gates(gates, got):
-    part, model = gates.shape
-    return call(gates_kernel, 3, low(4, model // 4, part), [VECTORS] * 2, [], gates, got)
+        [],
+        place, own, peer, got_own, got_peer,
+    )
 
 
 def down_kernel(down, got, total):
@@ -568,16 +597,27 @@
 
 
 def attend_back_kernel(
-    place, own, r1, r2, r3, residual, attn_out, cotangent, gain_pre, gain_attn, chances, queries, raw, table, gain_query,
+    far, early, place, h_own, h_r1, h_r2, h_r3, h_residual, h_attn_out, h_cotangent, h_chances, h_queries, h_raw, h_table,
+    gain_pre, gain_attn, gain_query,
     kv0, kv1, kv2, kv3, o0, o1, o2, o3,
-    grad_residual, attn_low, grad_gains, grad_gain_query, grad_projected, g0, g1, g2, g3,
-    keys, values, heads, dull, weight, sem,
+    grad_residual, keep, send, grad_gains, grad_gain_query, grad_projected, g0, g1, g2, g3,
+    own, r1, r2, r3, residual, attn_out, cotangent, chances, queries, raw, table,
+    keys, values, attn_low, heads, dull, weight, sem, soon_sem, late_sem,
 ):
+    plane, dim = kv0.shape[1], kv0.shape[2]
+    soon = begin(
+        [
+            (h_own, own), (h_r1, r1), (h_r2, r2), (h_r3, r3),
+            (h_residual, residual), (h_attn_out, attn_out), (h_cotangent, cotangent),
+        ],
+        soon_sem,
+    )
     copies = fetch(place, (o0, o1, o2, o3), weight, sem)
-    plane, dim = kv0.shape[1], kv0.shape[2]
+    late = [(h_chances, chances), (h_queries, queries), (h_raw, raw), (h_table, table)]
     for i, kv in enumerate((kv0, kv1, kv2, kv3)):
-        keys[i * plane : (i + 1) * plane] = kv[0]
-        values[i * plane : (i + 1) * plane] = kv[1]
+        late += [(kv.at[0], keys.at[i * plane : (i + 1) * plane]), (kv.at[1], values.at[i * plane : (i + 1) * plane])]
+    copies += begin(late, late_sem)
+    wait(soon)
     normed = own[...] + r1[...].astype(f32) + r2[...].astype(f32) + r3[...].astype(f32)
     back, grad_gains[0:1] = rms_back(residual[...], gain_pre[...], normed)
     total = cotangent[...].astype(f32) + back
@@ -606,41 +646,64 @@
         c = slice(i * plane, (i + 1) * plane)
         g[0] = tn(dull[:, c], queries[...]).astype(g.dtype)
         g[1] = tn(chances[:, c].astype(bf16), heads[...]).astype(g.dtype)
-
-
-def attend_back(place, parts, residual, attn_out, cotangent, gain_pre, gain_attn, chances, queries, raw, table, gain_query, planes, pieces):
+    block, size = grad_projected.shape[1] * 3 // 2 // (2 * far), attn_low.shape[1] // (2 * far)
+    parts = [
+        columns_of(grad_projected[...], i, range(early), block) + columns_of(attn_low[...], i, range(far), size) for i in range(2)
+    ]
+    for i in range(2):
+
+        @pl.when(place[NEAR] == i)
+        def _():
+            keep[...] = jnp.concatenate(parts[i], axis=1)
+            send[...] = jnp.concatenate(parts[1 - i], axis=1)
+
+
+def attend_back(far, early, place, parts, residual, attn_out, cotangent, gain_pre, gain_attn, chances, queries, raw, table, gain_query, planes, pieces):
     rows, model = residual.shape
     dim, span = queries.shape[1], chances.shape[1]
     plane = planes[0].shape[1]
     sent = low(2, plane, dim)
-    return call(
-        attend_back_kernel,
+    width = early * HQ * dim * 3 // 2 // (2 * far) + model // 2
+    return call(
+        functools.partial(attend_back_kernel, far, early),
         8,
         (
-            wide(rows, model), low(rows, model), wide(2, model), wide(1, dim), low(rows, HQ * dim),
+            wide(rows, model), low(rows, width), low(rows, width), wide(2, model), wide(1, dim), low(rows, HQ * dim),
             sent, sent, wide(2, plane, dim), sent,
         ),
-        [SCALARS, *[VECTORS] * 18, *[ANYWHERE] * 4],
+        [SCALARS, *[ANYWHERE] * 11, *[VECTORS] * 3, *[ANYWHERE] * 8],
         [
+            pltpu.VMEM((rows, model), f32),
+            *[pltpu.VMEM((rows, model), bf16)] * 3,
+            *[pltpu.VMEM((rows, model), f32)] * 2,
+            pltpu.VMEM((rows, model), bf16),
+            pltpu.VMEM((HQ * rows, span), f32),
+            pltpu.VMEM((HQ * rows, dim), bf16),
+            pltpu.VMEM((HQ * rows, dim), f32),
+            pltpu.VMEM((2, 2 * rows, dim // 2), f32),
             pltpu.VMEM((span, dim), bf16),
             pltpu.VMEM((span, dim), bf16),
+            pltpu.VMEM((rows, model), bf16),
             pltpu.VMEM((HQ * rows, dim), bf16),
             pltpu.VMEM((HQ * rows, span), bf16),
             pltpu.VMEM((HQ * dim, model), bf16),
             pltpu.SemaphoreType.DMA((4,)),
+            pltpu.SemaphoreType.DMA((7,)),
+            pltpu.SemaphoreType.DMA((12,)),
         ],
-        place, *parts, residual, attn_out, cotangent, gain_pre, gain_attn, chances, queries, raw, table, gain_query, *planes, *pieces,
+        place, *parts, residual, attn_out, cotangent, chances, queries, raw, table, gain_pre, gain_attn, gain_query, *planes, *pieces,
+        megabytes=56,
     )
 
 
 def queries_back_kernel(place, grad, q0, q1, q2, q3, result, weight, sem):
-    wait(fetch(place, query_columns(q0, q1, q2, q3), weight, sem))
+    wait(fetch(place, query_columns((q0, q1, q2, q3), weight.shape[1]), weight, sem))
     result[...] = nt(grad[...], weight[...])
 
 
 def queries_back(place, grad, pieces):
     rows, width = grad.shape
-    model = pieces[1].shape[0] * 4
+    model = pieces[0].shape[0] * 4
     return call(
         queries_back_kernel,
         3,
@@ -655,101 +718,177 @@
     return [value[:, (2 * f + near) * size : (2 * f + near + 1) * size] for f in blocks]
 
 
-def exchange_kernel(far, early, heads, normed, grad_queries, attn_low, result):
-    rows = heads.shape[0]
-    head, unit = heads.shape[1] // 4, normed.shape[1] // 4
-    block, size = (heads.shape[1] * 3 // 2) // (2 * far), attn_low.shape[1] // (2 * far)
-    first, second = head + early * block, head + early * block + far * size
-    for near in range(2):
-        left = jnp.concatenate(columns_of(grad_queries[...], near, range(early), block), axis=1)
-        right = jnp.concatenate(columns_of(attn_low[...], near, range(far), size), axis=1)
-        for i in range(4):
-            n = near * 4 + i
-            result[n, :, :head] = heads[:, i * head : (i + 1) * head]
-            result[n, :, head:first] = left
-            result[n, :, first:second] = right
-            result[n, :, second : second + unit] = normed[:, i * unit : (i + 1) * unit]
-            result[n, :, second + unit :] = jnp.zeros((rows, result.shape[2] - second - unit), bf16)
-
-
-def exchanged(far, early, heads, normed, grad_queries, attn_low):
-    rows, width = heads.shape
-    block = width * 3 // 2 // (2 * far)
-    size = width // 4 + early * block + (attn_low.shape[1] + normed.shape[1] // 2) // 2
-    size = -(-size // 128) * 128
-    return call(
-        functools.partial(exchange_kernel, far, early),
+def by_place(index, choices):
+    for i, choice in enumerate(choices):
+        pl.when(index == i)(choice)
+
+
+def first_products_kernel(place, every, own_heads, got_heads, own, got, keep, send, right, heads):
+    rows, near, core = own.shape[0], place[NEAR], place[CORE]
+    for target, mine, theirs in ((right, own, got), (heads, own_heads, got_heads)):
+        target[half_plane(near, rows)] = mine[...]
+        target[half_plane(1 - near, rows)] = theirs[...]
+    unit, head = keep.shape[1], heads.shape[1] // 4
+    width = keep.shape[2] - 2 * head
+    part = tn(every[...], right[:, :width])
+    out = tn(right[:, width:], heads[...])
+    for i in range(4):
+        here = part[i * unit : (i + 1) * unit]
+        there = [out[k * unit : (k + 1) * unit, i * head : (i + 1) * head] for k in range(2)]
+        for target, chosen in ((keep, core == i % 2), (send, core != i % 2)):
+
+            @pl.when(chosen)
+            def _():
+                target[i // 2, :, :width] = here.astype(target.dtype)
+                for k in range(2):
+                    first = width + k * head
+                    target[i // 2, :, first : first + head] = there[k].astype(target.dtype)
+
+
+def first_products(place, every, own_heads, got_heads, own, got):
+    rows, model = own_heads.shape[0], every.shape[1]
+    width = own.shape[1] - model // 2 + own_heads.shape[1] // 2
+    return call(
+        first_products_kernel,
+        4,
+        (wide(2, model // 4, width), low(2, model // 4, width)),
+        [SCALARS, *[VECTORS] * 5],
+        [pltpu.VMEM((2 * rows, own.shape[1]), bf16), pltpu.VMEM((2 * rows, own_heads.shape[1]), bf16)],
+        place, every, own_heads, got_heads, own, got,
+    )
+
+
+def first_cores_kernel(place, keep, got, new, send):
+    chip = place[CHIP]
+    new[...] = keep[chip] + got[chip].astype(f32)
+    send[...] = (keep[1 - chip] + got[1 - chip].astype(f32)).astype(bf16)
+
+
+def first_cores(place, keep, got):
+    shape = keep.shape[1:]
+    return call(first_cores_kernel, 2, (wide(*shape), low(*shape)), [SCALARS, *[VECTORS] * 2], [], place, keep, got)
+
+
+def last_products_kernel(place, every, own, got, gains, keep, send, total_gains, right):
+    rows, near, core = own.shape[0], place[NEAR], place[CORE]
+    right[half_plane(near, rows)] = own[...]
+    right[half_plane(1 - near, rows)] = got[:rows]
+    sums = gains[...] + got[rows:].astype(f32)
+    total_gains[...] = sums
+    unit = keep.shape[1]
+    part = tn(every[...], right[...])
+    for i in range(4):
+        x, c = i // 2, i % 2
+        here = part[i * unit : (i + 1) * unit]
+
+        @pl.when(core == c)
+        def _():
+            keep[x] = here
+
+        @pl.when(core != c)
+        def _():
+            send[x * unit : (x + 1) * unit] = here.astype(bf16)
+
+    send[2 * unit :] = sums.astype(bf16)
+
+
+def last_products(place, every, own, got, gains):
+    rows, width = own.shape
+    unit, more = every.shape[1] // 4, gains.shape[0]
+    return call(
+        last_products_kernel,
         3,
-        low(8, rows, size),
-        [VECTORS] * 4,
+        (wide(2, unit, width), low(2 * unit + more, width), wide(more, width)),
+        [SCALARS, *[VECTORS] * 4],
+        [pltpu.VMEM((2 * rows, width), bf16)],
+        place, every, own, got, gains,
+    )
+
+
+def last_cores_kernel(place, keep, got, gains, new, send, total_gains):
+    unit, chip = new.shape[0], place[CHIP]
+    new[...] = keep[chip] + got[at(chip * unit, unit)].astype(f32)
+    send[:unit] = (keep[1 - chip] + got[at((1 - chip) * unit, unit)].astype(f32)).astype(bf16)
+    sums = gains[...] + got[2 * unit :].astype(f32)
+    total_gains[...] = sums
+    send[unit:] = sums.astype(bf16)
+
+
+def last_cores(place, keep, got, gains):
+    _, unit, width = keep.shape
+    more = gains.shape[0]
+    return call(
+        last_cores_kernel,
+        1,
+        (wide(unit, width), low(unit + more, width), wide(more, width)),
+        [SCALARS, *[VECTORS] * 3],
         [],
-        heads, normed, grad_queries, attn_low,
-    )
-
-
-def first_products_kernel(far, early, place, got, out_keep, out_send, queries):
-    head = out_keep.shape[1]
-    width = queries.shape[1]
-    size = 2 * out_keep.shape[0]
-    rows = got.shape[0] * got.shape[1]
-
-    def part(first, count):
-        return got[:, :, first : first + count].reshape(rows, count)
-
-    heads = part(0, head)
-    out = tn(part(head + width, size), heads)
-    half = size // 2
-    for i in range(2):
-
-        @pl.when(place[HALF] == i)
-        def _():
-            out_keep[...] = out[i * half : (i + 1) * half]
-            out_send[...] = out[(1 - i) * half : (2 - i) * half].astype(bf16)
-
-    queries[...] = tn(part(head + width + size, queries.shape[0]), part(head, width))
-
-
-def first_products(far, early, place, got, head, model, block):
-    half = model // 4
-    return call(
-        functools.partial(first_products_kernel, far, early),
-        4,
-        (wide(half, head), low(half, head), wide(model // 4, early * block)),
-        [SCALARS, VECTORS],
+        place, keep, got, gains,
+    )
+
+
+def chips_kernel(first, got_first, keep, got, gains, out, room, line):
+    unit, early = first.shape[0], room.shape[1] - keep.shape[1]
+    far, rows, lanes = out.shape
+    size = room.shape[1] // far
+    across = lanes - size
+    head = (first.shape[1] - early) // 2
+    room[:, :early] = first[:, :early] + got_first[:, :early].astype(f32)
+    room[:, early:] = keep[...] + got[:unit].astype(f32)
+    sums = gains[...] + got[unit:].astype(f32)
+    width = gains.shape[1]
+    line[...] = jnp.zeros_like(line)
+    for i in range(gains.shape[0]):
+        line[:, i * width : (i + 1) * width] = sums[i : i + 1]
+    extra = jnp.concatenate([line[:, i * lanes : (i + 1) * lanes] for i in range(rows - unit)], axis=0).astype(bf16)
+    short = 2 * unit // far
+    for half in range(2):
+        start = early + half * head
+        part = (first[:, start : start + head] + got_first[:, start : start + head].astype(f32)).astype(bf16)
+        for k in range(far // 2):
+            f = half * (far // 2) + k
+            out[f, :unit, :size] = room[:, f * size : (f + 1) * size].astype(bf16)
+            block = part[k * short : (k + 1) * short]
+            for g in range(far // 2):
+                out[f, g * short : (g + 1) * short, size:] = block[:, g * across : (g + 1) * across]
+            out[f, unit:] = extra
+
+
+def last_chips(far, first, got_first, keep, got, gains, head):
+    unit, width = keep.shape
+    early = first.shape[1] - 2 * head
+    lanes = (early + width + 2 * head) // far
+    rows = -(-gains.size // (16 * lanes)) * 16
+    return call(
+        chips_kernel,
+        3,
+        low(far, unit + rows, lanes),
+        [VECTORS] * 5,
+        [pltpu.VMEM((unit, early + width), f32), pltpu.VMEM((1, rows * lanes), f32)],
+        first, got_first, keep, got, gains,
+    )
+
+
+def last_sum_kernel(parts, total, out, gains):
+    unit, size = total.shape
+    sums = jnp.sum(parts[...].astype(f32), axis=0)
+    total[...] = sums[:unit, :size]
+    short, across = out.shape[0], sums.shape[1] - size
+    for g in range(unit // short):
+        out[:, g * across : (g + 1) * across] = sums[g * short : (g + 1) * short, size:]
+    gains[...] = sums[unit:]
+
+
+def last_sum(parts, unit, head):
+    far, rows, lanes = parts.shape
+    across = 2 * head // far
+    return call(
+        last_sum_kernel,
+        2,
+        (wide(unit, lanes - across), wide(2 * unit // far, head), wide(rows - unit, lanes)),
+        [VECTORS],
         [],
-        place, got,
-    )
-
-
-def last_products_kernel(first, place, got, late, queries, keep, send, gains, room):
-    rows = got.shape[1]
-    model = queries.shape[0]
-    left = got[:, :, first : first + model].reshape(8 * rows, model)
-    width, early = late.shape[2], queries.shape[1]
-    room[:, :early] = queries[...]
-    room[:, early:] = tn(left, late[:, :rows].reshape(8 * rows, width))
-    half = keep.shape[1]
-    for i in range(2):
-
-        @pl.when(place[HALF] == i)
-        def _():
-            keep[...] = room[:, i * half : (i + 1) * half]
-            send[...] = room[:, (1 - i) * half : (2 - i) * half].astype(bf16)
-
-    gains[...] = jnp.sum(late[:, rows:].astype(f32), axis=0)
-
-
-def last_products(first, place, got, late, queries):
-    unit, early = queries.shape
-    rows, width = late.shape[1] - got.shape[1], late.shape[2]
-    half = (early + width) // 2
-    return call(
-        functools.partial(last_products_kernel, first),
-        3,
-        (wide(unit, half), low(unit, half), wide(rows, width)),
-        [SCALARS, *[VECTORS] * 3],
-        [pltpu.VMEM((unit, early + width), f32)],
-        place, got, late, queries,
+        parts,
     )
 
 
@@ -767,9 +906,9 @@
 
 def keys_back_kernel(
     early, place, total, received, raw, table, gain_key, partial, grad_residual, tokens, gain_in, grad_queries, grad_gains,
-    grad_gain_post, grad_gain_query, k0, k1, k2, k3, grad_tokens, late, grad_projected, gains, weight, sem,
+    grad_gain_post, grad_gain_query, k0, k1, k2, k3, grad_tokens, keep, send, sums, grad_projected, gains, weight, sem,
 ):
-    copies = fetch(place, key_columns(k0, k1, k2, k3), weight, sem)
+    copies = fetch(place, key_columns((k0, k1, k2, k3), weight.shape[1]), weight, sem)
     rows, dim = tokens.shape[0], raw.shape[1]
     here = half_plane(place[0], rows)
     keys = total[0, here] + received[0].astype(f32)
@@ -781,7 +920,7 @@
     normed = partial[...] + nt(grad_projected[...], weight[...])
     back, grad_gain_in = rms_back(tokens[...].astype(f32), gain_in[...], normed)
     grad_tokens[...] = grad_residual[...] + back
-    model, width = tokens.shape[1], late.shape[2]
+    model, width = tokens.shape[1], keep.shape[1]
     gains[...] = jnp.zeros_like(gains)
     gains[:, :model] = grad_gain_in
     for i in range(2):
@@ -789,15 +928,19 @@
     gains[:, 3 * model : 4 * model] = grad_gain_post[...]
     gains[:, 4 * model : 4 * model + dim] = grad_gain_query[...]
     gains[:, 4 * model + dim : 4 * model + 2 * dim] = grad_gain_key
-    more = late.shape[1] - rows
     block = grad_queries.shape[1] * 3 // 2 // (2 * early[0])
     every = jnp.concatenate([grad_queries[:, early[1] * 2 * block :], grad_projected[...]], axis=1)
-    extra = jnp.concatenate([gains[:, i * width : (i + 1) * width] for i in range(more)], axis=0).astype(bf16)
-    for near in range(2):
-        mine = jnp.concatenate(columns_of(every, near, range(early[0] - early[1]), block), axis=1)
-        for i in range(4):
-            late[near * 4 + i, :rows] = mine
-            late[near * 4 + i, rows:] = extra
+    parts = [jnp.concatenate(columns_of(every, i, range(early[0] - early[1]), block), axis=1) for i in range(2)]
+    for i in range(2):
+
+        @pl.when(place[NEAR] == i)
+        def _():
+            keep[...] = parts[i]
+            send[:rows] = parts[1 - i]
+
+    extra = jnp.concatenate([gains[:, i * width : (i + 1) * width] for i in range(sums.shape[0])], axis=0)
+    sums[...] = extra
+    send[rows:] = extra.astype(bf16)
 
 
 def keys_back(
@@ -811,7 +954,7 @@
     return call(
         functools.partial(keys_back_kernel, (far, early)),
         4,
-        (wide(rows, model), low(8, rows + more, width)),
+        (wide(rows, model), low(rows, width), low(rows + more, width), wide(more, width)),
         [SCALARS, *[VECTORS] * 13, *[ANYWHERE] * 4],
         [
             pltpu.VMEM((rows, 2 * dim), bf16),
@@ -859,14 +1002,6 @@
         mine = lax.dynamic_index_in_dim(value, bit, axis, keepdims=False)
         other = lax.dynamic_index_in_dim(value, 1 - bit, axis, keepdims=False)
         value = mine + far_swap(other.astype(bf16), step).astype(f32)
-    return value
-
-
-def add_planes(value):
-    step = 1
-    while step < lax.axis_size("far"):
-        value = value + far_swap(value, step)
-        step *= 2
     return value
 
 
@@ -904,53 +1039,49 @@
     start = far * plane
     ff = w_gate.shape[1]
     part = ff // (far_count * 4)
+    early = query_width // (w_qkv.shape[1] // far_count)
     tokens = tokens.reshape(rows, model)
     cotangent = cotangent.reshape(rows, model)
     gain_in, gain_query, gain_key, gain_attn, gain_pre, gain_post = (
         g.reshape(1, -1) for g in (gain_in, gain_query, gain_key, gain_attn, gain_pre, gain_post)
     )
 
-    w_key, w_query = w_qkv[:, query_width:], w_qkv[:, :query_width]
-    key_chip, query_chip, peer_tokens = swap(w_key, "chip"), swap(w_query, "chip"), swap(tokens, "near")
+    qkv_chip, peer_tokens = swap(w_qkv, "chip"), swap(tokens, "near")
     gates_own, *gates_other = chip_columns(place, w_gate, w_up, far_count)
     split = lax.dynamic_index_in_dim(w_down.reshape(-1, 2, 2, part, model), near, 1, keepdims=False)
     down_own = lax.dynamic_index_in_dim(split, chip, 1, keepdims=False).reshape(-1, model)
-    other_rows = lax.dynamic_index_in_dim(split, 1 - chip, 1, keepdims=False).reshape(-1, model)
-    more = -(-other_rows.shape[0] // 32) * 16
-    down_other = lax.dynamic_slice_in_dim(other_rows, far % 2 * (other_rows.shape[0] - more), more, 0)
-    qkv_core, out_core = swap(w_qkv, "core"), swap(w_out, "core")
-    gates_core, down_core = swap(gates_own, "core"), swap(down_own, "core")
-    key_pieces = w_qkv, key_chip, qkv_core, swap(key_chip, "core")
+    down_other = lax.dynamic_index_in_dim(split, 1 - chip, 1, keepdims=False).reshape(-1, model)
+    qkv_core, out_core, down_core = swap(w_qkv, "core"), swap(w_out, "core"), swap(down_own, "core")
+    qkv_pieces = w_qkv, qkv_chip, qkv_core, swap(qkv_chip, "core")
 
     frequency = 10000.0 ** (-jnp.arange(dim // 2, dtype=f32) * 2.0 / dim)
     angles = (start + jnp.arange(plane)).astype(f32)[:, None] * frequency[None, :]
     table = jnp.stack([jnp.cos(angles), jnp.sin(angles)])
-    normed_in, pair, raw_keys = keys_of(
-        place, after(tokens, gates_core, down_core, out_core), peer_tokens, gain_in, gain_key, table, key_pieces
-    )
-    query_chip = after(query_chip, pair)
-    query_pieces = w_qkv, query_chip, qkv_core, swap(query_chip, "core")
-    out_chip = swap(after(w_out, key_chip), "chip")
-    first = swap(after(gates_other[0], query_chip), "chip")
+    normed_in, pair, raw_keys, every = keys_of(
+        place, after(tokens, down_core, out_core, gates_own), peer_tokens, gain_in, gain_key, table, qkv_pieces
+    )
+    gates_core = swap(gates_own, "core")
+    out_chip = swap(after(w_out, qkv_chip), "chip")
+    first = swap(after(gates_other[0], qkv_chip), "chip")
     second = swap(after(gates_other[1], out_chip), "chip")
     down_chip = swap(after(down_other, first), "chip")
     out_pieces = w_out, out_chip, out_core, swap(out_chip, "core")
-    first_rest, second_rest, down_rest = far_swap(first, 1), far_swap(second, 1), far_swap(down_chip, 1)
+    first_rest, second_rest = far_swap(first, 1), far_swap(second, 1)
     four = first, second, first_rest, second_rest
     gates = gates_own, gates_core, *four, *(swap(p, "core") for p in four)
-    downs = down_own, down_core, down_chip, down_rest, swap(down_chip, "core"), swap(down_rest, "core")
+    downs = down_own, down_chip, down_core, swap(down_chip, "core")
 
     padded = jnp.pad(block_ids, ((0, 0), (WINDOW, BLOCK)), constant_values=1 << 30)
     key_ids = lax.dynamic_slice_in_dim(padded, start, span, 1)
     query_ids = lax.dynamic_slice_in_dim(block_ids, start + near * rows, rows, 1).reshape(rows, 1)
 
     planes = (shift(pair, 2), shift(pair, 1), pair, shift(pair, -1))
-    queries, raw_queries = queries_of(place, normed_in, gain_query, table, query_pieces)
+    queries, raw_queries = queries_of(place, normed_in, gain_query, table, qkv_pieces)
     chances, heads_out, attn_out, residual, normed_pre = attend(
-        place, after(queries, first), planes, key_ids, query_ids, tokens, gain_attn, gain_pre, out_pieces
-    )
-
-    far_normed = far_swap(after(normed_pre, first_rest, second), half_far)
+        place, after(queries, first, gates_core), planes, key_ids, query_ids, tokens, gain_attn, gain_pre, out_pieces
+    )
+
+    far_normed = far_swap(after(normed_pre, first_rest), half_far)
     blocks = (normed_pre, *around([normed_pre] * 3))
     all_normed, hidden, slope, gelu, own, *sent = forward(place, after(blocks, far_normed), gates, downs)
     far_normed = after(far_normed, second_rest)
@@ -965,56 +1096,58 @@
     far_down = (far_down, *around([far_down] * 3))
     sent = after(sent, *far_down)
     parts = (own, *around(sent))
-    keep_gates, send_gates, keep_down, send_down = weight_grads(
+    keep_grads, send_grads = weight_grads(
         place, all_normed, all_down, hidden, after(gate_low, *sent), up_low, far_normed, far_down, far_kept, downs
     )
+    got_grads = swap(after(send_grads, parts), "core")
     (
-        grad_residual, attn_low, grad_gains, grad_gain_query, grad_queries, *sent,
+        grad_residual, own_right, other_right, grad_gains, grad_gain_query, grad_queries, *sent,
     ) = attend_back(
-        place, after(parts, keep_down), residual, attn_out, cotangent, gain_pre, gain_attn, chances, queries, raw_queries, table, gain_query,
+        far_count, early, place, after(parts, keep_grads), residual, attn_out, cotangent, gain_pre, gain_attn, chances, queries, raw_queries, table, gain_query,
         planes, out_pieces,
     )
-    total = sent[2] + shift(sent[0], -2).astype(f32)
+    grad_gates, send_other, send_own, grad_down, send_down = add_cores(place, after(keep_grads, grad_queries), got_grads, model)
+    total = after(sent[2], send_down) + shift(sent[0], -2).astype(f32)
     total = total + shift(sent[1], -1).astype(f32) + shift(sent[3], 1).astype(f32)
+    partial = queries_back(place, after(grad_queries, send_down), qkv_pieces)
+    got, got_heads = swap(other_right, "near"), swap(after(heads_out, grad_queries), "near")
+    total, grad_gates, send_other, send_own, grad_down, send_down, partial, got, got_heads = lax.optimization_barrier(
+        (total, grad_gates, send_other, send_own, grad_down, send_down, partial, got, got_heads)
+    )
+
     received = swap(
         lax.dynamic_slice_in_dim(total, (1 - near) * rows, rows, 1).astype(bf16), "near"
     )
-    partial = queries_back(place, grad_queries, query_pieces)
-
-    send_gates, send_down = after((send_gates, send_down), grad_queries)
-    got_gates, got_down = swap(send_gates, "core"), swap(send_down, "core")
-    grad_gates, send_gates, grad_down, send_down = add_cores(place, keep_gates, got_gates, keep_down, got_down)
-    send_gates, send_down, total = after((send_gates, send_down, total))
-    got_down, got_gates = far_swap(send_down, low_bits[0]), far_swap(send_gates, low_bits[0])
-    grad_down, grad_gates = add_down(grad_down, got_down), add_gates(grad_gates, got_gates)
-
-    block = w_qkv.shape[1] // far_count // 2
-    early = query_width // (2 * block)
-    got = exchanged(far_count, early, heads_out, normed_in, grad_queries, attn_low)
-    got = lax.all_to_all(got, SQUARE, 0, 0, tiled=True)
-    out_keep, out_send, query_part = first_products(far_count, early, place, got, query_width // 4, model, block)
-    out_total = halving(out_keep + far_swap(out_send, half_far).astype(f32), 0, low_bits).T
-
-    grad_tokens, late = keys_back(
-        far_count, early, place, total, received, raw_keys, table, gain_key, partial, grad_residual, tokens, gain_in,
-        grad_queries, grad_gains, grad_gain_post, grad_gain_query, key_pieces,
-    )
-    late = lax.all_to_all(after(late, got, got_down), SQUARE, 0, 0, tiled=True)
-    keep, send, gains = last_products(query_width // 4 + early * block + model // 2, place, got, late, query_part)
-    qkv_total = halving(keep + far_swap(send, half_far).astype(f32), 1, low_bits)
-    gains = add_planes(gains.reshape(-1))
-
+    got_down, got_other, got_own = (far_swap(g, low_bits[0]) for g in (send_down, send_other, send_own))
+    keep_first, send_first = first_products(place, every, heads_out, got_heads, own_right, got)
+    keep_first, send_first = first_cores(place, keep_first, swap(send_first, "core"))
+    got_first = swap(send_first, "chip")
+    grad_tokens, own_right, other_right, gains = keys_back(
+        far_count, early, place, after(total, send_first), received, raw_keys, table, gain_key, partial, grad_residual, tokens, gain_in,
+        grad_queries, grad_gains, grad_gain_post, grad_gain_query, qkv_pieces,
+    )
+    keep, send, gains = last_products(place, every, after(own_right, got_down), swap(other_right, "near"), gains)
+    keep, send, gains = last_cores(place, after(keep, got_other), swap(send, "core"), gains)
+    grad_down = add_down(grad_down, got_down)
+    sums = last_chips(
+        far_count, after(keep_first, got_own), got_first, keep, swap(send, "chip"), gains, query_width // 4
+    )
     columns = model // far_count // 2
     down_parts = halving(grad_down, 1, low_bits[1:]).astype(bf16).reshape(2, 2, columns, -1)
     down_parts = down_parts.transpose(1, 0, 2, 3).reshape(4, columns, -1)
     down_parts = lax.all_to_all(down_parts, ("near", "chip"), 0, 0, tiled=True)
+    other_gates = add_gates(True, place, after(grad_gates, send), got_other)
+    peer_gates = swap(halving(other_gates, 2, low_bits[1:]).astype(bf16), "chip")
+    sums, got_own = lax.optimization_barrier((sums, got_own))
+
+    sums = lax.all_to_all(sums, "far", 0, 0, tiled=True)
+    qkv_total, out_total, gains = last_sum(sums, model // 4, query_width // 4)
+    out_total, gains = out_total.T, gains.reshape(-1)
+    own_gates = halving(add_gates(False, place, grad_gates, got_own), 2, low_bits[1:]).astype(bf16)
+    mine = [lax.dynamic_index_in_dim(g, core, 0, keepdims=False) for g in (own_gates, peer_gates)]
+    theirs = [lax.dynamic_index_in_dim(g, 1 - core, 0, keepdims=False) for g in (own_gates, peer_gates)]
+    gate_total, up_total = gather_gates(place, *mine, *(swap(g, "core") for g in theirs))
     down_total = down_rows(down_parts, part).T
-
-    gate_parts = halving(grad_gates, 2, low_bits[1:]).astype(bf16)
-    gate_parts = lax.all_to_all(gate_parts, DP, 0, 0, tiled=True)
-    gate_parts = gate_parts.reshape(2, 2, -1, part)
-    gate_total = jnp.concatenate([gate_parts[0, 0], gate_parts[1, 0]], axis=1).astype(f32)
-    up_total = jnp.concatenate([gate_parts[0, 1], gate_parts[1, 1]], axis=1).astype(f32)
 
     gain_in, gain_pre, gain_attn, gain_post = (gains[i * model : (i + 1) * model] for i in range(4))
     gain_query, gain_key = gains[4 * model :][:dim], gains[4 * model + dim :][:dim]

time: 360 us -> 324 us (0.900)
  waiting for transfers between devices: 117 us -> 85 us
  Pallas kernels: 110 us -> 118 us
  other arithmetic: 6.83 us -> 0.67 us
  starting transfers between devices: 86.4 us -> 80.3 us
    ppermute x13 -> x7, waiting for transfers between devices: 41.5 us -> 21.2 us  [far_swap(): lax.ppermute(value, 'far', [(i, i ^ step) for i in range(lax.axis_size('f...]
    ppermute x6, waiting for transfers between devices: 17.9 us -> 7.89 us  [shift(): return lax.ppermute(value, 'far', pairs)]
    pallas_call x19 -> x24, Pallas kernels: 110 us -> 118 us  [call(): pl.pallas_call(kernel, out_shape=out_shape, in_specs=in_specs, out_specs=...]
    all_to_all x3 -> x1, starting transfers between devices: 11.4 us -> 3.51 us  [shards(): sums = lax.all_to_all(sums, 'far', 0, 0, tiled=True)]
    all_to_all x3 -> x1, waiting for transfers between devices: 6.67 us -> 2.74 us  [shards(): sums = lax.all_to_all(sums, 'far', 0, 0, tiled=True)]
    unnamed x127 -> x158, local copies, waits for them, and re-layouts: 25.6 us -> 29.3 us
    ppermute x35 -> x41, starting transfers between devices: 30.3 us -> 33.4 us  [swap(): return lax.ppermute(value, axis, [(0, 1), (1, 0)])]
    ppermute x13 -> x7, starting transfers between devices: 15.8 us -> 14.2 us  [far_swap(): lax.ppermute(value, 'far', [(i, i ^ step) for i in range(lax.axis_size('f...]
  transfers between devices with their start and end apart: 64 -> 62, of which waited for: 25 -> 19; matrix products, arithmetic and copies ran while one was open for 4% -> 1% of each run, Pallas kernels for 26% -> 36%
where the time goes in v1:
time: 324 us; the launch traced here: 320 us
  Pallas kernels  118 us (36%)
  waiting for transfers between devices  85 us (26%)
  starting transfers between devices  80.3 us (25%)
  local copies, waits for them, and re-layouts  34.5 us (11%)
    pallas_call x24, Pallas kernels, call(): pl.pallas_call(kernel, out_shape=out_shape, in_specs=in_specs, out_specs=...  118 us
    ppermute x41, waiting for transfers between devices, swap(): return lax.ppermute(value, axis, [(0, 1), (1, 0)])  50 us
    ppermute x41, starting transfers between devices, swap(): return lax.ppermute(value, axis, [(0, 1), (1, 0)])  33.4 us
    unnamed x158, local copies, waits for them, and re-layouts  29.3 us
    ppermute x7, waiting for transfers between devices, far_swap(): lax.ppermute(value, 'far', [(i, i ^ step) for i in range(lax.axis_size('f...  21.2 us
    ppermute x6, starting transfers between devices, shift(): return lax.ppermute(value, 'far', pairs)  17.8 us
    ppermute x7, starting transfers between devices, far_swap(): lax.ppermute(value, 'far', [(i, i ^ step) for i in range(lax.axis_size('f...  14.2 us
    ppermute x6, waiting for transfers between devices, shift(): return lax.ppermute(value, 'far', pairs)  7.89 us
  transfers between devices with their start and end apart: 62, of which 19 were waited for; matrix products, arithmetic and copies ran while one was open for 1% of the time, Pallas kernels for 36%

profile of v1, /device:TPU:0, one launch (start us, length us, event | category | flops | bytes accessed | tf_op | source)
XLA Modules:
  0.0 320.0 jit_solution(6414666847859771080)
XLA Ops:
  0.6 3.0 collective-permute-start.3
  3.7 8.2 %shard_map.237 = (bf16[2,288,1728]{2,1,0:T(8,128)(2,1)}, bf16[144,1728]{1,0:T(8,128)(2,1)S(1)}, bf16[144,1728]{1,0:T(8,128)(2,1)S(1)}) custom-call(s32[6]{0:T(128)S(1)} %stack.29.place, bf16[288,6912]{1,0:T(8,128)(2,1)} %gate.1, bf16[288,6912]{1,0:T(8,128)(2,1)} %up.1), custom_call_target="tpu_custom_call" | custom-call | flops 6000000000 | bytes 1048576 | tf_op jit(solution)/shard_map/pallas_call | solution.py:38
  13.5 2.7 dynamic-slice_bitcast_fusion
  16.8 1.6 collective-permute-start.2
  18.3 7.7 %collective-permute-done.2.peer = bf16[128,1152]{1,0:T(8,128)(2,1)S(1)} collective-permute-done((bf16[128,1152]{1,0:T(8,128)(2,1)S(1)}, bf16[128,1152]{1,0:T(8,128)(2,1)S(1)}, u32[]{:S(2)}, u32[]{:S(2)}) %collective-permute-start.2) | collective-permute-done | bytes 294944 | tf_op jit(solution)/shard_map/ppermute | solution.py:977
  28.5 1.8 collective-permute-start.6
  30.8 13.8 %collective-permute-done.11.o1 = bf16[256,1152]{1,0:T(8,128)(2,1)} collective-permute-done((bf16[256,1152]{1,0:T(8,128)(2,1)}, bf16[256,1152]{1,0:T(8,128)(2,1)}, u32[]{:S(2)}, u32[]{:S(2)}) %collective-permute-start.11) | collective-permute-done | bytes 589856 | tf_op jit(solution)/shard_map/ppermute | solution.py:977
  45.6 3.2 shard_map.238
  52.4 2.4 collective-permute-done.6.refs_2_
  55.3 1.9 collective-permute-start.16
  57.2 4.5 %collective-permute-start.8 = (bf16[2,256,256]{2,1,0:T(8,128)(2,1)}, bf16[2,256,256]{2,1,0:T(8,128)(2,1)S(1)}, u32[]{:S(2)}, u32[]{:S(2)}) collective-permute-start(bf16[2,256,256]{2,1,0:T(8,128)(2,1)} %get-tuple-element.143.kv2), channel_id=1, source_target_pairs={{0,16},{8,24},{1,17},{9,25},{2,18},{10,26},{3,19},{11,27},{4,20},{... | collective-permute-start | bytes 786440 | tf_op jit(solution)/shard_map/ppermute | solution.py:973
  62.2 3.3 %collective-permute-start.9 = (bf16[2,256,256]{2,1,0:T(8,128)(2,1)}, bf16[2,256,256]{2,1,0:T(8,128)(2,1)S(1)}, u32[]{:S(2)}, u32[]{:S(2)}) collective-permute-start(bf16[2,256,256]{2,1,0:T(8,128)(2,1)} %get-tuple-element.143.kv2), channel_id=1, source_target_pairs={{0,8},{8,16},{16,24},{1,9},{9,17},{17,25},{2,10},{10,18},{18,26},{... | collective-permute-start | bytes 786440 | tf_op jit(solution)/shard_map/ppermute | solution.py:973
  66.6 2.7 shard_map.239
  70.1 5.3 %collective-permute-done.8.kv0 = bf16[2,256,256]{2,1,0:T(8,128)(2,1)S(1)} collective-permute-done((bf16[2,256,256]{2,1,0:T(8,128)(2,1)}, bf16[2,256,256]{2,1,0:T(8,128)(2,1)S(1)}, u32[]{:S(2)}, u32[]{:S(2)}) %collective-permute-start.8) | collective-permute-done | bytes 262176 | tf_op jit(solution)/shard_map/ppermute | solution.py:973
  75.4 1.5 collective-permute-start.18
  76.9 2.0 collective-permute-done.9.kv1
  79.0 6.1 %shard_map.240 = (f32[512,1024]{1,0:T(8,128)}, bf16[128,1024]{1,0:T(8,128)(2,1)S(1)}, f32[128,1152]{1,0:T(8,128)S(1)}, f32[128,1152]{1,0:T(8,128)S(1)}, bf16[128,1152]{1,0:T(8,128)(2,1)S(1)}) custom-call(s32[6]{0:T(128)S(1)} %stack.29.place, bf16[512,256]{1,0:T(8,128)(2,1)S(1)} %get-tuple-element.142.queries.h_queries, ...), custom_call_target="tpu_custom_call" | custom-call | flops 5000000000 | bytes 1048576 | tf_op jit(solution)/shard_map/pallas_call | solution.py:38
  85.9 2.5 collective-permute-start.17
  89.2 1.6 collective-permute-start.19
  90.9 1.6 collective-permute-start.13
  92.4 1.5 collective-permute-start.14
  93.9 6.2 %collective-permute-done.17.n0 = bf16[128,1152]{1,0:T(8,128)(2,1)S(1)} collective-permute-done((bf16[128,1152]{1,0:T(8,128)(2,1)S(1)}, bf16[128,1152]{1,0:T(8,128)(2,1)S(1)}, u32[]{:S(2)}, u32[]{:S(2)}) %collective-permute-start.17) | collective-permute-done | bytes 294944 | tf_op jit(solution)/shard_map/ppermute | solution.py:989
  100.2 2.5 collective-permute-start.15
  102.7 2.0 collective-permute-done.14.x2
  104.7 3.2 collective-permute-done.15.x3
  108.3 1.5 collective-permute-start.26
  109.8 1.5 collective-permute-start.27
  113.2 13.8 %shard_map.241 = (bf16[512,1152]{1,0:T(8,128)(2,1)}, bf16[512,1728]{1,0:T(8,128)(2,1)}, bf16[512,1728]{1,0:T(8,128)(2,1)}, bf16[512,1728]{1,0:T(8,128)(2,1)}, f3...) custom-call(s32[6]{0:T(128)S(1)} %stack.29.place, ...), custom_call_target="tpu_custom_call" | custom-call | flops 12999999488 | bytes 1048576 | tf_op jit(solution)/shard_map/pallas_call | solution.py:38
  128.3 1.5 collective-permute-start.30
  130.6 6.4 %collective-permute-done.29.r1 = bf16[128,1152]{1,0:T(8,128)(2,1)S(1)} collective-permute-done((bf16[128,1152]{1,0:T(8,128)(2,1)S(1)}, bf16[128,1152]{1,0:T(8,128)(2,1)S(1)}, u32[]{:S(2)}, u32[]{:S(2)}) %collective-permute-start.29) | collective-permute-done | bytes 294944 | tf_op jit(solution)/shard_map/ppermute | solution.py:977
  137.0 5.4 %collective-permute-done.30.r2 = bf16[128,1152]{1,0:T(8,128)(2,1)S(1)} collective-permute-done((bf16[128,1152]{1,0:T(8,128)(2,1)S(1)}, bf16[128,1152]{1,0:T(8,128)(2,1)S(1)}, u32[]{:S(2)}, u32[]{:S(2)}) %collective-permute-start.30) | collective-permute-done | bytes 294944 | tf_op jit(solution)/shard_map/ppermute | solution.py:977
  145.4 1.5 collective-permute-start.32
  147.5 1.4 collective-permute-start.34
  148.9 2.5 collective-permute-start.35
  151.4 11.5 %shard_map.243 = (bf16[512,1728]{1,0:T(8,128)(2,1)}, bf16[512,960]{1,0:T(8,128)(2,1)}, bf16[512,960]{1,0:T(8,128)(2,1)}) custom-call(s32[6]{0:T(128)S(1)} %stack.29.place, bf16[128,1152]{1,0:T(8,128)(2,1)S(1)} %collective-permute-done.17.n0, bf16[128,1152]{1,0:T(8,128)(2,1)S(1)} %collective-permute-done.26.n1, ...), custom_call_target="tpu_custom_call" | custom-call | flops 11000000512 | bytes 1048576 | tf_op jit(solution)/shard_map/pallas_call | solution.py:38
  163.0 1.4 collective-permute-start.36
  166.5 15.0 %shard_map.244 = (bf16[512,1152]{1,0:T(8,128)(2,1)}, bf16[512,1728]{1,0:T(8,128)(2,1)}, bf16[512,1728]{1,0:T(8,128)(2,1)}, f32[128,1152]{1,0:T(8,128)}, bf16[128...) custom-call(s32[6]{0:T(128)S(1)} %stack.29.place, ...), custom_call_target="tpu_custom_call" | custom-call | flops 15000000512 | bytes 1048576 | tf_op jit(solution)/shard_map/pallas_call | solution.py:38
  181.6 1.4 collective-permute-start.39
  185.1 21.7 %shard_map.245 = (bf16[2,432,1792]{2,1,0:T(8,128)(2,1)}, bf16[2,432,1792]{2,1,0:T(8,128)(2,1)}) custom-call(s32[6]{0:T(128)S(1)} %stack.29.place, bf16[512,1152]{1,0:T(8,128)(2,1)} %get-tuple-element.185.normed, bf16[512,1152]{1,0:T(8,128)(2,1)} %get-tuple-element.186.down, bf16[512,1728]{1,0:T(8,128)(2,1)} %get-tuple-element.187.hidden, ...), custom_call_target="tpu_custom_call" | custom-call | flops 16000000000 | bytes 1048576 | tf_op jit(solution)/shard_map/pallas_call | solution.py:38
  207.7 10.8 %shard_map.246 = (f32[128,1152]{1,0:T(8,128)}, bf16[128,960]{1,0:T(8,128)(2,1)}, bf16[128,960]{1,0:T(8,128)(2,1)}, f32[2,1152]{1,0:T(2,128)}, f32[1,256]{1,0:T(1...) custom-call(s32[6]{0:T(128)} %copy-done.6, ...), custom_call_target="tpu_custom_call" | custom-call | flops 8000000000 | bytes 1048576 | tf_op jit(solution)/shard_map/pallas_call | solution.py:38
  218.6 1.5 collective-permute-start.47
  222.6 6.1 %collective-permute-start.45 = (bf16[2,256,256]{2,1,0:T(8,128)(2,1)}, bf16[2,256,256]{2,1,0:T(8,128)(2,1)S(1)}, u32[]{:S(2)}, u32[]{:S(2)}) collective-permute-start(bf16[2,256,256]{2,1,0:T(8,128)(2,1)} %get-tuple-element.208), channel_id=1, source_target_pairs={{0,8},{8,16},{16,24},{1,9},{9,17},{17,25},{2,10},{10,18},{18,26},{... | collective-permute-start | bytes 786440 | tf_op jit(solution)/shard_map/ppermute | solution.py:973
  229.4 4.5 %shard_map.247 = (f32[432,1152]{1,0:T(8,128)S(1)}, bf16[432,576]{1,0:T(8,128)(2,1)S(1)}, bf16[432,576]{1,0:T(8,128)(2,1)S(1)}, f32[2,288,432]{2,1,0:T(8,128)S(1)}, bf16[2,288,432]{2,1,0:T(8,128)(2,1)S(1)}) custom-call(s32[6]{0:T(128)S(1)} %copy-done.7, bf16[2,432,1792]{2,1,0:T(8,128)(2,1)} %get-tuple-element.201.keep, ...), custom_call_target="tpu_custom_call" | custom-call | flops 4000000000 | bytes 1048576 | tf_op jit(solution)/shard_map/pallas_call | solution.py:38
  235.7 1.3 copy-done.44
  237.0 2.9 shard_map.248.partial
  240.2 1.6 shard_map.249
  241.9 1.3 copy-done.42
  243.2 2.5 collective-permute-start.52
  246.8 1.6 copy-done.43
  248.4 1.6 shard_map.250
  251.5 3.5 %shard_map.251 = (f32[128,1152]{1,0:T(8,128)}, bf16[128,384]{1,0:T(8,128)(2,1)S(1)}, bf16[144,384]{1,0:T(8,128)(2,1)S(1)}, f32[16,384]{1,0:T(8,128)S(1)}) custom-call(s32[6]{0:T(128)S(1)} %copy-done.7, f32[2,256,256]{2,1,0:T(8,128)S(1)} %convert_add_fusion.total, bf16[2,128,256]{2,1,0:T(8,128)(2,1)S(1)} %collective-permute-done.49.received, ...), custom_call_target="tpu_custom_call" | custom-call | flops 4000000000 | bytes 1048576 | tf_op jit(solution)/shard_map/pallas_call | solution.py:38
  257.3 2.6 collective-permute-done.52.got
  262.2 1.9 collective-permute-start.50
  264.2 7.6 %collective-permute-done.54.got = bf16[432,576]{1,0:T(8,128)(2,1)S(1)} collective-permute-done((bf16[432,576]{1,0:T(8,128)(2,1)S(1)}, bf16[432,576]{1,0:T(8,128)(2,1)S(1)}, u32[]{:S(2)}, u32[]{:S(2)}) %collective-permute-start.54) | collective-permute-done | bytes 497696 | tf_op jit(solution)/shard_map/ppermute | solution.py:989
  275.2 3.5 %all-to-all-start.1 = ((bf16[4,144,432]{2,1,0:T(8,128)(2,1)}), bf16[4,144,432]{2,1,0:T(8,128)(2,1)S(1)}, u32[]{:S(2)}, u32[]{:S(2)}) async-start(bf16[4,144,432]{2,1,0:T(8,128)(2,1)} %bitcast.43), calls=%async_computation.1 | async-start | bytes 1179648 | tf_op jit(solution)/shard_map/all_to_all | solution.py:1138
  278.7 4.7 %collective-permute-done.50.got = bf16[432,576]{1,0:T(8,128)(2,1)S(1)} collective-permute-done((bf16[432,576]{1,0:T(8,128)(2,1)S(1)}, bf16[432,576]{1,0:T(8,128)(2,1)S(1)}, u32[]{:S(2)}, u32[]{:S(2)}) %collective-permute-start.50) | collective-permute-done | bytes 497696 | tf_op jit(solution)/shard_map/ppermute | solution.py:989
  288.1 1.3 shard_map.254
  289.4 3.5 %all-to-all-start = ((bf16[4,320,320]{2,1,0:T(8,128)(2,1)}), bf16[4,320,320]{2,1,0:T(8,128)(2,1)S(1)}, u32[]{:S(2)}, u32[]{:S(2)}) async-start(bf16[4,320,320]{2,1,0:T(8,128)(2,1)} %shard_map.254), calls=%async_computation | async-start | bytes 1966080 | tf_op jit(solution)/shard_map/all_to_all | solution.py:1143
  293.0 1.5 copy-done.45
  294.5 1.3 shard_map.257
  298.1 1.6 copy-done.46
  300.6 10.5 %collective-permute-done.57 = bf16[2,288,432]{2,1,0:T(8,128)(2,1)S(1)} collective-permute-done((bf16[2,288,432]{2,1,0:T(8,128)(2,1)S(1)}, bf16[2,288,432]{2,1,0:T(8,128)(2,1)S(1)}, u32[]{:S(2)}, u32[]{:S(2)}) %collective-permute-start.57) | collective-permute-done | bytes 497696 | tf_op jit(solution)/shard_map/ppermute | solution.py:977
  312.7 2.1 shard_map.258
  314.8 2.7 all-to-all-done.parts
  (263 shorter events, 54.6 us)
Async XLA Ops:
  0.6 26.1 %collective-permute-start.3 = (bf16[288,1536]{1,0:T(8,128)(2,1)}, bf16[288,1536]{1,0:T(8,128)(2,1)}, u32[]{:S(2)}, u32[]{:S(2)}) collective-permute-start(bf16[288,1536]{1,0:T(8,128)(2,1)} %k0.3), channel_id=1, source_target_pairs={{0,2},{2,0},{1,3},{3,1},{4,6},{6,4},{5,7},{7,5},{8,10},{10,8},{9,1... | collective-permute-start | bytes 2654216 | tf_op jit(solution)/shard_map/ppermute | solution.py:977
  3.7 181.4 %copy-start.6 = (s32[6]{0:T(128)}, s32[6]{0:T(128)S(1)}, u32[]{:S(2)}) copy-start(s32[6]{0:T(128)S(1)} %stack.29.place) | copy-start | bytes 76
  13.5 43.7 %collective-permute-start.7 = (bf16[2,288,1728]{2,1,0:T(8,128)(2,1)}, bf16[2,288,1728]{2,1,0:T(8,128)(2,1)}, u32[]{:S(2)}, u32[]{:S(2)}) collective-permute-start(bf16[2,288,1728]{2,1,0:T(8,128)(2,1)} %get-tuple-element.136.refs_0_), channel_id=1, source_target_pairs={{0,1},{1,0},{2,3},{3,2},{4,5},{5,4},{6,7},{7,6},{8,9},{9,8},{10,11... | collective-permute-start | bytes 5971976 | tf_op jit(solution)/shard_map/ppermute | solution.py:977
  16.2 12.2 %collective-permute-start = (bf16[432,1152]{1,0:T(8,128)(2,1)S(1)}, bf16[432,1152]{1,0:T(8,128)(2,1)S(1)}, u32[]{:S(2)}, u32[]{:S(2)}) collective-permute-start(bf16[432,1152]{1,0:T(8,128)(2,1)S(1)} %get-tuple-element.260.refs_10_.refs_0_), channel_id=1, source_target_pairs={{0,1},{1,0},{2,3},{3,2},{4,5},{5,4},{6,7},{7,6},{8,9},{9,8},{10,11... | collective-permute-start | bytes 2985992 | tf_op jit(solution)/shard_map/ppermute | solution.py:977
  16.6 10.7 %collective-permute-start.1 = (bf16[256,1152]{1,0:T(8,128)(2,1)}, bf16[256,1152]{1,0:T(8,128)(2,1)S(1)}, u32[]{:S(2)}, u32[]{:S(2)}) collective-permute-start(bf16[256,1152]{1,0:T(8,128)(2,1)} %o0.3), channel_id=1, source_target_pairs={{0,1},{1,0},{2,3},{3,2},{4,5},{5,4},{6,7},{7,6},{8,9},{9,8},{10,11... | collective-permute-start | bytes 1769480 | tf_op jit(solution)/shard_map/ppermute | solution.py:977
  16.8 9.3 %collective-permute-start.2 = (bf16[128,1152]{1,0:T(8,128)(2,1)S(1)}, bf16[128,1152]{1,0:T(8,128)(2,1)S(1)}, u32[]{:S(2)}, u32[]{:S(2)}) collective-permute-start(bf16[128,1152]{1,0:T(8,128)(2,1)S(1)} %bitcast.35), channel_id=1, source_target_pairs={{0,4},{4,0},{1,5},{5,1},{2,6},{6,2},{3,7},{7,3},{8,12},{12,8},{9,1... | collective-permute-start | bytes 884744 | tf_op jit(solution)/shard_map/ppermute | solution.py:977
  26.8 17.8 %collective-permute-start.4 = (bf16[288,1536]{1,0:T(8,128)(2,1)S(1)}, bf16[288,1536]{1,0:T(8,128)(2,1)}, u32[]{:S(2)}, u32[]{:S(2)}) collective-permute-start(bf16[288,1536]{1,0:T(8,128)(2,1)S(1)} %copy-done.12), channel_id=1, source_target_pairs={{0,1},{1,0},{2,3},{3,2},{4,5},{5,4},{6,7},{7,6},{8,9},{9,8},{10,11... | collective-permute-start | bytes 2654216 | tf_op jit(solution)/shard_map/ppermute | solution.py:977
  26.8 17.8 %collective-permute-start.5 = (bf16[288,1536]{1,0:T(8,128)(2,1)}, bf16[288,1536]{1,0:T(8,128)(2,1)}, u32[]{:S(2)}, u32[]{:S(2)}) collective-permute-start(bf16[288,1536]{1,0:T(8,128)(2,1)} %collective-permute-done.3.k1.q1), channel_id=1, source_target_pairs={{0,1},{1,0},{2,3},{3,2},{4,5},{5,4},{6,7},{7,6},{8,9},{9,8},{10,11... | collective-permute-start | bytes 2654216 | tf_op jit(solution)/shard_map/ppermute | solution.py:977
  28.1 16.5 %collective-permute-start.11 = (bf16[256,1152]{1,0:T(8,128)(2,1)}, bf16[256,1152]{1,0:T(8,128)(2,1)}, u32[]{:S(2)}, u32[]{:S(2)}) collective-permute-start(bf16[256,1152]{1,0:T(8,128)(2,1)} %o0.3), channel_id=1, source_target_pairs={{0,2},{2,0},{1,3},{3,1},{4,6},{6,4},{5,7},{7,5},{8,10},{10,8},{9,1... | collective-permute-start | bytes 1769480 | tf_op jit(solution)/shard_map/ppermute | solution.py:977
  28.5 26.3 %collective-permute-start.6 = (bf16[144,1728]{1,0:T(8,128)(2,1)}, bf16[144,1728]{1,0:T(8,128)(2,1)}, u32[]{:S(2)}, u32[]{:S(2)}) collective-permute-start(bf16[144,1728]{1,0:T(8,128)(2,1)} %copy-done.26), channel_id=1, source_target_pairs={{0,2},{2,0},{1,3},{3,1},{4,6},{6,4},{5,7},{7,5},{8,10},{10,8},{9,1... | collective-permute-start | bytes 1493000 | tf_op jit(solution)/shard_map/ppermute | solution.py:977
  44.6 34.3 %collective-permute-start.12 = (bf16[256,1152]{1,0:T(8,128)(2,1)}, bf16[256,1152]{1,0:T(8,128)(2,1)}, u32[]{:S(2)}, u32[]{:S(2)}) collective-permute-start(bf16[256,1152]{1,0:T(8,128)(2,1)} %collective-permute-done.11.o1), channel_id=1, source_target_pairs={{0,1},{1,0},{2,3},{3,2},{4,5},{5,4},{6,7},{7,6},{8,9},{9,8},{10,11... | collective-permute-start | bytes 1769480 | tf_op jit(solution)/shard_map/ppermute | solution.py:977
  51.1 11.2 %collective-permute-start.10 = (bf16[2,256,256]{2,1,0:T(8,128)(2,1)}, bf16[2,256,256]{2,1,0:T(8,128)(2,1)S(1)}, u32[]{:S(2)}, u32[]{:S(2)}) collective-permute-start(bf16[2,256,256]{2,1,0:T(8,128)(2,1)} %get-tuple-element.143.kv2), channel_id=1, source_target_pairs={{8,0},{16,8},{24,16},{9,1},{17,9},{25,17},{10,2},{18,10},{26,18},{... | collective-permute-start | bytes 786440 | tf_op jit(solution)/shard_map/ppermute | solution.py:973
  54.8 36.0 %collective-permute-start.24 = (bf16[432,1152]{1,0:T(8,128)(2,1)}, bf16[432,1152]{1,0:T(8,128)(2,1)S(1)}, u32[]{:S(2)}, u32[]{:S(2)}) collective-permute-start(bf16[432,1152]{1,0:T(8,128)(2,1)} %get-tuple-element.153), channel_id=1, source_target_pairs={{0,2},{2,0},{1,3},{3,1},{4,6},{6,4},{5,7},{7,5},{8,10},{10,8},{9,1... | collective-permute-start | bytes 2985992 | tf_op jit(solution)/shard_map/ppermute | solution.py:977
  55.3 30.6 %collective-permute-start.16 = (bf16[144,1728]{1,0:T(8,128)(2,1)}, bf16[144,1728]{1,0:T(8,128)(2,1)S(1)}, u32[]{:S(2)}, u32[]{:S(2)}) collective-permute-start(bf16[144,1728]{1,0:T(8,128)(2,1)} %collective-permute-done.6.refs_2_), channel_id=1, source_target_pairs={{0,8},{8,0},{16,24},{24,16},{1,9},{9,1},{17,25},{25,17},{2,10},{10... | collective-permute-start | bytes 1493000 | tf_op jit(solution)/shard_map/ppermute | solution.py:989
  57.2 18.2 %collective-permute-start.8 = (bf16[2,256,256]{2,1,0:T(8,128)(2,1)}, bf16[2,256,256]{2,1,0:T(8,128)(2,1)S(1)}, u32[]{:S(2)}, u32[]{:S(2)}) collective-permute-start(bf16[2,256,256]{2,1,0:T(8,128)(2,1)} %get-tuple-element.143.kv2), channel_id=1, source_target_pairs={{0,16},{8,24},{1,17},{9,25},{2,18},{10,26},{3,19},{11,27},{4,20},{... | collective-permute-start | bytes 786440 | tf_op jit(solution)/shard_map/ppermute | solution.py:973
  62.2 16.7 %collective-permute-start.9 = (bf16[2,256,256]{2,1,0:T(8,128)(2,1)}, bf16[2,256,256]{2,1,0:T(8,128)(2,1)S(1)}, u32[]{:S(2)}, u32[]{:S(2)}) collective-permute-start(bf16[2,256,256]{2,1,0:T(8,128)(2,1)} %get-tuple-element.143.kv2), channel_id=1, source_target_pairs={{0,8},{8,16},{16,24},{1,9},{9,17},{17,25},{2,10},{10,18},{18,26},{... | collective-permute-start | bytes 786440 | tf_op jit(solution)/shard_map/ppermute | solution.py:973
  75.4 13.8 %collective-permute-start.18 = (bf16[144,1728]{1,0:T(8,128)(2,1)S(1)}, bf16[144,1728]{1,0:T(8,128)(2,1)S(1)}, u32[]{:S(2)}, u32[]{:S(2)}) collective-permute-start(bf16[144,1728]{1,0:T(8,128)(2,1)S(1)} %copy-done.25), channel_id=1, source_target_pairs={{0,2},{2,0},{1,3},{3,1},{4,6},{6,4},{5,7},{7,5},{8,10},{10,8},{9,1... | collective-permute-start | bytes 1493000 | tf_op jit(solution)/shard_map/ppermute | solution.py:977
  85.9 56.5 %copy-start.27 = (bf16[1,128,1152]{2,1,0:T(8,128)(2,1)S(1)}, bf16[1,128,1152]{2,1,0:T(8,128)(2,1)}, u32[]{:S(2)}) copy-start(bf16[1,128,1152]{2,1,0:T(8,128)(2,1)} %param.27) | copy-start | bytes 884740
  85.9 14.3 %collective-permute-start.17 = (bf16[128,1152]{1,0:T(8,128)(2,1)S(1)}, bf16[128,1152]{1,0:T(8,128)(2,1)S(1)}, u32[]{:S(2)}, u32[]{:S(2)}) collective-permute-start(bf16[128,1152]{1,0:T(8,128)(2,1)S(1)} %get-tuple-element.147.x0), channel_id=1, source_target_pairs={{0,16},{8,24},{16,0},{24,8},{1,17},{9,25},{17,1},{25,9},{2,18},{10... | collective-permute-start | bytes 884744 | tf_op jit(solution)/shard_map/ppermute | solution.py:989
  89.2 18.6 %collective-permute-start.19 = (bf16[144,1728]{1,0:T(8,128)(2,1)S(1)}, bf16[144,1728]{1,0:T(8,128)(2,1)S(1)}, u32[]{:S(2)}, u32[]{:S(2)}) collective-permute-start(bf16[144,1728]{1,0:T(8,128)(2,1)S(1)} %collective-permute-done.18.refs_3_), channel_id=1, source_target_pairs={{0,8},{8,0},{16,24},{24,16},{1,9},{9,1},{17,25},{25,17},{2,10},{10... | collective-permute-start | bytes 1493000 | tf_op jit(solution)/shard_map/ppermute | solution.py:989
  90.8 21.3 %collective-permute-start.25 = (bf16[432,1152]{1,0:T(8,128)(2,1)S(1)}, bf16[432,1152]{1,0:T(8,128)(2,1)S(1)}, u32[]{:S(2)}, u32[]{:S(2)}) collective-permute-start(bf16[432,1152]{1,0:T(8,128)(2,1)S(1)} %collective-permute-done.24.refs_11_.refs_1_), channel_id=1, source_target_pairs={{0,1},{1,0},{2,3},{3,2},{4,5},{5,4},{6,7},{7,6},{8,9},{9,8},{10,11... | collective-permute-start | bytes 2985992 | tf_op jit(solution)/shard_map/ppermute | solution.py:977
  90.9 11.8 %collective-permute-start.13 = (bf16[128,1152]{1,0:T(8,128)(2,1)S(1)}, bf16[128,1152]{1,0:T(8,128)(2,1)S(1)}, u32[]{:S(2)}, u32[]{:S(2)}) collective-permute-start(bf16[128,1152]{1,0:T(8,128)(2,1)S(1)} %get-tuple-element.147.x0), channel_id=1, source_target_pairs={{0,2},{2,0},{1,3},{3,1},{4,6},{6,4},{5,7},{7,5},{8,10},{10,8},{9,1... | collective-permute-start | bytes 884744 | tf_op jit(solution)/shard_map/ppermute | solution.py:977
  92.4 12.2 %collective-permute-start.14 = (bf16[128,1152]{1,0:T(8,128)(2,1)S(1)}, bf16[128,1152]{1,0:T(8,128)(2,1)S(1)}, u32[]{:S(2)}, u32[]{:S(2)}) collective-permute-start(bf16[128,1152]{1,0:T(8,128)(2,1)S(1)} %get-tuple-element.147.x0), channel_id=1, source_target_pairs={{0,4},{4,0},{1,5},{5,1},{2,6},{6,2},{3,7},{7,3},{8,12},{12,8},{9,1... | collective-permute-start | bytes 884744 | tf_op jit(solution)/shard_map/ppermute | solution.py:977
  100.2 7.6 %collective-permute-start.15 = (bf16[128,1152]{1,0:T(8,128)(2,1)S(1)}, bf16[128,1152]{1,0:T(8,128)(2,1)S(1)}, u32[]{:S(2)}, u32[]{:S(2)}) collective-permute-start(bf16[128,1152]{1,0:T(8,128)(2,1)S(1)} %get-tuple-element.147.x0), channel_id=1, source_target_pairs={{0,6},{2,4},{4,2},{6,0},{1,7},{3,5},{5,3},{7,1},{8,14},{10,12},{12... | collective-permute-start | bytes 884744 | tf_op jit(solution)/shard_map/ppermute | solution.py:981
  102.6 5.7 %collective-permute-start.20 = (bf16[144,1728]{1,0:T(8,128)(2,1)}, bf16[144,1728]{1,0:T(8,128)(2,1)S(1)}, u32[]{:S(2)}, u32[]{:S(2)}) collective-permute-start(bf16[144,1728]{1,0:T(8,128)(2,1)} %collective-permute-done.6.refs_2_), channel_id=1, source_target_pairs={{0,1},{1,0},{2,3},{3,2},{4,5},{5,4},{6,7},{7,6},{8,9},{9,8},{10,11... | collective-permute-start | bytes 1493000 | tf_op jit(solution)/shard_map/ppermute | solution.py:977
  104.6 5.2 %collective-permute-start.22 = (bf16[144,1728]{1,0:T(8,128)(2,1)S(1)}, bf16[144,1728]{1,0:T(8,128)(2,1)S(1)}, u32[]{:S(2)}, u32[]{:S(2)}) collective-permute-start(bf16[144,1728]{1,0:T(8,128)(2,1)S(1)} %collective-permute-done.16.refs_4_), channel_id=1, source_target_pairs={{0,1},{1,0},{2,3},{3,2},{4,5},{5,4},{6,7},{7,6},{8,9},{9,8},{10,11... | collective-permute-start | bytes 1493000 | tf_op jit(solution)/shard_map/ppermute | solution.py:977
  107.8 3.5 %collective-permute-start.21 = (bf16[144,1728]{1,0:T(8,128)(2,1)S(1)}, bf16[144,1728]{1,0:T(8,128)(2,1)S(1)}, u32[]{:S(2)}, u32[]{:S(2)}) collective-permute-start(bf16[144,1728]{1,0:T(8,128)(2,1)S(1)} %collective-permute-done.18.refs_3_), channel_id=1, source_target_pairs={{0,1},{1,0},{2,3},{3,2},{4,5},{5,4},{6,7},{7,6},{8,9},{9,8},{10,11... | collective-permute-start | bytes 1493000 | tf_op jit(solution)/shard_map/ppermute | solution.py:977
  107.8 4.4 %collective-permute-start.23 = (bf16[144,1728]{1,0:T(8,128)(2,1)S(1)}, bf16[144,1728]{1,0:T(8,128)(2,1)S(1)}, u32[]{:S(2)}, u32[]{:S(2)}) collective-permute-start(bf16[144,1728]{1,0:T(8,128)(2,1)S(1)} %collective-permute-done.19.refs_5_), channel_id=1, source_target_pairs={{0,1},{1,0},{2,3},{3,2},{4,5},{5,4},{6,7},{7,6},{8,9},{9,8},{10,11... | collective-permute-start | bytes 1493000 | tf_op jit(solution)/shard_map/ppermute | solution.py:977
  108.3 18.7 %collective-permute-start.26 = (bf16[128,1152]{1,0:T(8,128)(2,1)S(1)}, bf16[128,1152]{1,0:T(8,128)(2,1)S(1)}, u32[]{:S(2)}, u32[]{:S(2)}) collective-permute-start(bf16[128,1152]{1,0:T(8,128)(2,1)S(1)} %collective-permute-done.17.n0), channel_id=1, source_target_pairs={{0,2},{2,0},{1,3},{3,1},{4,6},{6,4},{5,7},{7,5},{8,10},{10,8},{9,1... | collective-permute-start | bytes 884744 | tf_op jit(solution)/shard_map/ppermute | solution.py:977
  109.8 17.2 %collective-permute-start.27 = (bf16[128,1152]{1,0:T(8,128)(2,1)S(1)}, bf16[128,1152]{1,0:T(8,128)(2,1)S(1)}, u32[]{:S(2)}, u32[]{:S(2)}) collective-permute-start(bf16[128,1152]{1,0:T(8,128)(2,1)S(1)} %collective-permute-done.17.n0), channel_id=1, source_target_pairs={{0,4},{4,0},{1,5},{5,1},{2,6},{6,2},{3,7},{7,3},{8,12},{12,8},{9,1... | collective-permute-start | bytes 884744 | tf_op jit(solution)/shard_map/ppermute | solution.py:977
  111.4 15.7 %collective-permute-start.28 = (bf16[128,1152]{1,0:T(8,128)(2,1)S(1)}, bf16[128,1152]{1,0:T(8,128)(2,1)S(1)}, u32[]{:S(2)}, u32[]{:S(2)}) collective-permute-start(bf16[128,1152]{1,0:T(8,128)(2,1)S(1)} %collective-permute-done.17.n0), channel_id=1, source_target_pairs={{0,6},{2,4},{4,2},{6,0},{1,7},{3,5},{5,3},{7,1},{8,14},{10,12},{12... | collective-permute-start | bytes 884744 | tf_op jit(solution)/shard_map/ppermute | solution.py:981
  127.0 10.0 %collective-permute-start.29 = (bf16[128,1152]{1,0:T(8,128)(2,1)S(1)}, bf16[128,1152]{1,0:T(8,128)(2,1)S(1)}, u32[]{:S(2)}, u32[]{:S(2)}) collective-permute-start(bf16[128,1152]{1,0:T(8,128)(2,1)S(1)} %get-tuple-element.159), channel_id=1, source_target_pairs={{0,2},{2,0},{1,3},{3,1},{4,6},{6,4},{5,7},{7,5},{8,10},{10,8},{9,1... | collective-permute-start | bytes 884744 | tf_op jit(solution)/shard_map/ppermute | solution.py:977
  128.3 14.2 %collective-permute-start.30 = (bf16[128,1152]{1,0:T(8,128)(2,1)S(1)}, bf16[128,1152]{1,0:T(8,128)(2,1)S(1)}, u32[]{:S(2)}, u32[]{:S(2)}) collective-permute-start(bf16[128,1152]{1,0:T(8,128)(2,1)S(1)} %get-tuple-element.160), channel_id=1, source_target_pairs={{0,4},{4,0},{1,5},{5,1},{2,6},{6,2},{3,7},{7,3},{8,12},{12,8},{9,1... | collective-permute-start | bytes 884744 | tf_op jit(solution)/shard_map/ppermute | solution.py:977
  129.8 12.7 %collective-permute-start.31 = (bf16[128,1152]{1,0:T(8,128)(2,1)S(1)}, bf16[128,1152]{1,0:T(8,128)(2,1)S(1)}, u32[]{:S(2)}, u32[]{:S(2)}) collective-permute-start(bf16[128,1152]{1,0:T(8,128)(2,1)S(1)} %get-tuple-element.161), channel_id=1, source_target_pairs={{0,6},{2,4},{4,2},{6,0},{1,7},{3,5},{5,3},{7,1},{8,14},{10,12},{12... | collective-permute-start | bytes 884744 | tf_op jit(solution)/shard_map/ppermute | solution.py:981
  145.4 17.5 %collective-permute-start.32 = (bf16[128,1152]{1,0:T(8,128)(2,1)S(1)}, bf16[128,1152]{1,0:T(8,128)(2,1)S(1)}, u32[]{:S(2)}, u32[]{:S(2)}) collective-permute-start(bf16[128,1152]{1,0:T(8,128)(2,1)S(1)} %get-tuple-element.172.x0), channel_id=1, source_target_pairs={{0,2},{2,0},{1,3},{3,1},{4,6},{6,4},{5,7},{7,5},{8,10},{10,8},{9,1... | collective-permute-start | bytes 884744 | tf_op jit(solution)/shard_map/ppermute | solution.py:977
  146.9 16.0 %collective-permute-start.33 = (bf16[128,1152]{1,0:T(8,128)(2,1)S(1)}, bf16[128,1152]{1,0:T(8,128)(2,1)S(1)}, u32[]{:S(2)}, u32[]{:S(2)}) collective-permute-start(bf16[128,1152]{1,0:T(8,128)(2,1)S(1)} %get-tuple-element.172.x0), channel_id=1, source_target_pairs={{0,4},{4,0},{1,5},{5,1},{2,6},{6,2},{3,7},{7,3},{8,12},{12,8},{9,1... | collective-permute-start | bytes 884744 | tf_op jit(solution)/shard_map/ppermute | solution.py:977
  147.5 15.5 %collective-permute-start.34 = (bf16[128,1152]{1,0:T(8,128)(2,1)S(1)}, bf16[128,1152]{1,0:T(8,128)(2,1)S(1)}, u32[]{:S(2)}, u32[]{:S(2)}) collective-permute-start(bf16[128,1152]{1,0:T(8,128)(2,1)S(1)} %get-tuple-element.172.x0), channel_id=1, source_target_pairs={{0,6},{2,4},{4,2},{6,0},{1,7},{3,5},{5,3},{7,1},{8,14},{10,12},{12... | collective-permute-start | bytes 884744 | tf_op jit(solution)/shard_map/ppermute | solution.py:981
  148.9 14.0 %collective-permute-start.35 = (bf16[128,1152]{1,0:T(8,128)(2,1)S(1)}, bf16[128,1152]{1,0:T(8,128)(2,1)S(1)}, u32[]{:S(2)}, u32[]{:S(2)}) collective-permute-start(bf16[128,1152]{1,0:T(8,128)(2,1)S(1)} %get-tuple-element.172.x0), channel_id=1, source_target_pairs={{0,16},{8,24},{16,0},{24,8},{1,17},{9,25},{17,1},{25,9},{2,18},{10... | collective-permute-start | bytes 884744 | tf_op jit(solution)/shard_map/ppermute | solution.py:989
  163.0 18.6 %collective-permute-start.36 = (bf16[128,1152]{1,0:T(8,128)(2,1)S(1)}, bf16[128,1152]{1,0:T(8,128)(2,1)S(1)}, u32[]{:S(2)}, u32[]{:S(2)}) collective-permute-start(bf16[128,1152]{1,0:T(8,128)(2,1)S(1)} %collective-permute-done.35.d0), channel_id=1, source_target_pairs={{0,2},{2,0},{1,3},{3,1},{4,6},{6,4},{5,7},{7,5},{8,10},{10,8},{9,1... | collective-permute-start | bytes 884744 | tf_op jit(solution)/shard_map/ppermute | solution.py:977
  164.3 17.2 %collective-permute-start.37 = (bf16[128,1152]{1,0:T(8,128)(2,1)S(1)}, bf16[128,1152]{1,0:T(8,128)(2,1)S(1)}, u32[]{:S(2)}, u32[]{:S(2)}) collective-permute-start(bf16[128,1152]{1,0:T(8,128)(2,1)S(1)} %collective-permute-done.35.d0), channel_id=1, source_target_pairs={{0,4},{4,0},{1,5},{5,1},{2,6},{6,2},{3,7},{7,3},{8,12},{12,8},{9,1... | collective-permute-start | bytes 884744 | tf_op jit(solution)/shard_map/ppermute | solution.py:977
  165.3 16.2 %collective-permute-start.38 = (bf16[128,1152]{1,0:T(8,128)(2,1)S(1)}, bf16[128,1152]{1,0:T(8,128)(2,1)S(1)}, u32[]{:S(2)}, u32[]{:S(2)}) collective-permute-start(bf16[128,1152]{1,0:T(8,128)(2,1)S(1)} %collective-permute-done.35.d0), channel_id=1, source_target_pairs={{0,6},{2,4},{4,2},{6,0},{1,7},{3,5},{5,3},{7,1},{8,14},{10,12},{12... | collective-permute-start | bytes 884744 | tf_op jit(solution)/shard_map/ppermute | solution.py:981
  181.6 25.3 %collective-permute-start.39 = (bf16[128,1152]{1,0:T(8,128)(2,1)S(1)}, bf16[128,1152]{1,0:T(8,128)(2,1)S(1)}, u32[]{:S(2)}, u32[]{:S(2)}) collective-permute-start(bf16[128,1152]{1,0:T(8,128)(2,1)S(1)} %get-tuple-element.182), channel_id=1, source_target_pairs={{0,2},{2,0},{1,3},{3,1},{4,6},{6,4},{5,7},{7,5},{8,10},{10,8},{9,1... | collective-permute-start | bytes 884744 | tf_op jit(solution)/shard_map/ppermute | solution.py:977
  182.9 23.9 %collective-permute-start.40 = (bf16[128,1152]{1,0:T(8,128)(2,1)S(1)}, bf16[128,1152]{1,0:T(8,128)(2,1)S(1)}, u32[]{:S(2)}, u32[]{:S(2)}) collective-permute-start(bf16[128,1152]{1,0:T(8,128)(2,1)S(1)} %get-tuple-element.183), channel_id=1, source_target_pairs={{0,4},{4,0},{1,5},{5,1},{2,6},{6,2},{3,7},{7,3},{8,12},{12,8},{9,1... | collective-permute-start | bytes 884744 | tf_op jit(solution)/shard_map/ppermute | solution.py:977
  183.9 22.9 %collective-permute-start.41 = (bf16[128,1152]{1,0:T(8,128)(2,1)S(1)}, bf16[128,1152]{1,0:T(8,128)(2,1)S(1)}, u32[]{:S(2)}, u32[]{:S(2)}) collective-permute-start(bf16[128,1152]{1,0:T(8,128)(2,1)S(1)} %get-tuple-element.184), channel_id=1, source_target_pairs={{0,6},{2,4},{4,2},{6,0},{1,7},{3,5},{5,3},{7,1},{8,14},{10,12},{12... | collective-permute-start | bytes 884744 | tf_op jit(solution)/shard_map/ppermute | solution.py:981
  206.9 21.9 %collective-permute-start.42 = (bf16[2,432,1792]{2,1,0:T(8,128)(2,1)}, bf16[2,432,1792]{2,1,0:T(8,128)(2,1)}, u32[]{:S(2)}, u32[]{:S(2)}) collective-permute-start(bf16[2,432,1792]{2,1,0:T(8,128)(2,1)} %get-tuple-element.203), channel_id=1, source_target_pairs={{0,1},{1,0},{2,3},{3,2},{4,5},{5,4},{6,7},{7,6},{8,9},{9,8},{10,11... | collective-permute-start | bytes 9289736 | tf_op jit(solution)/shard_map/ppermute | solution.py:977
  218.6 21.6 %collective-permute-start.47 = (bf16[128,1024]{1,0:T(8,128)(2,1)S(1)}, bf16[128,1024]{1,0:T(8,128)(2,1)S(1)}, u32[]{:S(2)}, u32[]{:S(2)}) collective-permute-start(bf16[128,1024]{1,0:T(8,128)(2,1)S(1)} %get-tuple-element.216.own_heads), channel_id=1, source_target_pairs={{0,4},{4,0},{1,5},{5,1},{2,6},{6,2},{3,7},{7,3},{8,12},{12,8},{9,1... | collective-permute-start | bytes 786440 | tf_op jit(solution)/shard_map/ppermute | solution.py:977
  220.0 20.0 %collective-permute-start.43 = (bf16[2,256,256]{2,1,0:T(8,128)(2,1)}, bf16[2,256,256]{2,1,0:T(8,128)(2,1)S(1)}, u32[]{:S(2)}, u32[]{:S(2)}) collective-permute-start(bf16[2,256,256]{2,1,0:T(8,128)(2,1)} %get-tuple-element.206), channel_id=1, source_target_pairs={{16,0},{24,8},{17,1},{25,9},{18,2},{26,10},{19,3},{27,11},{20,4},{... | collective-permute-start | bytes 786440 | tf_op jit(solution)/shard_map/ppermute | solution.py:973
  221.3 18.7 %collective-permute-start.44 = (bf16[2,256,256]{2,1,0:T(8,128)(2,1)}, bf16[2,256,256]{2,1,0:T(8,128)(2,1)S(1)}, u32[]{:S(2)}, u32[]{:S(2)}) collective-permute-start(bf16[2,256,256]{2,1,0:T(8,128)(2,1)} %get-tuple-element.207), channel_id=1, source_target_pairs={{8,0},{16,8},{24,16},{9,1},{17,9},{25,17},{10,2},{18,10},{26,18},{... | collective-permute-start | bytes 786440 | tf_op jit(solution)/shard_map/ppermute | solution.py:973
  222.6 17.4 %collective-permute-start.45 = (bf16[2,256,256]{2,1,0:T(8,128)(2,1)}, bf16[2,256,256]{2,1,0:T(8,128)(2,1)S(1)}, u32[]{:S(2)}, u32[]{:S(2)}) collective-permute-start(bf16[2,256,256]{2,1,0:T(8,128)(2,1)} %get-tuple-element.208), channel_id=1, source_target_pairs={{0,8},{8,16},{16,24},{1,9},{9,17},{17,25},{2,10},{10,18},{18,26},{... | collective-permute-start | bytes 786440 | tf_op jit(solution)/shard_map/ppermute | solution.py:973
  228.8 11.4 %collective-permute-start.46 = (bf16[128,960]{1,0:T(8,128)(2,1)}, bf16[128,960]{1,0:T(8,128)(2,1)S(1)}, u32[]{:S(2)}, u32[]{:S(2)}) collective-permute-start(bf16[128,960]{1,0:T(8,128)(2,1)} %get-tuple-element.214), channel_id=1, source_target_pairs={{0,4},{4,0},{1,5},{5,1},{2,6},{6,2},{3,7},{7,3},{8,12},{12,8},{9,1... | collective-permute-start | bytes 737288 | tf_op jit(solution)/shard_map/ppermute | solution.py:977
  243.2 3.6 %collective-permute-start.48 = (bf16[2,288,896]{2,1,0:T(8,128)(2,1)S(1)}, bf16[2,288,896]{2,1,0:T(8,128)(2,1)}, u32[]{:S(2)}, u32[]{:S(2)}) collective-permute-start(bf16[2,288,896]{2,1,0:T(8,128)(2,1)S(1)} %get-tuple-element.223), channel_id=1, source_target_pairs={{0,1},{1,0},{2,3},{3,2},{4,5},{5,4},{6,7},{7,6},{8,9},{9,8},{10,11... | collective-permute-start | bytes 3096584 | tf_op jit(solution)/shard_map/ppermute | solution.py:977
  243.2 16.7 %collective-permute-start.52 = (bf16[2,288,432]{2,1,0:T(8,128)(2,1)S(1)}, bf16[2,288,432]{2,1,0:T(8,128)(2,1)S(1)}, u32[]{:S(2)}, u32[]{:S(2)}) collective-permute-start(bf16[2,288,432]{2,1,0:T(8,128)(2,1)S(1)} %get-tuple-element.237), channel_id=1, source_target_pairs={{0,8},{8,0},{16,24},{24,16},{1,9},{9,1},{17,25},{25,17},{2,10},{10... | collective-permute-start | bytes 1493000 | tf_op jit(solution)/shard_map/ppermute | solution.py:989
  245.7 5.7 %collective-permute-start.49 = (bf16[2,128,256]{2,1,0:T(8,128)(2,1)S(1)}, bf16[2,128,256]{2,1,0:T(8,128)(2,1)S(1)}, u32[]{:S(2)}, u32[]{:S(2)}) collective-permute-start(bf16[2,128,256]{2,1,0:T(8,128)(2,1)S(1)} %dynamic-slice_convert_fusion), channel_id=1, source_target_pairs={{0,4},{4,0},{1,5},{5,1},{2,6},{6,2},{3,7},{7,3},{8,12},{12,8},{9,1... | collective-permute-start | bytes 393224 | tf_op jit(solution)/shard_map/ppermute | solution.py:977
  255.0 4.9 %collective-permute-start.53 = (bf16[144,384]{1,0:T(8,128)(2,1)S(1)}, bf16[144,384]{1,0:T(8,128)(2,1)S(1)}, u32[]{:S(2)}, u32[]{:S(2)}) collective-permute-start(bf16[144,384]{1,0:T(8,128)(2,1)S(1)} %get-tuple-element.239), channel_id=1, source_target_pairs={{0,4},{4,0},{1,5},{5,1},{2,6},{6,2},{3,7},{7,3},{8,12},{12,8},{9,1... | collective-permute-start | bytes 331784 | tf_op jit(solution)/shard_map/ppermute | solution.py:977
  256.0 15.7 %collective-permute-start.54 = (bf16[432,576]{1,0:T(8,128)(2,1)S(1)}, bf16[432,576]{1,0:T(8,128)(2,1)S(1)}, u32[]{:S(2)}, u32[]{:S(2)}) collective-permute-start(bf16[432,576]{1,0:T(8,128)(2,1)S(1)} %copy-done.19), channel_id=1, source_target_pairs={{0,8},{8,0},{16,24},{24,16},{1,9},{9,1},{17,25},{25,17},{2,10},{10... | collective-permute-start | bytes 1493000 | tf_op jit(solution)/shard_map/ppermute | solution.py:989
  261.1 10.7 %collective-permute-start.55 = (bf16[592,384]{1,0:T(8,128)(2,1)S(1)}, bf16[592,384]{1,0:T(8,128)(2,1)S(1)}, u32[]{:S(2)}, u32[]{:S(2)}) collective-permute-start(bf16[592,384]{1,0:T(8,128)(2,1)S(1)} %get-tuple-element.244), channel_id=1, source_target_pairs={{0,1},{1,0},{2,3},{3,2},{4,5},{5,4},{6,7},{7,6},{8,9},{9,8},{10,11... | collective-permute-start | bytes 1363976 | tf_op jit(solution)/shard_map/ppermute | solution.py:977
  261.1 23.1 %collective-permute-start.51 = (bf16[288,896]{1,0:T(8,128)(2,1)S(1)}, bf16[288,896]{1,0:T(8,128)(2,1)S(1)}, u32[]{:S(2)}, u32[]{:S(2)}) collective-permute-start(bf16[288,896]{1,0:T(8,128)(2,1)S(1)} %get-tuple-element.224), channel_id=1, source_target_pairs={{0,2},{2,0},{1,3},{3,1},{4,6},{6,4},{5,7},{7,5},{8,10},{10,8},{9,1... | collective-permute-start | bytes 1548296 | tf_op jit(solution)/shard_map/ppermute | solution.py:977
  262.2 21.2 %collective-permute-start.50 = (bf16[432,576]{1,0:T(8,128)(2,1)S(1)}, bf16[432,576]{1,0:T(8,128)(2,1)S(1)}, u32[]{:S(2)}, u32[]{:S(2)}) collective-permute-start(bf16[432,576]{1,0:T(8,128)(2,1)S(1)} %copy-done.17), channel_id=1, source_target_pairs={{0,8},{8,0},{16,24},{24,16},{1,9},{9,1},{17,25},{25,17},{2,10},{10... | collective-permute-start | bytes 1493000 | tf_op jit(solution)/shard_map/ppermute | solution.py:989
  273.2 11.1 %collective-permute-start.56 = (bf16[304,384]{1,0:T(8,128)(2,1)S(1)}, bf16[304,384]{1,0:T(8,128)(2,1)S(1)}, u32[]{:S(2)}, u32[]{:S(2)}) collective-permute-start(bf16[304,384]{1,0:T(8,128)(2,1)S(1)} %get-tuple-element.247), channel_id=1, source_target_pairs={{0,2},{2,0},{1,3},{3,1},{4,6},{6,4},{5,7},{7,5},{8,10},{10,8},{9,1... | collective-permute-start | bytes 700424 | tf_op jit(solution)/shard_map/ppermute | solution.py:977
  275.2 14.2 %all-to-all-start.1 = ((bf16[4,144,432]{2,1,0:T(8,128)(2,1)}), bf16[4,144,432]{2,1,0:T(8,128)(2,1)S(1)}, u32[]{:S(2)}, u32[]{:S(2)}) async-start(bf16[4,144,432]{2,1,0:T(8,128)(2,1)} %bitcast.43), calls=%async_computation.1 | async-start | bytes 1179648 | tf_op jit(solution)/shard_map/all_to_all | solution.py:1138
  289.4 28.2 %all-to-all-start = ((bf16[4,320,320]{2,1,0:T(8,128)(2,1)}), bf16[4,320,320]{2,1,0:T(8,128)(2,1)S(1)}, u32[]{:S(2)}, u32[]{:S(2)}) async-start(bf16[4,320,320]{2,1,0:T(8,128)(2,1)} %shard_map.254), calls=%async_computation | async-start | bytes 1966080 | tf_op jit(solution)/shard_map/all_to_all | solution.py:1143
  295.8 15.2 %collective-permute-start.57 = (bf16[2,288,432]{2,1,0:T(8,128)(2,1)S(1)}, bf16[2,288,432]{2,1,0:T(8,128)(2,1)S(1)}, u32[]{:S(2)}, u32[]{:S(2)}) collective-permute-start(bf16[2,288,432]{2,1,0:T(8,128)(2,1)S(1)} %shard_map.257), channel_id=1, source_target_pairs={{0,2},{2,0},{1,3},{3,1},{4,6},{6,4},{5,7},{7,5},{8,10},{10,8},{9,1... | collective-permute-start | bytes 1493000 | tf_op jit(solution)/shard_map/ppermute | solution.py:977
  300.5 11.8 %collective-permute-start.58 = (bf16[288,432]{1,0:T(8,128)(2,1)S(1)}, bf16[288,432]{1,0:T(8,128)(2,1)S(1)}, u32[]{:S(2)}, u32[]{:S(2)}) collective-permute-start(bf16[288,432]{1,0:T(8,128)(2,1)S(1)} %get-tuple-element.263), channel_id=1, source_target_pairs={{0,1},{1,0},{2,3},{3,2},{4,5},{5,4},{6,7},{7,6},{8,9},{9,8},{10,11... | collective-permute-start | bytes 746504 | tf_op jit(solution)/shard_map/ppermute | solution.py:977
  311.1 1.6 collective-permute-start.59
  (77 other events, 581.2 us)

commit v2 on v1

--- a/solution.py
+++ b/solution.py
@@ -257,13 +257,15 @@
     column = lax.broadcasted_iota(jnp.int32, (rows, span), 1)
     same = key_ids[...] == query_ids[...]
     allowed = same | ((key_ids[...] < query_ids[...]) & (column >= row))
+    chances[...] = nt(queries[...], keys[...])
     for h in range(HQ):
         here = slice(h * rows, (h + 1) * rows)
-        scores = jnp.where(allowed, nt(queries[here], keys[...]), -1e30)
+        scores = jnp.where(allowed, chances[here], -1e30)
         grown = jnp.exp(scores - jnp.max(scores, axis=-1, keepdims=True))
-        share = grown / jnp.sum(grown, axis=-1, keepdims=True)
-        chances[here] = share
-        heads[:, h * dim : (h + 1) * dim] = nn(share.astype(bf16), values[...]).astype(bf16)
+        chances[here] = grown / jnp.sum(grown, axis=-1, keepdims=True)
+    seen = nn(chances[...].astype(bf16), values[...]).astype(bf16)
+    for h in range(HQ):
+        heads[:, h * dim : (h + 1) * dim] = seen[h * rows : (h + 1) * rows]
     wait(copies)
     out = nn(heads[...], weight[...])
     attn_out[...] = out
@@ -378,18 +380,20 @@
     )
 
 
-def far_kernel(window, place, n0, n1, n2, n3, *refs):
-    gates, (hidden, slope, gelu, w_gates, tokens, room, sem) = refs[:10], refs[10:]
+def far_kernel(window, place, own, n0, n1, n2, n3, *refs):
+    gates, (hiddens, slope, gelu, w_gates, tokens, room, sem) = refs[:10], refs[10:]
     start, width = window
     copies = fetch_gates(place, gates, w_gates, sem)
     rows = n0.shape[0]
     for i, n in enumerate((n0, n1, n2, n3)):
         tokens[i * rows : (i + 1) * rows] = n[...]
+    hiddens[:, : 4 * rows] = own[...].T
     wait(copies)
-    for first, last in steps(hidden.shape[1], 256):
+    for first, last in steps(hiddens.shape[0], 256):
         gate = nn(tokens[...], w_gates[0, :, first:last])
         up = nn(tokens[...], w_gates[1, :, first:last])
-        hidden[:, first:last], room[0, :, first:last], room[1, :, first:last] = gated(gate, up)
+        value, room[0, :, first:last], room[1, :, first:last] = gated(gate, up)
+        hiddens[first:last, 4 * rows :] = value.T
     here = at(place[HALF] * start, width, 128)
     slope[...] = room[0, :, here]
     gelu[...] = room[1, :, here]
@@ -400,62 +404,68 @@
     return start, ff - start
 
 
-def far_hidden(place, far_normed, gates):
+def far_hidden(place, hidden, far_normed, gates):
     rows, model = far_normed[0].shape
     ff = gates[0].shape[2]
     start, width = window_of(ff)
     return call(
         functools.partial(far_kernel, (start, width)),
         11,
-        (low(4 * rows, ff), low(4 * rows, width), low(4 * rows, width)),
-        [SCALARS, *[VECTORS] * 4, *[ANYWHERE] * 10],
+        (low(ff, 8 * rows), low(4 * rows, width), low(4 * rows, width)),
+        [SCALARS, *[VECTORS] * 5, *[ANYWHERE] * 10],
         [
             pltpu.VMEM((2, model, ff), bf16),
             pltpu.VMEM((4 * rows, model), bf16),
             pltpu.VMEM((2, 4 * rows, ff), bf16),
             pltpu.SemaphoreType.DMA((10,)),
         ],
-        place, *far_normed, *gates,
+        place, hidden, *far_normed, *gates,
     )
 
 
 def weights_kernel(
-    window, place, normed, down, hidden, gate_low, up_low, n0, n1, n2, n3, d0, d1, d2, d3, far_hiddens, slope, gelu, *refs
+    window, place, h_normed, h_down, h_gate, h_up, n0, n1, n2, n3, d0, d1, d2, d3, h_hiddens, h_slope, h_gelu, w0, w1, w2, w3,
+    h_keep, h_send, w_down, grads, tokens, backs, gate_low, up_low, hiddens, slope, gelu, keep, send,
+    sem, soon_sem, late_sem, out_sem,
 ):
-    downs = refs[:4]
-    keep, send = refs[4:6]
-    w_down, hiddens, grads, tokens, backs, sem = refs[6:]
-    model = normed.shape[1]
     start, width = window
     half, core, bit = place[HALF], place[CORE], place[BIT]
+    own, model = h_normed.shape
+    rows = own // 4
     columns = at(half * start, width, 128)
-    copies = fetch(place, downs, w_down, sem)
-    rows, own = n0.shape[0], normed.shape[0]
-    kept = hidden.shape[1] // 2
-    hiddens[:, :own] = hidden[...].T
+
+    def blocks(parts, target):
+        return [(p, target.at[own + i * rows : own + (i + 1) * rows]) for i, p in enumerate(parts)]
+
+    first = begin([(h_gate, gate_low), (h_up, up_low)], sem)
+    soon = [*blocks((d0, d1, d2, d3), backs), (h_slope, slope), (h_gelu, gelu), (h_down, backs.at[:own])]
+    for slot, piece in zip(slots(place), (w0, w1, w2, w3)):
+        soon.append((piece, w_down.at[at(slot * piece.shape[0], piece.shape[0])]))
+    soon = begin(soon, soon_sem)
+    late = begin([*blocks((n0, n1, n2, n3), tokens), (h_normed, tokens.at[:own]), (h_hiddens, hiddens)], late_sem)
+    wait(first)
     grads[core, :, :own] = gate_low[:, columns].T
     grads[1 - core, :, :own] = up_low[:, columns].T
-    hiddens[:, own:] = far_hiddens[...].T
-    tokens[:own] = normed[...]
-    backs[:own] = down[...]
-    for i, (n, d) in enumerate(zip((n0, n1, n2, n3), (d0, d1, d2, d3))):
-        here = slice(own + i * rows, own + (i + 1) * rows)
-        tokens[here] = n[...]
-        backs[here] = d[...]
-    wait(copies)
+    wait(soon)
     for first, last in steps(width, 256):
         back = nt(backs[own:], w_down[at(half * start + first, last - first)])
         c = slice(first, last)
         grads[core, c, own:] = (back * slope[:, c].astype(f32)).astype(bf16).T
         grads[1 - core, c, own:] = (back * gelu[:, c].astype(f32)).astype(bf16).T
+    wait(late)
+    kept = hiddens.shape[0] // 2
     part = kept // 2
+    results = []
     for i in range(2):
         r = at(half * (kept - start) + i * part, part)
         slot = i ^ bit
         keep[slot, :, :model] = nn(grads[0, r], tokens[...]).astype(bf16)
         send[slot, :, :model] = nn(grads[1, r], tokens[...]).astype(bf16)
+    gates = pl.ds(0, model)
+    results += [(keep.at[:, :, gates], h_keep.at[:, :, gates]), (send.at[:, :, gates], h_send.at[:, :, gates])]
+    done = begin(results, out_sem)
     span = keep.shape[2] - model
-    columns = at(half * (backs.shape[1] - span), span, 128)
+    columns = at(half * (model - span), span, 128)
     for i in range(4):
         result = nn(hiddens[i * part : (i + 1) * part], backs[:, columns]).astype(bf16)
 
@@ -467,28 +477,46 @@
         def _():
             send[i // 2, :, model:] = result
 
-
-def weight_grads(place, normed, down, hidden, gate_low, up_low, far_normed, far_down, far_kept, downs):
+    rest = pl.ds(model, span)
+    for i, (a, b) in enumerate(((keep, h_keep), (send, h_send))):
+        copy = pltpu.make_async_copy(a.at[:, :, rest], b.at[:, :, rest], out_sem.at[2 + i])
+        copy.start()
+        done.append(copy)
+    wait(done)
+
+
+def weight_grads(place, normed, down, gate_low, up_low, far_normed, far_down, far_kept, downs):
     own, model = normed.shape
-    ff = hidden.shape[1]
+    ff = gate_low.shape[1]
     start, width = window_of(ff)
     part = ff // 4
     span = -(-model // 256) * 128
-    return call(
+    shape = (2, part, model + span)
+    return pl.pallas_call(
         functools.partial(weights_kernel, (start, width)),
-        16,
-        (low(2, part, model + span), low(2, part, model + span)),
-        [SCALARS, *[VECTORS] * 16, *[ANYWHERE] * 4],
-        [
+        out_shape=(low(*shape), low(*shape)),
+        in_specs=[SCALARS, *[ANYWHERE] * 19],
+        out_specs=(ANYWHERE, ANYWHERE),
+        scratch_shapes=[
             pltpu.VMEM((ff, model), bf16),
-            pltpu.VMEM((ff, 2 * own), bf16),
             pltpu.VMEM((2, width, 2 * own), bf16),
             pltpu.VMEM((2 * own, model), bf16),
             pltpu.VMEM((2 * own, model), bf16),
+            pltpu.VMEM((own, ff), bf16),
+            pltpu.VMEM((own, ff), bf16),
+            pltpu.VMEM((ff, 2 * own), bf16),
+            pltpu.VMEM((own, width), bf16),
+            pltpu.VMEM((own, width), bf16),
+            pltpu.VMEM(shape, bf16),
+            pltpu.VMEM(shape, bf16),
+            pltpu.SemaphoreType.DMA((2,)),
+            pltpu.SemaphoreType.DMA((11,)),
             pltpu.SemaphoreType.DMA((6,)),
+            pltpu.SemaphoreType.DMA((4,)),
         ],
-        place, normed, down, hidden, gate_low, up_low, *far_normed, *far_down, *far_kept, *downs,
-    )
+        cost_estimate=pl.CostEstimate(flops=16_000_000_000, bytes_accessed=1 << 20, transcendentals=0),
+        compiler_params=pltpu.CompilerParams(vmem_limit_bytes=48 << 20),
+    )(place, normed, down, gate_low, up_low, *far_normed, *far_down, *far_kept, *downs)
 
 
 def turning_kernel(own, r1, r2, r3, residual, cotangent, gain, output, grad, grad_gain):
@@ -513,21 +541,23 @@
 def cores_kernel(place, keep, got, gates, send_other, send_own, down, send_down, turned):
     model = gates.shape[1]
     gates[...] = keep[0, :, :model].astype(f32) + got[0, :, :model].astype(f32)
-    sent = (keep[1, :, :model].astype(f32) + got[1, :, :model].astype(f32)).astype(bf16)
-    half = send_own.shape[1]
+    sent = keep[1, :, :model].astype(f32) + got[1, :, :model].astype(f32)
+    half, short = model // 2, send_own.shape[0]
     for i in range(2):
 
         @pl.when(place[CHIP] == i)
         def _():
-            send_own[...] = sent[:, i * half : (i + 1) * half]
-            send_other[...] = sent[:, (1 - i) * half : (2 - i) * half]
-
-    part = down.shape[1]
-    first = place[HALF] * (turned.shape[1] - 2 * part)
+            for target, j in ((send_own, i), (send_other, 1 - i)):
+                for k in range(2):
+                    block = sent[k * short : (k + 1) * short, j * half : (j + 1) * half]
+                    target[:, k * half : (k + 1) * half] = block.astype(bf16)
+
+    unit, part = down.shape[0], turned.shape[2]
+    first = place[HALF] * (turned.shape[1] - 2 * unit)
     for i in range(2):
         turned[i] = (keep[i, :, model:].astype(f32) + got[i, :, model:].astype(f32)).T
         for target, bit in ((down, place[BIT]), (send_down, 1 - place[BIT])):
-            target[i] = turned[i, at(first + bit * part, part)].astype(target.dtype)
+            target[:, i * part : (i + 1) * part] = turned[i, at(first + bit * unit, unit)].astype(target.dtype)
 
 
 def add_cores(place, keep, got, model):
@@ -536,8 +566,8 @@
         cores_kernel,
         4,
         (
-            wide(part, model), low(part, model // 2), low(part, model // 2),
-            wide(2, model // 4, part), low(2, model // 4, part),
+            wide(part, model), low(part // 2, model), low(part // 2, model),
+            wide(model // 4, 2 * part), low(model // 4, 2 * part),
         ),
         [SCALARS, *[VECTORS] * 2],
         [pltpu.VMEM((2, keep.shape[2] - model, part), f32)],
@@ -546,20 +576,21 @@
 
 
 def gates_kernel(flip, place, gates, got, total):
-    half, unit = got.shape[1], total.shape[1]
+    half, unit = got.shape[1] // 2, total.shape[1]
+    both = jnp.concatenate([got[:, :half].astype(f32), got[:, half:].astype(f32)], axis=0)
     for i in range(2):
 
         @pl.when(place[CHIP] == (1 - i if flip else i))
         def _():
-            turned = (gates[:, i * half : (i + 1) * half] + got[...].astype(f32)).T.astype(bf16)
+            turned = (gates[:, i * half : (i + 1) * half] + both).T.astype(bf16)
             for k in range(2):
                 total[k] = turned[k * unit : (k + 1) * unit]
 
 
 def add_gates(flip, place, gates, got):
-    part, half = got.shape
-    return call(
-        functools.partial(gates_kernel, flip), 2, low(2, half // 2, part), [SCALARS, *[VECTORS] * 2], [], place, gates, got
+    part, model = gates.shape
+    return call(
+        functools.partial(gates_kernel, flip), 2, low(2, model // 4, part), [SCALARS, *[VECTORS] * 2], [], place, gates, got
     )
 
 
@@ -589,11 +620,15 @@
 
 
 def down_kernel(down, got, total):
-    total[...] = (down[...] + got[...].astype(f32)).astype(bf16)
+    part = total.shape[2]
+    for i in range(2):
+        c = slice(i * part, (i + 1) * part)
+        total[i] = (down[:, c] + got[:, c].astype(f32)).astype(bf16)
 
 
 def add_down(down, got):
-    return call(down_kernel, 1, low(*down.shape), [VECTORS] * 2, [], down, got)
+    rows, width = down.shape
+    return call(down_kernel, 1, low(2, rows, width // 2), [VECTORS] * 2, [], down, got)
 
 
 def attend_back_kernel(
@@ -602,7 +637,7 @@
     kv0, kv1, kv2, kv3, o0, o1, o2, o3,
     grad_residual, keep, send, grad_gains, grad_gain_query, grad_projected, g0, g1, g2, g3,
     own, r1, r2, r3, residual, attn_out, cotangent, chances, queries, raw, table,
-    keys, values, attn_low, heads, dull, weight, sem, soon_sem, late_sem,
+    keys, values, attn_low, heads, dull, grad_share, weight, sem, soon_sem, late_sem,
 ):
     plane, dim = kv0.shape[1], kv0.shape[2]
     soon = begin(
@@ -628,17 +663,19 @@
     rows = own.shape[0]
     here = half_plane(place[0], rows)
     cosine, sine = table[0, here], table[1, here]
+    grad_heads = nt(attn_low[...], weight[...]).astype(bf16)
+    for h in range(HQ):
+        heads[h * rows : (h + 1) * rows] = grad_heads[:, h * dim : (h + 1) * dim]
+    grad_share[...] = nt(heads[...], values[...])
+    for h in range(HQ):
+        r = slice(h * rows, (h + 1) * rows)
+        share, back = chances[r], grad_share[r]
+        dull[r] = (share * (back - jnp.sum(share * back, axis=-1, keepdims=True))).astype(bf16)
+    turned = nn(dull[...], keys[...]) * (dim**-0.5)
     gain_total = jnp.zeros_like(grad_gain_query)
     for h in range(HQ):
         r = slice(h * rows, (h + 1) * rows)
-        heads[r] = nt(attn_low[...], weight[h * dim : (h + 1) * dim]).astype(bf16)
-        share = chances[r]
-        grad_share = nt(heads[r], values[...])
-        mean = jnp.sum(share * grad_share, axis=-1, keepdims=True)
-        grad_scores = (share * (grad_share - mean)).astype(bf16)
-        dull[r] = grad_scores
-        turned = nn(grad_scores, keys[...]) * (dim**-0.5)
-        back, gain_part = rms_back(raw[r], gain_query[...], turn(turned, cosine, -sine))
+        back, gain_part = rms_back(raw[r], gain_query[...], turn(turned[r], cosine, -sine))
         gain_total = gain_total + gain_part
         grad_projected[:, h * dim : (h + 1) * dim] = back.astype(bf16)
     grad_gain_query[...] = gain_total
@@ -686,6 +723,7 @@
             pltpu.VMEM((rows, model), bf16),
             pltpu.VMEM((HQ * rows, dim), bf16),
             pltpu.VMEM((HQ * rows, span), bf16),
+            pltpu.VMEM((HQ * rows, span), f32),
             pltpu.VMEM((HQ * dim, model), bf16),
             pltpu.SemaphoreType.DMA((4,)),
             pltpu.SemaphoreType.DMA((7,)),
@@ -827,65 +865,81 @@
     )
 
 
-def chips_kernel(first, got_first, keep, got, gains, out, room, line):
+def layout(far, unit, columns, head, gains):
+    size, short = columns // far, 2 * unit // far
+    lanes = -(-size // 128) * 128
+    free = lanes - size
+    beside = unit // (head // free) if free and head % free == 0 else 0
+    beside = beside if beside <= short and beside * (head // max(free, 1)) == unit else 0
+    rest = (short - beside) * head // lanes
+    return size, short, lanes, beside, rest, -(-(unit + rest + -(-gains // lanes)) // 16) * 16
+
+
+def chips_kernel(count, first, got_first, keep, got, gains, out, room, line, block):
     unit, early = first.shape[0], room.shape[1] - keep.shape[1]
-    far, rows, lanes = out.shape
-    size = room.shape[1] // far
-    across = lanes - size
-    head = (first.shape[1] - early) // 2
+    far, head = out.shape[0], (first.shape[1] - early) // 2
+    size, short, lanes, beside, rest, _ = layout(far, unit, room.shape[1], head, count)
     room[:, :early] = first[:, :early] + got_first[:, :early].astype(f32)
     room[:, early:] = keep[...] + got[:unit].astype(f32)
     sums = gains[...] + got[unit:].astype(f32)
-    width = gains.shape[1]
+    width, more = gains.shape[1], -(-count // lanes)
     line[...] = jnp.zeros_like(line)
-    for i in range(gains.shape[0]):
-        line[:, i * width : (i + 1) * width] = sums[i : i + 1]
-    extra = jnp.concatenate([line[:, i * lanes : (i + 1) * lanes] for i in range(rows - unit)], axis=0).astype(bf16)
-    short = 2 * unit // far
+    for i in range(0, more * lanes, width):
+        here = min(width, more * lanes - i)
+        line[:, i : i + here] = sums[i // width : i // width + 1, :here]
+    block[...] = jnp.zeros_like(block)
+    for i in range(more):
+        block[unit + rest + i : unit + rest + i + 1] = line[:, i * lanes : (i + 1) * lanes]
     for half in range(2):
         start = early + half * head
-        part = (first[:, start : start + head] + got_first[:, start : start + head].astype(f32)).astype(bf16)
+        part = first[:, start : start + head] + got_first[:, start : start + head].astype(f32)
         for k in range(far // 2):
             f = half * (far // 2) + k
-            out[f, :unit, :size] = room[:, f * size : (f + 1) * size].astype(bf16)
-            block = part[k * short : (k + 1) * short]
-            for g in range(far // 2):
-                out[f, g * short : (g + 1) * short, size:] = block[:, g * across : (g + 1) * across]
-            out[f, unit:] = extra
-
-
-def last_chips(far, first, got_first, keep, got, gains, head):
+            mine = part[k * short : (k + 1) * short]
+            block[:unit, :size] = room[:, f * size : (f + 1) * size]
+            for g in range(unit // beside if beside else 0):
+                block[g * beside : (g + 1) * beside, size:] = mine[:beside, g * (lanes - size) : (g + 1) * (lanes - size)]
+            for j in range(head // lanes):
+                start_row = unit + j * (short - beside)
+                block[start_row : start_row + short - beside] = mine[beside:, j * lanes : (j + 1) * lanes]
+            out[f] = block[...].astype(bf16)
+
+
+def last_chips(far, first, got_first, keep, got, gains, head, count):
     unit, width = keep.shape
-    early = first.shape[1] - 2 * head
-    lanes = (early + width + 2 * head) // far
-    rows = -(-gains.size // (16 * lanes)) * 16
-    return call(
-        chips_kernel,
+    columns = first.shape[1] - 2 * head + width
+    _, _, lanes, _, _, rows = layout(far, unit, columns, head, count)
+    return call(
+        functools.partial(chips_kernel, count),
         3,
-        low(far, unit + rows, lanes),
+        low(far, rows, lanes),
         [VECTORS] * 5,
-        [pltpu.VMEM((unit, early + width), f32), pltpu.VMEM((1, rows * lanes), f32)],
+        [pltpu.VMEM((unit, columns), f32), pltpu.VMEM((1, -(-count // lanes) * lanes), f32), pltpu.VMEM((rows, lanes), f32)],
         first, got_first, keep, got, gains,
     )
 
 
-def last_sum_kernel(parts, total, out, gains):
-    unit, size = total.shape
+def last_sum_kernel(count, parts, total, out, gains):
+    unit, head = total.shape[0], out.shape[1]
+    far = parts.shape[0]
+    size, short, lanes, beside, rest, _ = layout(far, unit, total.shape[1] * far, head, count)
     sums = jnp.sum(parts[...].astype(f32), axis=0)
     total[...] = sums[:unit, :size]
-    short, across = out.shape[0], sums.shape[1] - size
-    for g in range(unit // short):
-        out[:, g * across : (g + 1) * across] = sums[g * short : (g + 1) * short, size:]
-    gains[...] = sums[unit:]
-
-
-def last_sum(parts, unit, head):
-    far, rows, lanes = parts.shape
-    across = 2 * head // far
-    return call(
-        last_sum_kernel,
+    for g in range(unit // beside if beside else 0):
+        out[:beside, g * (lanes - size) : (g + 1) * (lanes - size)] = sums[g * beside : (g + 1) * beside, size:]
+    for j in range(head // lanes):
+        start_row = unit + j * (short - beside)
+        out[beside:, j * lanes : (j + 1) * lanes] = sums[start_row : start_row + short - beside]
+    for i in range(-(-count // lanes)):
+        gains[:, i * lanes : (i + 1) * lanes] = sums[unit + rest + i : unit + rest + i + 1]
+
+
+def last_sum(parts, unit, columns, head, count):
+    far, _, lanes = parts.shape
+    return call(
+        functools.partial(last_sum_kernel, count),
         2,
-        (wide(unit, lanes - across), wide(2 * unit // far, head), wide(rows - unit, lanes)),
+        (wide(unit, columns // far), wide(2 * unit // far, head), wide(1, -(-count // lanes) * lanes)),
         [VECTORS],
         [],
         parts,
@@ -1090,14 +1144,14 @@
     output, grad_down_proj, grad_gain_post = turning((own, *around(sent)), residual, cotangent, gain_post)
     far_down = far_swap(grad_down_proj, half_far)
     blocks = (grad_down_proj, *around([grad_down_proj] * 3))
-    far_kept = far_hidden(place, after(far_normed, grad_down_proj), gates)
+    far_kept = far_hidden(place, hidden, after(far_normed, grad_down_proj), gates)
     blocks = after(blocks, far_down, *far_kept)
     all_down, gate_low, up_low, own, *sent = backward(place, blocks, slope, gelu, gates, downs)
     far_down = (far_down, *around([far_down] * 3))
     sent = after(sent, *far_down)
     parts = (own, *around(sent))
     keep_grads, send_grads = weight_grads(
-        place, all_normed, all_down, hidden, after(gate_low, *sent), up_low, far_normed, far_down, far_kept, downs
+        place, all_normed, all_down, after(gate_low, *sent), up_low, far_normed, far_down, far_kept, downs
     )
     got_grads = swap(after(send_grads, parts), "core")
     (
@@ -1130,7 +1184,7 @@
     keep, send, gains = last_cores(place, after(keep, got_other), swap(send, "core"), gains)
     grad_down = add_down(grad_down, got_down)
     sums = last_chips(
-        far_count, after(keep_first, got_own), got_first, keep, swap(send, "chip"), gains, query_width // 4
+        far_count, keep_first, got_first, keep, swap(send, "chip"), gains, query_width // 4, 4 * model + 2 * dim
     )
     columns = model // far_count // 2
     down_parts = halving(grad_down, 1, low_bits[1:]).astype(bf16).reshape(2, 2, columns, -1)
@@ -1141,7 +1195,7 @@
     sums, got_own = lax.optimization_barrier((sums, got_own))
 
     sums = lax.all_to_all(sums, "far", 0, 0, tiled=True)
-    qkv_total, out_total, gains = last_sum(sums, model // 4, query_width // 4)
+    qkv_total, out_total, gains = last_sum(sums, model // 4, w_qkv.shape[1] // 2, query_width // 4, 4 * model + 2 * dim)
     out_total, gains = out_total.T, gains.reshape(-1)
     own_gates = halving(add_gates(False, place, grad_gates, got_own), 2, low_bits[1:]).astype(bf16)
     mine = [lax.dynamic_index_in_dim(g, core, 0, keepdims=False) for g in (own_gates, peer_gates)]

time: 324 us -> 313 us (0.966)
  Pallas kernels: 118 us -> 111 us
  waiting for transfers between devices: 85 us -> 80.1 us
    pallas_call x24 -> x23, Pallas kernels: 118 us -> 93.9 us  [call(): pl.pallas_call(kernel, out_shape=out_shape, in_specs=in_specs, out_specs=...]
    pallas_call x0 -> x1, Pallas kernels: none -> 17.3 us  [weight_grads(): pl.pallas_call(functools.partial(weights_kernel, (start, width)), out_sha...]
    ppermute x7, waiting for transfers between devices: 21.2 us -> 15.2 us  [far_swap(): lax.ppermute(value, 'far', [(i, i ^ step) for i in range(lax.axis_size('f...]
    unnamed x158 -> x150, local copies, waits for them, and re-layouts: 29.3 us -> 27.1 us
  transfers between devices with their start and end apart: 62 -> 62, of which waited for: 19 -> 20; matrix products, arithmetic and copies ran while one was open for 1% -> 2% of each run, Pallas kernels for 36% -> 35%
where the time goes in v2:
time: 313 us; the launch traced here: 310 us
  Pallas kernels  111 us (35%)
  starting transfers between devices  82.6 us (26%)
  waiting for transfers between devices  80.1 us (26%)
  local copies, waits for them, and re-layouts  32.9 us (11%)
    pallas_call x23, Pallas kernels, call(): pl.pallas_call(kernel, out_shape=out_shape, in_specs=in_specs, out_specs=...  93.9 us
    ppermute x41, waiting for transfers between devices, swap(): return lax.ppermute(value, axis, [(0, 1), (1, 0)])  50 us
    ppermute x41, starting transfers between devices, swap(): return lax.ppermute(value, axis, [(0, 1), (1, 0)])  34.6 us
    unnamed x150, local copies, waits for them, and re-layouts  27.1 us
    ppermute x6, starting transfers between devices, shift(): return lax.ppermute(value, 'far', pairs)  18.2 us
    pallas_call x1, Pallas kernels, weight_grads(): pl.pallas_call(functools.partial(weights_kernel, (start, width)), out_sha...  17.3 us
    ppermute x7, waiting for transfers between devices, far_swap(): lax.ppermute(value, 'far', [(i, i ^ step) for i in range(lax.axis_size('f...  15.2 us
    ppermute x7, starting transfers between devices, far_swap(): lax.ppermute(value, 'far', [(i, i ^ step) for i in range(lax.axis_size('f...  14.6 us
  transfers between devices with their start and end apart: 62, of which 20 were waited for; matrix products, arithmetic and copies ran while one was open for 2% of the time, Pallas kernels for 35%

profile of v2, /device:TPU:0, one launch (start us, length us, event | category | flops | bytes accessed | tf_op | source)
XLA Modules:
  0.0 309.5 jit_solution(7969445772758056756)
XLA Ops:
  0.6 3.0 collective-permute-start.3
  3.7 6.9 %shard_map.237 = (bf16[2,288,1728]{2,1,0:T(8,128)(2,1)S(1)}, bf16[144,1728]{1,0:T(8,128)(2,1)S(1)}, bf16[144,1728]{1,0:T(8,128)(2,1)S(1)}) custom-call(s32[6]{0:T(128)S(1)} %stack.29.place, bf16[288,6912]{1,0:T(8,128)(2,1)} %gate.1, bf16[288,6912]{1,0:T(8,128)(2,1)} %up.1), custom_call_target="tpu_custom_call" | custom-call | flops 6000000000 | bytes 1048576 | tf_op jit(solution)/shard_map/pallas_call | solution.py:38
  12.2 3.4 %dynamic-slice_bitcast_fusion = (bf16[432,1152]{1,0:T(8,128)(2,1)}, bf16[432,1152]{1,0:T(8,128)(2,1)S(1)}) fusion(bf16[1,2,2,432,1152]{4,3,2,1,0:T(8,128)(2,1)} %bitcast.46, s32[]{:T(128)S(6)} %select_n.52, s32[]{:T(128)S(6)} %select_n.58, s32[]{:T(128)S(6)} %select_n.54), kind=kLoop, calls=%fused_computation | loop fusion | bytes 3981324 | tf_op jit(solution)/shard_map/reshape | solution.py:1107
  16.1 1.5 collective-permute-start.2
  17.6 7.6 %collective-permute-done.2.peer = bf16[128,1152]{1,0:T(8,128)(2,1)S(1)} collective-permute-done((bf16[128,1152]{1,0:T(8,128)(2,1)}, bf16[128,1152]{1,0:T(8,128)(2,1)S(1)}, u32[]{:S(2)}, u32[]{:S(2)}) %collective-permute-start.2) | collective-permute-done | bytes 294944 | tf_op jit(solution)/shard_map/ppermute | solution.py:1031
  27.6 1.8 collective-permute-start.6
  30.0 13.8 %collective-permute-done.11.o1 = bf16[256,1152]{1,0:T(8,128)(2,1)} collective-permute-done((bf16[256,1152]{1,0:T(8,128)(2,1)}, bf16[256,1152]{1,0:T(8,128)(2,1)}, u32[]{:S(2)}, u32[]{:S(2)}) %collective-permute-start.11) | collective-permute-done | bytes 589856 | tf_op jit(solution)/shard_map/ppermute | solution.py:1031
  46.9 3.2 %shard_map.238 = (bf16[128,1152]{1,0:T(8,128)(2,1)S(1)}, bf16[2,256,256]{2,1,0:T(8,128)(2,1)}, f32[256,256]{1,0:T(8,128)S(1)}, bf16[256,1152]{1,0:T(8,128)(2,1)S(1)}) custom-call(s32[6]{0:T(128)S(1)} %stack.29.place, bf16[128,1152]{1,0:T(8,128)(2,1)S(1)} %bitcast.38, bf16[128,1152]{1,0:T(8,128)(2,1)S(1)} %copy-done.28, f32[1,1152]{1,0:T(1,128)S(1)} %reshape.191.gain_in, ...), custom_call_target="tpu_custom_call" | custom-call | flops 2000000000 | bytes 1048576 | tf_op jit(solution)/shard_map/pallas_call | solution.py:38
  54.4 2.5 collective-permute-start.16
  56.9 4.7 %collective-permute-start.8 = (bf16[2,256,256]{2,1,0:T(8,128)(2,1)}, bf16[2,256,256]{2,1,0:T(8,128)(2,1)S(1)}, u32[]{:S(2)}, u32[]{:S(2)}) collective-permute-start(bf16[2,256,256]{2,1,0:T(8,128)(2,1)} %get-tuple-element.142.kv2), channel_id=1, source_target_pairs={{0,16},{8,24},{1,17},{9,25},{2,18},{10,26},{3,19},{11,27},{4,20},{... | collective-permute-start | bytes 786440 | tf_op jit(solution)/shard_map/ppermute | solution.py:1027
  61.7 1.8 collective-permute-done.10.kv3
  63.5 3.6 %collective-permute-start.9 = (bf16[2,256,256]{2,1,0:T(8,128)(2,1)}, bf16[2,256,256]{2,1,0:T(8,128)(2,1)S(1)}, u32[]{:S(2)}, u32[]{:S(2)}) collective-permute-start(bf16[2,256,256]{2,1,0:T(8,128)(2,1)} %get-tuple-element.142.kv2), channel_id=1, source_target_pairs={{0,8},{8,16},{16,24},{1,9},{9,17},{17,25},{2,10},{10,18},{18,26},{... | collective-permute-start | bytes 786440 | tf_op jit(solution)/shard_map/ppermute | solution.py:1027
  69.3 2.7 shard_map.239
  72.0 3.1 collective-permute-done.8.kv0
  75.0 1.7 collective-permute-start.18
  76.8 2.9 collective-permute-done.9.kv1
  79.8 4.3 %shard_map.240 = (f32[512,1024]{1,0:T(8,128)}, bf16[128,1024]{1,0:T(8,128)(2,1)S(1)}, f32[128,1152]{1,0:T(8,128)S(1)}, f32[128,1152]{1,0:T(8,128)S(1)}, bf16[128,1152]{1,0:T(8,128)(2,1)S(1)}) custom-call(s32[6]{0:T(128)S(1)} %stack.29.place, bf16[512,256]{1,0:T(8,128)(2,1)S(1)} %get-tuple-element.141.queries.h_queries, ...), custom_call_target="tpu_custom_call" | custom-call | flops 5000000000 | bytes 1048576 | tf_op jit(solution)/shard_map/pallas_call | solution.py:38
  85.0 2.8 collective-permute-start.17
  87.8 1.6 collective-permute-done.18.refs_3_
  89.4 2.4 collective-permute-start.19
  92.1 1.7 collective-permute-start.14
  93.8 6.6 %collective-permute-done.17.n0 = bf16[128,1152]{1,0:T(8,128)(2,1)S(1)} collective-permute-done((bf16[128,1152]{1,0:T(8,128)(2,1)S(1)}, bf16[128,1152]{1,0:T(8,128)(2,1)S(1)}, u32[]{:S(2)}, u32[]{:S(2)}) %collective-permute-start.17) | collective-permute-done | bytes 294944 | tf_op jit(solution)/shard_map/ppermute | solution.py:1043
  100.4 2.6 collective-permute-start.15
  103.5 5.0 %collective-permute-done.15.x3 = bf16[128,1152]{1,0:T(8,128)(2,1)S(1)} collective-permute-done((bf16[128,1152]{1,0:T(8,128)(2,1)S(1)}, bf16[128,1152]{1,0:T(8,128)(2,1)S(1)}, u32[]{:S(2)}, u32[]{:S(2)}) %collective-permute-start.15) | collective-permute-done | bytes 294944 | tf_op jit(solution)/shard_map/ppermute | solution.py:1035
  109.0 1.4 collective-permute-start.26
  110.4 1.5 collective-permute-start.27
  113.7 13.8 %shard_map.241 = (bf16[512,1152]{1,0:T(8,128)(2,1)}, bf16[512,1728]{1,0:T(8,128)(2,1)}, bf16[512,1728]{1,0:T(8,128)(2,1)}, bf16[512,1728]{1,0:T(8,128)(2,1)}, f3...) custom-call(s32[6]{0:T(128)S(1)} %stack.29.place, ...), custom_call_target="tpu_custom_call" | custom-call | flops 12999999488 | bytes 1048576 | tf_op jit(solution)/shard_map/pallas_call | solution.py:38
  128.7 1.5 collective-permute-start.30
  131.1 6.4 %collective-permute-done.29.r1 = bf16[128,1152]{1,0:T(8,128)(2,1)S(1)} collective-permute-done((bf16[128,1152]{1,0:T(8,128)(2,1)S(1)}, bf16[128,1152]{1,0:T(8,128)(2,1)S(1)}, u32[]{:S(2)}, u32[]{:S(2)}) %collective-permute-start.29) | collective-permute-done | bytes 294944 | tf_op jit(solution)/shard_map/ppermute | solution.py:1031
  137.5 5.4 %collective-permute-done.30.r2 = bf16[128,1152]{1,0:T(8,128)(2,1)S(1)} collective-permute-done((bf16[128,1152]{1,0:T(8,128)(2,1)S(1)}, bf16[128,1152]{1,0:T(8,128)(2,1)S(1)}, u32[]{:S(2)}, u32[]{:S(2)}) %collective-permute-start.30) | collective-permute-done | bytes 294944 | tf_op jit(solution)/shard_map/ppermute | solution.py:1031
  145.1 1.5 collective-permute-start.32
  147.1 1.4 collective-permute-start.34
  148.6 2.9 collective-permute-start.35
  151.5 13.5 %shard_map.243 = (bf16[1728,1024]{1,0:T(8,128)(2,1)}, bf16[512,960]{1,0:T(8,128)(2,1)}, bf16[512,960]{1,0:T(8,128)(2,1)}) custom-call(s32[6]{0:T(128)S(1)} %stack.29.place, bf16[512,1728]{1,0:T(8,128)(2,1)} %get-tuple-element.164.own, bf16[128,1152]{1,0:T(8,128)(2,1)S(1)} %collective-permute-done.17.n0, bf16[128,1152]{1,0:T(8,128)(2,1)S(1)} %collective-permute-done.26.n1, ...), custom_call_target="tpu_custom_call" | custom-call | flops 11000000512 | bytes 1048576 | tf_op jit(solution)/shard_map/pallas_call | solution.py:38
  165.0 1.4 collective-permute-start.36
  168.6 14.9 %shard_map.244 = (bf16[512,1152]{1,0:T(8,128)(2,1)}, bf16[512,1728]{1,0:T(8,128)(2,1)}, bf16[512,1728]{1,0:T(8,128)(2,1)}, f32[128,1152]{1,0:T(8,128)}, bf16[128...) custom-call(s32[6]{0:T(128)S(1)} %stack.29.place, ...), custom_call_target="tpu_custom_call" | custom-call | flops 15000000512 | bytes 1048576 | tf_op jit(solution)/shard_map/pallas_call | solution.py:38
  183.6 1.4 collective-permute-start.39
  187.1 17.3 %shard_map.245 = (bf16[2,432,1792]{2,1,0:T(8,128)(2,1)}, bf16[2,432,1792]{2,1,0:T(8,128)(2,1)}) custom-call(s32[6]{0:T(128)S(1)} %stack.29.place, bf16[512,1152]{1,0:T(8,128)(2,1)} %get-tuple-element.185.h_normed, bf16[512,1152]{1,0:T(8,128)(2,1)} %get-tuple-element.186.h_down, bf16[512,1728]{1,0:T(8,128)(2,1)} %get-tuple-element.188.h_gate, ...), custom_call_target="tpu_custom_call" | custom-call | flops 16000000000 | bytes 1048576 | tf_op jit(solution)/shard_map/pallas_call | solution.py:495
  205.3 9.5 %shard_map.246 = (f32[128,1152]{1,0:T(8,128)}, bf16[128,960]{1,0:T(8,128)(2,1)}, bf16[128,960]{1,0:T(8,128)(2,1)}, f32[2,1152]{1,0:T(2,128)}, f32[1,256]{1,0:T(1...) custom-call(s32[6]{0:T(128)} %copy-done.6, ...), custom_call_target="tpu_custom_call" | custom-call | flops 8000000000 | bytes 1048576 | tf_op jit(solution)/shard_map/pallas_call | solution.py:38
  218.6 6.1 %collective-permute-start.45 = (bf16[2,256,256]{2,1,0:T(8,128)(2,1)}, bf16[2,256,256]{2,1,0:T(8,128)(2,1)S(1)}, u32[]{:S(2)}, u32[]{:S(2)}) collective-permute-start(bf16[2,256,256]{2,1,0:T(8,128)(2,1)} %get-tuple-element.207), channel_id=1, source_target_pairs={{0,8},{8,16},{16,24},{1,9},{9,17},{17,25},{2,10},{10,18},{18,26},{... | collective-permute-start | bytes 786440 | tf_op jit(solution)/shard_map/ppermute | solution.py:1027
  225.2 4.7 %shard_map.247 = (f32[432,1152]{1,0:T(8,128)S(1)}, bf16[216,1152]{1,0:T(8,128)(2,1)S(1)}, bf16[216,1152]{1,0:T(8,128)(2,1)S(1)}, f32[288,864]{1,0:T(8,128)S(1)}, bf16[288,864]{1,0:T(8,128)(2,1)S(1)}) custom-call(s32[6]{0:T(128)S(1)} %copy-done.7, bf16[2,432,1792]{2,1,0:T(8,128)(2,1)} %get-tuple-element.200.keep, ...), custom_call_target="tpu_custom_call" | custom-call | flops 4000000000 | bytes 1048576 | tf_op jit(solution)/shard_map/pallas_call | solution.py:38
  233.1 3.1 shard_map.248.partial
  237.0 1.6 shard_map.249
  239.9 2.0 collective-permute-start.51
  242.0 1.6 collective-permute-start.49
  243.6 1.6 copy-done.39
  247.7 3.4 %shard_map.251 = (f32[128,1152]{1,0:T(8,128)}, bf16[128,384]{1,0:T(8,128)(2,1)S(1)}, bf16[144,384]{1,0:T(8,128)(2,1)S(1)}, f32[16,384]{1,0:T(8,128)S(1)}) custom-call(s32[6]{0:T(128)S(1)} %copy-done.7, f32[2,256,256]{2,1,0:T(8,128)S(1)} %convert_add_fusion.total, bf16[2,128,256]{2,1,0:T(8,128)(2,1)S(1)} %collective-permute-done.49.received, ...), custom_call_target="tpu_custom_call" | custom-call | flops 4000000000 | bytes 1048576 | tf_op jit(solution)/shard_map/pallas_call | solution.py:38
  251.2 1.6 collective-permute-start.52
  253.1 1.5 collective-permute-done.51.got
  254.6 1.4 collective-permute-done.52.got
  257.3 1.6 collective-permute-start.50
  258.8 6.4 %collective-permute-done.53.got = bf16[216,1152]{1,0:T(8,128)(2,1)S(1)} collective-permute-done((bf16[216,1152]{1,0:T(8,128)(2,1)S(1)}, bf16[216,1152]{1,0:T(8,128)(2,1)S(1)}, u32[]{:S(2)}, u32[]{:S(2)}) %collective-permute-start.53) | collective-permute-done | bytes 497696 | tf_op jit(solution)/shard_map/ppermute | solution.py:1043
  265.2 1.3 shard_map.253
  266.6 1.5 collective-permute-start.55
  268.0 1.7 collective-permute-start.56
  270.9 3.5 %all-to-all-start.1 = ((bf16[4,144,432]{2,1,0:T(8,128)(2,1)}), bf16[4,144,432]{2,1,0:T(8,128)(2,1)S(1)}, u32[]{:S(2)}, u32[]{:S(2)}) async-start(bf16[4,144,432]{2,1,0:T(8,128)(2,1)} %bitcast.45), calls=%async_computation.1 | async-start | bytes 1179648 | tf_op jit(solution)/shard_map/all_to_all | solution.py:1192
  274.4 2.2 collective-permute-done.55.got
  280.8 2.1 all-to-all-done.1.parts
  282.8 3.7 %all-to-all-start = ((bf16[4,384,256]{2,1,0:T(8,128)(2,1)}), bf16[4,384,256]{2,1,0:T(8,128)(2,1)S(1)}, u32[]{:S(2)}, u32[]{:S(2)}) async-start(bf16[4,384,256]{2,1,0:T(8,128)(2,1)} %shard_map.254), calls=%async_computation | async-start | bytes 1572864 | tf_op jit(solution)/shard_map/all_to_all | solution.py:1197
  286.5 1.6 copy-done.41
  288.0 1.3 shard_map.257
  290.5 1.6 copy-done.42
  293.1 10.1 %collective-permute-done.57 = bf16[2,288,432]{2,1,0:T(8,128)(2,1)S(1)} collective-permute-done((bf16[2,288,432]{2,1,0:T(8,128)(2,1)S(1)}, bf16[2,288,432]{2,1,0:T(8,128)(2,1)S(1)}, u32[]{:S(2)}, u32[]{:S(2)}) %collective-permute-start.57) | collective-permute-done | bytes 497696 | tf_op jit(solution)/shard_map/ppermute | solution.py:1031
  304.9 2.1 shard_map.258
  (254 shorter events, 53.2 us)
Async XLA Ops:
  0.6 25.3 %collective-permute-start.3 = (bf16[288,1536]{1,0:T(8,128)(2,1)}, bf16[288,1536]{1,0:T(8,128)(2,1)}, u32[]{:S(2)}, u32[]{:S(2)}) collective-permute-start(bf16[288,1536]{1,0:T(8,128)(2,1)} %k0.3), channel_id=1, source_target_pairs={{0,2},{2,0},{1,3},{3,1},{4,6},{6,4},{5,7},{7,5},{8,10},{10,8},{9,1... | collective-permute-start | bytes 2654216 | tf_op jit(solution)/shard_map/ppermute | solution.py:1031
  3.7 183.4 %copy-start.6 = (s32[6]{0:T(128)}, s32[6]{0:T(128)S(1)}, u32[]{:S(2)}) copy-start(s32[6]{0:T(128)S(1)} %stack.29.place) | copy-start | bytes 76
  12.2 44.7 %collective-permute-start.7 = (bf16[2,288,1728]{2,1,0:T(8,128)(2,1)S(1)}, bf16[2,288,1728]{2,1,0:T(8,128)(2,1)}, u32[]{:S(2)}, u32[]{:S(2)}) collective-permute-start(bf16[2,288,1728]{2,1,0:T(8,128)(2,1)S(1)} %get-tuple-element.135.refs_0_), channel_id=1, source_target_pairs={{0,1},{1,0},{2,3},{3,2},{4,5},{5,4},{6,7},{7,6},{8,9},{9,8},{10,11... | collective-permute-start | bytes 5971976 | tf_op jit(solution)/shard_map/ppermute | solution.py:1031
  15.6 12.0 %collective-permute-start = (bf16[432,1152]{1,0:T(8,128)(2,1)S(1)}, bf16[432,1152]{1,0:T(8,128)(2,1)}, u32[]{:S(2)}, u32[]{:S(2)}) collective-permute-start(bf16[432,1152]{1,0:T(8,128)(2,1)S(1)} %get-tuple-element.262.refs_10_.w0), channel_id=1, source_target_pairs={{0,1},{1,0},{2,3},{3,2},{4,5},{5,4},{6,7},{7,6},{8,9},{9,8},{10,11... | collective-permute-start | bytes 2985992 | tf_op jit(solution)/shard_map/ppermute | solution.py:1031
  15.6 10.9 %collective-permute-start.1 = (bf16[256,1152]{1,0:T(8,128)(2,1)}, bf16[256,1152]{1,0:T(8,128)(2,1)S(1)}, u32[]{:S(2)}, u32[]{:S(2)}) collective-permute-start(bf16[256,1152]{1,0:T(8,128)(2,1)} %o0.3), channel_id=1, source_target_pairs={{0,1},{1,0},{2,3},{3,2},{4,5},{5,4},{6,7},{7,6},{8,9},{9,8},{10,11... | collective-permute-start | bytes 1769480 | tf_op jit(solution)/shard_map/ppermute | solution.py:1031
  16.1 9.1 %collective-permute-start.2 = (bf16[128,1152]{1,0:T(8,128)(2,1)}, bf16[128,1152]{1,0:T(8,128)(2,1)S(1)}, u32[]{:S(2)}, u32[]{:S(2)}) collective-permute-start(bf16[128,1152]{1,0:T(8,128)(2,1)} %bitcast.37), channel_id=1, source_target_pairs={{0,4},{4,0},{1,5},{5,1},{2,6},{6,2},{3,7},{7,3},{8,12},{12,8},{9,1... | collective-permute-start | bytes 884744 | tf_op jit(solution)/shard_map/ppermute | solution.py:1031
  25.9 17.9 %collective-permute-start.4 = (bf16[288,1536]{1,0:T(8,128)(2,1)}, bf16[288,1536]{1,0:T(8,128)(2,1)}, u32[]{:S(2)}, u32[]{:S(2)}) collective-permute-start(bf16[288,1536]{1,0:T(8,128)(2,1)} %k0.3), channel_id=1, source_target_pairs={{0,1},{1,0},{2,3},{3,2},{4,5},{5,4},{6,7},{7,6},{8,9},{9,8},{10,11... | collective-permute-start | bytes 2654216 | tf_op jit(solution)/shard_map/ppermute | solution.py:1031
  25.9 17.8 %collective-permute-start.5 = (bf16[288,1536]{1,0:T(8,128)(2,1)}, bf16[288,1536]{1,0:T(8,128)(2,1)}, u32[]{:S(2)}, u32[]{:S(2)}) collective-permute-start(bf16[288,1536]{1,0:T(8,128)(2,1)} %collective-permute-done.3.k1.q1), channel_id=1, source_target_pairs={{0,1},{1,0},{2,3},{3,2},{4,5},{5,4},{6,7},{7,6},{8,9},{9,8},{10,11... | collective-permute-start | bytes 2654216 | tf_op jit(solution)/shard_map/ppermute | solution.py:1031
  27.3 16.5 %collective-permute-start.11 = (bf16[256,1152]{1,0:T(8,128)(2,1)}, bf16[256,1152]{1,0:T(8,128)(2,1)}, u32[]{:S(2)}, u32[]{:S(2)}) collective-permute-start(bf16[256,1152]{1,0:T(8,128)(2,1)} %o0.3), channel_id=1, source_target_pairs={{0,2},{2,0},{1,3},{3,1},{4,6},{6,4},{5,7},{7,5},{8,10},{10,8},{9,1... | collective-permute-start | bytes 1769480 | tf_op jit(solution)/shard_map/ppermute | solution.py:1031
  27.6 26.3 %collective-permute-start.6 = (bf16[144,1728]{1,0:T(8,128)(2,1)}, bf16[144,1728]{1,0:T(8,128)(2,1)}, u32[]{:S(2)}, u32[]{:S(2)}) collective-permute-start(bf16[144,1728]{1,0:T(8,128)(2,1)} %copy-done.17), channel_id=1, source_target_pairs={{0,2},{2,0},{1,3},{3,1},{4,6},{6,4},{5,7},{7,5},{8,10},{10,8},{9,1... | collective-permute-start | bytes 1493000 | tf_op jit(solution)/shard_map/ppermute | solution.py:1031
  43.8 35.9 %collective-permute-start.12 = (bf16[256,1152]{1,0:T(8,128)(2,1)}, bf16[256,1152]{1,0:T(8,128)(2,1)}, u32[]{:S(2)}, u32[]{:S(2)}) collective-permute-start(bf16[256,1152]{1,0:T(8,128)(2,1)} %collective-permute-done.11.o1), channel_id=1, source_target_pairs={{0,1},{1,0},{2,3},{3,2},{4,5},{5,4},{6,7},{7,6},{8,9},{9,8},{10,11... | collective-permute-start | bytes 1769480 | tf_op jit(solution)/shard_map/ppermute | solution.py:1031
  52.3 11.2 %collective-permute-start.10 = (bf16[2,256,256]{2,1,0:T(8,128)(2,1)}, bf16[2,256,256]{2,1,0:T(8,128)(2,1)S(1)}, u32[]{:S(2)}, u32[]{:S(2)}) collective-permute-start(bf16[2,256,256]{2,1,0:T(8,128)(2,1)} %get-tuple-element.142.kv2), channel_id=1, source_target_pairs={{8,0},{16,8},{24,16},{9,1},{17,9},{25,17},{10,2},{18,10},{26,18},{... | collective-permute-start | bytes 786440 | tf_op jit(solution)/shard_map/ppermute | solution.py:1027
  53.9 37.9 %collective-permute-start.24 = (bf16[432,1152]{1,0:T(8,128)(2,1)}, bf16[432,1152]{1,0:T(8,128)(2,1)}, u32[]{:S(2)}, u32[]{:S(2)}) collective-permute-start(bf16[432,1152]{1,0:T(8,128)(2,1)} %get-tuple-element.152), channel_id=1, source_target_pairs={{0,2},{2,0},{1,3},{3,1},{4,6},{6,4},{5,7},{7,5},{8,10},{10,8},{9,1... | collective-permute-start | bytes 2985992 | tf_op jit(solution)/shard_map/ppermute | solution.py:1031
  54.4 30.6 %collective-permute-start.16 = (bf16[144,1728]{1,0:T(8,128)(2,1)}, bf16[144,1728]{1,0:T(8,128)(2,1)S(1)}, u32[]{:S(2)}, u32[]{:S(2)}) collective-permute-start(bf16[144,1728]{1,0:T(8,128)(2,1)} %collective-permute-done.6.refs_2_), channel_id=1, source_target_pairs={{0,8},{8,0},{16,24},{24,16},{1,9},{9,1},{17,25},{25,17},{2,10},{10... | collective-permute-start | bytes 1493000 | tf_op jit(solution)/shard_map/ppermute | solution.py:1043
  56.9 18.1 %collective-permute-start.8 = (bf16[2,256,256]{2,1,0:T(8,128)(2,1)}, bf16[2,256,256]{2,1,0:T(8,128)(2,1)S(1)}, u32[]{:S(2)}, u32[]{:S(2)}) collective-permute-start(bf16[2,256,256]{2,1,0:T(8,128)(2,1)} %get-tuple-element.142.kv2), channel_id=1, source_target_pairs={{0,16},{8,24},{1,17},{9,25},{2,18},{10,26},{3,19},{11,27},{4,20},{... | collective-permute-start | bytes 786440 | tf_op jit(solution)/shard_map/ppermute | solution.py:1027
  63.5 16.2 %collective-permute-start.9 = (bf16[2,256,256]{2,1,0:T(8,128)(2,1)}, bf16[2,256,256]{2,1,0:T(8,128)(2,1)S(1)}, u32[]{:S(2)}, u32[]{:S(2)}) collective-permute-start(bf16[2,256,256]{2,1,0:T(8,128)(2,1)} %get-tuple-element.142.kv2), channel_id=1, source_target_pairs={{0,8},{8,16},{16,24},{1,9},{9,17},{17,25},{2,10},{10,18},{18,26},{... | collective-permute-start | bytes 786440 | tf_op jit(solution)/shard_map/ppermute | solution.py:1027
  75.0 14.3 %collective-permute-start.18 = (bf16[144,1728]{1,0:T(8,128)(2,1)S(1)}, bf16[144,1728]{1,0:T(8,128)(2,1)S(1)}, u32[]{:S(2)}, u32[]{:S(2)}) collective-permute-start(bf16[144,1728]{1,0:T(8,128)(2,1)S(1)} %copy-done.16), channel_id=1, source_target_pairs={{0,2},{2,0},{1,3},{3,1},{4,6},{6,4},{5,7},{7,5},{8,10},{10,8},{9,1... | collective-permute-start | bytes 1493000 | tf_op jit(solution)/shard_map/ppermute | solution.py:1031
  85.0 58.0 %copy-start.36 = (f32[128,1152]{1,0:T(8,128)}, f32[128,1152]{1,0:T(8,128)S(1)}, u32[]{:S(2)}) copy-start(f32[128,1152]{1,0:T(8,128)S(1)} %get-tuple-element.161.residual.h_residual) | copy-start | bytes 1769476
  85.0 15.5 %collective-permute-start.17 = (bf16[128,1152]{1,0:T(8,128)(2,1)S(1)}, bf16[128,1152]{1,0:T(8,128)(2,1)S(1)}, u32[]{:S(2)}, u32[]{:S(2)}) collective-permute-start(bf16[128,1152]{1,0:T(8,128)(2,1)S(1)} %get-tuple-element.146.x0), channel_id=1, source_target_pairs={{0,16},{8,24},{16,0},{24,8},{1,17},{9,25},{17,1},{25,9},{2,18},{10... | collective-permute-start | bytes 884744 | tf_op jit(solution)/shard_map/ppermute | solution.py:1043
  89.4 19.1 %collective-permute-start.19 = (bf16[144,1728]{1,0:T(8,128)(2,1)S(1)}, bf16[144,1728]{1,0:T(8,128)(2,1)S(1)}, u32[]{:S(2)}, u32[]{:S(2)}) collective-permute-start(bf16[144,1728]{1,0:T(8,128)(2,1)S(1)} %collective-permute-done.18.refs_3_), channel_id=1, source_target_pairs={{0,8},{8,0},{16,24},{24,16},{1,9},{9,1},{17,25},{25,17},{2,10},{10... | collective-permute-start | bytes 1493000 | tf_op jit(solution)/shard_map/ppermute | solution.py:1043
  91.7 21.0 %collective-permute-start.25 = (bf16[432,1152]{1,0:T(8,128)(2,1)}, bf16[432,1152]{1,0:T(8,128)(2,1)S(1)}, u32[]{:S(2)}, u32[]{:S(2)}) collective-permute-start(bf16[432,1152]{1,0:T(8,128)(2,1)} %collective-permute-done.24.refs_11_.w1), channel_id=1, source_target_pairs={{0,1},{1,0},{2,3},{3,2},{4,5},{5,4},{6,7},{7,6},{8,9},{9,8},{10,11... | collective-permute-start | bytes 2985992 | tf_op jit(solution)/shard_map/ppermute | solution.py:1031
  91.7 11.3 %collective-permute-start.13 = (bf16[128,1152]{1,0:T(8,128)(2,1)S(1)}, bf16[128,1152]{1,0:T(8,128)(2,1)S(1)}, u32[]{:S(2)}, u32[]{:S(2)}) collective-permute-start(bf16[128,1152]{1,0:T(8,128)(2,1)S(1)} %get-tuple-element.146.x0), channel_id=1, source_target_pairs={{0,2},{2,0},{1,3},{3,1},{4,6},{6,4},{5,7},{7,5},{8,10},{10,8},{9,1... | collective-permute-start | bytes 884744 | tf_op jit(solution)/shard_map/ppermute | solution.py:1031
  92.1 10.9 %collective-permute-start.14 = (bf16[128,1152]{1,0:T(8,128)(2,1)S(1)}, bf16[128,1152]{1,0:T(8,128)(2,1)S(1)}, u32[]{:S(2)}, u32[]{:S(2)}) collective-permute-start(bf16[128,1152]{1,0:T(8,128)(2,1)S(1)} %get-tuple-element.146.x0), channel_id=1, source_target_pairs={{0,4},{4,0},{1,5},{5,1},{2,6},{6,2},{3,7},{7,3},{8,12},{12,8},{9,1... | collective-permute-start | bytes 884744 | tf_op jit(solution)/shard_map/ppermute | solution.py:1031
  100.4 8.0 %collective-permute-start.15 = (bf16[128,1152]{1,0:T(8,128)(2,1)S(1)}, bf16[128,1152]{1,0:T(8,128)(2,1)S(1)}, u32[]{:S(2)}, u32[]{:S(2)}) collective-permute-start(bf16[128,1152]{1,0:T(8,128)(2,1)S(1)} %get-tuple-element.146.x0), channel_id=1, source_target_pairs={{0,6},{2,4},{4,2},{6,0},{1,7},{3,5},{5,3},{7,1},{8,14},{10,12},{12... | collective-permute-start | bytes 884744 | tf_op jit(solution)/shard_map/ppermute | solution.py:1035
  103.0 6.0 %collective-permute-start.20 = (bf16[144,1728]{1,0:T(8,128)(2,1)}, bf16[144,1728]{1,0:T(8,128)(2,1)S(1)}, u32[]{:S(2)}, u32[]{:S(2)}) collective-permute-start(bf16[144,1728]{1,0:T(8,128)(2,1)} %collective-permute-done.6.refs_2_), channel_id=1, source_target_pairs={{0,1},{1,0},{2,3},{3,2},{4,5},{5,4},{6,7},{7,6},{8,9},{9,8},{10,11... | collective-permute-start | bytes 1493000 | tf_op jit(solution)/shard_map/ppermute | solution.py:1031
  103.0 7.4 %collective-permute-start.22 = (bf16[144,1728]{1,0:T(8,128)(2,1)S(1)}, bf16[144,1728]{1,0:T(8,128)(2,1)S(1)}, u32[]{:S(2)}, u32[]{:S(2)}) collective-permute-start(bf16[144,1728]{1,0:T(8,128)(2,1)S(1)} %collective-permute-done.16.refs_4_), channel_id=1, source_target_pairs={{0,1},{1,0},{2,3},{3,2},{4,5},{5,4},{6,7},{7,6},{8,9},{9,8},{10,11... | collective-permute-start | bytes 1493000 | tf_op jit(solution)/shard_map/ppermute | solution.py:1031
  108.5 3.5 %collective-permute-start.21 = (bf16[144,1728]{1,0:T(8,128)(2,1)S(1)}, bf16[144,1728]{1,0:T(8,128)(2,1)S(1)}, u32[]{:S(2)}, u32[]{:S(2)}) collective-permute-start(bf16[144,1728]{1,0:T(8,128)(2,1)S(1)} %collective-permute-done.18.refs_3_), channel_id=1, source_target_pairs={{0,1},{1,0},{2,3},{3,2},{4,5},{5,4},{6,7},{7,6},{8,9},{9,8},{10,11... | collective-permute-start | bytes 1493000 | tf_op jit(solution)/shard_map/ppermute | solution.py:1031
  108.5 4.3 %collective-permute-start.23 = (bf16[144,1728]{1,0:T(8,128)(2,1)S(1)}, bf16[144,1728]{1,0:T(8,128)(2,1)S(1)}, u32[]{:S(2)}, u32[]{:S(2)}) collective-permute-start(bf16[144,1728]{1,0:T(8,128)(2,1)S(1)} %collective-permute-done.19.refs_5_), channel_id=1, source_target_pairs={{0,1},{1,0},{2,3},{3,2},{4,5},{5,4},{6,7},{7,6},{8,9},{9,8},{10,11... | collective-permute-start | bytes 1493000 | tf_op jit(solution)/shard_map/ppermute | solution.py:1031
  109.0 18.5 %collective-permute-start.26 = (bf16[128,1152]{1,0:T(8,128)(2,1)S(1)}, bf16[128,1152]{1,0:T(8,128)(2,1)S(1)}, u32[]{:S(2)}, u32[]{:S(2)}) collective-permute-start(bf16[128,1152]{1,0:T(8,128)(2,1)S(1)} %collective-permute-done.17.n0), channel_id=1, source_target_pairs={{0,2},{2,0},{1,3},{3,1},{4,6},{6,4},{5,7},{7,5},{8,10},{10,8},{9,1... | collective-permute-start | bytes 884744 | tf_op jit(solution)/shard_map/ppermute | solution.py:1031
  110.4 17.1 %collective-permute-start.27 = (bf16[128,1152]{1,0:T(8,128)(2,1)S(1)}, bf16[128,1152]{1,0:T(8,128)(2,1)S(1)}, u32[]{:S(2)}, u32[]{:S(2)}) collective-permute-start(bf16[128,1152]{1,0:T(8,128)(2,1)S(1)} %collective-permute-done.17.n0), channel_id=1, source_target_pairs={{0,4},{4,0},{1,5},{5,1},{2,6},{6,2},{3,7},{7,3},{8,12},{12,8},{9,1... | collective-permute-start | bytes 884744 | tf_op jit(solution)/shard_map/ppermute | solution.py:1031
  112.0 15.6 %collective-permute-start.28 = (bf16[128,1152]{1,0:T(8,128)(2,1)S(1)}, bf16[128,1152]{1,0:T(8,128)(2,1)S(1)}, u32[]{:S(2)}, u32[]{:S(2)}) collective-permute-start(bf16[128,1152]{1,0:T(8,128)(2,1)S(1)} %collective-permute-done.17.n0), channel_id=1, source_target_pairs={{0,6},{2,4},{4,2},{6,0},{1,7},{3,5},{5,3},{7,1},{8,14},{10,12},{12... | collective-permute-start | bytes 884744 | tf_op jit(solution)/shard_map/ppermute | solution.py:1035
  127.5 10.0 %collective-permute-start.29 = (bf16[128,1152]{1,0:T(8,128)(2,1)S(1)}, bf16[128,1152]{1,0:T(8,128)(2,1)S(1)}, u32[]{:S(2)}, u32[]{:S(2)}) collective-permute-start(bf16[128,1152]{1,0:T(8,128)(2,1)S(1)} %get-tuple-element.158), channel_id=1, source_target_pairs={{0,2},{2,0},{1,3},{3,1},{4,6},{6,4},{5,7},{7,5},{8,10},{10,8},{9,1... | collective-permute-start | bytes 884744 | tf_op jit(solution)/shard_map/ppermute | solution.py:1031
  128.7 14.2 %collective-permute-start.30 = (bf16[128,1152]{1,0:T(8,128)(2,1)S(1)}, bf16[128,1152]{1,0:T(8,128)(2,1)S(1)}, u32[]{:S(2)}, u32[]{:S(2)}) collective-permute-start(bf16[128,1152]{1,0:T(8,128)(2,1)S(1)} %get-tuple-element.159), channel_id=1, source_target_pairs={{0,4},{4,0},{1,5},{5,1},{2,6},{6,2},{3,7},{7,3},{8,12},{12,8},{9,1... | collective-permute-start | bytes 884744 | tf_op jit(solution)/shard_map/ppermute | solution.py:1031
  130.3 12.6 %collective-permute-start.31 = (bf16[128,1152]{1,0:T(8,128)(2,1)S(1)}, bf16[128,1152]{1,0:T(8,128)(2,1)S(1)}, u32[]{:S(2)}, u32[]{:S(2)}) collective-permute-start(bf16[128,1152]{1,0:T(8,128)(2,1)S(1)} %get-tuple-element.160), channel_id=1, source_target_pairs={{0,6},{2,4},{4,2},{6,0},{1,7},{3,5},{5,3},{7,1},{8,14},{10,12},{12... | collective-permute-start | bytes 884744 | tf_op jit(solution)/shard_map/ppermute | solution.py:1035
  145.1 19.9 %collective-permute-start.32 = (bf16[128,1152]{1,0:T(8,128)(2,1)S(1)}, bf16[128,1152]{1,0:T(8,128)(2,1)S(1)}, u32[]{:S(2)}, u32[]{:S(2)}) collective-permute-start(bf16[128,1152]{1,0:T(8,128)(2,1)S(1)} %get-tuple-element.172.x0), channel_id=1, source_target_pairs={{0,2},{2,0},{1,3},{3,1},{4,6},{6,4},{5,7},{7,5},{8,10},{10,8},{9,1... | collective-permute-start | bytes 884744 | tf_op jit(solution)/shard_map/ppermute | solution.py:1031
  146.6 18.4 %collective-permute-start.33 = (bf16[128,1152]{1,0:T(8,128)(2,1)S(1)}, bf16[128,1152]{1,0:T(8,128)(2,1)S(1)}, u32[]{:S(2)}, u32[]{:S(2)}) collective-permute-start(bf16[128,1152]{1,0:T(8,128)(2,1)S(1)} %get-tuple-element.172.x0), channel_id=1, source_target_pairs={{0,4},{4,0},{1,5},{5,1},{2,6},{6,2},{3,7},{7,3},{8,12},{12,8},{9,1... | collective-permute-start | bytes 884744 | tf_op jit(solution)/shard_map/ppermute | solution.py:1031
  147.1 17.9 %collective-permute-start.34 = (bf16[128,1152]{1,0:T(8,128)(2,1)S(1)}, bf16[128,1152]{1,0:T(8,128)(2,1)S(1)}, u32[]{:S(2)}, u32[]{:S(2)}) collective-permute-start(bf16[128,1152]{1,0:T(8,128)(2,1)S(1)} %get-tuple-element.172.x0), channel_id=1, source_target_pairs={{0,6},{2,4},{4,2},{6,0},{1,7},{3,5},{5,3},{7,1},{8,14},{10,12},{12... | collective-permute-start | bytes 884744 | tf_op jit(solution)/shard_map/ppermute | solution.py:1035
  148.6 16.5 %collective-permute-start.35 = (bf16[128,1152]{1,0:T(8,128)(2,1)S(1)}, bf16[128,1152]{1,0:T(8,128)(2,1)S(1)}, u32[]{:S(2)}, u32[]{:S(2)}) collective-permute-start(bf16[128,1152]{1,0:T(8,128)(2,1)S(1)} %get-tuple-element.172.x0), channel_id=1, source_target_pairs={{0,16},{8,24},{16,0},{24,8},{1,17},{9,25},{17,1},{25,9},{2,18},{10... | collective-permute-start | bytes 884744 | tf_op jit(solution)/shard_map/ppermute | solution.py:1043
  165.0 18.5 %collective-permute-start.36 = (bf16[128,1152]{1,0:T(8,128)(2,1)S(1)}, bf16[128,1152]{1,0:T(8,128)(2,1)S(1)}, u32[]{:S(2)}, u32[]{:S(2)}) collective-permute-start(bf16[128,1152]{1,0:T(8,128)(2,1)S(1)} %collective-permute-done.35.d0), channel_id=1, source_target_pairs={{0,2},{2,0},{1,3},{3,1},{4,6},{6,4},{5,7},{7,5},{8,10},{10,8},{9,1... | collective-permute-start | bytes 884744 | tf_op jit(solution)/shard_map/ppermute | solution.py:1031
  166.4 17.1 %collective-permute-start.37 = (bf16[128,1152]{1,0:T(8,128)(2,1)S(1)}, bf16[128,1152]{1,0:T(8,128)(2,1)S(1)}, u32[]{:S(2)}, u32[]{:S(2)}) collective-permute-start(bf16[128,1152]{1,0:T(8,128)(2,1)S(1)} %collective-permute-done.35.d0), channel_id=1, source_target_pairs={{0,4},{4,0},{1,5},{5,1},{2,6},{6,2},{3,7},{7,3},{8,12},{12,8},{9,1... | collective-permute-start | bytes 884744 | tf_op jit(solution)/shard_map/ppermute | solution.py:1031
  167.4 16.1 %collective-permute-start.38 = (bf16[128,1152]{1,0:T(8,128)(2,1)S(1)}, bf16[128,1152]{1,0:T(8,128)(2,1)S(1)}, u32[]{:S(2)}, u32[]{:S(2)}) collective-permute-start(bf16[128,1152]{1,0:T(8,128)(2,1)S(1)} %collective-permute-done.35.d0), channel_id=1, source_target_pairs={{0,6},{2,4},{4,2},{6,0},{1,7},{3,5},{5,3},{7,1},{8,14},{10,12},{12... | collective-permute-start | bytes 884744 | tf_op jit(solution)/shard_map/ppermute | solution.py:1035
  183.6 20.8 %collective-permute-start.39 = (bf16[128,1152]{1,0:T(8,128)(2,1)S(1)}, bf16[128,1152]{1,0:T(8,128)(2,1)S(1)}, u32[]{:S(2)}, u32[]{:S(2)}) collective-permute-start(bf16[128,1152]{1,0:T(8,128)(2,1)S(1)} %get-tuple-element.182), channel_id=1, source_target_pairs={{0,2},{2,0},{1,3},{3,1},{4,6},{6,4},{5,7},{7,5},{8,10},{10,8},{9,1... | collective-permute-start | bytes 884744 | tf_op jit(solution)/shard_map/ppermute | solution.py:1031
  184.9 19.5 %collective-permute-start.40 = (bf16[128,1152]{1,0:T(8,128)(2,1)S(1)}, bf16[128,1152]{1,0:T(8,128)(2,1)S(1)}, u32[]{:S(2)}, u32[]{:S(2)}) collective-permute-start(bf16[128,1152]{1,0:T(8,128)(2,1)S(1)} %get-tuple-element.183), channel_id=1, source_target_pairs={{0,4},{4,0},{1,5},{5,1},{2,6},{6,2},{3,7},{7,3},{8,12},{12,8},{9,1... | collective-permute-start | bytes 884744 | tf_op jit(solution)/shard_map/ppermute | solution.py:1031
  185.9 18.5 %collective-permute-start.41 = (bf16[128,1152]{1,0:T(8,128)(2,1)S(1)}, bf16[128,1152]{1,0:T(8,128)(2,1)S(1)}, u32[]{:S(2)}, u32[]{:S(2)}) collective-permute-start(bf16[128,1152]{1,0:T(8,128)(2,1)S(1)} %get-tuple-element.184), channel_id=1, source_target_pairs={{0,6},{2,4},{4,2},{6,0},{1,7},{3,5},{5,3},{7,1},{8,14},{10,12},{12... | collective-permute-start | bytes 884744 | tf_op jit(solution)/shard_map/ppermute | solution.py:1035
  204.5 20.2 %collective-permute-start.42 = (bf16[2,432,1792]{2,1,0:T(8,128)(2,1)}, bf16[2,432,1792]{2,1,0:T(8,128)(2,1)}, u32[]{:S(2)}, u32[]{:S(2)}) collective-permute-start(bf16[2,432,1792]{2,1,0:T(8,128)(2,1)} %get-tuple-element.202), channel_id=1, source_target_pairs={{0,1},{1,0},{2,3},{3,2},{4,5},{5,4},{6,7},{7,6},{8,9},{9,8},{10,11... | collective-permute-start | bytes 9289736 | tf_op jit(solution)/shard_map/ppermute | solution.py:1031
  214.9 21.5 %collective-permute-start.47 = (bf16[128,1024]{1,0:T(8,128)(2,1)S(1)}, bf16[128,1024]{1,0:T(8,128)(2,1)S(1)}, u32[]{:S(2)}, u32[]{:S(2)}) collective-permute-start(bf16[128,1024]{1,0:T(8,128)(2,1)S(1)} %get-tuple-element.215.own_heads), channel_id=1, source_target_pairs={{0,4},{4,0},{1,5},{5,1},{2,6},{6,2},{3,7},{7,3},{8,12},{12,8},{9,1... | collective-permute-start | bytes 786440 | tf_op jit(solution)/shard_map/ppermute | solution.py:1031
  216.0 20.2 %collective-permute-start.43 = (bf16[2,256,256]{2,1,0:T(8,128)(2,1)}, bf16[2,256,256]{2,1,0:T(8,128)(2,1)S(1)}, u32[]{:S(2)}, u32[]{:S(2)}) collective-permute-start(bf16[2,256,256]{2,1,0:T(8,128)(2,1)} %get-tuple-element.205), channel_id=1, source_target_pairs={{16,0},{24,8},{17,1},{25,9},{18,2},{26,10},{19,3},{27,11},{20,4},{... | collective-permute-start | bytes 786440 | tf_op jit(solution)/shard_map/ppermute | solution.py:1027
  217.3 18.9 %collective-permute-start.44 = (bf16[2,256,256]{2,1,0:T(8,128)(2,1)}, bf16[2,256,256]{2,1,0:T(8,128)(2,1)S(1)}, u32[]{:S(2)}, u32[]{:S(2)}) collective-permute-start(bf16[2,256,256]{2,1,0:T(8,128)(2,1)} %get-tuple-element.206), channel_id=1, source_target_pairs={{8,0},{16,8},{24,16},{9,1},{17,9},{25,17},{10,2},{18,10},{26,18},{... | collective-permute-start | bytes 786440 | tf_op jit(solution)/shard_map/ppermute | solution.py:1027
  218.6 17.6 %collective-permute-start.45 = (bf16[2,256,256]{2,1,0:T(8,128)(2,1)}, bf16[2,256,256]{2,1,0:T(8,128)(2,1)S(1)}, u32[]{:S(2)}, u32[]{:S(2)}) collective-permute-start(bf16[2,256,256]{2,1,0:T(8,128)(2,1)} %get-tuple-element.207), channel_id=1, source_target_pairs={{0,8},{8,16},{16,24},{1,9},{9,17},{17,25},{2,10},{10,18},{18,26},{... | collective-permute-start | bytes 786440 | tf_op jit(solution)/shard_map/ppermute | solution.py:1027
  224.7 11.7 %collective-permute-start.46 = (bf16[128,960]{1,0:T(8,128)(2,1)}, bf16[128,960]{1,0:T(8,128)(2,1)S(1)}, u32[]{:S(2)}, u32[]{:S(2)}) collective-permute-start(bf16[128,960]{1,0:T(8,128)(2,1)} %get-tuple-element.213), channel_id=1, source_target_pairs={{0,4},{4,0},{1,5},{5,1},{2,6},{6,2},{3,7},{7,3},{8,12},{12,8},{9,1... | collective-permute-start | bytes 737288 | tf_op jit(solution)/shard_map/ppermute | solution.py:1031
  239.9 3.6 %collective-permute-start.48 = (bf16[2,288,896]{2,1,0:T(8,128)(2,1)S(1)}, bf16[2,288,896]{2,1,0:T(8,128)(2,1)S(1)}, u32[]{:S(2)}, u32[]{:S(2)}) collective-permute-start(bf16[2,288,896]{2,1,0:T(8,128)(2,1)S(1)} %get-tuple-element.222), channel_id=1, source_target_pairs={{0,1},{1,0},{2,3},{3,2},{4,5},{5,4},{6,7},{7,6},{8,9},{9,8},{10,11... | collective-permute-start | bytes 3096584 | tf_op jit(solution)/shard_map/ppermute | solution.py:1031
  239.9 14.6 %collective-permute-start.51 = (bf16[288,864]{1,0:T(8,128)(2,1)}, bf16[288,864]{1,0:T(8,128)(2,1)S(1)}, u32[]{:S(2)}, u32[]{:S(2)}) collective-permute-start(bf16[288,864]{1,0:T(8,128)(2,1)} %copy-done.18), channel_id=1, source_target_pairs={{0,8},{8,0},{16,24},{24,16},{1,9},{9,1},{17,25},{25,17},{2,10},{10... | collective-permute-start | bytes 1493000 | tf_op jit(solution)/shard_map/ppermute | solution.py:1043
  242.0 5.7 %collective-permute-start.49 = (bf16[2,128,256]{2,1,0:T(8,128)(2,1)S(1)}, bf16[2,128,256]{2,1,0:T(8,128)(2,1)S(1)}, u32[]{:S(2)}, u32[]{:S(2)}) collective-permute-start(bf16[2,128,256]{2,1,0:T(8,128)(2,1)S(1)} %dynamic-slice_convert_fusion), channel_id=1, source_target_pairs={{0,4},{4,0},{1,5},{5,1},{2,6},{6,2},{3,7},{7,3},{8,12},{12,8},{9,1... | collective-permute-start | bytes 393224 | tf_op jit(solution)/shard_map/ppermute | solution.py:1031
  251.2 4.8 %collective-permute-start.52 = (bf16[144,384]{1,0:T(8,128)(2,1)S(1)}, bf16[144,384]{1,0:T(8,128)(2,1)S(1)}, u32[]{:S(2)}, u32[]{:S(2)}) collective-permute-start(bf16[144,384]{1,0:T(8,128)(2,1)S(1)} %get-tuple-element.236), channel_id=1, source_target_pairs={{0,4},{4,0},{1,5},{5,1},{2,6},{6,2},{3,7},{7,3},{8,12},{12,8},{9,1... | collective-permute-start | bytes 331784 | tf_op jit(solution)/shard_map/ppermute | solution.py:1031
  252.8 12.4 %collective-permute-start.53 = (bf16[216,1152]{1,0:T(8,128)(2,1)S(1)}, bf16[216,1152]{1,0:T(8,128)(2,1)S(1)}, u32[]{:S(2)}, u32[]{:S(2)}) collective-permute-start(bf16[216,1152]{1,0:T(8,128)(2,1)S(1)} %copy-done.22), channel_id=1, source_target_pairs={{0,8},{8,0},{16,24},{24,16},{1,9},{9,1},{17,25},{25,17},{2,10},{10... | collective-permute-start | bytes 1493000 | tf_op jit(solution)/shard_map/ppermute | solution.py:1043
  257.2 8.0 %collective-permute-start.54 = (bf16[592,384]{1,0:T(8,128)(2,1)S(1)}, bf16[592,384]{1,0:T(8,128)(2,1)S(1)}, u32[]{:S(2)}, u32[]{:S(2)}) collective-permute-start(bf16[592,384]{1,0:T(8,128)(2,1)S(1)} %get-tuple-element.241), channel_id=1, source_target_pairs={{0,1},{1,0},{2,3},{3,2},{4,5},{5,4},{6,7},{7,6},{8,9},{9,8},{10,11... | collective-permute-start | bytes 1363976 | tf_op jit(solution)/shard_map/ppermute | solution.py:1031
  257.3 17.1 %collective-permute-start.50 = (bf16[288,896]{1,0:T(8,128)(2,1)S(1)}, bf16[288,896]{1,0:T(8,128)(2,1)S(1)}, u32[]{:S(2)}, u32[]{:S(2)}) collective-permute-start(bf16[288,896]{1,0:T(8,128)(2,1)S(1)} %get-tuple-element.223), channel_id=1, source_target_pairs={{0,2},{2,0},{1,3},{3,1},{4,6},{6,4},{5,7},{7,5},{8,10},{10,8},{9,1... | collective-permute-start | bytes 1548296 | tf_op jit(solution)/shard_map/ppermute | solution.py:1031
  266.6 10.0 %collective-permute-start.55 = (bf16[304,384]{1,0:T(8,128)(2,1)}, bf16[304,384]{1,0:T(8,128)(2,1)S(1)}, u32[]{:S(2)}, u32[]{:S(2)}) collective-permute-start(bf16[304,384]{1,0:T(8,128)(2,1)} %get-tuple-element.244), channel_id=1, source_target_pairs={{0,2},{2,0},{1,3},{3,1},{4,6},{6,4},{5,7},{7,5},{8,10},{10,8},{9,1... | collective-permute-start | bytes 700424 | tf_op jit(solution)/shard_map/ppermute | solution.py:1031
  268.0 12.7 %collective-permute-start.56 = (bf16[216,1152]{1,0:T(8,128)(2,1)S(1)}, bf16[216,1152]{1,0:T(8,128)(2,1)S(1)}, u32[]{:S(2)}, u32[]{:S(2)}) collective-permute-start(bf16[216,1152]{1,0:T(8,128)(2,1)S(1)} %copy-done.20), channel_id=1, source_target_pairs={{0,8},{8,0},{16,24},{24,16},{1,9},{9,1},{17,25},{25,17},{2,10},{10... | collective-permute-start | bytes 1493000 | tf_op jit(solution)/shard_map/ppermute | solution.py:1043
  270.9 11.9 %all-to-all-start.1 = ((bf16[4,144,432]{2,1,0:T(8,128)(2,1)}), bf16[4,144,432]{2,1,0:T(8,128)(2,1)S(1)}, u32[]{:S(2)}, u32[]{:S(2)}) async-start(bf16[4,144,432]{2,1,0:T(8,128)(2,1)} %bitcast.45), calls=%async_computation.1 | async-start | bytes 1179648 | tf_op jit(solution)/shard_map/all_to_all | solution.py:1192
  282.8 24.2 %all-to-all-start = ((bf16[4,384,256]{2,1,0:T(8,128)(2,1)}), bf16[4,384,256]{2,1,0:T(8,128)(2,1)S(1)}, u32[]{:S(2)}, u32[]{:S(2)}) async-start(bf16[4,384,256]{2,1,0:T(8,128)(2,1)} %shard_map.254), calls=%async_computation | async-start | bytes 1572864 | tf_op jit(solution)/shard_map/all_to_all | solution.py:1197
  289.4 13.9 %collective-permute-start.57 = (bf16[2,288,432]{2,1,0:T(8,128)(2,1)S(1)}, bf16[2,288,432]{2,1,0:T(8,128)(2,1)S(1)}, u32[]{:S(2)}, u32[]{:S(2)}) collective-permute-start(bf16[2,288,432]{2,1,0:T(8,128)(2,1)S(1)} %shard_map.257), channel_id=1, source_target_pairs={{0,2},{2,0},{1,3},{3,1},{4,6},{6,4},{5,7},{7,5},{8,10},{10,8},{9,1... | collective-permute-start | bytes 1493000 | tf_op jit(solution)/shard_map/ppermute | solution.py:1031
  293.1 11.4 %collective-permute-start.58 = (bf16[288,432]{1,0:T(8,128)(2,1)S(1)}, bf16[288,432]{1,0:T(8,128)(2,1)S(1)}, u32[]{:S(2)}, u32[]{:S(2)}) collective-permute-start(bf16[288,432]{1,0:T(8,128)(2,1)S(1)} %get-tuple-element.265), channel_id=1, source_target_pairs={{0,1},{1,0},{2,3},{3,2},{4,5},{5,4},{6,7},{7,6},{8,9},{9,8},{10,11... | collective-permute-start | bytes 746504 | tf_op jit(solution)/shard_map/ppermute | solution.py:1031
  303.3 1.6 collective-permute-start.59
  (73 other events, 587.2 us)

commit v3 on v2

--- a/solution.py
+++ b/solution.py
@@ -235,7 +235,7 @@
     dim = gain.shape[1]
     return call(
         queries_kernel,
-        3,
+        6,
         (low(HQ * rows, dim), wide(HQ * rows, dim)),
         [SCALARS, *[VECTORS] * 3, *[ANYWHERE] * 4],
         [pltpu.VMEM((model, HQ * dim), bf16), pltpu.SemaphoreType.DMA((4,))],
@@ -279,7 +279,7 @@
     dim, span = queries.shape[1], key_ids.shape[1]
     return call(
         attend_kernel,
-        5,
+        2,
         (wide(HQ * rows, span), low(rows, HQ * dim), wide(rows, model), wide(rows, model), low(rows, model)),
         [SCALARS, *[VECTORS] * 10, *[ANYWHERE] * 4],
         [
@@ -744,7 +744,7 @@
     model = pieces[0].shape[0] * 4
     return call(
         queries_back_kernel,
-        3,
+        4,
         wide(rows, model),
         [SCALARS, VECTORS, *[ANYWHERE] * 4],
         [pltpu.VMEM((model, width), bf16), pltpu.SemaphoreType.DMA((4,))],
@@ -835,7 +835,7 @@
     unit, more = every.shape[1] // 4, gains.shape[0]
     return call(
         last_products_kernel,
-        3,
+        2,
         (wide(2, unit, width), low(2 * unit + more, width), wide(more, width)),
         [SCALARS, *[VECTORS] * 4],
         [pltpu.VMEM((2 * rows, width), bf16)],

time: 313 us -> 308 us (0.984)
  starting transfers between devices: 82.6 us -> 77.9 us
    ppermute x41, waiting for transfers between devices: 50 us -> 42.7 us  [swap(): return lax.ppermute(value, axis, [(0, 1), (1, 0)])]
    ppermute x6, waiting for transfers between devices: 4.97 us -> 12.3 us  [diagonal(): return lax.ppermute(value, ('near', 'chip'), [(i, 3 - i) for i in range(4)])]
    unnamed x150 -> x146, local copies, waits for them, and re-layouts: 27.1 us -> 27.2 us
where the time goes in v3:
time: 308 us; the launch traced here: 304 us
  Pallas kernels  111 us (36%)
  waiting for transfers between devices  79.5 us (26%)
  starting transfers between devices  77.9 us (25%)
  local copies, waits for them, and re-layouts  32.9 us (11%)
    pallas_call x23, Pallas kernels, call(): pl.pallas_call(kernel, out_shape=out_shape, in_specs=in_specs, out_specs=...  94.1 us
    ppermute x41, waiting for transfers between devices, swap(): return lax.ppermute(value, axis, [(0, 1), (1, 0)])  42.7 us
    ppermute x41, starting transfers between devices, swap(): return lax.ppermute(value, axis, [(0, 1), (1, 0)])  31.8 us
    unnamed x146, local copies, waits for them, and re-layouts  27.2 us
    ppermute x6, starting transfers between devices, shift(): return lax.ppermute(value, 'far', pairs)  18.2 us
    pallas_call x1, Pallas kernels, weight_grads(): pl.pallas_call(functools.partial(weights_kernel, (start, width)), out_sha...  17.3 us
    ppermute x7, waiting for transfers between devices, far_swap(): lax.ppermute(value, 'far', [(i, i ^ step) for i in range(lax.axis_size('f...  15 us
    ppermute x7, starting transfers between devices, far_swap(): lax.ppermute(value, 'far', [(i, i ^ step) for i in range(lax.axis_size('f...  12.9 us
  transfers between devices with their start and end apart: 62, of which 20 were waited for; matrix products, arithmetic and copies ran while one was open for 2% of the time, Pallas kernels for 35%

profile of v3, /device:TPU:0, one launch (start us, length us, event | category | flops | bytes accessed | tf_op | source)
XLA Modules:
  0.0 304.4 jit_solution(2530680146723959637)
XLA Ops:
  0.6 3.0 collective-permute-start.3
  3.7 6.9 %shard_map.237 = (bf16[2,288,1728]{2,1,0:T(8,128)(2,1)S(1)}, bf16[144,1728]{1,0:T(8,128)(2,1)S(1)}, bf16[144,1728]{1,0:T(8,128)(2,1)S(1)}) custom-call(s32[6]{0:T(128)S(1)} %stack.29.place, bf16[288,6912]{1,0:T(8,128)(2,1)} %gate.1, bf16[288,6912]{1,0:T(8,128)(2,1)} %up.1), custom_call_target="tpu_custom_call" | custom-call | flops 6000000000 | bytes 1048576 | tf_op jit(solution)/shard_map/pallas_call | solution.py:38
  12.2 3.4 %dynamic-slice_bitcast_fusion = (bf16[432,1152]{1,0:T(8,128)(2,1)}, bf16[432,1152]{1,0:T(8,128)(2,1)S(1)}) fusion(bf16[1,2,2,432,1152]{4,3,2,1,0:T(8,128)(2,1)} %bitcast.46, s32[]{:T(128)S(6)} %select_n.52, s32[]{:T(128)S(6)} %select_n.58, s32[]{:T(128)S(6)} %select_n.54), kind=kLoop, calls=%fused_computation | loop fusion | bytes 3981324 | tf_op jit(solution)/shard_map/reshape | solution.py:1107
  15.6 1.5 collective-permute-start.2
  17.3 7.9 %collective-permute-done.2.peer = bf16[128,1152]{1,0:T(8,128)(2,1)S(1)} collective-permute-done((bf16[128,1152]{1,0:T(8,128)(2,1)}, bf16[128,1152]{1,0:T(8,128)(2,1)S(1)}, u32[]{:S(2)}, u32[]{:S(2)}) %collective-permute-start.2) | collective-permute-done | bytes 294944 | tf_op jit(solution)/shard_map/ppermute | solution.py:1031
  26.8 1.7 collective-permute-start.11
  33.0 3.2 %shard_map.238 = (bf16[128,1152]{1,0:T(8,128)(2,1)S(1)}, bf16[2,256,256]{2,1,0:T(8,128)(2,1)}, f32[256,256]{1,0:T(8,128)S(1)}, bf16[256,1152]{1,0:T(8,128)(2,1)S(1)}) custom-call(s32[6]{0:T(128)S(1)} %stack.29.place, bf16[128,1152]{1,0:T(8,128)(2,1)S(1)} %bitcast.38, bf16[128,1152]{1,0:T(8,128)(2,1)S(1)} %copy-done.26, f32[1,1152]{1,0:T(1,128)S(1)} %reshape.191.gain_in, ...), custom_call_target="tpu_custom_call" | custom-call | flops 2000000000 | bytes 1048576 | tf_op jit(solution)/shard_map/pallas_call | solution.py:38
  39.7 5.6 %collective-permute-start.8 = (bf16[2,256,256]{2,1,0:T(8,128)(2,1)}, bf16[2,256,256]{2,1,0:T(8,128)(2,1)S(1)}, u32[]{:S(2)}, u32[]{:S(2)}) collective-permute-start(bf16[2,256,256]{2,1,0:T(8,128)(2,1)} %get-tuple-element.142.kv2), channel_id=1, source_target_pairs={{0,16},{8,24},{1,17},{9,25},{2,18},{10,26},{3,19},{11,27},{4,20},{... | collective-permute-start | bytes 786440 | tf_op jit(solution)/shard_map/ppermute | solution.py:1027
  46.0 8.1 %collective-permute-done.11.o1 = bf16[256,1152]{1,0:T(8,128)(2,1)} collective-permute-done((bf16[256,1152]{1,0:T(8,128)(2,1)}, bf16[256,1152]{1,0:T(8,128)(2,1)}, u32[]{:S(2)}, u32[]{:S(2)}) %collective-permute-start.11) | collective-permute-done | bytes 589856 | tf_op jit(solution)/shard_map/ppermute | solution.py:1031
  54.3 1.6 collective-permute-start.16
  56.5 4.2 %collective-permute-start.9 = (bf16[2,256,256]{2,1,0:T(8,128)(2,1)}, bf16[2,256,256]{2,1,0:T(8,128)(2,1)S(1)}, u32[]{:S(2)}, u32[]{:S(2)}) collective-permute-start(bf16[2,256,256]{2,1,0:T(8,128)(2,1)} %get-tuple-element.142.kv2), channel_id=1, source_target_pairs={{0,8},{8,16},{16,24},{1,9},{9,17},{17,25},{2,10},{10,18},{18,26},{... | collective-permute-start | bytes 786440 | tf_op jit(solution)/shard_map/ppermute | solution.py:1027
  62.8 2.7 shard_map.239
  66.3 7.2 %collective-permute-done.9.kv1 = bf16[2,256,256]{2,1,0:T(8,128)(2,1)S(1)} collective-permute-done((bf16[2,256,256]{2,1,0:T(8,128)(2,1)}, bf16[2,256,256]{2,1,0:T(8,128)(2,1)S(1)}, u32[]{:S(2)}, u32[]{:S(2)}) %collective-permute-start.9) | collective-permute-done | bytes 262176 | tf_op jit(solution)/shard_map/ppermute | solution.py:1027
  73.6 4.5 %shard_map.240 = (f32[512,1024]{1,0:T(8,128)}, bf16[128,1024]{1,0:T(8,128)(2,1)S(1)}, f32[128,1152]{1,0:T(8,128)S(1)}, f32[128,1152]{1,0:T(8,128)S(1)}, bf16[128,1152]{1,0:T(8,128)(2,1)S(1)}) custom-call(s32[6]{0:T(128)S(1)} %stack.29.place, bf16[512,256]{1,0:T(8,128)(2,1)S(1)} %get-tuple-element.141.queries.h_queries, ...), custom_call_target="tpu_custom_call" | custom-call | flops 2000000000 | bytes 1048576 | tf_op jit(solution)/shard_map/pallas_call | solution.py:38
  79.0 2.7 collective-permute-start.17
  81.6 3.8 %collective-permute-done.18.refs_3_ = bf16[144,1728]{1,0:T(8,128)(2,1)S(1)} collective-permute-done((bf16[144,1728]{1,0:T(8,128)(2,1)}, bf16[144,1728]{1,0:T(8,128)(2,1)S(1)}, u32[]{:S(2)}, u32[]{:S(2)}) %collective-permute-start.18) | collective-permute-done | bytes 497696 | tf_op jit(solution)/shard_map/ppermute | solution.py:1031
  85.4 1.6 collective-permute-start.19
  87.6 1.5 collective-permute-start.14
  89.1 5.9 %collective-permute-done.17.n0 = bf16[128,1152]{1,0:T(8,128)(2,1)S(1)} collective-permute-done((bf16[128,1152]{1,0:T(8,128)(2,1)S(1)}, bf16[128,1152]{1,0:T(8,128)(2,1)S(1)}, u32[]{:S(2)}, u32[]{:S(2)}) %collective-permute-start.17) | collective-permute-done | bytes 294944 | tf_op jit(solution)/shard_map/ppermute | solution.py:1043
  95.0 1.5 collective-permute-start.15
  97.0 6.7 %collective-permute-done.15.x3 = bf16[128,1152]{1,0:T(8,128)(2,1)S(1)} collective-permute-done((bf16[128,1152]{1,0:T(8,128)(2,1)S(1)}, bf16[128,1152]{1,0:T(8,128)(2,1)S(1)}, u32[]{:S(2)}, u32[]{:S(2)}) %collective-permute-start.15) | collective-permute-done | bytes 294944 | tf_op jit(solution)/shard_map/ppermute | solution.py:1035
  105.1 1.5 collective-permute-start.27
  106.6 1.5 collective-permute-start.28
  109.1 13.8 %shard_map.241 = (bf16[512,1152]{1,0:T(8,128)(2,1)}, bf16[512,1728]{1,0:T(8,128)(2,1)}, bf16[512,1728]{1,0:T(8,128)(2,1)}, bf16[512,1728]{1,0:T(8,128)(2,1)}, f3...) custom-call(s32[6]{0:T(128)S(1)} %stack.29.place, ...), custom_call_target="tpu_custom_call" | custom-call | flops 12999999488 | bytes 1048576 | tf_op jit(solution)/shard_map/pallas_call | solution.py:38
  123.4 1.5 collective-permute-start.30
  124.9 1.5 collective-permute-start.31
  126.4 6.4 %collective-permute-done.29.r1 = bf16[128,1152]{1,0:T(8,128)(2,1)S(1)} collective-permute-done((bf16[128,1152]{1,0:T(8,128)(2,1)S(1)}, bf16[128,1152]{1,0:T(8,128)(2,1)S(1)}, u32[]{:S(2)}, u32[]{:S(2)}) %collective-permute-start.29) | collective-permute-done | bytes 294944 | tf_op jit(solution)/shard_map/ppermute | solution.py:1031
  132.9 5.6 %collective-permute-done.31.r3 = bf16[128,1152]{1,0:T(8,128)(2,1)S(1)} collective-permute-done((bf16[128,1152]{1,0:T(8,128)(2,1)S(1)}, bf16[128,1152]{1,0:T(8,128)(2,1)S(1)}, u32[]{:S(2)}, u32[]{:S(2)}) %collective-permute-start.31) | collective-permute-done | bytes 294944 | tf_op jit(solution)/shard_map/ppermute | solution.py:1035
  140.6 1.3 collective-permute-start.32
  144.1 2.6 collective-permute-start.35
  146.7 13.6 %shard_map.243 = (bf16[1728,1024]{1,0:T(8,128)(2,1)}, bf16[512,960]{1,0:T(8,128)(2,1)}, bf16[512,960]{1,0:T(8,128)(2,1)}) custom-call(s32[6]{0:T(128)S(1)} %stack.29.place, bf16[512,1728]{1,0:T(8,128)(2,1)} %get-tuple-element.164.own, bf16[128,1152]{1,0:T(8,128)(2,1)S(1)} %collective-permute-done.17.n0, bf16[128,1152]{1,0:T(8,128)(2,1)S(1)} %collective-permute-done.26.n1, ...), custom_call_target="tpu_custom_call" | custom-call | flops 11000000512 | bytes 1048576 | tf_op jit(solution)/shard_map/pallas_call | solution.py:38
  160.3 1.4 collective-permute-start.36
  163.9 14.9 %shard_map.244 = (bf16[512,1152]{1,0:T(8,128)(2,1)}, bf16[512,1728]{1,0:T(8,128)(2,1)}, bf16[512,1728]{1,0:T(8,128)(2,1)}, f32[128,1152]{1,0:T(8,128)}, bf16[128...) custom-call(s32[6]{0:T(128)S(1)} %stack.29.place, ...), custom_call_target="tpu_custom_call" | custom-call | flops 15000000512 | bytes 1048576 | tf_op jit(solution)/shard_map/pallas_call | solution.py:38
  178.8 1.4 collective-permute-start.39
  182.4 17.3 %shard_map.245 = (bf16[2,432,1792]{2,1,0:T(8,128)(2,1)}, bf16[2,432,1792]{2,1,0:T(8,128)(2,1)}) custom-call(s32[6]{0:T(128)S(1)} %stack.29.place, bf16[512,1152]{1,0:T(8,128)(2,1)} %get-tuple-element.185.h_normed, bf16[512,1152]{1,0:T(8,128)(2,1)} %get-tuple-element.186.h_down, bf16[512,1728]{1,0:T(8,128)(2,1)} %get-tuple-element.188.h_gate, ...), custom_call_target="tpu_custom_call" | custom-call | flops 16000000000 | bytes 1048576 | tf_op jit(solution)/shard_map/pallas_call | solution.py:495
  200.6 9.6 %shard_map.246 = (f32[128,1152]{1,0:T(8,128)}, bf16[128,960]{1,0:T(8,128)(2,1)}, bf16[128,960]{1,0:T(8,128)(2,1)}, f32[2,1152]{1,0:T(2,128)}, f32[1,256]{1,0:T(1...) custom-call(s32[6]{0:T(128)} %copy-done.6, ...), custom_call_target="tpu_custom_call" | custom-call | flops 8000000000 | bytes 1048576 | tf_op jit(solution)/shard_map/pallas_call | solution.py:38
  212.6 1.3 collective-permute-start.44
  213.9 4.6 %collective-permute-start.45 = (bf16[2,256,256]{2,1,0:T(8,128)(2,1)}, bf16[2,256,256]{2,1,0:T(8,128)(2,1)S(1)}, u32[]{:S(2)}, u32[]{:S(2)}) collective-permute-start(bf16[2,256,256]{2,1,0:T(8,128)(2,1)} %get-tuple-element.207), channel_id=1, source_target_pairs={{0,8},{8,16},{16,24},{1,9},{9,17},{17,25},{2,10},{10,18},{18,26},{... | collective-permute-start | bytes 786440 | tf_op jit(solution)/shard_map/ppermute | solution.py:1027
  218.5 1.3 collective-permute-start.46
  219.8 4.7 %shard_map.247 = (f32[432,1152]{1,0:T(8,128)S(1)}, bf16[216,1152]{1,0:T(8,128)(2,1)S(1)}, bf16[216,1152]{1,0:T(8,128)(2,1)S(1)}, f32[288,864]{1,0:T(8,128)S(1)}, bf16[288,864]{1,0:T(8,128)(2,1)S(1)}) custom-call(s32[6]{0:T(128)S(1)} %copy-done.7, bf16[2,432,1792]{2,1,0:T(8,128)(2,1)} %get-tuple-element.200.keep, ...), custom_call_target="tpu_custom_call" | custom-call | flops 4000000000 | bytes 1048576 | tf_op jit(solution)/shard_map/pallas_call | solution.py:38
  226.3 1.3 copy-done.38
  227.6 3.1 %shard_map.248.partial = f32[128,1152]{1,0:T(8,128)S(1)} custom-call(s32[6]{0:T(128)S(1)} %copy-done.7, bf16[128,1024]{1,0:T(8,128)(2,1)S(1)} %copy-done.57, bf16[288,1536]{1,0:T(8,128)(2,1)S(1)} %copy-done.11, bf16[288,1536]{1,0:T(8,128)(2,1)} %collective-permute-done.3.k1.q1, bf16[288,1536]{1,0:T(8,128)(2,1)} %collective-permute-done.4.k2.q2, ...), custom_call_target="tpu_custom_call" | custom-call | flops 4000000000 | bytes 1048576 | tf_op jit(solution)/shard_map/pallas_call | solution.py:38
  231.6 1.6 shard_map.249
  233.2 1.3 copy-done.36
  234.5 2.4 collective-permute-start.51
  238.0 1.6 copy-done.37
  242.7 3.5 %shard_map.251 = (f32[128,1152]{1,0:T(8,128)}, bf16[128,384]{1,0:T(8,128)(2,1)S(1)}, bf16[144,384]{1,0:T(8,128)(2,1)S(1)}, f32[16,384]{1,0:T(8,128)S(1)}) custom-call(s32[6]{0:T(128)S(1)} %copy-done.7, f32[2,256,256]{2,1,0:T(8,128)S(1)} %convert_add_fusion.total, bf16[2,128,256]{2,1,0:T(8,128)(2,1)S(1)} %collective-permute-done.49.received, ...), custom_call_target="tpu_custom_call" | custom-call | flops 4000000000 | bytes 1048576 | tf_op jit(solution)/shard_map/pallas_call | solution.py:38
  247.5 2.2 collective-permute-done.51.got
  252.3 1.4 collective-permute-start.50
  253.6 6.6 %collective-permute-done.53.got = bf16[216,1152]{1,0:T(8,128)(2,1)S(1)} collective-permute-done((bf16[216,1152]{1,0:T(8,128)(2,1)S(1)}, bf16[216,1152]{1,0:T(8,128)(2,1)S(1)}, u32[]{:S(2)}, u32[]{:S(2)}) %collective-permute-start.53) | collective-permute-done | bytes 497696 | tf_op jit(solution)/shard_map/ppermute | solution.py:1043
  260.2 1.3 shard_map.253
  261.5 1.3 collective-permute-start.55
  262.8 1.7 collective-permute-start.56
  265.6 3.5 %all-to-all-start.1 = ((bf16[4,144,432]{2,1,0:T(8,128)(2,1)}), bf16[4,144,432]{2,1,0:T(8,128)(2,1)S(1)}, u32[]{:S(2)}, u32[]{:S(2)}) async-start(bf16[4,144,432]{2,1,0:T(8,128)(2,1)} %bitcast.45), calls=%async_computation.1 | async-start | bytes 1179648 | tf_op jit(solution)/shard_map/all_to_all | solution.py:1192
  269.1 2.6 collective-permute-done.55.got
  274.0 1.3 shard_map.254
  275.5 2.3 all-to-all-done.1.parts
  277.8 3.6 %all-to-all-start = ((bf16[4,384,256]{2,1,0:T(8,128)(2,1)}), bf16[4,384,256]{2,1,0:T(8,128)(2,1)S(1)}, u32[]{:S(2)}, u32[]{:S(2)}) async-start(bf16[4,384,256]{2,1,0:T(8,128)(2,1)} %shard_map.254), calls=%async_computation | async-start | bytes 1572864 | tf_op jit(solution)/shard_map/all_to_all | solution.py:1197
  281.4 1.6 copy-done.39
  282.9 1.3 shard_map.257
  284.3 1.4 collective-permute-start.57
  285.7 1.6 copy-done.40
  288.3 9.8 %collective-permute-done.57 = bf16[2,288,432]{2,1,0:T(8,128)(2,1)S(1)} collective-permute-done((bf16[2,288,432]{2,1,0:T(8,128)(2,1)S(1)}, bf16[2,288,432]{2,1,0:T(8,128)(2,1)S(1)}, u32[]{:S(2)}, u32[]{:S(2)}) %collective-permute-start.57) | collective-permute-done | bytes 497696 | tf_op jit(solution)/shard_map/ppermute | solution.py:1031
  299.8 2.1 shard_map.258
  (250 shorter events, 51.5 us)
Async XLA Ops:
  0.6 25.3 %collective-permute-start.3 = (bf16[288,1536]{1,0:T(8,128)(2,1)}, bf16[288,1536]{1,0:T(8,128)(2,1)}, u32[]{:S(2)}, u32[]{:S(2)}) collective-permute-start(bf16[288,1536]{1,0:T(8,128)(2,1)} %k0.3), channel_id=1, source_target_pairs={{0,2},{2,0},{1,3},{3,1},{4,6},{6,4},{5,7},{7,5},{8,10},{10,8},{9,1... | collective-permute-start | bytes 2654216 | tf_op jit(solution)/shard_map/ppermute | solution.py:1031
  3.7 178.6 %copy-start.6 = (s32[6]{0:T(128)}, s32[6]{0:T(128)S(1)}, u32[]{:S(2)}) copy-start(s32[6]{0:T(128)S(1)} %stack.29.place) | copy-start | bytes 76
  12.2 42.1 %collective-permute-start.7 = (bf16[2,288,1728]{2,1,0:T(8,128)(2,1)S(1)}, bf16[2,288,1728]{2,1,0:T(8,128)(2,1)}, u32[]{:S(2)}, u32[]{:S(2)}) collective-permute-start(bf16[2,288,1728]{2,1,0:T(8,128)(2,1)S(1)} %get-tuple-element.135.refs_0_), channel_id=1, source_target_pairs={{0,1},{1,0},{2,3},{3,2},{4,5},{5,4},{6,7},{7,6},{8,9},{9,8},{10,11... | collective-permute-start | bytes 5971976 | tf_op jit(solution)/shard_map/ppermute | solution.py:1031
  15.6 11.3 %collective-permute-start = (bf16[432,1152]{1,0:T(8,128)(2,1)S(1)}, bf16[432,1152]{1,0:T(8,128)(2,1)}, u32[]{:S(2)}, u32[]{:S(2)}) collective-permute-start(bf16[432,1152]{1,0:T(8,128)(2,1)S(1)} %get-tuple-element.262.refs_10_.w0), channel_id=1, source_target_pairs={{0,1},{1,0},{2,3},{3,2},{4,5},{5,4},{6,7},{7,6},{8,9},{9,8},{10,11... | collective-permute-start | bytes 2985992 | tf_op jit(solution)/shard_map/ppermute | solution.py:1031
  15.6 9.6 %collective-permute-start.2 = (bf16[128,1152]{1,0:T(8,128)(2,1)}, bf16[128,1152]{1,0:T(8,128)(2,1)S(1)}, u32[]{:S(2)}, u32[]{:S(2)}) collective-permute-start(bf16[128,1152]{1,0:T(8,128)(2,1)} %bitcast.37), channel_id=1, source_target_pairs={{0,4},{4,0},{1,5},{5,1},{2,6},{6,2},{3,7},{7,3},{8,12},{12,8},{9,1... | collective-permute-start | bytes 884744 | tf_op jit(solution)/shard_map/ppermute | solution.py:1031
  17.1 9.4 %collective-permute-start.1 = (bf16[256,1152]{1,0:T(8,128)(2,1)}, bf16[256,1152]{1,0:T(8,128)(2,1)}, u32[]{:S(2)}, u32[]{:S(2)}) collective-permute-start(bf16[256,1152]{1,0:T(8,128)(2,1)} %o0.3), channel_id=1, source_target_pairs={{0,1},{1,0},{2,3},{3,2},{4,5},{5,4},{6,7},{7,6},{8,9},{9,8},{10,11... | collective-permute-start | bytes 1769480 | tf_op jit(solution)/shard_map/ppermute | solution.py:1031
  25.9 3.2 %collective-permute-start.4 = (bf16[288,1536]{1,0:T(8,128)(2,1)}, bf16[288,1536]{1,0:T(8,128)(2,1)}, u32[]{:S(2)}, u32[]{:S(2)}) collective-permute-start(bf16[288,1536]{1,0:T(8,128)(2,1)} %k0.3), channel_id=1, source_target_pairs={{0,1},{1,0},{2,3},{3,2},{4,5},{5,4},{6,7},{7,6},{8,9},{9,8},{10,11... | collective-permute-start | bytes 2654216 | tf_op jit(solution)/shard_map/ppermute | solution.py:1031
  25.9 4.0 %collective-permute-start.5 = (bf16[288,1536]{1,0:T(8,128)(2,1)}, bf16[288,1536]{1,0:T(8,128)(2,1)}, u32[]{:S(2)}, u32[]{:S(2)}) collective-permute-start(bf16[288,1536]{1,0:T(8,128)(2,1)} %collective-permute-done.3.k1.q1), channel_id=1, source_target_pairs={{0,1},{1,0},{2,3},{3,2},{4,5},{5,4},{6,7},{7,6},{8,9},{9,8},{10,11... | collective-permute-start | bytes 2654216 | tf_op jit(solution)/shard_map/ppermute | solution.py:1031
  26.5 18.9 %collective-permute-start.6 = (bf16[144,1728]{1,0:T(8,128)(2,1)}, bf16[144,1728]{1,0:T(8,128)(2,1)}, u32[]{:S(2)}, u32[]{:S(2)}) collective-permute-start(bf16[144,1728]{1,0:T(8,128)(2,1)} %copy-done.15), channel_id=1, source_target_pairs={{0,2},{2,0},{1,3},{3,1},{4,6},{6,4},{5,7},{7,5},{8,10},{10,8},{9,1... | collective-permute-start | bytes 1493000 | tf_op jit(solution)/shard_map/ppermute | solution.py:1031
  26.8 27.2 %collective-permute-start.11 = (bf16[256,1152]{1,0:T(8,128)(2,1)}, bf16[256,1152]{1,0:T(8,128)(2,1)}, u32[]{:S(2)}, u32[]{:S(2)}) collective-permute-start(bf16[256,1152]{1,0:T(8,128)(2,1)} %o0.3), channel_id=1, source_target_pairs={{0,2},{2,0},{1,3},{3,1},{4,6},{6,4},{5,7},{7,5},{8,10},{10,8},{9,1... | collective-permute-start | bytes 1769480 | tf_op jit(solution)/shard_map/ppermute | solution.py:1031
  38.5 17.5 %collective-permute-start.10 = (bf16[2,256,256]{2,1,0:T(8,128)(2,1)}, bf16[2,256,256]{2,1,0:T(8,128)(2,1)S(1)}, u32[]{:S(2)}, u32[]{:S(2)}) collective-permute-start(bf16[2,256,256]{2,1,0:T(8,128)(2,1)} %get-tuple-element.142.kv2), channel_id=1, source_target_pairs={{8,0},{16,8},{24,16},{9,1},{17,9},{25,17},{10,2},{18,10},{26,18},{... | collective-permute-start | bytes 786440 | tf_op jit(solution)/shard_map/ppermute | solution.py:1027
  39.7 16.7 %collective-permute-start.8 = (bf16[2,256,256]{2,1,0:T(8,128)(2,1)}, bf16[2,256,256]{2,1,0:T(8,128)(2,1)S(1)}, u32[]{:S(2)}, u32[]{:S(2)}) collective-permute-start(bf16[2,256,256]{2,1,0:T(8,128)(2,1)} %get-tuple-element.142.kv2), channel_id=1, source_target_pairs={{0,16},{8,24},{1,17},{9,25},{2,18},{10,26},{3,19},{11,27},{4,20},{... | collective-permute-start | bytes 786440 | tf_op jit(solution)/shard_map/ppermute | solution.py:1027
  45.3 41.7 %collective-permute-start.24 = (bf16[432,1152]{1,0:T(8,128)(2,1)}, bf16[432,1152]{1,0:T(8,128)(2,1)}, u32[]{:S(2)}, u32[]{:S(2)}) collective-permute-start(bf16[432,1152]{1,0:T(8,128)(2,1)} %get-tuple-element.152), channel_id=1, source_target_pairs={{0,2},{2,0},{1,3},{3,1},{4,6},{6,4},{5,7},{7,5},{8,10},{10,8},{9,1... | collective-permute-start | bytes 2985992 | tf_op jit(solution)/shard_map/ppermute | solution.py:1031
  54.1 19.5 %collective-permute-start.12 = (bf16[256,1152]{1,0:T(8,128)(2,1)}, bf16[256,1152]{1,0:T(8,128)(2,1)S(1)}, u32[]{:S(2)}, u32[]{:S(2)}) collective-permute-start(bf16[256,1152]{1,0:T(8,128)(2,1)} %collective-permute-done.11.o1), channel_id=1, source_target_pairs={{0,1},{1,0},{2,3},{3,2},{4,5},{5,4},{6,7},{7,6},{8,9},{9,8},{10,11... | collective-permute-start | bytes 1769480 | tf_op jit(solution)/shard_map/ppermute | solution.py:1031
  54.3 24.7 %collective-permute-start.16 = (bf16[144,1728]{1,0:T(8,128)(2,1)}, bf16[144,1728]{1,0:T(8,128)(2,1)S(1)}, u32[]{:S(2)}, u32[]{:S(2)}) collective-permute-start(bf16[144,1728]{1,0:T(8,128)(2,1)} %collective-permute-done.6.refs_2_), channel_id=1, source_target_pairs={{0,8},{8,0},{16,24},{24,16},{1,9},{9,1},{17,25},{25,17},{2,10},{10... | collective-permute-start | bytes 1493000 | tf_op jit(solution)/shard_map/ppermute | solution.py:1043
  55.9 29.5 %collective-permute-start.18 = (bf16[144,1728]{1,0:T(8,128)(2,1)}, bf16[144,1728]{1,0:T(8,128)(2,1)S(1)}, u32[]{:S(2)}, u32[]{:S(2)}) collective-permute-start(bf16[144,1728]{1,0:T(8,128)(2,1)} %copy-done.14), channel_id=1, source_target_pairs={{0,2},{2,0},{1,3},{3,1},{4,6},{6,4},{5,7},{7,5},{8,10},{10,8},{9,1... | collective-permute-start | bytes 1493000 | tf_op jit(solution)/shard_map/ppermute | solution.py:1031
  56.5 17.1 %collective-permute-start.9 = (bf16[2,256,256]{2,1,0:T(8,128)(2,1)}, bf16[2,256,256]{2,1,0:T(8,128)(2,1)S(1)}, u32[]{:S(2)}, u32[]{:S(2)}) collective-permute-start(bf16[2,256,256]{2,1,0:T(8,128)(2,1)} %get-tuple-element.142.kv2), channel_id=1, source_target_pairs={{0,8},{8,16},{16,24},{1,9},{9,17},{17,25},{2,10},{10,18},{18,26},{... | collective-permute-start | bytes 786440 | tf_op jit(solution)/shard_map/ppermute | solution.py:1027
  79.0 59.5 %copy-start.34 = (f32[128,1152]{1,0:T(8,128)}, f32[128,1152]{1,0:T(8,128)S(1)}, u32[]{:S(2)}) copy-start(f32[128,1152]{1,0:T(8,128)S(1)} %get-tuple-element.161.residual.h_residual) | copy-start | bytes 1769476
  79.0 16.0 %collective-permute-start.17 = (bf16[128,1152]{1,0:T(8,128)(2,1)S(1)}, bf16[128,1152]{1,0:T(8,128)(2,1)S(1)}, u32[]{:S(2)}, u32[]{:S(2)}) collective-permute-start(bf16[128,1152]{1,0:T(8,128)(2,1)S(1)} %get-tuple-element.146.x0), channel_id=1, source_target_pairs={{0,16},{8,24},{16,0},{24,8},{1,17},{9,25},{17,1},{25,9},{2,18},{10... | collective-permute-start | bytes 884744 | tf_op jit(solution)/shard_map/ppermute | solution.py:1043
  85.4 18.3 %collective-permute-start.19 = (bf16[144,1728]{1,0:T(8,128)(2,1)S(1)}, bf16[144,1728]{1,0:T(8,128)(2,1)S(1)}, u32[]{:S(2)}, u32[]{:S(2)}) collective-permute-start(bf16[144,1728]{1,0:T(8,128)(2,1)S(1)} %collective-permute-done.18.refs_3_), channel_id=1, source_target_pairs={{0,8},{8,0},{16,24},{24,16},{1,9},{9,1},{17,25},{25,17},{2,10},{10... | collective-permute-start | bytes 1493000 | tf_op jit(solution)/shard_map/ppermute | solution.py:1043
  87.0 21.1 %collective-permute-start.25 = (bf16[432,1152]{1,0:T(8,128)(2,1)}, bf16[432,1152]{1,0:T(8,128)(2,1)S(1)}, u32[]{:S(2)}, u32[]{:S(2)}) collective-permute-start(bf16[432,1152]{1,0:T(8,128)(2,1)} %collective-permute-done.24.refs_11_.w1), channel_id=1, source_target_pairs={{0,1},{1,0},{2,3},{3,2},{4,5},{5,4},{6,7},{7,6},{8,9},{9,8},{10,11... | collective-permute-start | bytes 2985992 | tf_op jit(solution)/shard_map/ppermute | solution.py:1031
  87.0 9.5 %collective-permute-start.13 = (bf16[128,1152]{1,0:T(8,128)(2,1)S(1)}, bf16[128,1152]{1,0:T(8,128)(2,1)S(1)}, u32[]{:S(2)}, u32[]{:S(2)}) collective-permute-start(bf16[128,1152]{1,0:T(8,128)(2,1)S(1)} %get-tuple-element.146.x0), channel_id=1, source_target_pairs={{0,2},{2,0},{1,3},{3,1},{4,6},{6,4},{5,7},{7,5},{8,10},{10,8},{9,1... | collective-permute-start | bytes 884744 | tf_op jit(solution)/shard_map/ppermute | solution.py:1031
  87.6 9.1 %collective-permute-start.14 = (bf16[128,1152]{1,0:T(8,128)(2,1)S(1)}, bf16[128,1152]{1,0:T(8,128)(2,1)S(1)}, u32[]{:S(2)}, u32[]{:S(2)}) collective-permute-start(bf16[128,1152]{1,0:T(8,128)(2,1)S(1)} %get-tuple-element.146.x0), channel_id=1, source_target_pairs={{0,4},{4,0},{1,5},{5,1},{2,6},{6,2},{3,7},{7,3},{8,12},{12,8},{9,1... | collective-permute-start | bytes 884744 | tf_op jit(solution)/shard_map/ppermute | solution.py:1031
  95.0 8.7 %collective-permute-start.15 = (bf16[128,1152]{1,0:T(8,128)(2,1)S(1)}, bf16[128,1152]{1,0:T(8,128)(2,1)S(1)}, u32[]{:S(2)}, u32[]{:S(2)}) collective-permute-start(bf16[128,1152]{1,0:T(8,128)(2,1)S(1)} %get-tuple-element.146.x0), channel_id=1, source_target_pairs={{0,6},{2,4},{4,2},{6,0},{1,7},{3,5},{5,3},{7,1},{8,14},{10,12},{12... | collective-permute-start | bytes 884744 | tf_op jit(solution)/shard_map/ppermute | solution.py:1035
  96.5 7.7 %collective-permute-start.20 = (bf16[144,1728]{1,0:T(8,128)(2,1)}, bf16[144,1728]{1,0:T(8,128)(2,1)S(1)}, u32[]{:S(2)}, u32[]{:S(2)}) collective-permute-start(bf16[144,1728]{1,0:T(8,128)(2,1)} %collective-permute-done.6.refs_2_), channel_id=1, source_target_pairs={{0,1},{1,0},{2,3},{3,2},{4,5},{5,4},{6,7},{7,6},{8,9},{9,8},{10,11... | collective-permute-start | bytes 1493000 | tf_op jit(solution)/shard_map/ppermute | solution.py:1031
  96.7 8.4 %collective-permute-start.22 = (bf16[144,1728]{1,0:T(8,128)(2,1)S(1)}, bf16[144,1728]{1,0:T(8,128)(2,1)S(1)}, u32[]{:S(2)}, u32[]{:S(2)}) collective-permute-start(bf16[144,1728]{1,0:T(8,128)(2,1)S(1)} %collective-permute-done.16.refs_4_), channel_id=1, source_target_pairs={{0,1},{1,0},{2,3},{3,2},{4,5},{5,4},{6,7},{7,6},{8,9},{9,8},{10,11... | collective-permute-start | bytes 1493000 | tf_op jit(solution)/shard_map/ppermute | solution.py:1031
  103.7 2.9 collective-permute-start.21
  103.7 4.4 %collective-permute-start.23 = (bf16[144,1728]{1,0:T(8,128)(2,1)S(1)}, bf16[144,1728]{1,0:T(8,128)(2,1)S(1)}, u32[]{:S(2)}, u32[]{:S(2)}) collective-permute-start(bf16[144,1728]{1,0:T(8,128)(2,1)S(1)} %collective-permute-done.19.refs_5_), channel_id=1, source_target_pairs={{0,1},{1,0},{2,3},{3,2},{4,5},{5,4},{6,7},{7,6},{8,9},{9,8},{10,11... | collective-permute-start | bytes 1493000 | tf_op jit(solution)/shard_map/ppermute | solution.py:1031
  104.2 18.6 %collective-permute-start.26 = (bf16[128,1152]{1,0:T(8,128)(2,1)S(1)}, bf16[128,1152]{1,0:T(8,128)(2,1)S(1)}, u32[]{:S(2)}, u32[]{:S(2)}) collective-permute-start(bf16[128,1152]{1,0:T(8,128)(2,1)S(1)} %collective-permute-done.17.n0), channel_id=1, source_target_pairs={{0,2},{2,0},{1,3},{3,1},{4,6},{6,4},{5,7},{7,5},{8,10},{10,8},{9,1... | collective-permute-start | bytes 884744 | tf_op jit(solution)/shard_map/ppermute | solution.py:1031
  105.1 17.7 %collective-permute-start.27 = (bf16[128,1152]{1,0:T(8,128)(2,1)S(1)}, bf16[128,1152]{1,0:T(8,128)(2,1)S(1)}, u32[]{:S(2)}, u32[]{:S(2)}) collective-permute-start(bf16[128,1152]{1,0:T(8,128)(2,1)S(1)} %collective-permute-done.17.n0), channel_id=1, source_target_pairs={{0,4},{4,0},{1,5},{5,1},{2,6},{6,2},{3,7},{7,3},{8,12},{12,8},{9,1... | collective-permute-start | bytes 884744 | tf_op jit(solution)/shard_map/ppermute | solution.py:1031
  106.6 16.2 %collective-permute-start.28 = (bf16[128,1152]{1,0:T(8,128)(2,1)S(1)}, bf16[128,1152]{1,0:T(8,128)(2,1)S(1)}, u32[]{:S(2)}, u32[]{:S(2)}) collective-permute-start(bf16[128,1152]{1,0:T(8,128)(2,1)S(1)} %collective-permute-done.17.n0), channel_id=1, source_target_pairs={{0,6},{2,4},{4,2},{6,0},{1,7},{3,5},{5,3},{7,1},{8,14},{10,12},{12... | collective-permute-start | bytes 884744 | tf_op jit(solution)/shard_map/ppermute | solution.py:1035
  122.9 10.0 %collective-permute-start.29 = (bf16[128,1152]{1,0:T(8,128)(2,1)S(1)}, bf16[128,1152]{1,0:T(8,128)(2,1)S(1)}, u32[]{:S(2)}, u32[]{:S(2)}) collective-permute-start(bf16[128,1152]{1,0:T(8,128)(2,1)S(1)} %get-tuple-element.158), channel_id=1, source_target_pairs={{0,2},{2,0},{1,3},{3,1},{4,6},{6,4},{5,7},{7,5},{8,10},{10,8},{9,1... | collective-permute-start | bytes 884744 | tf_op jit(solution)/shard_map/ppermute | solution.py:1031
  123.4 9.5 %collective-permute-start.30 = (bf16[128,1152]{1,0:T(8,128)(2,1)S(1)}, bf16[128,1152]{1,0:T(8,128)(2,1)S(1)}, u32[]{:S(2)}, u32[]{:S(2)}) collective-permute-start(bf16[128,1152]{1,0:T(8,128)(2,1)S(1)} %get-tuple-element.159), channel_id=1, source_target_pairs={{0,4},{4,0},{1,5},{5,1},{2,6},{6,2},{3,7},{7,3},{8,12},{12,8},{9,1... | collective-permute-start | bytes 884744 | tf_op jit(solution)/shard_map/ppermute | solution.py:1031
  124.9 13.5 %collective-permute-start.31 = (bf16[128,1152]{1,0:T(8,128)(2,1)S(1)}, bf16[128,1152]{1,0:T(8,128)(2,1)S(1)}, u32[]{:S(2)}, u32[]{:S(2)}) collective-permute-start(bf16[128,1152]{1,0:T(8,128)(2,1)S(1)} %get-tuple-element.160), channel_id=1, source_target_pairs={{0,6},{2,4},{4,2},{6,0},{1,7},{3,5},{5,3},{7,1},{8,14},{10,12},{12... | collective-permute-start | bytes 884744 | tf_op jit(solution)/shard_map/ppermute | solution.py:1035
  140.6 19.6 %collective-permute-start.32 = (bf16[128,1152]{1,0:T(8,128)(2,1)S(1)}, bf16[128,1152]{1,0:T(8,128)(2,1)S(1)}, u32[]{:S(2)}, u32[]{:S(2)}) collective-permute-start(bf16[128,1152]{1,0:T(8,128)(2,1)S(1)} %get-tuple-element.172.x0), channel_id=1, source_target_pairs={{0,2},{2,0},{1,3},{3,1},{4,6},{6,4},{5,7},{7,5},{8,10},{10,8},{9,1... | collective-permute-start | bytes 884744 | tf_op jit(solution)/shard_map/ppermute | solution.py:1031
  141.9 18.4 %collective-permute-start.33 = (bf16[128,1152]{1,0:T(8,128)(2,1)S(1)}, bf16[128,1152]{1,0:T(8,128)(2,1)S(1)}, u32[]{:S(2)}, u32[]{:S(2)}) collective-permute-start(bf16[128,1152]{1,0:T(8,128)(2,1)S(1)} %get-tuple-element.172.x0), channel_id=1, source_target_pairs={{0,4},{4,0},{1,5},{5,1},{2,6},{6,2},{3,7},{7,3},{8,12},{12,8},{9,1... | collective-permute-start | bytes 884744 | tf_op jit(solution)/shard_map/ppermute | solution.py:1031
  142.9 17.3 %collective-permute-start.34 = (bf16[128,1152]{1,0:T(8,128)(2,1)S(1)}, bf16[128,1152]{1,0:T(8,128)(2,1)S(1)}, u32[]{:S(2)}, u32[]{:S(2)}) collective-permute-start(bf16[128,1152]{1,0:T(8,128)(2,1)S(1)} %get-tuple-element.172.x0), channel_id=1, source_target_pairs={{0,6},{2,4},{4,2},{6,0},{1,7},{3,5},{5,3},{7,1},{8,14},{10,12},{12... | collective-permute-start | bytes 884744 | tf_op jit(solution)/shard_map/ppermute | solution.py:1035
  144.1 16.2 %collective-permute-start.35 = (bf16[128,1152]{1,0:T(8,128)(2,1)S(1)}, bf16[128,1152]{1,0:T(8,128)(2,1)S(1)}, u32[]{:S(2)}, u32[]{:S(2)}) collective-permute-start(bf16[128,1152]{1,0:T(8,128)(2,1)S(1)} %get-tuple-element.172.x0), channel_id=1, source_target_pairs={{0,16},{8,24},{16,0},{24,8},{1,17},{9,25},{17,1},{25,9},{2,18},{10... | collective-permute-start | bytes 884744 | tf_op jit(solution)/shard_map/ppermute | solution.py:1043
  160.3 18.5 %collective-permute-start.36 = (bf16[128,1152]{1,0:T(8,128)(2,1)S(1)}, bf16[128,1152]{1,0:T(8,128)(2,1)S(1)}, u32[]{:S(2)}, u32[]{:S(2)}) collective-permute-start(bf16[128,1152]{1,0:T(8,128)(2,1)S(1)} %collective-permute-done.35.d0), channel_id=1, source_target_pairs={{0,2},{2,0},{1,3},{3,1},{4,6},{6,4},{5,7},{7,5},{8,10},{10,8},{9,1... | collective-permute-start | bytes 884744 | tf_op jit(solution)/shard_map/ppermute | solution.py:1031
  161.7 17.1 %collective-permute-start.37 = (bf16[128,1152]{1,0:T(8,128)(2,1)S(1)}, bf16[128,1152]{1,0:T(8,128)(2,1)S(1)}, u32[]{:S(2)}, u32[]{:S(2)}) collective-permute-start(bf16[128,1152]{1,0:T(8,128)(2,1)S(1)} %collective-permute-done.35.d0), channel_id=1, source_target_pairs={{0,4},{4,0},{1,5},{5,1},{2,6},{6,2},{3,7},{7,3},{8,12},{12,8},{9,1... | collective-permute-start | bytes 884744 | tf_op jit(solution)/shard_map/ppermute | solution.py:1031
  162.7 16.1 %collective-permute-start.38 = (bf16[128,1152]{1,0:T(8,128)(2,1)S(1)}, bf16[128,1152]{1,0:T(8,128)(2,1)S(1)}, u32[]{:S(2)}, u32[]{:S(2)}) collective-permute-start(bf16[128,1152]{1,0:T(8,128)(2,1)S(1)} %collective-permute-done.35.d0), channel_id=1, source_target_pairs={{0,6},{2,4},{4,2},{6,0},{1,7},{3,5},{5,3},{7,1},{8,14},{10,12},{12... | collective-permute-start | bytes 884744 | tf_op jit(solution)/shard_map/ppermute | solution.py:1035
  178.8 20.8 %collective-permute-start.39 = (bf16[128,1152]{1,0:T(8,128)(2,1)S(1)}, bf16[128,1152]{1,0:T(8,128)(2,1)S(1)}, u32[]{:S(2)}, u32[]{:S(2)}) collective-permute-start(bf16[128,1152]{1,0:T(8,128)(2,1)S(1)} %get-tuple-element.182), channel_id=1, source_target_pairs={{0,2},{2,0},{1,3},{3,1},{4,6},{6,4},{5,7},{7,5},{8,10},{10,8},{9,1... | collective-permute-start | bytes 884744 | tf_op jit(solution)/shard_map/ppermute | solution.py:1031
  180.2 19.5 %collective-permute-start.40 = (bf16[128,1152]{1,0:T(8,128)(2,1)S(1)}, bf16[128,1152]{1,0:T(8,128)(2,1)S(1)}, u32[]{:S(2)}, u32[]{:S(2)}) collective-permute-start(bf16[128,1152]{1,0:T(8,128)(2,1)S(1)} %get-tuple-element.183), channel_id=1, source_target_pairs={{0,4},{4,0},{1,5},{5,1},{2,6},{6,2},{3,7},{7,3},{8,12},{12,8},{9,1... | collective-permute-start | bytes 884744 | tf_op jit(solution)/shard_map/ppermute | solution.py:1031
  181.2 18.5 %collective-permute-start.41 = (bf16[128,1152]{1,0:T(8,128)(2,1)S(1)}, bf16[128,1152]{1,0:T(8,128)(2,1)S(1)}, u32[]{:S(2)}, u32[]{:S(2)}) collective-permute-start(bf16[128,1152]{1,0:T(8,128)(2,1)S(1)} %get-tuple-element.184), channel_id=1, source_target_pairs={{0,6},{2,4},{4,2},{6,0},{1,7},{3,5},{5,3},{7,1},{8,14},{10,12},{12... | collective-permute-start | bytes 884744 | tf_op jit(solution)/shard_map/ppermute | solution.py:1035
  199.7 18.7 %collective-permute-start.42 = (bf16[2,432,1792]{2,1,0:T(8,128)(2,1)}, bf16[2,432,1792]{2,1,0:T(8,128)(2,1)}, u32[]{:S(2)}, u32[]{:S(2)}) collective-permute-start(bf16[2,432,1792]{2,1,0:T(8,128)(2,1)} %get-tuple-element.202), channel_id=1, source_target_pairs={{0,1},{1,0},{2,3},{3,2},{4,5},{5,4},{6,7},{7,6},{8,9},{9,8},{10,11... | collective-permute-start | bytes 9289736 | tf_op jit(solution)/shard_map/ppermute | solution.py:1031
  210.2 20.8 %collective-permute-start.47 = (bf16[128,1024]{1,0:T(8,128)(2,1)S(1)}, bf16[128,1024]{1,0:T(8,128)(2,1)S(1)}, u32[]{:S(2)}, u32[]{:S(2)}) collective-permute-start(bf16[128,1024]{1,0:T(8,128)(2,1)S(1)} %get-tuple-element.215.own_heads), channel_id=1, source_target_pairs={{0,4},{4,0},{1,5},{5,1},{2,6},{6,2},{3,7},{7,3},{8,12},{12,8},{9,1... | collective-permute-start | bytes 786440 | tf_op jit(solution)/shard_map/ppermute | solution.py:1031
  211.3 19.5 %collective-permute-start.43 = (bf16[2,256,256]{2,1,0:T(8,128)(2,1)}, bf16[2,256,256]{2,1,0:T(8,128)(2,1)S(1)}, u32[]{:S(2)}, u32[]{:S(2)}) collective-permute-start(bf16[2,256,256]{2,1,0:T(8,128)(2,1)} %get-tuple-element.205), channel_id=1, source_target_pairs={{16,0},{24,8},{17,1},{25,9},{18,2},{26,10},{19,3},{27,11},{20,4},{... | collective-permute-start | bytes 786440 | tf_op jit(solution)/shard_map/ppermute | solution.py:1027
  212.6 18.2 %collective-permute-start.44 = (bf16[2,256,256]{2,1,0:T(8,128)(2,1)}, bf16[2,256,256]{2,1,0:T(8,128)(2,1)S(1)}, u32[]{:S(2)}, u32[]{:S(2)}) collective-permute-start(bf16[2,256,256]{2,1,0:T(8,128)(2,1)} %get-tuple-element.206), channel_id=1, source_target_pairs={{8,0},{16,8},{24,16},{9,1},{17,9},{25,17},{10,2},{18,10},{26,18},{... | collective-permute-start | bytes 786440 | tf_op jit(solution)/shard_map/ppermute | solution.py:1027
  213.9 16.9 %collective-permute-start.45 = (bf16[2,256,256]{2,1,0:T(8,128)(2,1)}, bf16[2,256,256]{2,1,0:T(8,128)(2,1)S(1)}, u32[]{:S(2)}, u32[]{:S(2)}) collective-permute-start(bf16[2,256,256]{2,1,0:T(8,128)(2,1)} %get-tuple-element.207), channel_id=1, source_target_pairs={{0,8},{8,16},{16,24},{1,9},{9,17},{17,25},{2,10},{10,18},{18,26},{... | collective-permute-start | bytes 786440 | tf_op jit(solution)/shard_map/ppermute | solution.py:1027
  218.5 12.5 %collective-permute-start.46 = (bf16[128,960]{1,0:T(8,128)(2,1)}, bf16[128,960]{1,0:T(8,128)(2,1)S(1)}, u32[]{:S(2)}, u32[]{:S(2)}) collective-permute-start(bf16[128,960]{1,0:T(8,128)(2,1)} %get-tuple-element.213), channel_id=1, source_target_pairs={{0,4},{4,0},{1,5},{5,1},{2,6},{6,2},{3,7},{7,3},{8,12},{12,8},{9,1... | collective-permute-start | bytes 737288 | tf_op jit(solution)/shard_map/ppermute | solution.py:1031
  234.5 3.5 %collective-permute-start.48 = (bf16[2,288,896]{2,1,0:T(8,128)(2,1)S(1)}, bf16[2,288,896]{2,1,0:T(8,128)(2,1)S(1)}, u32[]{:S(2)}, u32[]{:S(2)}) collective-permute-start(bf16[2,288,896]{2,1,0:T(8,128)(2,1)S(1)} %get-tuple-element.222), channel_id=1, source_target_pairs={{0,1},{1,0},{2,3},{3,2},{4,5},{5,4},{6,7},{7,6},{8,9},{9,8},{10,11... | collective-permute-start | bytes 3096584 | tf_op jit(solution)/shard_map/ppermute | solution.py:1031
  234.5 15.2 %collective-permute-start.51 = (bf16[288,864]{1,0:T(8,128)(2,1)}, bf16[288,864]{1,0:T(8,128)(2,1)S(1)}, u32[]{:S(2)}, u32[]{:S(2)}) collective-permute-start(bf16[288,864]{1,0:T(8,128)(2,1)} %copy-done.16), channel_id=1, source_target_pairs={{0,8},{8,0},{16,24},{24,16},{1,9},{9,1},{17,25},{25,17},{2,10},{10... | collective-permute-start | bytes 1493000 | tf_op jit(solution)/shard_map/ppermute | solution.py:1043
  236.9 5.7 %collective-permute-start.49 = (bf16[2,128,256]{2,1,0:T(8,128)(2,1)S(1)}, bf16[2,128,256]{2,1,0:T(8,128)(2,1)S(1)}, u32[]{:S(2)}, u32[]{:S(2)}) collective-permute-start(bf16[2,128,256]{2,1,0:T(8,128)(2,1)S(1)} %dynamic-slice_convert_fusion), channel_id=1, source_target_pairs={{0,4},{4,0},{1,5},{5,1},{2,6},{6,2},{3,7},{7,3},{8,12},{12,8},{9,1... | collective-permute-start | bytes 393224 | tf_op jit(solution)/shard_map/ppermute | solution.py:1031
  246.2 4.8 %collective-permute-start.52 = (bf16[144,384]{1,0:T(8,128)(2,1)S(1)}, bf16[144,384]{1,0:T(8,128)(2,1)S(1)}, u32[]{:S(2)}, u32[]{:S(2)}) collective-permute-start(bf16[144,384]{1,0:T(8,128)(2,1)S(1)} %get-tuple-element.236), channel_id=1, source_target_pairs={{0,4},{4,0},{1,5},{5,1},{2,6},{6,2},{3,7},{7,3},{8,12},{12,8},{9,1... | collective-permute-start | bytes 331784 | tf_op jit(solution)/shard_map/ppermute | solution.py:1031
  247.2 13.0 %collective-permute-start.53 = (bf16[216,1152]{1,0:T(8,128)(2,1)S(1)}, bf16[216,1152]{1,0:T(8,128)(2,1)S(1)}, u32[]{:S(2)}, u32[]{:S(2)}) collective-permute-start(bf16[216,1152]{1,0:T(8,128)(2,1)S(1)} %copy-done.20), channel_id=1, source_target_pairs={{0,8},{8,0},{16,24},{24,16},{1,9},{9,1},{17,25},{25,17},{2,10},{10... | collective-permute-start | bytes 1493000 | tf_op jit(solution)/shard_map/ppermute | solution.py:1043
  252.2 8.0 %collective-permute-start.54 = (bf16[592,384]{1,0:T(8,128)(2,1)S(1)}, bf16[592,384]{1,0:T(8,128)(2,1)S(1)}, u32[]{:S(2)}, u32[]{:S(2)}) collective-permute-start(bf16[592,384]{1,0:T(8,128)(2,1)S(1)} %get-tuple-element.241), channel_id=1, source_target_pairs={{0,1},{1,0},{2,3},{3,2},{4,5},{5,4},{6,7},{7,6},{8,9},{9,8},{10,11... | collective-permute-start | bytes 1363976 | tf_op jit(solution)/shard_map/ppermute | solution.py:1031
  252.3 16.9 %collective-permute-start.50 = (bf16[288,896]{1,0:T(8,128)(2,1)S(1)}, bf16[288,896]{1,0:T(8,128)(2,1)S(1)}, u32[]{:S(2)}, u32[]{:S(2)}) collective-permute-start(bf16[288,896]{1,0:T(8,128)(2,1)S(1)} %get-tuple-element.223), channel_id=1, source_target_pairs={{0,2},{2,0},{1,3},{3,1},{4,6},{6,4},{5,7},{7,5},{8,10},{10,8},{9,1... | collective-permute-start | bytes 1548296 | tf_op jit(solution)/shard_map/ppermute | solution.py:1031
  261.5 10.2 %collective-permute-start.55 = (bf16[304,384]{1,0:T(8,128)(2,1)}, bf16[304,384]{1,0:T(8,128)(2,1)S(1)}, u32[]{:S(2)}, u32[]{:S(2)}) collective-permute-start(bf16[304,384]{1,0:T(8,128)(2,1)} %get-tuple-element.244), channel_id=1, source_target_pairs={{0,2},{2,0},{1,3},{3,1},{4,6},{6,4},{5,7},{7,5},{8,10},{10,8},{9,1... | collective-permute-start | bytes 700424 | tf_op jit(solution)/shard_map/ppermute | solution.py:1031
  262.8 12.7 %collective-permute-start.56 = (bf16[216,1152]{1,0:T(8,128)(2,1)S(1)}, bf16[216,1152]{1,0:T(8,128)(2,1)S(1)}, u32[]{:S(2)}, u32[]{:S(2)}) collective-permute-start(bf16[216,1152]{1,0:T(8,128)(2,1)S(1)} %copy-done.18), channel_id=1, source_target_pairs={{0,8},{8,0},{16,24},{24,16},{1,9},{9,1},{17,25},{25,17},{2,10},{10... | collective-permute-start | bytes 1493000 | tf_op jit(solution)/shard_map/ppermute | solution.py:1043
  265.6 12.2 %all-to-all-start.1 = ((bf16[4,144,432]{2,1,0:T(8,128)(2,1)}), bf16[4,144,432]{2,1,0:T(8,128)(2,1)S(1)}, u32[]{:S(2)}, u32[]{:S(2)}) async-start(bf16[4,144,432]{2,1,0:T(8,128)(2,1)} %bitcast.45), calls=%async_computation.1 | async-start | bytes 1179648 | tf_op jit(solution)/shard_map/all_to_all | solution.py:1192
  277.8 24.1 %all-to-all-start = ((bf16[4,384,256]{2,1,0:T(8,128)(2,1)}), bf16[4,384,256]{2,1,0:T(8,128)(2,1)S(1)}, u32[]{:S(2)}, u32[]{:S(2)}) async-start(bf16[4,384,256]{2,1,0:T(8,128)(2,1)} %shard_map.254), calls=%async_computation | async-start | bytes 1572864 | tf_op jit(solution)/shard_map/all_to_all | solution.py:1197
  284.3 13.9 %collective-permute-start.57 = (bf16[2,288,432]{2,1,0:T(8,128)(2,1)S(1)}, bf16[2,288,432]{2,1,0:T(8,128)(2,1)S(1)}, u32[]{:S(2)}, u32[]{:S(2)}) collective-permute-start(bf16[2,288,432]{2,1,0:T(8,128)(2,1)S(1)} %shard_map.257), channel_id=1, source_target_pairs={{0,2},{2,0},{1,3},{3,1},{4,6},{6,4},{5,7},{7,5},{8,10},{10,8},{9,1... | collective-permute-start | bytes 1493000 | tf_op jit(solution)/shard_map/ppermute | solution.py:1031
  288.2 11.2 %collective-permute-start.58 = (bf16[288,432]{1,0:T(8,128)(2,1)S(1)}, bf16[288,432]{1,0:T(8,128)(2,1)S(1)}, u32[]{:S(2)}, u32[]{:S(2)}) collective-permute-start(bf16[288,432]{1,0:T(8,128)(2,1)S(1)} %get-tuple-element.265), channel_id=1, source_target_pairs={{0,1},{1,0},{2,3},{3,2},{4,5},{5,4},{6,7},{7,6},{8,9},{9,8},{10,11... | collective-permute-start | bytes 746504 | tf_op jit(solution)/shard_map/ppermute | solution.py:1031
  298.2 1.6 collective-permute-start.59
  (71 other events, 573.4 us)

commit v4 on v3

--- a/solution.py
+++ b/solution.py
@@ -392,8 +392,16 @@
     for first, last in steps(hiddens.shape[0], 256):
         gate = nn(tokens[...], w_gates[0, :, first:last])
         up = nn(tokens[...], w_gates[1, :, first:last])
-        value, room[0, :, first:last], room[1, :, first:last] = gated(gate, up)
+        value, bend, share = gated(gate, up)
         hiddens[first:last, 4 * rows :] = value.T
+        if first >= width or last <= start:
+
+            @pl.when(place[HALF] == int(first >= width))
+            def _():
+                room[0, :, first:last], room[1, :, first:last] = bend, share
+
+        else:
+            room[0, :, first:last], room[1, :, first:last] = bend, share
     here = at(place[HALF] * start, width, 128)
     slope[...] = room[0, :, here]
     gelu[...] = room[1, :, here]

time: 308 us -> 310 us (level)
  transfers between devices with their start and end apart: 62 -> 62, of which waited for: 20 -> 19; matrix products, arithmetic and copies ran while one was open for 2% -> 2% of each run, Pallas kernels for 35% -> 36%
where the time goes in v4:
time: 310 us; the launch traced here: 306 us
  Pallas kernels  113 us (36%)
  waiting for transfers between devices  79.8 us (26%)
  starting transfers between devices  77.7 us (25%)
  local copies, waits for them, and re-layouts  32.9 us (11%)
    pallas_call x23, Pallas kernels, call(): pl.pallas_call(kernel, out_shape=out_shape, in_specs=in_specs, out_specs=...  95.9 us
    ppermute x41, waiting for transfers between devices, swap(): return lax.ppermute(value, axis, [(0, 1), (1, 0)])  43.4 us
    ppermute x41, starting transfers between devices, swap(): return lax.ppermute(value, axis, [(0, 1), (1, 0)])  31.9 us
    unnamed x146, local copies, waits for them, and re-layouts  27.2 us
    ppermute x6, starting transfers between devices, shift(): return lax.ppermute(value, 'far', pairs)  17.9 us
    pallas_call x1, Pallas kernels, weight_grads(): pl.pallas_call(functools.partial(weights_kernel, (start, width)), out_sha...  17.4 us
    ppermute x7, waiting for transfers between devices, far_swap(): lax.ppermute(value, 'far', [(i, i ^ step) for i in range(lax.axis_size('f...  14.3 us
    ppermute x7, starting transfers between devices, far_swap(): lax.ppermute(value, 'far', [(i, i ^ step) for i in range(lax.axis_size('f...  12.9 us
  transfers between devices with their start and end apart: 62, of which 19 were waited for; matrix products, arithmetic and copies ran while one was open for 2% of the time, Pallas kernels for 36%

profile of v4, /device:TPU:0, one launch (start us, length us, event | category | flops | bytes accessed | tf_op | source)
XLA Modules:
  0.0 306.3 jit_solution(3140113075150125474)
XLA Ops:
  0.6 3.0 collective-permute-start.3
  3.7 6.9 %shard_map.237 = (bf16[2,288,1728]{2,1,0:T(8,128)(2,1)S(1)}, bf16[144,1728]{1,0:T(8,128)(2,1)S(1)}, bf16[144,1728]{1,0:T(8,128)(2,1)S(1)}) custom-call(s32[6]{0:T(128)S(1)} %stack.29.place, bf16[288,6912]{1,0:T(8,128)(2,1)} %gate.1, bf16[288,6912]{1,0:T(8,128)(2,1)} %up.1), custom_call_target="tpu_custom_call" | custom-call | flops 6000000000 | bytes 1048576 | tf_op jit(solution)/shard_map/pallas_call | solution.py:38
  12.2 3.4 %dynamic-slice_bitcast_fusion = (bf16[432,1152]{1,0:T(8,128)(2,1)}, bf16[432,1152]{1,0:T(8,128)(2,1)S(1)}) fusion(bf16[1,2,2,432,1152]{4,3,2,1,0:T(8,128)(2,1)} %bitcast.46, s32[]{:T(128)S(6)} %select_n.52, s32[]{:T(128)S(6)} %select_n.58, s32[]{:T(128)S(6)} %select_n.54), kind=kLoop, calls=%fused_computation | loop fusion | bytes 3981324 | tf_op jit(solution)/shard_map/reshape | solution.py:1115
  15.6 1.5 collective-permute-start.2
  17.3 7.9 %collective-permute-done.2.peer = bf16[128,1152]{1,0:T(8,128)(2,1)S(1)} collective-permute-done((bf16[128,1152]{1,0:T(8,128)(2,1)}, bf16[128,1152]{1,0:T(8,128)(2,1)S(1)}, u32[]{:S(2)}, u32[]{:S(2)}) %collective-permute-start.2) | collective-permute-done | bytes 294944 | tf_op jit(solution)/shard_map/ppermute | solution.py:1039
  26.8 1.7 collective-permute-start.11
  33.0 3.2 %shard_map.238 = (bf16[128,1152]{1,0:T(8,128)(2,1)S(1)}, bf16[2,256,256]{2,1,0:T(8,128)(2,1)}, f32[256,256]{1,0:T(8,128)S(1)}, bf16[256,1152]{1,0:T(8,128)(2,1)S(1)}) custom-call(s32[6]{0:T(128)S(1)} %stack.29.place, bf16[128,1152]{1,0:T(8,128)(2,1)S(1)} %bitcast.38, bf16[128,1152]{1,0:T(8,128)(2,1)S(1)} %copy-done.26, f32[1,1152]{1,0:T(1,128)S(1)} %reshape.191.gain_in, ...), custom_call_target="tpu_custom_call" | custom-call | flops 2000000000 | bytes 1048576 | tf_op jit(solution)/shard_map/pallas_call | solution.py:38
  39.7 5.6 %collective-permute-start.8 = (bf16[2,256,256]{2,1,0:T(8,128)(2,1)}, bf16[2,256,256]{2,1,0:T(8,128)(2,1)S(1)}, u32[]{:S(2)}, u32[]{:S(2)}) collective-permute-start(bf16[2,256,256]{2,1,0:T(8,128)(2,1)} %get-tuple-element.142.kv2), channel_id=1, source_target_pairs={{0,16},{8,24},{1,17},{9,25},{2,18},{10,26},{3,19},{11,27},{4,20},{... | collective-permute-start | bytes 786440 | tf_op jit(solution)/shard_map/ppermute | solution.py:1035
  46.0 8.1 %collective-permute-done.11.o1 = bf16[256,1152]{1,0:T(8,128)(2,1)} collective-permute-done((bf16[256,1152]{1,0:T(8,128)(2,1)}, bf16[256,1152]{1,0:T(8,128)(2,1)}, u32[]{:S(2)}, u32[]{:S(2)}) %collective-permute-start.11) | collective-permute-done | bytes 589856 | tf_op jit(solution)/shard_map/ppermute | solution.py:1039
  54.3 1.6 collective-permute-start.16
  56.5 3.9 %collective-permute-start.9 = (bf16[2,256,256]{2,1,0:T(8,128)(2,1)}, bf16[2,256,256]{2,1,0:T(8,128)(2,1)S(1)}, u32[]{:S(2)}, u32[]{:S(2)}) collective-permute-start(bf16[2,256,256]{2,1,0:T(8,128)(2,1)} %get-tuple-element.142.kv2), channel_id=1, source_target_pairs={{0,8},{8,16},{16,24},{1,9},{9,17},{17,25},{2,10},{10,18},{18,26},{... | collective-permute-start | bytes 786440 | tf_op jit(solution)/shard_map/ppermute | solution.py:1035
  62.6 2.7 shard_map.239
  66.1 7.5 %collective-permute-done.9.kv1 = bf16[2,256,256]{2,1,0:T(8,128)(2,1)S(1)} collective-permute-done((bf16[2,256,256]{2,1,0:T(8,128)(2,1)}, bf16[2,256,256]{2,1,0:T(8,128)(2,1)S(1)}, u32[]{:S(2)}, u32[]{:S(2)}) %collective-permute-start.9) | collective-permute-done | bytes 262176 | tf_op jit(solution)/shard_map/ppermute | solution.py:1035
  73.6 4.5 %shard_map.240 = (f32[512,1024]{1,0:T(8,128)}, bf16[128,1024]{1,0:T(8,128)(2,1)S(1)}, f32[128,1152]{1,0:T(8,128)S(1)}, f32[128,1152]{1,0:T(8,128)S(1)}, bf16[128,1152]{1,0:T(8,128)(2,1)S(1)}) custom-call(s32[6]{0:T(128)S(1)} %stack.29.place, bf16[512,256]{1,0:T(8,128)(2,1)S(1)} %get-tuple-element.141.queries.h_queries, ...), custom_call_target="tpu_custom_call" | custom-call | flops 2000000000 | bytes 1048576 | tf_op jit(solution)/shard_map/pallas_call | solution.py:38
  79.0 2.6 collective-permute-start.17
  81.6 3.8 %collective-permute-done.18.refs_3_ = bf16[144,1728]{1,0:T(8,128)(2,1)S(1)} collective-permute-done((bf16[144,1728]{1,0:T(8,128)(2,1)}, bf16[144,1728]{1,0:T(8,128)(2,1)S(1)}, u32[]{:S(2)}, u32[]{:S(2)}) %collective-permute-start.18) | collective-permute-done | bytes 497696 | tf_op jit(solution)/shard_map/ppermute | solution.py:1039
  85.4 1.6 collective-permute-start.19
  87.6 1.5 collective-permute-start.14
  89.1 5.9 %collective-permute-done.17.n0 = bf16[128,1152]{1,0:T(8,128)(2,1)S(1)} collective-permute-done((bf16[128,1152]{1,0:T(8,128)(2,1)S(1)}, bf16[128,1152]{1,0:T(8,128)(2,1)S(1)}, u32[]{:S(2)}, u32[]{:S(2)}) %collective-permute-start.17) | collective-permute-done | bytes 294944 | tf_op jit(solution)/shard_map/ppermute | solution.py:1051
  95.0 1.5 collective-permute-start.15
  97.0 6.7 %collective-permute-done.15.x3 = bf16[128,1152]{1,0:T(8,128)(2,1)S(1)} collective-permute-done((bf16[128,1152]{1,0:T(8,128)(2,1)S(1)}, bf16[128,1152]{1,0:T(8,128)(2,1)S(1)}, u32[]{:S(2)}, u32[]{:S(2)}) %collective-permute-start.15) | collective-permute-done | bytes 294944 | tf_op jit(solution)/shard_map/ppermute | solution.py:1043
  105.1 1.5 collective-permute-start.27
  106.6 1.5 collective-permute-start.28
  109.1 13.8 %shard_map.241 = (bf16[512,1152]{1,0:T(8,128)(2,1)}, bf16[512,1728]{1,0:T(8,128)(2,1)}, bf16[512,1728]{1,0:T(8,128)(2,1)}, bf16[512,1728]{1,0:T(8,128)(2,1)}, f3...) custom-call(s32[6]{0:T(128)S(1)} %stack.29.place, ...), custom_call_target="tpu_custom_call" | custom-call | flops 12999999488 | bytes 1048576 | tf_op jit(solution)/shard_map/pallas_call | solution.py:38
  123.4 1.5 collective-permute-start.30
  124.9 1.5 collective-permute-start.31
  126.4 6.4 %collective-permute-done.29.r1 = bf16[128,1152]{1,0:T(8,128)(2,1)S(1)} collective-permute-done((bf16[128,1152]{1,0:T(8,128)(2,1)S(1)}, bf16[128,1152]{1,0:T(8,128)(2,1)S(1)}, u32[]{:S(2)}, u32[]{:S(2)}) %collective-permute-start.29) | collective-permute-done | bytes 294944 | tf_op jit(solution)/shard_map/ppermute | solution.py:1039
  132.9 5.5 %collective-permute-done.31.r3 = bf16[128,1152]{1,0:T(8,128)(2,1)S(1)} collective-permute-done((bf16[128,1152]{1,0:T(8,128)(2,1)S(1)}, bf16[128,1152]{1,0:T(8,128)(2,1)S(1)}, u32[]{:S(2)}, u32[]{:S(2)}) %collective-permute-start.31) | collective-permute-done | bytes 294944 | tf_op jit(solution)/shard_map/ppermute | solution.py:1043
  140.6 1.3 collective-permute-start.32
  144.1 2.6 collective-permute-start.35
  146.7 15.4 %shard_map.243 = (bf16[1728,1024]{1,0:T(8,128)(2,1)}, bf16[512,960]{1,0:T(8,128)(2,1)}, bf16[512,960]{1,0:T(8,128)(2,1)}) custom-call(s32[6]{0:T(128)S(1)} %stack.29.place, bf16[512,1728]{1,0:T(8,128)(2,1)} %get-tuple-element.164.own, bf16[128,1152]{1,0:T(8,128)(2,1)S(1)} %collective-permute-done.17.n0, bf16[128,1152]{1,0:T(8,128)(2,1)S(1)} %collective-permute-done.26.n1, ...), custom_call_target="tpu_custom_call" | custom-call | flops 11000000512 | bytes 1048576 | tf_op jit(solution)/shard_map/pallas_call | solution.py:38
  162.1 1.4 collective-permute-start.36
  165.7 14.9 %shard_map.244 = (bf16[512,1152]{1,0:T(8,128)(2,1)}, bf16[512,1728]{1,0:T(8,128)(2,1)}, bf16[512,1728]{1,0:T(8,128)(2,1)}, f32[128,1152]{1,0:T(8,128)}, bf16[128...) custom-call(s32[6]{0:T(128)S(1)} %stack.29.place, ...), custom_call_target="tpu_custom_call" | custom-call | flops 15000000512 | bytes 1048576 | tf_op jit(solution)/shard_map/pallas_call | solution.py:38
  180.6 1.4 collective-permute-start.39
  184.2 17.4 %shard_map.245 = (bf16[2,432,1792]{2,1,0:T(8,128)(2,1)}, bf16[2,432,1792]{2,1,0:T(8,128)(2,1)}) custom-call(s32[6]{0:T(128)S(1)} %stack.29.place, bf16[512,1152]{1,0:T(8,128)(2,1)} %get-tuple-element.185.h_normed, bf16[512,1152]{1,0:T(8,128)(2,1)} %get-tuple-element.186.h_down, bf16[512,1728]{1,0:T(8,128)(2,1)} %get-tuple-element.188.h_gate, ...), custom_call_target="tpu_custom_call" | custom-call | flops 16000000000 | bytes 1048576 | tf_op jit(solution)/shard_map/pallas_call | solution.py:503
  202.6 9.3 %shard_map.246 = (f32[128,1152]{1,0:T(8,128)}, bf16[128,960]{1,0:T(8,128)(2,1)}, bf16[128,960]{1,0:T(8,128)(2,1)}, f32[2,1152]{1,0:T(2,128)}, f32[1,256]{1,0:T(1...) custom-call(s32[6]{0:T(128)} %copy-done.6, ...), custom_call_target="tpu_custom_call" | custom-call | flops 8000000000 | bytes 1048576 | tf_op jit(solution)/shard_map/pallas_call | solution.py:38
  214.3 1.3 collective-permute-start.44
  215.6 4.6 %collective-permute-start.45 = (bf16[2,256,256]{2,1,0:T(8,128)(2,1)}, bf16[2,256,256]{2,1,0:T(8,128)(2,1)S(1)}, u32[]{:S(2)}, u32[]{:S(2)}) collective-permute-start(bf16[2,256,256]{2,1,0:T(8,128)(2,1)} %get-tuple-element.207), channel_id=1, source_target_pairs={{0,8},{8,16},{16,24},{1,9},{9,17},{17,25},{2,10},{10,18},{18,26},{... | collective-permute-start | bytes 786440 | tf_op jit(solution)/shard_map/ppermute | solution.py:1035
  220.2 1.4 collective-permute-start.46
  221.6 4.7 %shard_map.247 = (f32[432,1152]{1,0:T(8,128)S(1)}, bf16[216,1152]{1,0:T(8,128)(2,1)S(1)}, bf16[216,1152]{1,0:T(8,128)(2,1)S(1)}, f32[288,864]{1,0:T(8,128)S(1)}, bf16[288,864]{1,0:T(8,128)(2,1)S(1)}) custom-call(s32[6]{0:T(128)S(1)} %copy-done.7, bf16[2,432,1792]{2,1,0:T(8,128)(2,1)} %get-tuple-element.200.keep, ...), custom_call_target="tpu_custom_call" | custom-call | flops 4000000000 | bytes 1048576 | tf_op jit(solution)/shard_map/pallas_call | solution.py:38
  228.1 1.3 copy-done.38
  229.4 3.1 shard_map.248.partial
  233.3 1.6 shard_map.249
  235.0 1.3 copy-done.36
  236.3 2.4 collective-permute-start.51
  239.8 1.6 copy-done.37
  244.5 3.7 %shard_map.251 = (f32[128,1152]{1,0:T(8,128)}, bf16[128,384]{1,0:T(8,128)(2,1)S(1)}, bf16[144,384]{1,0:T(8,128)(2,1)S(1)}, f32[16,384]{1,0:T(8,128)S(1)}) custom-call(s32[6]{0:T(128)S(1)} %copy-done.7, f32[2,256,256]{2,1,0:T(8,128)S(1)} %convert_add_fusion.total, bf16[2,128,256]{2,1,0:T(8,128)(2,1)S(1)} %collective-permute-done.49.received, ...), custom_call_target="tpu_custom_call" | custom-call | flops 4000000000 | bytes 1048576 | tf_op jit(solution)/shard_map/pallas_call | solution.py:38
  249.5 2.0 collective-permute-done.51.got
  251.5 1.5 collective-permute-done.52.got
  254.2 1.4 collective-permute-start.50
  255.6 6.4 %collective-permute-done.53.got = bf16[216,1152]{1,0:T(8,128)(2,1)S(1)} collective-permute-done((bf16[216,1152]{1,0:T(8,128)(2,1)S(1)}, bf16[216,1152]{1,0:T(8,128)(2,1)S(1)}, u32[]{:S(2)}, u32[]{:S(2)}) %collective-permute-start.53) | collective-permute-done | bytes 497696 | tf_op jit(solution)/shard_map/ppermute | solution.py:1051
  262.0 1.3 shard_map.253
  263.3 1.3 collective-permute-start.55
  264.6 1.7 collective-permute-start.56
  267.4 3.5 %all-to-all-start.1 = ((bf16[4,144,432]{2,1,0:T(8,128)(2,1)}), bf16[4,144,432]{2,1,0:T(8,128)(2,1)S(1)}, u32[]{:S(2)}, u32[]{:S(2)}) async-start(bf16[4,144,432]{2,1,0:T(8,128)(2,1)} %bitcast.45), calls=%async_computation.1 | async-start | bytes 1179648 | tf_op jit(solution)/shard_map/all_to_all | solution.py:1200
  270.9 2.9 collective-permute-done.55.got
  277.4 2.4 all-to-all-done.1.parts
  279.8 3.6 %all-to-all-start = ((bf16[4,384,256]{2,1,0:T(8,128)(2,1)}), bf16[4,384,256]{2,1,0:T(8,128)(2,1)S(1)}, u32[]{:S(2)}, u32[]{:S(2)}) async-start(bf16[4,384,256]{2,1,0:T(8,128)(2,1)} %shard_map.254), calls=%async_computation | async-start | bytes 1572864 | tf_op jit(solution)/shard_map/all_to_all | solution.py:1205
  283.3 1.6 copy-done.39
  284.9 1.3 shard_map.257
  286.2 1.4 collective-permute-start.57
  287.7 1.6 copy-done.40
  290.3 10.0 %collective-permute-done.57 = bf16[2,288,432]{2,1,0:T(8,128)(2,1)S(1)} collective-permute-done((bf16[2,288,432]{2,1,0:T(8,128)(2,1)S(1)}, bf16[2,288,432]{2,1,0:T(8,128)(2,1)S(1)}, u32[]{:S(2)}, u32[]{:S(2)}) %collective-permute-start.57) | collective-permute-done | bytes 497696 | tf_op jit(solution)/shard_map/ppermute | solution.py:1039
  302.0 2.1 shard_map.258
  (250 shorter events, 51.3 us)
Async XLA Ops:
  0.6 25.3 %collective-permute-start.3 = (bf16[288,1536]{1,0:T(8,128)(2,1)}, bf16[288,1536]{1,0:T(8,128)(2,1)}, u32[]{:S(2)}, u32[]{:S(2)}) collective-permute-start(bf16[288,1536]{1,0:T(8,128)(2,1)} %k0.3), channel_id=1, source_target_pairs={{0,2},{2,0},{1,3},{3,1},{4,6},{6,4},{5,7},{7,5},{8,10},{10,8},{9,1... | collective-permute-start | bytes 2654216 | tf_op jit(solution)/shard_map/ppermute | solution.py:1039
  3.7 180.5 %copy-start.6 = (s32[6]{0:T(128)}, s32[6]{0:T(128)S(1)}, u32[]{:S(2)}) copy-start(s32[6]{0:T(128)S(1)} %stack.29.place) | copy-start | bytes 76
  12.2 42.1 %collective-permute-start.7 = (bf16[2,288,1728]{2,1,0:T(8,128)(2,1)S(1)}, bf16[2,288,1728]{2,1,0:T(8,128)(2,1)}, u32[]{:S(2)}, u32[]{:S(2)}) collective-permute-start(bf16[2,288,1728]{2,1,0:T(8,128)(2,1)S(1)} %get-tuple-element.135.refs_0_), channel_id=1, source_target_pairs={{0,1},{1,0},{2,3},{3,2},{4,5},{5,4},{6,7},{7,6},{8,9},{9,8},{10,11... | collective-permute-start | bytes 5971976 | tf_op jit(solution)/shard_map/ppermute | solution.py:1039
  15.6 11.3 %collective-permute-start = (bf16[432,1152]{1,0:T(8,128)(2,1)S(1)}, bf16[432,1152]{1,0:T(8,128)(2,1)}, u32[]{:S(2)}, u32[]{:S(2)}) collective-permute-start(bf16[432,1152]{1,0:T(8,128)(2,1)S(1)} %get-tuple-element.262.refs_10_.w0), channel_id=1, source_target_pairs={{0,1},{1,0},{2,3},{3,2},{4,5},{5,4},{6,7},{7,6},{8,9},{9,8},{10,11... | collective-permute-start | bytes 2985992 | tf_op jit(solution)/shard_map/ppermute | solution.py:1039
  15.6 9.6 %collective-permute-start.2 = (bf16[128,1152]{1,0:T(8,128)(2,1)}, bf16[128,1152]{1,0:T(8,128)(2,1)S(1)}, u32[]{:S(2)}, u32[]{:S(2)}) collective-permute-start(bf16[128,1152]{1,0:T(8,128)(2,1)} %bitcast.37), channel_id=1, source_target_pairs={{0,4},{4,0},{1,5},{5,1},{2,6},{6,2},{3,7},{7,3},{8,12},{12,8},{9,1... | collective-permute-start | bytes 884744 | tf_op jit(solution)/shard_map/ppermute | solution.py:1039
  17.1 9.4 %collective-permute-start.1 = (bf16[256,1152]{1,0:T(8,128)(2,1)}, bf16[256,1152]{1,0:T(8,128)(2,1)}, u32[]{:S(2)}, u32[]{:S(2)}) collective-permute-start(bf16[256,1152]{1,0:T(8,128)(2,1)} %o0.3), channel_id=1, source_target_pairs={{0,1},{1,0},{2,3},{3,2},{4,5},{5,4},{6,7},{7,6},{8,9},{9,8},{10,11... | collective-permute-start | bytes 1769480 | tf_op jit(solution)/shard_map/ppermute | solution.py:1039
  25.9 3.2 %collective-permute-start.4 = (bf16[288,1536]{1,0:T(8,128)(2,1)}, bf16[288,1536]{1,0:T(8,128)(2,1)}, u32[]{:S(2)}, u32[]{:S(2)}) collective-permute-start(bf16[288,1536]{1,0:T(8,128)(2,1)} %k0.3), channel_id=1, source_target_pairs={{0,1},{1,0},{2,3},{3,2},{4,5},{5,4},{6,7},{7,6},{8,9},{9,8},{10,11... | collective-permute-start | bytes 2654216 | tf_op jit(solution)/shard_map/ppermute | solution.py:1039
  25.9 4.0 %collective-permute-start.5 = (bf16[288,1536]{1,0:T(8,128)(2,1)}, bf16[288,1536]{1,0:T(8,128)(2,1)}, u32[]{:S(2)}, u32[]{:S(2)}) collective-permute-start(bf16[288,1536]{1,0:T(8,128)(2,1)} %collective-permute-done.3.k1.q1), channel_id=1, source_target_pairs={{0,1},{1,0},{2,3},{3,2},{4,5},{5,4},{6,7},{7,6},{8,9},{9,8},{10,11... | collective-permute-start | bytes 2654216 | tf_op jit(solution)/shard_map/ppermute | solution.py:1039
  26.5 18.9 %collective-permute-start.6 = (bf16[144,1728]{1,0:T(8,128)(2,1)}, bf16[144,1728]{1,0:T(8,128)(2,1)}, u32[]{:S(2)}, u32[]{:S(2)}) collective-permute-start(bf16[144,1728]{1,0:T(8,128)(2,1)} %copy-done.15), channel_id=1, source_target_pairs={{0,2},{2,0},{1,3},{3,1},{4,6},{6,4},{5,7},{7,5},{8,10},{10,8},{9,1... | collective-permute-start | bytes 1493000 | tf_op jit(solution)/shard_map/ppermute | solution.py:1039
  26.8 27.2 %collective-permute-start.11 = (bf16[256,1152]{1,0:T(8,128)(2,1)}, bf16[256,1152]{1,0:T(8,128)(2,1)}, u32[]{:S(2)}, u32[]{:S(2)}) collective-permute-start(bf16[256,1152]{1,0:T(8,128)(2,1)} %o0.3), channel_id=1, source_target_pairs={{0,2},{2,0},{1,3},{3,1},{4,6},{6,4},{5,7},{7,5},{8,10},{10,8},{9,1... | collective-permute-start | bytes 1769480 | tf_op jit(solution)/shard_map/ppermute | solution.py:1039
  38.5 17.5 %collective-permute-start.10 = (bf16[2,256,256]{2,1,0:T(8,128)(2,1)}, bf16[2,256,256]{2,1,0:T(8,128)(2,1)S(1)}, u32[]{:S(2)}, u32[]{:S(2)}) collective-permute-start(bf16[2,256,256]{2,1,0:T(8,128)(2,1)} %get-tuple-element.142.kv2), channel_id=1, source_target_pairs={{8,0},{16,8},{24,16},{9,1},{17,9},{25,17},{10,2},{18,10},{26,18},{... | collective-permute-start | bytes 786440 | tf_op jit(solution)/shard_map/ppermute | solution.py:1035
  39.7 16.7 %collective-permute-start.8 = (bf16[2,256,256]{2,1,0:T(8,128)(2,1)}, bf16[2,256,256]{2,1,0:T(8,128)(2,1)S(1)}, u32[]{:S(2)}, u32[]{:S(2)}) collective-permute-start(bf16[2,256,256]{2,1,0:T(8,128)(2,1)} %get-tuple-element.142.kv2), channel_id=1, source_target_pairs={{0,16},{8,24},{1,17},{9,25},{2,18},{10,26},{3,19},{11,27},{4,20},{... | collective-permute-start | bytes 786440 | tf_op jit(solution)/shard_map/ppermute | solution.py:1035
  45.3 41.7 %collective-permute-start.24 = (bf16[432,1152]{1,0:T(8,128)(2,1)}, bf16[432,1152]{1,0:T(8,128)(2,1)}, u32[]{:S(2)}, u32[]{:S(2)}) collective-permute-start(bf16[432,1152]{1,0:T(8,128)(2,1)} %get-tuple-element.152), channel_id=1, source_target_pairs={{0,2},{2,0},{1,3},{3,1},{4,6},{6,4},{5,7},{7,5},{8,10},{10,8},{9,1... | collective-permute-start | bytes 2985992 | tf_op jit(solution)/shard_map/ppermute | solution.py:1039
  54.1 19.5 %collective-permute-start.12 = (bf16[256,1152]{1,0:T(8,128)(2,1)}, bf16[256,1152]{1,0:T(8,128)(2,1)S(1)}, u32[]{:S(2)}, u32[]{:S(2)}) collective-permute-start(bf16[256,1152]{1,0:T(8,128)(2,1)} %collective-permute-done.11.o1), channel_id=1, source_target_pairs={{0,1},{1,0},{2,3},{3,2},{4,5},{5,4},{6,7},{7,6},{8,9},{9,8},{10,11... | collective-permute-start | bytes 1769480 | tf_op jit(solution)/shard_map/ppermute | solution.py:1039
  54.3 24.7 %collective-permute-start.16 = (bf16[144,1728]{1,0:T(8,128)(2,1)}, bf16[144,1728]{1,0:T(8,128)(2,1)S(1)}, u32[]{:S(2)}, u32[]{:S(2)}) collective-permute-start(bf16[144,1728]{1,0:T(8,128)(2,1)} %collective-permute-done.6.refs_2_), channel_id=1, source_target_pairs={{0,8},{8,0},{16,24},{24,16},{1,9},{9,1},{17,25},{25,17},{2,10},{10... | collective-permute-start | bytes 1493000 | tf_op jit(solution)/shard_map/ppermute | solution.py:1051
  55.9 29.5 %collective-permute-start.18 = (bf16[144,1728]{1,0:T(8,128)(2,1)}, bf16[144,1728]{1,0:T(8,128)(2,1)S(1)}, u32[]{:S(2)}, u32[]{:S(2)}) collective-permute-start(bf16[144,1728]{1,0:T(8,128)(2,1)} %copy-done.14), channel_id=1, source_target_pairs={{0,2},{2,0},{1,3},{3,1},{4,6},{6,4},{5,7},{7,5},{8,10},{10,8},{9,1... | collective-permute-start | bytes 1493000 | tf_op jit(solution)/shard_map/ppermute | solution.py:1039
  56.5 17.1 %collective-permute-start.9 = (bf16[2,256,256]{2,1,0:T(8,128)(2,1)}, bf16[2,256,256]{2,1,0:T(8,128)(2,1)S(1)}, u32[]{:S(2)}, u32[]{:S(2)}) collective-permute-start(bf16[2,256,256]{2,1,0:T(8,128)(2,1)} %get-tuple-element.142.kv2), channel_id=1, source_target_pairs={{0,8},{8,16},{16,24},{1,9},{9,17},{17,25},{2,10},{10,18},{18,26},{... | collective-permute-start | bytes 786440 | tf_op jit(solution)/shard_map/ppermute | solution.py:1035
  79.0 59.5 %copy-start.34 = (f32[128,1152]{1,0:T(8,128)}, f32[128,1152]{1,0:T(8,128)S(1)}, u32[]{:S(2)}) copy-start(f32[128,1152]{1,0:T(8,128)S(1)} %get-tuple-element.161.residual.h_residual) | copy-start | bytes 1769476
  79.0 16.0 %collective-permute-start.17 = (bf16[128,1152]{1,0:T(8,128)(2,1)S(1)}, bf16[128,1152]{1,0:T(8,128)(2,1)S(1)}, u32[]{:S(2)}, u32[]{:S(2)}) collective-permute-start(bf16[128,1152]{1,0:T(8,128)(2,1)S(1)} %get-tuple-element.146.x0), channel_id=1, source_target_pairs={{0,16},{8,24},{16,0},{24,8},{1,17},{9,25},{17,1},{25,9},{2,18},{10... | collective-permute-start | bytes 884744 | tf_op jit(solution)/shard_map/ppermute | solution.py:1051
  85.4 18.3 %collective-permute-start.19 = (bf16[144,1728]{1,0:T(8,128)(2,1)S(1)}, bf16[144,1728]{1,0:T(8,128)(2,1)S(1)}, u32[]{:S(2)}, u32[]{:S(2)}) collective-permute-start(bf16[144,1728]{1,0:T(8,128)(2,1)S(1)} %collective-permute-done.18.refs_3_), channel_id=1, source_target_pairs={{0,8},{8,0},{16,24},{24,16},{1,9},{9,1},{17,25},{25,17},{2,10},{10... | collective-permute-start | bytes 1493000 | tf_op jit(solution)/shard_map/ppermute | solution.py:1051
  87.0 21.1 %collective-permute-start.25 = (bf16[432,1152]{1,0:T(8,128)(2,1)}, bf16[432,1152]{1,0:T(8,128)(2,1)S(1)}, u32[]{:S(2)}, u32[]{:S(2)}) collective-permute-start(bf16[432,1152]{1,0:T(8,128)(2,1)} %collective-permute-done.24.refs_11_.w1), channel_id=1, source_target_pairs={{0,1},{1,0},{2,3},{3,2},{4,5},{5,4},{6,7},{7,6},{8,9},{9,8},{10,11... | collective-permute-start | bytes 2985992 | tf_op jit(solution)/shard_map/ppermute | solution.py:1039
  87.0 9.5 %collective-permute-start.13 = (bf16[128,1152]{1,0:T(8,128)(2,1)S(1)}, bf16[128,1152]{1,0:T(8,128)(2,1)S(1)}, u32[]{:S(2)}, u32[]{:S(2)}) collective-permute-start(bf16[128,1152]{1,0:T(8,128)(2,1)S(1)} %get-tuple-element.146.x0), channel_id=1, source_target_pairs={{0,2},{2,0},{1,3},{3,1},{4,6},{6,4},{5,7},{7,5},{8,10},{10,8},{9,1... | collective-permute-start | bytes 884744 | tf_op jit(solution)/shard_map/ppermute | solution.py:1039
  87.6 9.1 %collective-permute-start.14 = (bf16[128,1152]{1,0:T(8,128)(2,1)S(1)}, bf16[128,1152]{1,0:T(8,128)(2,1)S(1)}, u32[]{:S(2)}, u32[]{:S(2)}) collective-permute-start(bf16[128,1152]{1,0:T(8,128)(2,1)S(1)} %get-tuple-element.146.x0), channel_id=1, source_target_pairs={{0,4},{4,0},{1,5},{5,1},{2,6},{6,2},{3,7},{7,3},{8,12},{12,8},{9,1... | collective-permute-start | bytes 884744 | tf_op jit(solution)/shard_map/ppermute | solution.py:1039
  95.0 8.7 %collective-permute-start.15 = (bf16[128,1152]{1,0:T(8,128)(2,1)S(1)}, bf16[128,1152]{1,0:T(8,128)(2,1)S(1)}, u32[]{:S(2)}, u32[]{:S(2)}) collective-permute-start(bf16[128,1152]{1,0:T(8,128)(2,1)S(1)} %get-tuple-element.146.x0), channel_id=1, source_target_pairs={{0,6},{2,4},{4,2},{6,0},{1,7},{3,5},{5,3},{7,1},{8,14},{10,12},{12... | collective-permute-start | bytes 884744 | tf_op jit(solution)/shard_map/ppermute | solution.py:1043
  96.5 7.7 %collective-permute-start.20 = (bf16[144,1728]{1,0:T(8,128)(2,1)}, bf16[144,1728]{1,0:T(8,128)(2,1)S(1)}, u32[]{:S(2)}, u32[]{:S(2)}) collective-permute-start(bf16[144,1728]{1,0:T(8,128)(2,1)} %collective-permute-done.6.refs_2_), channel_id=1, source_target_pairs={{0,1},{1,0},{2,3},{3,2},{4,5},{5,4},{6,7},{7,6},{8,9},{9,8},{10,11... | collective-permute-start | bytes 1493000 | tf_op jit(solution)/shard_map/ppermute | solution.py:1039
  96.7 8.4 %collective-permute-start.22 = (bf16[144,1728]{1,0:T(8,128)(2,1)S(1)}, bf16[144,1728]{1,0:T(8,128)(2,1)S(1)}, u32[]{:S(2)}, u32[]{:S(2)}) collective-permute-start(bf16[144,1728]{1,0:T(8,128)(2,1)S(1)} %collective-permute-done.16.refs_4_), channel_id=1, source_target_pairs={{0,1},{1,0},{2,3},{3,2},{4,5},{5,4},{6,7},{7,6},{8,9},{9,8},{10,11... | collective-permute-start | bytes 1493000 | tf_op jit(solution)/shard_map/ppermute | solution.py:1039
  103.7 2.9 collective-permute-start.21
  103.7 4.4 %collective-permute-start.23 = (bf16[144,1728]{1,0:T(8,128)(2,1)S(1)}, bf16[144,1728]{1,0:T(8,128)(2,1)S(1)}, u32[]{:S(2)}, u32[]{:S(2)}) collective-permute-start(bf16[144,1728]{1,0:T(8,128)(2,1)S(1)} %collective-permute-done.19.refs_5_), channel_id=1, source_target_pairs={{0,1},{1,0},{2,3},{3,2},{4,5},{5,4},{6,7},{7,6},{8,9},{9,8},{10,11... | collective-permute-start | bytes 1493000 | tf_op jit(solution)/shard_map/ppermute | solution.py:1039
  104.2 18.6 %collective-permute-start.26 = (bf16[128,1152]{1,0:T(8,128)(2,1)S(1)}, bf16[128,1152]{1,0:T(8,128)(2,1)S(1)}, u32[]{:S(2)}, u32[]{:S(2)}) collective-permute-start(bf16[128,1152]{1,0:T(8,128)(2,1)S(1)} %collective-permute-done.17.n0), channel_id=1, source_target_pairs={{0,2},{2,0},{1,3},{3,1},{4,6},{6,4},{5,7},{7,5},{8,10},{10,8},{9,1... | collective-permute-start | bytes 884744 | tf_op jit(solution)/shard_map/ppermute | solution.py:1039
  105.1 17.7 %collective-permute-start.27 = (bf16[128,1152]{1,0:T(8,128)(2,1)S(1)}, bf16[128,1152]{1,0:T(8,128)(2,1)S(1)}, u32[]{:S(2)}, u32[]{:S(2)}) collective-permute-start(bf16[128,1152]{1,0:T(8,128)(2,1)S(1)} %collective-permute-done.17.n0), channel_id=1, source_target_pairs={{0,4},{4,0},{1,5},{5,1},{2,6},{6,2},{3,7},{7,3},{8,12},{12,8},{9,1... | collective-permute-start | bytes 884744 | tf_op jit(solution)/shard_map/ppermute | solution.py:1039
  106.6 16.2 %collective-permute-start.28 = (bf16[128,1152]{1,0:T(8,128)(2,1)S(1)}, bf16[128,1152]{1,0:T(8,128)(2,1)S(1)}, u32[]{:S(2)}, u32[]{:S(2)}) collective-permute-start(bf16[128,1152]{1,0:T(8,128)(2,1)S(1)} %collective-permute-done.17.n0), channel_id=1, source_target_pairs={{0,6},{2,4},{4,2},{6,0},{1,7},{3,5},{5,3},{7,1},{8,14},{10,12},{12... | collective-permute-start | bytes 884744 | tf_op jit(solution)/shard_map/ppermute | solution.py:1043
  122.9 10.0 %collective-permute-start.29 = (bf16[128,1152]{1,0:T(8,128)(2,1)S(1)}, bf16[128,1152]{1,0:T(8,128)(2,1)S(1)}, u32[]{:S(2)}, u32[]{:S(2)}) collective-permute-start(bf16[128,1152]{1,0:T(8,128)(2,1)S(1)} %get-tuple-element.158), channel_id=1, source_target_pairs={{0,2},{2,0},{1,3},{3,1},{4,6},{6,4},{5,7},{7,5},{8,10},{10,8},{9,1... | collective-permute-start | bytes 884744 | tf_op jit(solution)/shard_map/ppermute | solution.py:1039
  123.4 9.5 %collective-permute-start.30 = (bf16[128,1152]{1,0:T(8,128)(2,1)S(1)}, bf16[128,1152]{1,0:T(8,128)(2,1)S(1)}, u32[]{:S(2)}, u32[]{:S(2)}) collective-permute-start(bf16[128,1152]{1,0:T(8,128)(2,1)S(1)} %get-tuple-element.159), channel_id=1, source_target_pairs={{0,4},{4,0},{1,5},{5,1},{2,6},{6,2},{3,7},{7,3},{8,12},{12,8},{9,1... | collective-permute-start | bytes 884744 | tf_op jit(solution)/shard_map/ppermute | solution.py:1039
  124.9 13.5 %collective-permute-start.31 = (bf16[128,1152]{1,0:T(8,128)(2,1)S(1)}, bf16[128,1152]{1,0:T(8,128)(2,1)S(1)}, u32[]{:S(2)}, u32[]{:S(2)}) collective-permute-start(bf16[128,1152]{1,0:T(8,128)(2,1)S(1)} %get-tuple-element.160), channel_id=1, source_target_pairs={{0,6},{2,4},{4,2},{6,0},{1,7},{3,5},{5,3},{7,1},{8,14},{10,12},{12... | collective-permute-start | bytes 884744 | tf_op jit(solution)/shard_map/ppermute | solution.py:1043
  140.6 21.5 %collective-permute-start.32 = (bf16[128,1152]{1,0:T(8,128)(2,1)S(1)}, bf16[128,1152]{1,0:T(8,128)(2,1)S(1)}, u32[]{:S(2)}, u32[]{:S(2)}) collective-permute-start(bf16[128,1152]{1,0:T(8,128)(2,1)S(1)} %get-tuple-element.172.x0), channel_id=1, source_target_pairs={{0,2},{2,0},{1,3},{3,1},{4,6},{6,4},{5,7},{7,5},{8,10},{10,8},{9,1... | collective-permute-start | bytes 884744 | tf_op jit(solution)/shard_map/ppermute | solution.py:1039
  141.9 20.2 %collective-permute-start.33 = (bf16[128,1152]{1,0:T(8,128)(2,1)S(1)}, bf16[128,1152]{1,0:T(8,128)(2,1)S(1)}, u32[]{:S(2)}, u32[]{:S(2)}) collective-permute-start(bf16[128,1152]{1,0:T(8,128)(2,1)S(1)} %get-tuple-element.172.x0), channel_id=1, source_target_pairs={{0,4},{4,0},{1,5},{5,1},{2,6},{6,2},{3,7},{7,3},{8,12},{12,8},{9,1... | collective-permute-start | bytes 884744 | tf_op jit(solution)/shard_map/ppermute | solution.py:1039
  142.9 19.2 %collective-permute-start.34 = (bf16[128,1152]{1,0:T(8,128)(2,1)S(1)}, bf16[128,1152]{1,0:T(8,128)(2,1)S(1)}, u32[]{:S(2)}, u32[]{:S(2)}) collective-permute-start(bf16[128,1152]{1,0:T(8,128)(2,1)S(1)} %get-tuple-element.172.x0), channel_id=1, source_target_pairs={{0,6},{2,4},{4,2},{6,0},{1,7},{3,5},{5,3},{7,1},{8,14},{10,12},{12... | collective-permute-start | bytes 884744 | tf_op jit(solution)/shard_map/ppermute | solution.py:1043
  144.1 18.0 %collective-permute-start.35 = (bf16[128,1152]{1,0:T(8,128)(2,1)S(1)}, bf16[128,1152]{1,0:T(8,128)(2,1)S(1)}, u32[]{:S(2)}, u32[]{:S(2)}) collective-permute-start(bf16[128,1152]{1,0:T(8,128)(2,1)S(1)} %get-tuple-element.172.x0), channel_id=1, source_target_pairs={{0,16},{8,24},{16,0},{24,8},{1,17},{9,25},{17,1},{25,9},{2,18},{10... | collective-permute-start | bytes 884744 | tf_op jit(solution)/shard_map/ppermute | solution.py:1051
  162.1 18.5 %collective-permute-start.36 = (bf16[128,1152]{1,0:T(8,128)(2,1)S(1)}, bf16[128,1152]{1,0:T(8,128)(2,1)S(1)}, u32[]{:S(2)}, u32[]{:S(2)}) collective-permute-start(bf16[128,1152]{1,0:T(8,128)(2,1)S(1)} %collective-permute-done.35.d0), channel_id=1, source_target_pairs={{0,2},{2,0},{1,3},{3,1},{4,6},{6,4},{5,7},{7,5},{8,10},{10,8},{9,1... | collective-permute-start | bytes 884744 | tf_op jit(solution)/shard_map/ppermute | solution.py:1039
  163.5 17.1 %collective-permute-start.37 = (bf16[128,1152]{1,0:T(8,128)(2,1)S(1)}, bf16[128,1152]{1,0:T(8,128)(2,1)S(1)}, u32[]{:S(2)}, u32[]{:S(2)}) collective-permute-start(bf16[128,1152]{1,0:T(8,128)(2,1)S(1)} %collective-permute-done.35.d0), channel_id=1, source_target_pairs={{0,4},{4,0},{1,5},{5,1},{2,6},{6,2},{3,7},{7,3},{8,12},{12,8},{9,1... | collective-permute-start | bytes 884744 | tf_op jit(solution)/shard_map/ppermute | solution.py:1039
  164.5 16.1 %collective-permute-start.38 = (bf16[128,1152]{1,0:T(8,128)(2,1)S(1)}, bf16[128,1152]{1,0:T(8,128)(2,1)S(1)}, u32[]{:S(2)}, u32[]{:S(2)}) collective-permute-start(bf16[128,1152]{1,0:T(8,128)(2,1)S(1)} %collective-permute-done.35.d0), channel_id=1, source_target_pairs={{0,6},{2,4},{4,2},{6,0},{1,7},{3,5},{5,3},{7,1},{8,14},{10,12},{12... | collective-permute-start | bytes 884744 | tf_op jit(solution)/shard_map/ppermute | solution.py:1043
  180.6 21.0 %collective-permute-start.39 = (bf16[128,1152]{1,0:T(8,128)(2,1)S(1)}, bf16[128,1152]{1,0:T(8,128)(2,1)S(1)}, u32[]{:S(2)}, u32[]{:S(2)}) collective-permute-start(bf16[128,1152]{1,0:T(8,128)(2,1)S(1)} %get-tuple-element.182), channel_id=1, source_target_pairs={{0,2},{2,0},{1,3},{3,1},{4,6},{6,4},{5,7},{7,5},{8,10},{10,8},{9,1... | collective-permute-start | bytes 884744 | tf_op jit(solution)/shard_map/ppermute | solution.py:1039
  182.0 19.6 %collective-permute-start.40 = (bf16[128,1152]{1,0:T(8,128)(2,1)S(1)}, bf16[128,1152]{1,0:T(8,128)(2,1)S(1)}, u32[]{:S(2)}, u32[]{:S(2)}) collective-permute-start(bf16[128,1152]{1,0:T(8,128)(2,1)S(1)} %get-tuple-element.183), channel_id=1, source_target_pairs={{0,4},{4,0},{1,5},{5,1},{2,6},{6,2},{3,7},{7,3},{8,12},{12,8},{9,1... | collective-permute-start | bytes 884744 | tf_op jit(solution)/shard_map/ppermute | solution.py:1039
  183.0 18.7 %collective-permute-start.41 = (bf16[128,1152]{1,0:T(8,128)(2,1)S(1)}, bf16[128,1152]{1,0:T(8,128)(2,1)S(1)}, u32[]{:S(2)}, u32[]{:S(2)}) collective-permute-start(bf16[128,1152]{1,0:T(8,128)(2,1)S(1)} %get-tuple-element.184), channel_id=1, source_target_pairs={{0,6},{2,4},{4,2},{6,0},{1,7},{3,5},{5,3},{7,1},{8,14},{10,12},{12... | collective-permute-start | bytes 884744 | tf_op jit(solution)/shard_map/ppermute | solution.py:1043
  201.7 18.5 %collective-permute-start.42 = (bf16[2,432,1792]{2,1,0:T(8,128)(2,1)}, bf16[2,432,1792]{2,1,0:T(8,128)(2,1)}, u32[]{:S(2)}, u32[]{:S(2)}) collective-permute-start(bf16[2,432,1792]{2,1,0:T(8,128)(2,1)} %get-tuple-element.202), channel_id=1, source_target_pairs={{0,1},{1,0},{2,3},{3,2},{4,5},{5,4},{6,7},{7,6},{8,9},{9,8},{10,11... | collective-permute-start | bytes 9289736 | tf_op jit(solution)/shard_map/ppermute | solution.py:1039
  211.9 20.8 %collective-permute-start.47 = (bf16[128,1024]{1,0:T(8,128)(2,1)S(1)}, bf16[128,1024]{1,0:T(8,128)(2,1)S(1)}, u32[]{:S(2)}, u32[]{:S(2)}) collective-permute-start(bf16[128,1024]{1,0:T(8,128)(2,1)S(1)} %get-tuple-element.215.own_heads), channel_id=1, source_target_pairs={{0,4},{4,0},{1,5},{5,1},{2,6},{6,2},{3,7},{7,3},{8,12},{12,8},{9,1... | collective-permute-start | bytes 786440 | tf_op jit(solution)/shard_map/ppermute | solution.py:1039
  213.0 19.5 %collective-permute-start.43 = (bf16[2,256,256]{2,1,0:T(8,128)(2,1)}, bf16[2,256,256]{2,1,0:T(8,128)(2,1)S(1)}, u32[]{:S(2)}, u32[]{:S(2)}) collective-permute-start(bf16[2,256,256]{2,1,0:T(8,128)(2,1)} %get-tuple-element.205), channel_id=1, source_target_pairs={{16,0},{24,8},{17,1},{25,9},{18,2},{26,10},{19,3},{27,11},{20,4},{... | collective-permute-start | bytes 786440 | tf_op jit(solution)/shard_map/ppermute | solution.py:1035
  214.3 18.2 %collective-permute-start.44 = (bf16[2,256,256]{2,1,0:T(8,128)(2,1)}, bf16[2,256,256]{2,1,0:T(8,128)(2,1)S(1)}, u32[]{:S(2)}, u32[]{:S(2)}) collective-permute-start(bf16[2,256,256]{2,1,0:T(8,128)(2,1)} %get-tuple-element.206), channel_id=1, source_target_pairs={{8,0},{16,8},{24,16},{9,1},{17,9},{25,17},{10,2},{18,10},{26,18},{... | collective-permute-start | bytes 786440 | tf_op jit(solution)/shard_map/ppermute | solution.py:1035
  215.6 16.9 %collective-permute-start.45 = (bf16[2,256,256]{2,1,0:T(8,128)(2,1)}, bf16[2,256,256]{2,1,0:T(8,128)(2,1)S(1)}, u32[]{:S(2)}, u32[]{:S(2)}) collective-permute-start(bf16[2,256,256]{2,1,0:T(8,128)(2,1)} %get-tuple-element.207), channel_id=1, source_target_pairs={{0,8},{8,16},{16,24},{1,9},{9,17},{17,25},{2,10},{10,18},{18,26},{... | collective-permute-start | bytes 786440 | tf_op jit(solution)/shard_map/ppermute | solution.py:1035
  220.2 12.5 %collective-permute-start.46 = (bf16[128,960]{1,0:T(8,128)(2,1)}, bf16[128,960]{1,0:T(8,128)(2,1)S(1)}, u32[]{:S(2)}, u32[]{:S(2)}) collective-permute-start(bf16[128,960]{1,0:T(8,128)(2,1)} %get-tuple-element.213), channel_id=1, source_target_pairs={{0,4},{4,0},{1,5},{5,1},{2,6},{6,2},{3,7},{7,3},{8,12},{12,8},{9,1... | collective-permute-start | bytes 737288 | tf_op jit(solution)/shard_map/ppermute | solution.py:1039
  236.3 3.5 %collective-permute-start.48 = (bf16[2,288,896]{2,1,0:T(8,128)(2,1)S(1)}, bf16[2,288,896]{2,1,0:T(8,128)(2,1)S(1)}, u32[]{:S(2)}, u32[]{:S(2)}) collective-permute-start(bf16[2,288,896]{2,1,0:T(8,128)(2,1)S(1)} %get-tuple-element.222), channel_id=1, source_target_pairs={{0,1},{1,0},{2,3},{3,2},{4,5},{5,4},{6,7},{7,6},{8,9},{9,8},{10,11... | collective-permute-start | bytes 3096584 | tf_op jit(solution)/shard_map/ppermute | solution.py:1039
  236.3 15.2 %collective-permute-start.51 = (bf16[288,864]{1,0:T(8,128)(2,1)}, bf16[288,864]{1,0:T(8,128)(2,1)S(1)}, u32[]{:S(2)}, u32[]{:S(2)}) collective-permute-start(bf16[288,864]{1,0:T(8,128)(2,1)} %copy-done.16), channel_id=1, source_target_pairs={{0,8},{8,0},{16,24},{24,16},{1,9},{9,1},{17,25},{25,17},{2,10},{10... | collective-permute-start | bytes 1493000 | tf_op jit(solution)/shard_map/ppermute | solution.py:1051
  238.7 5.7 %collective-permute-start.49 = (bf16[2,128,256]{2,1,0:T(8,128)(2,1)S(1)}, bf16[2,128,256]{2,1,0:T(8,128)(2,1)S(1)}, u32[]{:S(2)}, u32[]{:S(2)}) collective-permute-start(bf16[2,128,256]{2,1,0:T(8,128)(2,1)S(1)} %dynamic-slice_convert_fusion), channel_id=1, source_target_pairs={{0,4},{4,0},{1,5},{5,1},{2,6},{6,2},{3,7},{7,3},{8,12},{12,8},{9,1... | collective-permute-start | bytes 393224 | tf_op jit(solution)/shard_map/ppermute | solution.py:1039
  248.1 4.8 %collective-permute-start.52 = (bf16[144,384]{1,0:T(8,128)(2,1)S(1)}, bf16[144,384]{1,0:T(8,128)(2,1)S(1)}, u32[]{:S(2)}, u32[]{:S(2)}) collective-permute-start(bf16[144,384]{1,0:T(8,128)(2,1)S(1)} %get-tuple-element.236), channel_id=1, source_target_pairs={{0,4},{4,0},{1,5},{5,1},{2,6},{6,2},{3,7},{7,3},{8,12},{12,8},{9,1... | collective-permute-start | bytes 331784 | tf_op jit(solution)/shard_map/ppermute | solution.py:1039
  249.2 12.8 %collective-permute-start.53 = (bf16[216,1152]{1,0:T(8,128)(2,1)S(1)}, bf16[216,1152]{1,0:T(8,128)(2,1)S(1)}, u32[]{:S(2)}, u32[]{:S(2)}) collective-permute-start(bf16[216,1152]{1,0:T(8,128)(2,1)S(1)} %copy-done.20), channel_id=1, source_target_pairs={{0,8},{8,0},{16,24},{24,16},{1,9},{9,1},{17,25},{25,17},{2,10},{10... | collective-permute-start | bytes 1493000 | tf_op jit(solution)/shard_map/ppermute | solution.py:1051
  254.1 7.8 %collective-permute-start.54 = (bf16[592,384]{1,0:T(8,128)(2,1)S(1)}, bf16[592,384]{1,0:T(8,128)(2,1)S(1)}, u32[]{:S(2)}, u32[]{:S(2)}) collective-permute-start(bf16[592,384]{1,0:T(8,128)(2,1)S(1)} %get-tuple-element.241), channel_id=1, source_target_pairs={{0,1},{1,0},{2,3},{3,2},{4,5},{5,4},{6,7},{7,6},{8,9},{9,8},{10,11... | collective-permute-start | bytes 1363976 | tf_op jit(solution)/shard_map/ppermute | solution.py:1039
  254.2 16.7 %collective-permute-start.50 = (bf16[288,896]{1,0:T(8,128)(2,1)S(1)}, bf16[288,896]{1,0:T(8,128)(2,1)S(1)}, u32[]{:S(2)}, u32[]{:S(2)}) collective-permute-start(bf16[288,896]{1,0:T(8,128)(2,1)S(1)} %get-tuple-element.223), channel_id=1, source_target_pairs={{0,2},{2,0},{1,3},{3,1},{4,6},{6,4},{5,7},{7,5},{8,10},{10,8},{9,1... | collective-permute-start | bytes 1548296 | tf_op jit(solution)/shard_map/ppermute | solution.py:1039
  263.3 10.6 %collective-permute-start.55 = (bf16[304,384]{1,0:T(8,128)(2,1)}, bf16[304,384]{1,0:T(8,128)(2,1)S(1)}, u32[]{:S(2)}, u32[]{:S(2)}) collective-permute-start(bf16[304,384]{1,0:T(8,128)(2,1)} %get-tuple-element.244), channel_id=1, source_target_pairs={{0,2},{2,0},{1,3},{3,1},{4,6},{6,4},{5,7},{7,5},{8,10},{10,8},{9,1... | collective-permute-start | bytes 700424 | tf_op jit(solution)/shard_map/ppermute | solution.py:1039
  264.6 12.8 %collective-permute-start.56 = (bf16[216,1152]{1,0:T(8,128)(2,1)S(1)}, bf16[216,1152]{1,0:T(8,128)(2,1)S(1)}, u32[]{:S(2)}, u32[]{:S(2)}) collective-permute-start(bf16[216,1152]{1,0:T(8,128)(2,1)S(1)} %copy-done.18), channel_id=1, source_target_pairs={{0,8},{8,0},{16,24},{24,16},{1,9},{9,1},{17,25},{25,17},{2,10},{10... | collective-permute-start | bytes 1493000 | tf_op jit(solution)/shard_map/ppermute | solution.py:1051
  267.4 12.4 %all-to-all-start.1 = ((bf16[4,144,432]{2,1,0:T(8,128)(2,1)}), bf16[4,144,432]{2,1,0:T(8,128)(2,1)S(1)}, u32[]{:S(2)}, u32[]{:S(2)}) async-start(bf16[4,144,432]{2,1,0:T(8,128)(2,1)} %bitcast.45), calls=%async_computation.1 | async-start | bytes 1179648 | tf_op jit(solution)/shard_map/all_to_all | solution.py:1200
  279.8 24.3 %all-to-all-start = ((bf16[4,384,256]{2,1,0:T(8,128)(2,1)}), bf16[4,384,256]{2,1,0:T(8,128)(2,1)S(1)}, u32[]{:S(2)}, u32[]{:S(2)}) async-start(bf16[4,384,256]{2,1,0:T(8,128)(2,1)} %shard_map.254), calls=%async_computation | async-start | bytes 1572864 | tf_op jit(solution)/shard_map/all_to_all | solution.py:1205
  286.2 14.0 %collective-permute-start.57 = (bf16[2,288,432]{2,1,0:T(8,128)(2,1)S(1)}, bf16[2,288,432]{2,1,0:T(8,128)(2,1)S(1)}, u32[]{:S(2)}, u32[]{:S(2)}) collective-permute-start(bf16[2,288,432]{2,1,0:T(8,128)(2,1)S(1)} %shard_map.257), channel_id=1, source_target_pairs={{0,2},{2,0},{1,3},{3,1},{4,6},{6,4},{5,7},{7,5},{8,10},{10,8},{9,1... | collective-permute-start | bytes 1493000 | tf_op jit(solution)/shard_map/ppermute | solution.py:1039
  290.2 11.3 %collective-permute-start.58 = (bf16[288,432]{1,0:T(8,128)(2,1)S(1)}, bf16[288,432]{1,0:T(8,128)(2,1)S(1)}, u32[]{:S(2)}, u32[]{:S(2)}) collective-permute-start(bf16[288,432]{1,0:T(8,128)(2,1)S(1)} %get-tuple-element.265), channel_id=1, source_target_pairs={{0,1},{1,0},{2,3},{3,2},{4,5},{5,4},{6,7},{7,6},{8,9},{9,8},{10,11... | collective-permute-start | bytes 746504 | tf_op jit(solution)/shard_map/ppermute | solution.py:1039
  300.3 1.6 collective-permute-start.59
  (71 other events, 573.4 us)
